TPU v7x, 32 devices: a whole 2x2x4 slice. The times are simulated.
32 devices in a mesh: seq: 8 (over z, y), rep: 2 (over x), own: 2 (over core).
Axes of the slice: x: 2, y: 2, z: 4, core: 2. Of those that a mesh axis runs over, the one named last changes fastest.
Arguments:
- latent: bfloat16 [4096, 8, 1280], P('seq', ('rep', 'own')), may hold values from -40 to 40
- cotangent: bfloat16 [4096, 8, 1280], P('seq', ('rep', 'own')), may hold values from -16 to 16
- norm_gain: float32 [1280], replicated, may hold values from 0.1 to 1.9
- norm_shift: float32 [1280], replicated, may hold values from -3 to 3
- proj_qkv: bfloat16 [1280, 3072], P('own'), may hold values from -1 to 1
- proj_out: bfloat16 [1024, 1280], P('own'), may hold values from -0.1875 to 0.1875
Outputs:
- mixed: bfloat16 [4096, 8, 1280], P('seq', ('rep', 'own'))
- grad_latent: bfloat16 [4096, 8, 1280], P('seq', ('rep', 'own'))
- grad_proj_qkv: float32 [1280, 3072], P(('seq', 'rep', 'own'))
- grad_proj_out: float32 [1024, 1280], P(('seq', 'rep', 'own'))
All inputs are finite; a program needn't handle non-finite values.
Results may differ from a plain program's by a relative error of at most 0.0055.
The roundings to bfloat16 on the way count: a program that leaves them out, or rounds other values in their place, can miss the bound.
Values may be sent and summed in bfloat16 or wider, within the bound.
No kernel may reach another device: no remote copies, remote signals or barrier semaphores. Data moves between devices by JAX's collectives and lax.ppermute only.
A program may use at most 192 MiB of HBM per device.

v0:
```python
import jax
import jax.numpy as jnp
from jax import lax
from jax.sharding import PartitionSpec as P

HEADS = 16
HEAD = 64
GROUPS = 32


def shards(latent, cotangent, norm_gain, norm_shift, proj_qkv, proj_out):
    local_len, images, channels = latent.shape
    seq_count = lax.axis_size("seq")
    per_group = channels // GROUPS
    inner_width = HEADS * HEAD
    score_scale = HEAD ** (-0.5)
    total_count = local_len * seq_count * per_group
    full_qkv, full_out = (
        lax.all_gather(proj_qkv, "own", axis=0, tiled=True),
        lax.all_gather(proj_out, "own", axis=0, tiled=True),
    )
    values = latent.astype(jnp.float32)
    grouped = values.reshape(local_len, images, GROUPS, per_group)
    first_sum, second_sum = lax.psum(
        (jnp.sum(grouped, axis=(0, 3)), jnp.sum(grouped * grouped, axis=(0, 3))), "seq"
    )
    group_mean = first_sum / total_count
    inv_std = lax.rsqrt(second_sum / total_count - group_mean * group_mean + 1e-06)
    centred = (grouped - group_mean[None, :, :, None]) * inv_std[None, :, :, None]
    normed = (centred.reshape(local_len, images, channels) * norm_gain + norm_shift).astype(
        jnp.bfloat16
    )
    normed_rows = normed.reshape(local_len * images, channels)
    projected = jnp.dot(normed_rows, full_qkv, preferred_element_type=jnp.float32).astype(
        jnp.bfloat16
    )
    projected = projected.reshape(local_len, images, 3, inner_width)
    query_tok = projected[:, :, 0].reshape(local_len, images * inner_width)
    key_tok = projected[:, :, 1].reshape(local_len, images * inner_width)
    value_tok = projected[:, :, 2].reshape(local_len, images * inner_width)
    query_heads, key_heads, value_heads = (
        lax.all_to_all(query_tok, "seq", split_axis=1, concat_axis=0, tiled=True),
        lax.all_to_all(key_tok, "seq", split_axis=1, concat_axis=0, tiled=True),
        lax.all_to_all(value_tok, "seq", split_axis=1, concat_axis=0, tiled=True),
    )
    full_len, head_cols = query_heads.shape
    pair_count = head_cols // HEAD
    query_heads = query_heads.reshape(full_len, pair_count, HEAD)
    key_heads = key_heads.reshape(full_len, pair_count, HEAD)
    value_heads = value_heads.reshape(full_len, pair_count, HEAD)
    block_len = min(512, full_len)
    block_count = full_len // block_len

    def probabilities(query_block):
        scores = (
            jnp.einsum("qhd,khd->hqk", query_block, key_heads, preferred_element_type=jnp.float32)
            * score_scale
        )
        row_max = jnp.max(scores, axis=-1, keepdims=True)
        weights = jnp.exp(scores - row_max)
        return weights / jnp.sum(weights, axis=-1, keepdims=True)

    def attend_block(query_block):
        probs_low = probabilities(query_block).astype(jnp.bfloat16)
        return jnp.einsum(
            "hqk,khd->qhd", probs_low, value_heads, preferred_element_type=jnp.float32
        ).astype(jnp.bfloat16)

    query_blocks = query_heads.reshape(block_count, block_len, pair_count, HEAD)
    attended_heads = lax.map(attend_block, query_blocks).reshape(full_len, head_cols)
    attended_tok = lax.all_to_all(attended_heads, "seq", split_axis=0, concat_axis=1, tiled=True)
    attended_rows = attended_tok.reshape(local_len * images, inner_width)
    mixed_out = (
        values
        + jnp.dot(attended_rows, full_out, preferred_element_type=jnp.float32).reshape(
            local_len, images, channels
        )
    ).astype(jnp.bfloat16)
    back_qkv, back_out = (full_qkv, full_out)
    grad_rows = cotangent.reshape(local_len * images, channels)
    grad_attended = lax.dot_general(
        grad_rows, back_out, (((1,), (1,)), ((), ())), preferred_element_type=jnp.float32
    ).astype(jnp.bfloat16)
    grad_heads = lax.all_to_all(
        grad_attended.reshape(local_len, images * inner_width),
        "seq",
        split_axis=1,
        concat_axis=0,
        tiled=True,
    )
    grad_blocks = grad_heads.reshape(block_count, block_len, pair_count, HEAD)

    def backward_block(totals, operands):
        query_block, grad_block = operands
        probs_high = probabilities(query_block)
        probs_low = probs_high.astype(jnp.bfloat16)
        dprobs = jnp.einsum(
            "qhd,khd->hqk", grad_block, value_heads, preferred_element_type=jnp.float32
        )
        row_delta = jnp.sum(probs_high * dprobs, axis=-1, keepdims=True)
        dscores = (probs_high * (dprobs - row_delta) * score_scale).astype(jnp.bfloat16)
        grad_query = jnp.einsum(
            "hqk,khd->qhd", dscores, key_heads, preferred_element_type=jnp.float32
        ).astype(jnp.bfloat16)
        key_total = totals[0] + jnp.einsum(
            "hqk,qhd->khd", dscores, query_block, preferred_element_type=jnp.float32
        )
        value_total = totals[1] + jnp.einsum(
            "hqk,qhd->khd", probs_low, grad_block, preferred_element_type=jnp.float32
        )
        return ((key_total, value_total), grad_query)

    zeros_heads = jnp.zeros((full_len, pair_count, HEAD), jnp.float32)
    (key_total, value_total), grad_query = lax.scan(
        backward_block, (zeros_heads, zeros_heads), (query_blocks, grad_blocks)
    )
    grad_query = grad_query.reshape(full_len, head_cols)
    grad_key = key_total.astype(jnp.bfloat16).reshape(full_len, head_cols)
    grad_value = value_total.astype(jnp.bfloat16).reshape(full_len, head_cols)
    query_back, key_back, value_back = (
        lax.all_to_all(grad_query, "seq", split_axis=0, concat_axis=1, tiled=True),
        lax.all_to_all(grad_key, "seq", split_axis=0, concat_axis=1, tiled=True),
        lax.all_to_all(grad_value, "seq", split_axis=0, concat_axis=1, tiled=True),
    )
    grad_projected = jnp.stack(
        [
            query_back.reshape(local_len, images, inner_width),
            key_back.reshape(local_len, images, inner_width),
            value_back.reshape(local_len, images, inner_width),
        ],
        axis=2,
    )
    grad_projected = grad_projected.reshape(local_len * images, 3 * inner_width)
    grad_normed = lax.dot_general(
        grad_projected, back_qkv, (((1,), (1,)), ((), ())), preferred_element_type=jnp.float32
    )
    row_piece = normed_rows
    qkv_summed = lax.psum_scatter(
        lax.dot_general(
            row_piece, grad_projected, (((0,), (0,)), ((), ())), preferred_element_type=jnp.float32
        ),
        ("seq", "rep", "own"),
        scatter_dimension=0,
        tiled=True,
    )
    grad_centred = (grad_normed.reshape(local_len, images, channels) * norm_gain).reshape(
        local_len, images, GROUPS, per_group
    )
    sum_one, sum_two = lax.psum(
        (jnp.sum(grad_centred, axis=(0, 3)), jnp.sum(grad_centred * centred, axis=(0, 3))), "seq"
    )
    mean_one = sum_one / total_count
    mean_two = sum_two / total_count
    grad_values = inv_std[None, :, :, None] * (
        grad_centred - mean_one[None, :, :, None] - centred * mean_two[None, :, :, None]
    )
    grad_latent = (
        cotangent.astype(jnp.float32) + grad_values.reshape(local_len, images, channels)
    ).astype(jnp.bfloat16)
    row_piece = attended_rows
    out_summed = lax.psum_scatter(
        lax.dot_general(
            row_piece, grad_rows, (((0,), (0,)), ((), ())), preferred_element_type=jnp.float32
        ),
        ("seq", "rep", "own"),
        scatter_dimension=0,
        tiled=True,
    )
    return (mixed_out, grad_latent, qkv_summed, out_summed)


def solution(mesh):
    placed = (
        P("seq", ("rep", "own"), None),
        P("seq", ("rep", "own"), None),
        P(),
        P(),
        P("own", None),
        P("own", None),
    )
    return jax.shard_map(
        shards,
        mesh=mesh,
        in_specs=placed,
        out_specs=(
            P("seq", ("rep", "own"), None),
            P("seq", ("rep", "own"), None),
            P(("seq", "rep", "own"), None),
            P(("seq", "rep", "own"), None),
        ),
        check_vma=False,
    )
```

profile of v0, /device:TPU:0, one launch (start us, length us, event | category | flops | bytes accessed | tf_op | source)
XLA Modules:
  0.0 1955.4 jit_solution(17568246394729672420)
XLA Ops:
  10.0 23.1 %all-reduce.1 = (f32[2,32]{1,0:T(2,128)S(1)}, f32[2,32]{1,0:T(2,128)S(1)}) all-reduce(f32[2,32]{1,0:T(2,128)S(1)} %reduce_sum.96, f32[2,32]{1,0:T(2,128)S(1)} %reduce_sum.78), channel_id=1, replica_groups=mesh['seq'=8,'rep'=2,'own'=2] {'seq'}, use_global_device_ids=true, to_apply=%region_5.0 | all-reduce | flops 128 | bytes 1024 | tf_op jit(solution)/shard_map/psum | solution.py:24
  61.4 13.1 convolution_convert_fusion
  74.6 18.6 reshape.112
  93.2 20.9 %fusion.178 = (bf16[512,2,1,1024]{3,2,1,0:T(2,128)(2,1)}, bf16[512,2,1,1024]{3,2,1,0:T(2,128)(2,1)}, bf16[512,2,1,1024]{3,2,1,0:T(2,128)(2,1)}) fusion(bf16[512,2,3,1024]{3,2,1,0:T(4,128)(2,1)} %reshape.112), kind=kLoop, calls=%fused_computation.99 | loop fusion | bytes 12582912 | tf_op jit(solution)/shard_map/slice | solution.py:40
  140.9 34.2 %all-to-all-done.1 = bf16[512,8,256]{0,2,1:T(8,128)(2,1)} async-done(((bf16[512,8,256]{0,2,1:T(8,128)(2,1)}), bf16[512,8,256]{0,2,1:T(8,128)(2,1)}, u32[]{:S(2)}, u32[]{:S(2)}) %all-to-all-start.1) | async-done | bytes 2097184 | tf_op jit(solution)/shard_map/all_to_all | solution.py:43
  190.0 37.1 %all-to-all-done.2 = bf16[512,8,256]{0,2,1:T(8,128)(2,1)} async-done(((bf16[512,8,256]{0,2,1:T(8,128)(2,1)}), bf16[512,8,256]{0,2,1:T(8,128)(2,1)}, u32[]{:S(2)}, u32[]{:S(2)}) %all-to-all-start.2) | async-done | bytes 2097184 | tf_op jit(solution)/shard_map/all_to_all | solution.py:44
  246.1 33.2 %all-to-all-done = bf16[512,8,256]{0,2,1:T(8,128)(2,1)} async-done(((bf16[512,8,256]{0,2,1:T(8,128)(2,1)}), bf16[512,8,256]{0,2,1:T(8,128)(2,1)}, u32[]{:S(2)}, u32[]{:S(2)}) %all-to-all-start) | async-done | bytes 2097184 | tf_op jit(solution)/shard_map/all_to_all | solution.py:42
  280.9 202.2 %while.25 = (s32[]{:T(128)}, bf16[8,512,4,64]{1,3,2,0:T(8,128)(2,1)}, bf16[8,512,4,64]{1,3,2,0:T(8,128)(2,1)}, bf16[4096,4,64]{0,2,1:T(8,128)(2,1)}, bf16[4096,4,64]{0,2,1:T(8,128)(2,1)S(1)}, /*index=5*/s32[]{:T(128)}) while((s32[]{:T(128)}, bf16[8,512,4,64]{1,3,2,0:T(8,128)(2,1)}, bf16[8,512,4,64]{1,3,2,0:T(8,128)(2,1)}, ...), condition=%wide.region_9.10_spmd, body=%wide.region_6.9_spmd.sunk | while | flops 3280087040 | bytes 7095877 | solution.py:70
  292.9 13.6 fusion.235
  318.1 13.6 fusion.235
  343.3 13.6 fusion.235
  368.6 13.6 fusion.235
  393.8 13.6 fusion.235
  419.0 13.6 fusion.235
  444.2 13.6 fusion.235
  469.4 13.6 fusion.235
  489.0 1068.5 %while.26 = (s32[]{:T(128)}, f32[4096,4,64]{0,2,1:T(8,128)}, f32[4096,4,64]{0,2,1:T(8,128)}, bf16[8,512,4,64]{1,3,2,0:T(8,128)(2,1)}, bf16[8,512,4,64]{1,3,2,0:T...) while((s32[]{:T(128)}, f32[4096,4,64]{0,2,1:T(8,128)}, ...), condition=%wide.region_14.15_spmd.clone, body=%wide.region_10.14_spmd.clone.sunk | while | flops 6622959616 | bytes 362335296 | solution.py:114
  489.2 17.4 fusion.250
  506.5 14.0 fusion.249
  520.6 43.0 %fusion.253 = bf16[8,512,4,64]{1,3,2,0:T(8,128)(2,1)} fusion(bf16[8,512,4,64]{1,3,2,0:T(8,128)(2,1)} %get-tuple-element.297, s32[]{:T(128)} %get-tuple-element.294, bf16[4096,4,64]{0,2,1:T(8,128)(2,1)} %get-tuple-element.309, f32[4,512,4096]{2,1,0:T(8,128)} %fusion.249, f32[4,512,4096]{2,1,0:T(8,128)} %get-tuple-element.264, ...), kind=kOutput, calls=%fused_computation.45.clone.1 | convolution fusion | flops 1132599296 | bytes 136593920 | tf_op jit(solution)/shard_map/while/body/eval_jaxpr/hqk,khd->qhd/dot_general | solution.py:102
  563.5 43.4 %fusion.251 = f32[4096,4,64]{0,2,1:T(8,128)} fusion(f32[4,512,4096]{2,1,0:T(8,128)} %fusion.249, f32[4096,4,64]{0,2,1:T(8,128)} %get-tuple-element.295, pred[]{:T(512)S(6)} %compare.3, bf16[8,512,4,64]{1,3,2,0:T(8,128)(2,1)} %get-tuple-element.308, s32[]{:T(128)} %get-tuple-element.294, f32[4,512,4096]{2,1,0:T(8,128)} %get-tuple-element.264, ...), kind=kOutput, calls=%fused_computation.40.clone.1 | convolution fusion | flops 1134565376 | bytes 142885376 | tf_op jit(solution)/shard_map/while/body/eval_jaxpr/hqk,qhd->khd/dot_general | solution.py:105
  607.0 14.0 fusion.252
  621.0 17.3 fusion.250
  638.3 14.0 fusion.249
  652.4 43.0 %fusion.253 = bf16[8,512,4,64]{1,3,2,0:T(8,128)(2,1)} fusion(bf16[8,512,4,64]{1,3,2,0:T(8,128)(2,1)} %get-tuple-element.297, s32[]{:T(128)} %get-tuple-element.294, bf16[4096,4,64]{0,2,1:T(8,128)(2,1)} %get-tuple-element.309, f32[4,512,4096]{2,1,0:T(8,128)} %fusion.249, f32[4,512,4096]{2,1,0:T(8,128)} %get-tuple-element.264, ...), kind=kOutput, calls=%fused_computation.45.clone.1 | convolution fusion | flops 1132599296 | bytes 136593920 | tf_op jit(solution)/shard_map/while/body/eval_jaxpr/hqk,khd->qhd/dot_general | solution.py:102
  695.3 44.6 %fusion.251 = f32[4096,4,64]{0,2,1:T(8,128)} fusion(f32[4,512,4096]{2,1,0:T(8,128)} %fusion.249, f32[4096,4,64]{0,2,1:T(8,128)} %get-tuple-element.295, pred[]{:T(512)S(6)} %compare.3, bf16[8,512,4,64]{1,3,2,0:T(8,128)(2,1)} %get-tuple-element.308, s32[]{:T(128)} %get-tuple-element.294, f32[4,512,4096]{2,1,0:T(8,128)} %get-tuple-element.264, ...), kind=kOutput, calls=%fused_computation.40.clone.1 | convolution fusion | flops 1134565376 | bytes 142885376 | tf_op jit(solution)/shard_map/while/body/eval_jaxpr/hqk,qhd->khd/dot_general | solution.py:105
  740.0 14.7 fusion.252
  754.7 17.3 fusion.250
  772.0 14.0 fusion.249
  786.0 43.0 %fusion.253 = bf16[8,512,4,64]{1,3,2,0:T(8,128)(2,1)} fusion(bf16[8,512,4,64]{1,3,2,0:T(8,128)(2,1)} %get-tuple-element.297, s32[]{:T(128)} %get-tuple-element.294, bf16[4096,4,64]{0,2,1:T(8,128)(2,1)} %get-tuple-element.309, f32[4,512,4096]{2,1,0:T(8,128)} %fusion.249, f32[4,512,4096]{2,1,0:T(8,128)} %get-tuple-element.264, ...), kind=kOutput, calls=%fused_computation.45.clone.1 | convolution fusion | flops 1132599296 | bytes 136593920 | tf_op jit(solution)/shard_map/while/body/eval_jaxpr/hqk,khd->qhd/dot_general | solution.py:102
  829.0 44.7 %fusion.251 = f32[4096,4,64]{0,2,1:T(8,128)} fusion(f32[4,512,4096]{2,1,0:T(8,128)} %fusion.249, f32[4096,4,64]{0,2,1:T(8,128)} %get-tuple-element.295, pred[]{:T(512)S(6)} %compare.3, bf16[8,512,4,64]{1,3,2,0:T(8,128)(2,1)} %get-tuple-element.308, s32[]{:T(128)} %get-tuple-element.294, f32[4,512,4096]{2,1,0:T(8,128)} %get-tuple-element.264, ...), kind=kOutput, calls=%fused_computation.40.clone.1 | convolution fusion | flops 1134565376 | bytes 142885376 | tf_op jit(solution)/shard_map/while/body/eval_jaxpr/hqk,qhd->khd/dot_general | solution.py:105
  873.7 14.7 fusion.252
  888.4 17.3 fusion.250
  905.8 14.0 fusion.249
  919.8 43.0 %fusion.253 = bf16[8,512,4,64]{1,3,2,0:T(8,128)(2,1)} fusion(bf16[8,512,4,64]{1,3,2,0:T(8,128)(2,1)} %get-tuple-element.297, s32[]{:T(128)} %get-tuple-element.294, bf16[4096,4,64]{0,2,1:T(8,128)(2,1)} %get-tuple-element.309, f32[4,512,4096]{2,1,0:T(8,128)} %fusion.249, f32[4,512,4096]{2,1,0:T(8,128)} %get-tuple-element.264, ...), kind=kOutput, calls=%fused_computation.45.clone.1 | convolution fusion | flops 1132599296 | bytes 136593920 | tf_op jit(solution)/shard_map/while/body/eval_jaxpr/hqk,khd->qhd/dot_general | solution.py:102
  962.8 44.7 %fusion.251 = f32[4096,4,64]{0,2,1:T(8,128)} fusion(f32[4,512,4096]{2,1,0:T(8,128)} %fusion.249, f32[4096,4,64]{0,2,1:T(8,128)} %get-tuple-element.295, pred[]{:T(512)S(6)} %compare.3, bf16[8,512,4,64]{1,3,2,0:T(8,128)(2,1)} %get-tuple-element.308, s32[]{:T(128)} %get-tuple-element.294, f32[4,512,4096]{2,1,0:T(8,128)} %get-tuple-element.264, ...), kind=kOutput, calls=%fused_computation.40.clone.1 | convolution fusion | flops 1134565376 | bytes 142885376 | tf_op jit(solution)/shard_map/while/body/eval_jaxpr/hqk,qhd->khd/dot_general | solution.py:105
  1007.5 14.7 fusion.252
  1022.2 17.3 fusion.250
  1039.6 14.0 fusion.249
  1053.6 43.0 %fusion.253 = bf16[8,512,4,64]{1,3,2,0:T(8,128)(2,1)} fusion(bf16[8,512,4,64]{1,3,2,0:T(8,128)(2,1)} %get-tuple-element.297, s32[]{:T(128)} %get-tuple-element.294, bf16[4096,4,64]{0,2,1:T(8,128)(2,1)} %get-tuple-element.309, f32[4,512,4096]{2,1,0:T(8,128)} %fusion.249, f32[4,512,4096]{2,1,0:T(8,128)} %get-tuple-element.264, ...), kind=kOutput, calls=%fused_computation.45.clone.1 | convolution fusion | flops 1132599296 | bytes 136593920 | tf_op jit(solution)/shard_map/while/body/eval_jaxpr/hqk,khd->qhd/dot_general | solution.py:102
  1096.6 44.6 %fusion.251 = f32[4096,4,64]{0,2,1:T(8,128)} fusion(f32[4,512,4096]{2,1,0:T(8,128)} %fusion.249, f32[4096,4,64]{0,2,1:T(8,128)} %get-tuple-element.295, pred[]{:T(512)S(6)} %compare.3, bf16[8,512,4,64]{1,3,2,0:T(8,128)(2,1)} %get-tuple-element.308, s32[]{:T(128)} %get-tuple-element.294, f32[4,512,4096]{2,1,0:T(8,128)} %get-tuple-element.264, ...), kind=kOutput, calls=%fused_computation.40.clone.1 | convolution fusion | flops 1134565376 | bytes 142885376 | tf_op jit(solution)/shard_map/while/body/eval_jaxpr/hqk,qhd->khd/dot_general | solution.py:105
  1141.2 14.7 fusion.252
  1155.9 17.3 fusion.250
  1173.3 14.0 fusion.249
  1187.3 43.0 %fusion.253 = bf16[8,512,4,64]{1,3,2,0:T(8,128)(2,1)} fusion(bf16[8,512,4,64]{1,3,2,0:T(8,128)(2,1)} %get-tuple-element.297, s32[]{:T(128)} %get-tuple-element.294, bf16[4096,4,64]{0,2,1:T(8,128)(2,1)} %get-tuple-element.309, f32[4,512,4096]{2,1,0:T(8,128)} %fusion.249, f32[4,512,4096]{2,1,0:T(8,128)} %get-tuple-element.264, ...), kind=kOutput, calls=%fused_computation.45.clone.1 | convolution fusion | flops 1132599296 | bytes 136593920 | tf_op jit(solution)/shard_map/while/body/eval_jaxpr/hqk,khd->qhd/dot_general | solution.py:102
  1230.3 44.7 %fusion.251 = f32[4096,4,64]{0,2,1:T(8,128)} fusion(f32[4,512,4096]{2,1,0:T(8,128)} %fusion.249, f32[4096,4,64]{0,2,1:T(8,128)} %get-tuple-element.295, pred[]{:T(512)S(6)} %compare.3, bf16[8,512,4,64]{1,3,2,0:T(8,128)(2,1)} %get-tuple-element.308, s32[]{:T(128)} %get-tuple-element.294, f32[4,512,4096]{2,1,0:T(8,128)} %get-tuple-element.264, ...), kind=kOutput, calls=%fused_computation.40.clone.1 | convolution fusion | flops 1134565376 | bytes 142885376 | tf_op jit(solution)/shard_map/while/body/eval_jaxpr/hqk,qhd->khd/dot_general | solution.py:105
  1275.0 14.7 fusion.252
  1289.7 17.3 fusion.250
  1307.0 14.0 fusion.249
  1321.1 43.0 %fusion.253 = bf16[8,512,4,64]{1,3,2,0:T(8,128)(2,1)} fusion(bf16[8,512,4,64]{1,3,2,0:T(8,128)(2,1)} %get-tuple-element.297, s32[]{:T(128)} %get-tuple-element.294, bf16[4096,4,64]{0,2,1:T(8,128)(2,1)} %get-tuple-element.309, f32[4,512,4096]{2,1,0:T(8,128)} %fusion.249, f32[4,512,4096]{2,1,0:T(8,128)} %get-tuple-element.264, ...), kind=kOutput, calls=%fused_computation.45.clone.1 | convolution fusion | flops 1132599296 | bytes 136593920 | tf_op jit(solution)/shard_map/while/body/eval_jaxpr/hqk,khd->qhd/dot_general | solution.py:102
  1364.0 44.6 %fusion.251 = f32[4096,4,64]{0,2,1:T(8,128)} fusion(f32[4,512,4096]{2,1,0:T(8,128)} %fusion.249, f32[4096,4,64]{0,2,1:T(8,128)} %get-tuple-element.295, pred[]{:T(512)S(6)} %compare.3, bf16[8,512,4,64]{1,3,2,0:T(8,128)(2,1)} %get-tuple-element.308, s32[]{:T(128)} %get-tuple-element.294, f32[4,512,4096]{2,1,0:T(8,128)} %get-tuple-element.264, ...), kind=kOutput, calls=%fused_computation.40.clone.1 | convolution fusion | flops 1134565376 | bytes 142885376 | tf_op jit(solution)/shard_map/while/body/eval_jaxpr/hqk,qhd->khd/dot_general | solution.py:105
  1408.7 14.7 fusion.252
  1423.4 17.3 fusion.250
  1440.8 14.0 fusion.249
  1454.8 43.0 %fusion.253 = bf16[8,512,4,64]{1,3,2,0:T(8,128)(2,1)} fusion(bf16[8,512,4,64]{1,3,2,0:T(8,128)(2,1)} %get-tuple-element.297, s32[]{:T(128)} %get-tuple-element.294, bf16[4096,4,64]{0,2,1:T(8,128)(2,1)} %get-tuple-element.309, f32[4,512,4096]{2,1,0:T(8,128)} %fusion.249, f32[4,512,4096]{2,1,0:T(8,128)} %get-tuple-element.264, ...), kind=kOutput, calls=%fused_computation.45.clone.1 | convolution fusion | flops 1132599296 | bytes 136593920 | tf_op jit(solution)/shard_map/while/body/eval_jaxpr/hqk,khd->qhd/dot_general | solution.py:102
  1497.8 44.6 %fusion.251 = f32[4096,4,64]{0,2,1:T(8,128)} fusion(f32[4,512,4096]{2,1,0:T(8,128)} %fusion.249, f32[4096,4,64]{0,2,1:T(8,128)} %get-tuple-element.295, pred[]{:T(512)S(6)} %compare.3, bf16[8,512,4,64]{1,3,2,0:T(8,128)(2,1)} %get-tuple-element.308, s32[]{:T(128)} %get-tuple-element.294, f32[4,512,4096]{2,1,0:T(8,128)} %get-tuple-element.264, ...), kind=kOutput, calls=%fused_computation.40.clone.1 | convolution fusion | flops 1134565376 | bytes 142885376 | tf_op jit(solution)/shard_map/while/body/eval_jaxpr/hqk,qhd->khd/dot_general | solution.py:105
  1542.4 14.7 fusion.252
  1587.9 31.9 %all-to-all-done.6 = bf16[8,512,256]{1,2,0:T(8,128)(2,1)} async-done(((bf16[8,512,256]{1,2,0:T(8,128)(2,1)}), bf16[8,512,256]{1,2,0:T(8,128)(2,1)}, u32[]{:S(2)}, u32[]{:S(2)}) %all-to-all-start.6) | async-done | bytes 2097184 | tf_op jit(solution)/shard_map/all_to_all | solution.py:122
  1619.9 62.1 %all_to_all.128 = bf16[8,512,256]{1,2,0:T(8,128)(2,1)S(1)} all-to-all(bf16[8,512,256]{1,2,0:T(8,128)(2,1)} %copy.100), channel_id=1, replica_groups=mesh['seq'=8,'rep'=2,'own'=2] {'seq'}, dimensions={0} | all-to-all | bytes 4194304 | tf_op jit(solution)/shard_map/all_to_all | solution.py:123
  1681.9 60.8 %all_to_all.129 = bf16[8,512,256]{1,2,0:T(8,128)(2,1)S(1)} all-to-all(bf16[8,512,256]{1,2,0:T(8,128)(2,1)S(1)} %bitcast.179), channel_id=1, replica_groups=mesh['seq'=8,'rep'=2,'own'=2] {'seq'}, dimensions={0} | all-to-all | bytes 4194304 | tf_op jit(solution)/shard_map/all_to_all | solution.py:121
  1747.3 14.4 copy.103
  1784.3 14.5 fusion.167
  1799.1 18.2 all-reduce
  1835.6 113.1 %reduce-scatter.3.cloned.1.call-done = f32[40,3072]{1,0:T(8,128)} async-done(((f32[1280,3072]{1,0:T(8,128)}), f32[40,3072]{1,0:T(8,128)}) %reduce-scatter.3.cloned.1.call-update) | async-done | bytes 491536 | tf_op jit(solution)/shard_map/reduce_scatter | solution.py:138
  (108 shorter events, 267.8 us)
Async XLA Ops:
  7.2 1.7 copy-start
  7.2 26.3 %copy-start.10 = (f32[1280]{0:T(1024)S(1)}, f32[1280]{0:T(1024)}, u32[]{:S(2)}) copy-start(f32[1280]{0:T(1024)} %param.12) | copy-start | bytes 15364
  7.2 26.3 %copy-start.9 = (f32[1280]{0:T(1024)S(1)}, f32[1280]{0:T(1024)}, u32[]{:S(2)}) copy-start(f32[1280]{0:T(1024)} %param.13) | copy-start | bytes 15364
  7.2 38.2 %all-gather.5.cloned.1.call-start = ((), (), s32[]{:S(2)}) async-start(), calls=%async_computation.11 | async-start | bytes 3932160 | tf_op jit(solution)/shard_map/all_gather | solution.py:20
  7.9 53.5 %all-gather.3.cloned.1.call-start = ((), (), s32[]{:S(2)}) async-start(), calls=%async_computation.10 | async-start | bytes 11796480 | tf_op jit(solution)/shard_map/all_gather | solution.py:19
  33.3 3.9 copy-start.5
  33.5 3.7 copy-start.7
  45.3 1.5 copy-start.4
  57.6 66.9 %all-to-all-start.4 = ((bf16[512,8,256]{2,0,1:T(8,128)(2,1)}), bf16[512,8,256]{2,0,1:T(8,128)(2,1)S(1)}, u32[]{:S(2)}, u32[]{:S(2)}) async-start(bf16[512,8,256]{2,0,1:T(8,128)(2,1)} %copy.97), calls=%async_computation.4 | async-start | bytes 4194304 | tf_op jit(solution)/shard_map/all_to_all | solution.py:84
  124.5 50.7 %all-to-all-start.1 = ((bf16[512,8,256]{0,2,1:T(8,128)(2,1)}), bf16[512,8,256]{0,2,1:T(8,128)(2,1)}, u32[]{:S(2)}, u32[]{:S(2)}) async-start(bf16[512,8,256]{0,2,1:T(8,128)(2,1)} %bitcast.6), calls=%async_computation.1 | async-start | bytes 4194304 | tf_op jit(solution)/shard_map/all_to_all | solution.py:43
  175.2 51.9 %all-to-all-start.2 = ((bf16[512,8,256]{0,2,1:T(8,128)(2,1)}), bf16[512,8,256]{0,2,1:T(8,128)(2,1)}, u32[]{:S(2)}, u32[]{:S(2)}) async-start(bf16[512,8,256]{0,2,1:T(8,128)(2,1)} %bitcast.8), calls=%async_computation.2 | async-start | bytes 4194304 | tf_op jit(solution)/shard_map/all_to_all | solution.py:44
  227.1 52.2 %all-to-all-start = ((bf16[512,8,256]{0,2,1:T(8,128)(2,1)}), bf16[512,8,256]{0,2,1:T(8,128)(2,1)}, u32[]{:S(2)}, u32[]{:S(2)}) async-start(bf16[512,8,256]{0,2,1:T(8,128)(2,1)} %bitcast.3), calls=%async_computation | async-start | bytes 4194304 | tf_op jit(solution)/shard_map/all_to_all | solution.py:42
  483.1 1079.8 %all-to-all-start.3 = ((bf16[8,512,256]{1,2,0:T(8,128)(2,1)}), bf16[8,512,256]{1,2,0:T(8,128)(2,1)}, u32[]{:S(2)}, u32[]{:S(2)}) async-start(bf16[8,512,256]{1,2,0:T(8,128)(2,1)} %bitcast.180), calls=%async_computation.3 | async-start | bytes 4194304 | tf_op jit(solution)/shard_map/all_to_all | solution.py:71
  1562.9 57.0 %all-to-all-start.6 = ((bf16[8,512,256]{1,2,0:T(8,128)(2,1)}), bf16[8,512,256]{1,2,0:T(8,128)(2,1)}, u32[]{:S(2)}, u32[]{:S(2)}) async-start(bf16[8,512,256]{1,2,0:T(8,128)(2,1)} %copy.99), calls=%async_computation.6 | async-start | bytes 4194304 | tf_op jit(solution)/shard_map/all_to_all | solution.py:122
  1568.8 266.7 %reduce-scatter.5.cloned.1.call-start = ((), (), s32[]{:S(2)}) async-start(), calls=%async_computation.13 | async-start | bytes 5406720 | tf_op jit(solution)/shard_map/reduce_scatter | solution.py:161
  1582.5 366.1 %reduce-scatter.3.cloned.1.call-start = ((), (), s32[]{:S(2)}) async-start(), calls=%async_computation.12 | async-start | bytes 16220160 | tf_op jit(solution)/shard_map/reduce_scatter | solution.py:138
  1585.9 96.0 %copy-start.2 = (bf16[8,512,4,64]{1,3,2,0:T(8,128)(2,1)S(1)}, bf16[8,512,4,64]{1,3,2,0:T(8,128)(2,1)}, u32[]{:S(2)}) copy-start(bf16[8,512,4,64]{1,3,2,0:T(8,128)(2,1)} %get-tuple-element.76) | copy-start | bytes 6291460
  1761.6 7.6 copy-start.3
  1780.4 3.9 copy-start.1
  1780.4 3.8 copy-start.6
  1780.4 3.8 copy-start.8
  1780.4 3.8 copy-start.11
  1822.4 4.2 copy-start.12
Sparse Core Ops, SparseCore 0:
  9.6 14.0 all-gather.4
  25.2 20.2 all-gather.2
  1582.6 156.9 reduce-scatter.4
  1780.5 168.0 reduce-scatter.2
where the time goes:
time: 1970 us; the launch traced here: 1960 us
  matrix products  1330 us (68%)
  waiting for transfers between devices  251 us (13%)
  blocking collectives  164 us (8%)
  local copies, waits for them, and re-layouts  153 us (8%)
  starting transfers between devices  28.9 us (1%)
    dot_general x8, matrix products, backward_block(): jnp.einsum('hqk,qhd->khd', dscores, query_block, preferred_element_type=j...  356 us
    dot_general x8, matrix products, backward_block(): jnp.einsum('hqk,khd->qhd', dscores, key_heads, preferred_element_type=jnp...  344 us
    sub x16, matrix products, probabilities(): weights = jnp.exp(scores - row_max)  231 us
    dot_general x8, matrix products, backward_block(): jnp.einsum('hqk,qhd->khd', probs_low, grad_block, preferred_element_type=...  117 us
    reduce_scatter x1, waiting for transfers between devices, shards(): lax.psum_scatter(lax.dot_general(row_piece, grad_projected, (((0,), (0,))...  113 us
    dot_general x8, matrix products, backward_block(): jnp.einsum('qhd,khd->hqk', grad_block, value_heads, preferred_element_typ...  112 us
    dot_general x8, matrix products, attend_block(): jnp.einsum('hqk,khd->qhd', probs_low, value_heads, preferred_element_type...  109 us
    all_to_all x1, blocking collectives, shards(): lax.all_to_all(grad_value, 'seq', split_axis=0, concat_axis=1, tiled=True)  62.1 us
  transfers between devices with their start and end apart: 10, of which 5 were waited for; matrix products, arithmetic and copies ran while one was open for 66% of the time, Pallas kernels for 0%

commit v1 on v0

v1 whole, which is shorter than its diff:
```python
import functools
import math
import jax
import jax.numpy as jnp
from jax import lax
from jax.experimental import pallas as pl
from jax.experimental.pallas import tpu as pltpu
from jax.sharding import PartitionSpec as P

HEADS = 16
HEAD = 64
GROUPS = 32
EPS = 1e-06
LOG2E = math.log2(math.e)
PACK = 4 * HEAD
HALF = 2 * HEAD
ALL = ("seq", "rep", "own")
NT = (((1,), (1,)), ((), ()))
NN = (((1,), (0,)), ((), ()))
VMEM = 56 * 2**20


def dot(left, right, dims=NN):
    return lax.dot_general(left, right, dims, preferred_element_type=jnp.float32)


def low(array):
    return array.astype(jnp.bfloat16)


def eight_rows(array, op):
    return op(array.reshape(array.shape[0] // 8, 8, array.shape[1]), axis=0)


def pair_body(bq, kb, me_ref, *refs):
    ins, (o_ref, x_ref, kv_t, s_buf, dp_buf, acc, done) = refs[:-7], refs[-7:]
    length = x_ref.shape[0]
    piece = length // len(ins)
    for j, ref in enumerate(ins):
        x_ref[j * piece : (j + 1) * piece, :] = ref[...].reshape(piece, PACK)
    key_blocks, query_blocks = length // kb, length // bq
    step_len = min(512, length)
    first = lax.broadcasted_iota(jnp.int32, (1, HALF), 1) < HEAD
    zero = jnp.bfloat16(0)

    def prepare(j, carry):
        rows = pl.ds(pl.multiple_of(j * step_len, step_len), step_len)
        kv_t[:, rows] = low(x_ref[rows, 0:HALF].astype(jnp.float32).T)
        acc[rows, :] = jnp.zeros((step_len, HALF), jnp.float32)
        return carry

    lax.fori_loop(0, length // step_len, prepare, 0)

    def query_block(i):
        pair = x_ref[pl.ds(pl.multiple_of(i * bq, bq), bq), HALF:PACK]
        query = jnp.where(first, pair, zero) * jnp.bfloat16(HEAD**-0.5)
        return query, jnp.where(first, zero, pair)

    def score_block(j, query, buf, top):
        keys = slice(j * kb, (j + 1) * kb)
        scores = dot(x_ref[keys, 0:HALF], query, NT)
        s_buf[buf, keys, :] = scores
        return jnp.maximum(top, eight_rows(scores, jnp.max))

    def finish_top(top):
        return jnp.max(top, axis=0, keepdims=True) * LOG2E

    no_top = jnp.full((8, bq), -jnp.inf, jnp.float32)

    def step(i, top):
        buf = lax.rem(i, 2)
        query, grad = query_block(i)
        next_query, _ = query_block(lax.rem(i + 1, query_blocks))
        total = jnp.zeros((8, bq), jnp.float32)
        delta = jnp.zeros((8, bq), jnp.float32)
        for j in range(key_blocks):
            keys = slice(j * kb, (j + 1) * kb)
            dprobs = dot(x_ref[keys, 0:HALF], grad, NT)
            weights = jnp.exp2(s_buf[buf, keys, :] * LOG2E - top)
            s_buf[buf, keys, :] = weights
            dp_buf[keys, :] = dprobs
            total = total + eight_rows(weights, jnp.sum)
            delta = delta + eight_rows(weights * dprobs, jnp.sum)
        inverse = 1.0 / jnp.sum(total, axis=0, keepdims=True)
        delta = jnp.sum(delta, axis=0, keepdims=True) * inverse
        attended = jnp.zeros((HEAD, bq), jnp.float32)
        grad_query = jnp.zeros((HEAD, bq), jnp.float32)
        next_top = no_top
        for j in range(key_blocks):
            keys = slice(j * kb, (j + 1) * kb)
            probs = s_buf[buf, keys, :] * inverse
            probs_low = low(probs)
            dscores = low(probs * (dp_buf[keys, :] - delta))
            attended = attended + dot(kv_t[HEAD:HALF, keys], probs_low)
            grad_query = grad_query + dot(kv_t[0:HEAD, keys], dscores)
            acc[keys, :] += dot(dscores, query) + dot(probs_low, grad)
            next_top = score_block(j, next_query, 1 - buf, next_top)
        both = jnp.concatenate([grad_query * HEAD**-0.5, attended], axis=0)
        done[pl.ds(pl.multiple_of(i * bq, bq), bq), :] = low(both.T)
        return finish_top(next_top)

    top = no_top
    first_query, _ = query_block(0)
    for j in range(key_blocks):
        top = score_block(j, first_query, 0, top)
    lax.fori_loop(0, query_blocks, step, finish_top(top))

    tokens = o_ref.shape[1]
    for j in range(len(ins)):
        for half in range(2):
            rows = slice((2 * j + half) * tokens, (2 * j + half + 1) * tokens)
            owner = me_ref[0] ^ (half * len(ins) + j)
            o_ref[owner, :, 0:HALF] = low(acc[rows, :])
            o_ref[owner, :, HALF:PACK] = done[rows, :]


def attend_pair(pieces, me):
    tokens = pieces[0].shape[1]
    blocks = 2 * len(pieces)
    length = blocks * tokens
    bq, kb = min(256, length), min(256, length)
    vmem = pl.BlockSpec(memory_space=pltpu.VMEM)
    return pl.pallas_call(
        functools.partial(pair_body, bq, kb),
        out_shape=jax.ShapeDtypeStruct((blocks, tokens, PACK), jnp.bfloat16),
        in_specs=[pl.BlockSpec(memory_space=pltpu.SMEM)] + [vmem] * len(pieces),
        out_specs=vmem,
        scratch_shapes=[
            pltpu.VMEM((length, PACK), jnp.bfloat16),
            pltpu.VMEM((HALF, length), jnp.bfloat16),
            pltpu.VMEM((2, length, bq), jnp.float32),
            pltpu.VMEM((length, bq), jnp.float32),
            pltpu.VMEM((length, HALF), jnp.float32),
            pltpu.VMEM((length, HALF), jnp.bfloat16),
        ],
        compiler_params=pltpu.CompilerParams(vmem_limit_bytes=VMEM),
        cost_estimate=pl.CostEstimate(
            flops=6 * 2 * length * length * 256, bytes_accessed=4 * length * PACK, transcendentals=length * length
        ),
        name="attend_pair",
    )(me, *pieces)


def lane_piece(array, head, slot):
    piece = array[:, head * HEAD // HALF * HALF :][:, :HALF]
    return piece if head % 2 == slot % 2 else pltpu.roll(piece, HEAD, 1)


def project_body(count, groups, me_ref, norm_ref, grad_ref, wq_ref, wk_ref, wv_ref, *outs):
    first = lax.broadcasted_iota(jnp.int32, (1, HALF), 1) < HEAD
    width = count * HEAD
    weights = jnp.concatenate([wq_ref[...], wk_ref[...], wv_ref[...]], axis=1)
    projected = dot(norm_ref[0], weights)
    query, key, value = (projected[:, part * width : (part + 1) * width] for part in range(3))
    grad = grad_ref[0].astype(jnp.float32)
    packs = []
    for head in range(count):
        left = jnp.where(first, lane_piece(key, head, 0), lane_piece(value, head, 1))
        right = jnp.where(first, lane_piece(query, head, 0), lane_piece(grad, head, 1))
        packs.append(low(jnp.concatenate([left, right], axis=1)))
    for flip in range(groups):

        @pl.when(pl.program_id(1) == flip)
        def _():
            for head in range(count):
                outs[head * groups + flip][0] = packs[head]


def project(normed, grads, full_qkv, unit, heads, offset, count):
    halves, tokens, channels = normed.shape
    groups = HEADS // heads
    width = count * HEAD
    steps = heads // count
    rows = pl.BlockSpec((1, tokens, channels), lambda i, j, unit: (i, 0, 0))

    def columns(part):
        return pl.BlockSpec(
            (channels, width), lambda i, j, unit: (0, (part * groups + (j ^ unit[0])) * steps + offset // count)
        )

    results = pl.pallas_call(
        functools.partial(project_body, count, groups),
        out_shape=[jax.ShapeDtypeStruct((halves, tokens, PACK), jnp.bfloat16)] * (count * groups),
        grid_spec=pltpu.PrefetchScalarGridSpec(
            num_scalar_prefetch=1,
            grid=(halves, groups),
            in_specs=[
                rows,
                pl.BlockSpec((1, tokens, width), lambda i, j, unit: (i, 0, j ^ unit[0])),
                columns(0),
                columns(1),
                columns(2),
            ],
            out_specs=[pl.BlockSpec((1, tokens, PACK), lambda i, j, unit: (i, 0, 0))] * (count * groups),
        ),
        compiler_params=pltpu.CompilerParams(vmem_limit_bytes=VMEM),
        cost_estimate=pl.CostEstimate(
            flops=2 * halves * tokens * channels * 4 * groups * width, bytes_accessed=2**24, transcendentals=0
        ),
        name="project",
    )(unit, normed, grads, full_qkv, full_qkv, full_qkv)
    return [results[head * groups : (head + 1) * groups] for head in range(count)]


def project_plain(normed, grads, full_qkv, unit, heads, offset, count):
    halves, tokens, channels = normed.shape
    groups = HEADS // heads
    qkv = low(jnp.einsum("itc,cd->itd", normed, full_qkv, preferred_element_type=jnp.float32))
    split = qkv.reshape(halves, tokens, 3, groups, heads, HEAD)[:, :, :, :, offset : offset + count]
    grads = grads.reshape(halves, tokens, 1, groups, count, HEAD)
    packed = jnp.concatenate([split[:, :, 1:3], split[:, :, 0:1], grads], axis=2)
    packed = packed.transpose(4, 3, 0, 1, 2, 5).reshape(count, groups, halves, tokens, PACK)
    packed = jnp.take(packed, jnp.arange(groups) ^ unit[0], axis=1)
    return [[packed[head, flip] for flip in range(groups)] for head in range(count)]


def weight_body(images, norm_ref, cot_ref, *refs):
    grad_refs, o_ref = refs[:images], refs[images]
    grads = jnp.concatenate([ref[0] for ref in grad_refs], axis=0)
    split = lax.broadcasted_iota(jnp.int32, (1, PACK), 1) < 3 * HEAD
    zero = jnp.bfloat16(0)
    o_ref[...] = dot(norm_ref[...], jnp.where(split, grads, zero)) + dot(cot_ref[...], jnp.where(split, zero, grads))


def weight_grads(normed_t, cotangent_t, grads, images):
    channels, rows = normed_t.shape
    groups = grads.shape[0] // images
    tokens = grads.shape[1]
    whole = pl.BlockSpec((channels, rows), lambda g: (0, 0))

    def block(image):
        return pl.BlockSpec((1, tokens, PACK), lambda g: (image * groups + g, 0, 0))

    return pl.pallas_call(
        functools.partial(weight_body, images),
        out_shape=jax.ShapeDtypeStruct((channels, groups * PACK), jnp.float32),
        grid=(groups,),
        in_specs=[whole, whole] + [block(image) for image in range(images)],
        out_specs=pl.BlockSpec((channels, PACK), lambda g: (0, g)),
        compiler_params=pltpu.CompilerParams(vmem_limit_bytes=VMEM),
        cost_estimate=pl.CostEstimate(
            flops=4 * channels * rows * groups * PACK, bytes_accessed=2**23, transcendentals=0
        ),
        name="weight_grads",
    )(normed_t, cotangent_t, *([grads] * images))


def gather_heads(parts, slot):
    first = lax.broadcasted_iota(jnp.int32, (1, HALF), 1) < HEAD
    base = slot // 2 * HALF
    pieces = []
    for even in range(0, len(parts), 2):
        left, right = parts[even][:, base : base + HALF], parts[even + 1][:, base : base + HALF]
        if slot % 2 == 0:
            right = pltpu.roll(right, HEAD, 1)
        else:
            left = pltpu.roll(left, HEAD, 1)
        pieces.append(jnp.where(first, left, right))
    return low(jnp.concatenate(pieces, axis=1))


def back_body(heads, *refs):
    grads, (wq_ref, wk_ref, wv_ref, wo_ref, mix_ref, norm_ref) = refs[:heads], refs[heads:]
    g = pl.program_id(1)
    parts = [ref[0].astype(jnp.float32) for ref in grads]
    back = (
        dot(gather_heads(parts, 2), wq_ref[...], NT)
        + dot(gather_heads(parts, 0), wk_ref[...], NT)
        + dot(gather_heads(parts, 1), wv_ref[...], NT)
    )
    mixed = dot(gather_heads(parts, 3), wo_ref[...])

    @pl.when(g == 0)
    def _():
        norm_ref[0] = back
        mix_ref[0] = mixed

    @pl.when(g > 0)
    def _():
        norm_ref[0] += back
        mix_ref[0] += mixed


def project_back(grads, full_qkv, full_out, images):
    heads = len(grads)
    groups = HEADS // heads
    tokens = grads[0].shape[1]
    channels = full_qkv.shape[0]
    width = heads * HEAD

    def columns(part):
        return pl.BlockSpec((channels, width), lambda i, g: (0, part * groups + g))

    rows = pl.BlockSpec((1, tokens, channels), lambda i, g: (i, 0, 0))
    block = pl.BlockSpec((1, tokens, PACK), lambda i, g: (i * groups + g, 0, 0))
    return pl.pallas_call(
        functools.partial(back_body, heads),
        out_shape=[jax.ShapeDtypeStruct((images, tokens, channels), jnp.float32)] * 2,
        grid=(images, groups),
        in_specs=[block] * heads
        + [columns(0), columns(1), columns(2), pl.BlockSpec((width, channels), lambda i, g: (g, 0))],
        out_specs=[rows, rows],
        compiler_params=pltpu.CompilerParams(vmem_limit_bytes=VMEM),
        cost_estimate=pl.CostEstimate(
            flops=2 * images * tokens * channels * 4 * HEADS * HEAD, bytes_accessed=2**25, transcendentals=0
        ),
        name="project_back",
    )(*grads, full_qkv, full_qkv, full_qkv, full_out)


def project_back_plain(grads, full_qkv, full_out, images):
    heads = len(grads)
    groups = HEADS // heads
    tokens = grads[0].shape[1]
    packed = jnp.stack(grads).reshape(heads, images, groups, tokens, 4, HEAD)
    packed = packed.transpose(1, 3, 4, 2, 0, 5).reshape(images, tokens, 4, HEADS * HEAD)
    key, value, query, attended = (packed[:, :, slot] for slot in range(4))
    stacked = jnp.concatenate([query, key, value], axis=2)
    mixed = jnp.einsum("itd,dc->itc", attended, full_out, preferred_element_type=jnp.float32)
    back = jnp.einsum("itd,cd->itc", stacked, full_qkv, preferred_element_type=jnp.float32)
    return mixed, back


def flipped(array, axis, flip):
    return lax.ppermute(array, axis, [(i, i ^ flip) for i in range(lax.axis_size(axis))])


def sum_near(partial, seq_count):
    rep, own = lax.axis_size("rep"), lax.axis_size("own")
    columns = partial.shape[1]
    cut = partial.reshape(seq_count, rep * own, -1, columns)
    here = lax.axis_index("rep") * own + lax.axis_index("own")
    total = lax.dynamic_index_in_dim(cut, here, 1, keepdims=False)
    for flip in range(1, rep * own):
        sent = low(lax.dynamic_index_in_dim(cut, here ^ flip, 1, keepdims=False))
        total = total + flipped(sent, ("rep", "own"), flip).astype(jnp.float32)
    return low(total)


def sum_far(near):
    pieces = lax.all_to_all(near, "seq", split_axis=0, concat_axis=0, tiled=True)
    return jnp.sum(pieces.astype(jnp.float32), axis=0)


def shards(latent, cotangent, norm_gain, norm_shift, proj_qkv, proj_out):
    tokens, images, channels = latent.shape
    seq_count = lax.axis_size("seq")
    devices = seq_count * lax.axis_size("rep") * lax.axis_size("own")
    per_group = channels // GROUPS
    total_count = tokens * seq_count * per_group
    groups = seq_count // images
    heads = HEADS // groups
    aligned = heads * HEAD % HALF == 0

    full_qkv = lax.all_gather(proj_qkv, "own", axis=0, tiled=True)
    full_out = lax.all_gather(proj_out, "own", axis=0, tiled=True)

    def group_sums(*arrays):
        sums = jnp.stack([jnp.sum(a, axis=1).reshape(images, GROUPS, per_group).sum(axis=2) for a in arrays])
        return lax.psum(sums, "seq") / total_count

    def spread(array):
        return jnp.repeat(array, per_group, axis=1)[:, None, :]

    me = lax.axis_index("seq").astype(jnp.int32).reshape(1)
    unit = me % groups
    image = lax.axis_index("seq") // groups

    def pick(array, index):
        return lax.dynamic_index_in_dim(array, index, 0, keepdims=False)

    def swapped(array):
        return jnp.stack([pick(array, image), flipped(pick(array, 1 - image), "seq", groups)])

    rows = latent.transpose(1, 0, 2)
    cot_rows = cotangent.transpose(1, 0, 2)
    work = swapped(rows).astype(jnp.float32)
    count = 2 if aligned else heads
    offsets = range(0, heads, count)
    grad_parts = []
    for offset in offsets:
        part = full_out.reshape(groups, heads, HEAD, channels)[:, offset : offset + count]
        part = part.reshape(groups * count * HEAD, channels)
        grad_parts.append(swapped(low(jnp.einsum("itc,dc->itd", cot_rows, part, preferred_element_type=jnp.float32))))

    values = rows.astype(jnp.float32)
    group_mean, group_meansq = group_sums(values, values * values)
    group_inv = lax.rsqrt(group_meansq - group_mean * group_mean + EPS)
    mean, inv_std = spread(group_mean), spread(group_inv)
    centred = (values - mean) * inv_std
    normed = low(centred * norm_gain + norm_shift)
    normed_t = normed.reshape(images * tokens, channels).T
    cotangent_t = cot_rows.reshape(images * tokens, channels).T
    work_normed = low((work - pick(mean, image)) * pick(inv_std, image) * norm_gain + norm_shift)

    sends = []
    for offset, part in zip(offsets, grad_parts):
        sends += (project if aligned else project_plain)(work_normed, part, full_qkv, unit, heads, offset, count)
    grads, nears = [], []
    result = None
    for head in range(heads):
        pieces = [sends[head][0]] + [flipped(sends[head][flip], "seq", flip) for flip in range(1, groups)]
        if head == 0:
            pieces, normed_t, cotangent_t = lax.optimization_barrier((pieces, normed_t, cotangent_t))
        if head >= 1:
            pieces, result = lax.optimization_barrier((pieces, result))
            grads.append(lax.all_to_all(result, "seq", split_axis=0, concat_axis=0, tiled=True))
        if head + 1 < heads:
            pieces, sends[head + 1] = lax.optimization_barrier((pieces, sends[head + 1]))
        if head >= 2:
            partial = weight_grads(normed_t, cotangent_t, grads[head - 2], images)
            pieces, partial, grads[head - 2] = lax.optimization_barrier((pieces, partial, grads[head - 2]))
            nears.append(sum_near(partial, seq_count))
        if head >= 3:
            pieces, nears[head - 3] = lax.optimization_barrier((pieces, nears[head - 3]))
        result = attend_pair(pieces, me)
    if heads > 1:
        result, grads[-1] = lax.optimization_barrier((result, grads[-1]))
    grads.append(lax.all_to_all(result, "seq", split_axis=0, concat_axis=0, tiled=True))
    for grad in grads[len(nears) :]:
        nears.append(sum_near(weight_grads(normed_t, cotangent_t, grad, images), seq_count))
    weight_sums = []
    if heads > 1:
        early = sum_far(jnp.concatenate(nears[:-1], axis=2))
        early, nears[-1] = lax.optimization_barrier((early, nears[-1]))
        weight_sums = jnp.split(early, heads - 1, axis=1)
    weight_sums.append(sum_far(nears[-1]))

    mixed, back = (project_back if aligned else project_back_plain)(grads, full_qkv, full_out, images)
    mixed_out = low(values + mixed).transpose(1, 0, 2)
    grad_centred = back * norm_gain
    mean_one, mean_two = group_sums(grad_centred, grad_centred * centred)
    grad_values = inv_std * (grad_centred - spread(mean_one) - centred * spread(mean_two))
    grad_latent = low(cot_rows.astype(jnp.float32) + grad_values).transpose(1, 0, 2)

    own_rows = channels // devices
    summed = jnp.stack(weight_sums).reshape(heads, own_rows, groups, 4, HEAD)
    summed = summed.transpose(1, 3, 2, 0, 4).reshape(own_rows, 4, HEADS * HEAD)
    grad_qkv = jnp.concatenate([summed[:, 2], summed[:, 0], summed[:, 1]], axis=1)
    out_rows = HEADS * HEAD // devices
    pieces = summed[:, 3].reshape(own_rows, devices, out_rows).transpose(1, 2, 0)
    pieces = lax.all_to_all(pieces, ALL, split_axis=0, concat_axis=0, tiled=True)
    grad_out = pieces.transpose(1, 0, 2).reshape(out_rows, channels)
    return (mixed_out, grad_latent, grad_qkv, grad_out)


def solution(mesh):
    placed = (
        P("seq", ("rep", "own"), None),
        P("seq", ("rep", "own"), None),
        P(),
        P(),
        P("own", None),
        P("own", None),
    )
    return jax.shard_map(
        shards,
        mesh=mesh,
        in_specs=placed,
        out_specs=(
            P("seq", ("rep", "own"), None),
            P("seq", ("rep", "own"), None),
            P(ALL, None),
            P(ALL, None),
        ),
        check_vma=False,
    )
```

time: 1970 us -> 716 us (0.36)
  matrix products: 1330 us -> 3.09 us
  Pallas kernels: 0 us -> 354 us
  waiting for transfers between devices: 251 us -> 92.7 us
  local copies, waits for them, and re-layouts: 153 us -> 50.4 us
  blocking collectives: 164 us -> 64.2 us
  starting transfers between devices: 28.9 us -> 94.7 us
    dot_general x46 -> x2, matrix products: 1100 us -> 3.09 us  [shards(): jnp.einsum('itc,dc->itd', cot_rows, part, preferred_element_type=jnp.floa...]
    pallas_call x0 -> x11, Pallas kernels: none -> 354 us  [the longest x4 265 us: attend_pair(): pl.pallas_call(functools.partial(pair_body, bq, kb), out_shape=jax.ShapeD...]
    sub x16 -> x0, matrix products: 231 us -> none  [probabilities(): weights = jnp.exp(scores - row_max)]
    all_to_all x6 -> x7, waiting for transfers between devices: 136 us -> 7.78 us  [the longest x1 7.76 us: shards(): lax.all_to_all(pieces, ALL, split_axis=0, concat_axis=0, tiled=True)]
    all_to_all x2 -> x0, blocking collectives: 123 us -> none  [the longest x1 62.1 us: shards(): lax.all_to_all(grad_value, 'seq', split_axis=0, concat_axis=1, tiled=True)]
    reduce_scatter x2 -> x0, waiting for transfers between devices: 113 us -> none  [the longest x1 113 us: shards(): lax.psum_scatter(lax.dot_general(row_piece, grad_projected, (((0,), (0,))...]
    ppermute x0 -> x27, waiting for transfers between devices: none -> 83.5 us  [flipped(): lax.ppermute(array, axis, [(i, i ^ flip) for i in range(lax.axis_size(axi...]
    slice x4 -> x2, local copies, waits for them, and re-layouts: 52.3 us -> 2.14 us  [the longest x1 2.09 us: shards(): full_out.reshape(groups, heads, HEAD, channels)[:, offset:offset + count]]
  transfers between devices with their start and end apart: 10 -> 36, of which waited for: 5 -> 8; matrix products, arithmetic and copies ran while one was open for 66% -> 10% of each run, Pallas kernels for 0% -> 50%
where the time goes in v1:
time: 716 us; the launch traced here: 707 us
  Pallas kernels  354 us (49%)
  starting transfers between devices  94.7 us (13%)
  waiting for transfers between devices  92.7 us (13%)
  blocking collectives  64.2 us (9%)
  local copies, waits for them, and re-layouts  50.4 us (7%)
  other arithmetic  32.7 us (5%)
  between operations  15.1 us (2%)
    pallas_call x4, Pallas kernels, attend_pair(): pl.pallas_call(functools.partial(pair_body, bq, kb), out_shape=jax.ShapeD...  265 us
    ppermute x27, waiting for transfers between devices, flipped(): lax.ppermute(array, axis, [(i, i ^ flip) for i in range(lax.axis_size(axi...  83.5 us
    psum x2, blocking collectives, group_sums(): return lax.psum(sums, 'seq') / total_count  64.2 us
    ppermute x27, starting transfers between devices, flipped(): lax.ppermute(array, axis, [(i, i ^ flip) for i in range(lax.axis_size(axi...  46.9 us
    pallas_call x4, Pallas kernels, weight_grads(): pl.pallas_call(functools.partial(weight_body, images), out_shape=jax.Shap...  40.2 us
    all_to_all x4, starting transfers between devices, shards(): lax.all_to_all(result, 'seq', split_axis=0, concat_axis=0, tiled=True)  31.9 us
    pallas_call x2, Pallas kernels, project(): pl.pallas_call(functools.partial(project_body, count, groups), out_shape=...  25.9 us
    pallas_call x1, Pallas kernels, project_back(): pl.pallas_call(functools.partial(back_body, heads), out_shape=[jax.ShapeD...  23.3 us
  transfers between devices with their start and end apart: 36, of which 8 were waited for; matrix products, arithmetic and copies ran while one was open for 10% of the time, Pallas kernels for 50%

profile of v1, /device:TPU:0, one launch (start us, length us, event | category | flops | bytes accessed | tf_op | source)
XLA Modules:
  0.0 707.0 jit_solution(14931896155053210063)
XLA Ops:
  8.9 1.8 copy.86
  10.7 3.4 dynamic-slice_bitcast_fusion.1
  14.1 4.0 collective-permute-start
  19.2 42.3 %psum.14 = f32[2,2,32]{2,1,0:T(2,128)S(1)} all-reduce(f32[2,2,32]{2,1,0:T(2,128)S(1)} %pad_maximum_fusion.4), channel_id=1, replica_groups=mesh['seq'=8,'rep'=2,'own'=2] {'seq'}, use_global_device_ids=true, to_apply=%region_4.5 | all-reduce | flops 128 | bytes 1024 | tf_op jit(solution)/shard_map/psum | solution.py:360
  62.2 3.6 copy.89
  65.7 4.5 copy.108
  70.2 5.1 collective-permute-done
  75.4 4.8 fusion.6
  80.2 4.5 copy.107
  84.7 2.1 fusion.56
  87.2 1.5 fusion.19
  88.9 19.8 %collective-permute-start.1 = (bf16[512,512]{1,0:T(8,128)(2,1)S(1)}, bf16[512,512]{1,0:T(8,128)(2,1)S(1)}, u32[]{:S(2)}, u32[]{:S(2)}) collective-permute-start(bf16[512,512]{1,0:T(8,128)(2,1)S(1)} %get-tuple-element.217), channel_id=1, source_target_pairs={{0,16},{4,20},{8,24},{12,28},{16,0},{20,4},{24,8},{28,12},{1,17},{... | collective-permute-start | bytes 1572872 | tf_op jit(solution)/shard_map/ppermute | solution.py:325
  108.7 1.5 fusion.22
  110.4 31.5 %collective-permute-done.1 = bf16[512,512]{1,0:T(8,128)(2,1)S(1)} collective-permute-done((bf16[512,512]{1,0:T(8,128)(2,1)S(1)}, bf16[512,512]{1,0:T(8,128)(2,1)S(1)}, u32[]{:S(2)}, u32[]{:S(2)}) %collective-permute-start.1) | collective-permute-done | bytes 524320 | tf_op jit(solution)/shard_map/ppermute | solution.py:325
  143.0 12.8 %project.2 = (bf16[2,512,256]{2,1,0:T(8,128)(2,1)}, bf16[2,512,256]{2,1,0:T(8,128)(2,1)}, bf16[2,512,256]{2,1,0:T(8,128)(2,1)}, bf16[2,512,256]{2,1,0:T(8,128)(2...) custom-call(s32[1]{0:T(128)S(6)} %select_n.51.me_ref, ...), custom_call_target="tpu_custom_call" | custom-call | flops 5368709120 | bytes 16777216 | tf_op jit(solution)/shard_map/project/pallas_call | solution.py:181
  155.9 2.0 collective-permute-start.2
  157.9 1.5 collective-permute-start.4
  160.5 13.0 %project.3 = (bf16[2,512,256]{2,1,0:T(8,128)(2,1)}, bf16[2,512,256]{2,1,0:T(8,128)(2,1)}, bf16[2,512,256]{2,1,0:T(8,128)(2,1)}, bf16[2,512,256]{2,1,0:T(8,128)(2...) custom-call(s32[1]{0:T(128)S(6)} %select_n.51.me_ref, ...), custom_call_target="tpu_custom_call" | custom-call | flops 5368709120 | bytes 16777216 | tf_op jit(solution)/shard_map/project/pallas_call | solution.py:181
  173.6 6.6 collective-permute-done.4.refs_3_
  180.2 1.7 collective-permute-start.5
  182.2 1.5 collective-permute-start.7
  183.7 66.4 %attend_pair.4 = bf16[8,512,256]{2,1,0:T(8,128)(2,1)} custom-call(s32[1]{0:T(128)} %bitcast.1.me_ref, bf16[2,512,256]{2,1,0:T(8,128)(2,1)} %get-tuple-element.104.refs_0_, bf16[2,512,256]{2,1,0:T(8,128)(2,1)} %copy-done.21, bf16[2,512,256]{2,1,0:T(8,128)(2,1)} %copy-done.22, bf16[2,512,256]{2,1,0:T(8,128)(2,1)} %copy-done.23), custom_call_target="tpu_custom_call" | custom-call | flops 51539607552 | bytes 4194304 | tf_op jit(solution)/shard_map/attend_pair/pallas_call | solution.py:123
  251.7 5.2 all-to-all-start
  257.0 2.0 collective-permute-start.10
  259.0 1.5 collective-permute-start.11
  260.5 66.1 %attend_pair.5 = bf16[8,512,256]{2,1,0:T(8,128)(2,1)} custom-call(s32[1]{0:T(128)} %bitcast.1.me_ref, bf16[2,512,256]{2,1,0:T(8,128)(2,1)} %get-tuple-element.120.refs_0_, bf16[2,512,256]{2,1,0:T(8,128)(2,1)} %copy-done.24, bf16[2,512,256]{2,1,0:T(8,128)(2,1)} %copy-done.25, bf16[2,512,256]{2,1,0:T(8,128)(2,1)} %collective-permute-done.7.refs_3_), custom_call_target="tpu_custom_call" | custom-call | flops 51539607552 | bytes 4194304 | tf_op jit(solution)/shard_map/attend_pair/pallas_call | solution.py:123
  326.7 2.0 collective-permute-start.12
  328.7 1.5 collective-permute-start.13
  330.7 6.1 all-to-all-start.1
  336.8 10.1 %weight_grads.4 = f32[1280,1024]{1,0:T(8,128)} custom-call(bf16[1280,1024]{1,0:T(8,128)(2,1)} %bitcast.216, bf16[1280,1024]{1,0:T(8,128)(2,1)} %bitcast.212, bf16[8,512,256]{2,1,0:T(8,128)(2,1)} %copy-done.3, bf16[8,512,256]{2,1,0:T(8,128)(2,1)} %copy-done.3), custom_call_target="tpu_custom_call" | custom-call | flops 5368709120 | bytes 8388608 | tf_op jit(solution)/shard_map/weight_grads/pallas_call | solution.py:234
  346.8 3.5 fusion.39
  350.3 1.5 collective-permute-start.16
  352.2 66.2 %attend_pair.6 = bf16[8,512,256]{2,1,0:T(8,128)(2,1)} custom-call(s32[1]{0:T(128)} %bitcast.1.me_ref, bf16[2,512,256]{2,1,0:T(8,128)(2,1)} %get-tuple-element.144.refs_0_, bf16[2,512,256]{2,1,0:T(8,128)(2,1)} %copy-done.20, bf16[2,512,256]{2,1,0:T(8,128)(2,1)} %copy-done.16, bf16[2,512,256]{2,1,0:T(8,128)(2,1)} %copy-done.18), custom_call_target="tpu_custom_call" | custom-call | flops 51539607552 | bytes 4194304 | tf_op jit(solution)/shard_map/attend_pair/pallas_call | solution.py:123
  418.4 14.6 %all-to-all-start.2 = ((bf16[8,512,256]{2,1,0:T(8,128)(2,1)}), bf16[8,512,256]{2,1,0:T(8,128)(2,1)S(1)}, u32[]{:S(2)}, u32[]{:S(2)}) async-start(bf16[8,512,256]{2,1,0:T(8,128)(2,1)} %attend_pair.6), calls=%async_computation.2 | async-start | bytes 4194304 | tf_op jit(solution)/shard_map/all_to_all | solution.py:407
  433.0 10.0 %weight_grads.5 = f32[1280,1024]{1,0:T(8,128)} custom-call(bf16[1280,1024]{1,0:T(8,128)(2,1)} %bitcast.217, bf16[1280,1024]{1,0:T(8,128)(2,1)} %bitcast.213, bf16[8,512,256]{2,1,0:T(8,128)(2,1)} %all-to-all-done.1.refs_0_.refs_1_, bf16[8,512,256]{2,1,0:T(8,128)(2,1)} %all-to-all-done.1.refs_0_.refs_1_), custom_call_target="tpu_custom_call" | custom-call | flops 5368709120 | bytes 8388608 | tf_op jit(solution)/shard_map/weight_grads/pallas_call | solution.py:234
  443.1 2.1 fusion.36
  445.2 66.1 %attend_pair.7 = bf16[8,512,256]{2,1,0:T(8,128)(2,1)} custom-call(s32[1]{0:T(128)} %bitcast.1.me_ref, bf16[2,512,256]{2,1,0:T(8,128)(2,1)} %get-tuple-element.159.refs_0_, bf16[2,512,256]{2,1,0:T(8,128)(2,1)} %collective-permute-done.12.refs_1_, bf16[2,512,256]{2,1,0:T(8,128)(2,1)} %collective-permute-done.13.refs_2_, ...), custom_call_target="tpu_custom_call" | custom-call | flops 51539607552 | bytes 4194304 | tf_op jit(solution)/shard_map/attend_pair/pallas_call | solution.py:123
  511.3 6.0 all-to-all-start.3
  517.3 2.4 fusion.42
  522.1 10.0 %weight_grads.6 = f32[1280,1024]{1,0:T(8,128)} custom-call(bf16[1280,1024]{1,0:T(8,128)(2,1)} %bitcast.218, bf16[1280,1024]{1,0:T(8,128)(2,1)} %bitcast.214, bf16[8,512,256]{2,1,0:T(8,128)(2,1)} %copy-done.4, bf16[8,512,256]{2,1,0:T(8,128)(2,1)} %copy-done.4), custom_call_target="tpu_custom_call" | custom-call | flops 5368709120 | bytes 8388608 | tf_op jit(solution)/shard_map/weight_grads/pallas_call | solution.py:234
  532.1 2.4 fusion.45
  536.7 1.5 collective-permute-done.19
  538.2 12.3 %collective-permute-done.20 = bf16[8,40,1024]{2,1,0:T(8,128)(2,1)S(1)} collective-permute-done((bf16[8,40,1024]{2,1,0:T(8,128)(2,1)S(1)}, bf16[8,40,1024]{2,1,0:T(8,128)(2,1)S(1)}, u32[]{:S(2)}, u32[]{:S(2)}) %collective-permute-start.20) | collective-permute-done | bytes 655392 | tf_op jit(solution)/shard_map/ppermute | solution.py:325
  550.5 1.7 fusion.33
  552.3 14.1 %collective-permute-done.22 = bf16[8,40,1024]{2,1,0:T(8,128)(2,1)S(1)} collective-permute-done((bf16[8,40,1024]{2,1,0:T(8,128)(2,1)S(1)}, bf16[8,40,1024]{2,1,0:T(8,128)(2,1)S(1)}, u32[]{:S(2)}, u32[]{:S(2)}) %collective-permute-start.22) | collective-permute-done | bytes 655392 | tf_op jit(solution)/shard_map/ppermute | solution.py:325
  566.3 12.3 %collective-permute-done.23 = bf16[8,40,1024]{2,1,0:T(8,128)(2,1)S(1)} collective-permute-done((bf16[8,40,1024]{2,1,0:T(8,128)(2,1)S(1)}, bf16[8,40,1024]{2,1,0:T(8,128)(2,1)S(1)}, u32[]{:S(2)}, u32[]{:S(2)}) %collective-permute-start.23) | collective-permute-done | bytes 655392 | tf_op jit(solution)/shard_map/ppermute | solution.py:325
  578.6 1.7 fusion.30
  580.4 1.4 pad_maximum_fusion
  581.8 6.0 all-to-all-start.4
  587.7 10.1 %weight_grads.7 = f32[1280,1024]{1,0:T(8,128)} custom-call(bf16[1280,1024]{1,0:T(8,128)(2,1)} %bitcast.219, bf16[1280,1024]{1,0:T(8,128)(2,1)} %bitcast.215, bf16[8,512,256]{2,1,0:T(8,128)(2,1)} %all-to-all-done.3.refs_3_.refs_0_.refs_1_, bf16[8,512,256]{2,1,0:T(8,128)(2,1)} %all-to-all-done.3.refs_3_.refs_0_.refs_1_), custom_call_target="tpu_custom_call" | custom-call | flops 5368709120 | bytes 8388608 | tf_op jit(solution)/shard_map/weight_grads/pallas_call | solution.py:234
  597.8 3.5 fusion.47
  601.7 1.4 collective-permute-start.25
  603.3 23.3 %project_back.1 = (f32[2,512,1280]{2,1,0:T(8,128)}, f32[2,512,1280]{2,1,0:T(8,128)}) custom-call(bf16[8,512,256]{2,1,0:T(8,128)(2,1)} %copy-done.3, bf16[8,512,256]{2,1,0:T(8,128)(2,1)} %all-to-all-done.1.refs_0_.refs_1_, bf16[8,512,256]{2,1,0:T(8,128)(2,1)} %copy-done.4, bf16[8,512,256]{2,1,0:T(8,128)(2,1)} %all-to-all-done.3.refs_3_.refs_0_.refs_1_, ...), custom_call_target="tpu_custom_call" | custom-call | flops 10737418240 | bytes 33554432 | tf_op jit(solution)/shard_map/project_back/pallas_call | solution.py:296
  626.6 3.7 multiply_reduce_fusion
  630.7 21.8 %psum.15 = f32[2,2,32]{2,1,0:T(2,128)S(1)} all-reduce(f32[2,2,32]{2,1,0:T(2,128)S(1)} %pad_maximum_fusion.5), channel_id=1, replica_groups=mesh['seq'=8,'rep'=2,'own'=2] {'seq'}, use_global_device_ids=true, to_apply=%region_9.10 | all-reduce | flops 128 | bytes 1024 | tf_op jit(solution)/shard_map/psum | solution.py:360
  653.0 2.6 convert_reduce_fusion
  655.6 3.2 fusion.27
  658.8 3.8 all-to-all-start.5
  662.6 5.9 fusion.14
  668.5 4.2 copy.105
  672.6 4.2 copy.106
  680.7 1.1 reshape.109
  681.8 6.1 all-to-all-start.6
  688.7 7.8 %all-to-all-done.6 = f32[32,1,1280]{2,1,0:T(1,128)S(1)} async-done(((f32[32,1,1280]{2,1,0:T(1,128)}), f32[32,1,1280]{2,1,0:T(1,128)S(1)}, u32[]{:S(2)}, u32[]{:S(2)}) %all-to-all-start.6) | async-done | bytes 163872 | tf_op jit(solution)/shard_map/all_to_all | solution.py:442
  (148 shorter events, 22.7 us)
Async XLA Ops:
  7.2 1.7 copy-start
  7.2 77.5 %all-gather.3.cloned.1.call-start = ((), (), s32[]{:S(2)}) async-start(), calls=%async_computation.7 | async-start | bytes 3932160 | tf_op jit(solution)/shard_map/all_gather | solution.py:356
  7.9 135.1 %all-gather.5.cloned.1.call-start = ((), (), s32[]{:S(2)}) async-start(), calls=%async_computation.8 | async-start | bytes 11796480 | tf_op jit(solution)/shard_map/all_gather | solution.py:355
  14.1 61.3 %collective-permute-start = (bf16[512,1280]{1,0:T(8,128)(2,1)}, bf16[512,1280]{1,0:T(8,128)(2,1)}, u32[]{:S(2)}, u32[]{:S(2)}) collective-permute-start(bf16[512,1280]{1,0:T(8,128)(2,1)} %get-tuple-element.213), channel_id=1, source_target_pairs={{0,16},{4,20},{8,24},{12,28},{16,0},{20,4},{24,8},{28,12},{1,17},{... | collective-permute-start | bytes 3932168 | tf_op jit(solution)/shard_map/ppermute | solution.py:325
  61.8 13.5 %copy-start.6 = (f32[2,1280]{1,0:T(2,128)}, f32[2,1280]{1,0:T(2,128)S(1)}, u32[]{:S(2)}) copy-start(f32[2,1280]{1,0:T(2,128)S(1)} %mul.78) | copy-start | bytes 30724
  62.1 13.3 %copy-start.8 = (f32[2,1280]{1,0:T(2,128)}, f32[2,1280]{1,0:T(2,128)S(1)}, u32[]{:S(2)}) copy-start(f32[2,1280]{1,0:T(2,128)S(1)} %sub.51) | copy-start | bytes 30724
  65.7 9.7 %copy-start.10 = (f32[1280]{0:T(1024)S(1)}, f32[1280]{0:T(1024)}, u32[]{:S(2)}) copy-start(f32[1280]{0:T(1024)} %param.8) | copy-start | bytes 15364
  65.7 9.7 %copy-start.12 = (f32[1280]{0:T(1024)S(1)}, f32[1280]{0:T(1024)}, u32[]{:S(2)}) copy-start(f32[1280]{0:T(1024)} %param.9) | copy-start | bytes 15364
  84.7 2.5 copy-start.2
  88.9 53.1 %collective-permute-start.1 = (bf16[512,512]{1,0:T(8,128)(2,1)S(1)}, bf16[512,512]{1,0:T(8,128)(2,1)S(1)}, u32[]{:S(2)}, u32[]{:S(2)}) collective-permute-start(bf16[512,512]{1,0:T(8,128)(2,1)S(1)} %get-tuple-element.217), channel_id=1, source_target_pairs={{0,16},{4,20},{8,24},{12,28},{16,0},{20,4},{24,8},{28,12},{1,17},{... | collective-permute-start | bytes 1572872 | tf_op jit(solution)/shard_map/ppermute | solution.py:325
  110.3 49.1 %collective-permute-start.8 = (bf16[512,512]{1,0:T(8,128)(2,1)S(1)}, bf16[512,512]{1,0:T(8,128)(2,1)S(1)}, u32[]{:S(2)}, u32[]{:S(2)}) collective-permute-start(bf16[512,512]{1,0:T(8,128)(2,1)S(1)} %get-tuple-element.215), channel_id=1, source_target_pairs={{0,16},{4,20},{8,24},{12,28},{16,0},{20,4},{24,8},{28,12},{1,17},{... | collective-permute-start | bytes 1572872 | tf_op jit(solution)/shard_map/ppermute | solution.py:325
  155.9 17.7 %collective-permute-start.2 = (bf16[2,512,256]{2,1,0:T(8,128)(2,1)}, bf16[2,512,256]{2,1,0:T(8,128)(2,1)S(1)}, u32[]{:S(2)}, u32[]{:S(2)}) collective-permute-start(bf16[2,512,256]{2,1,0:T(8,128)(2,1)} %get-tuple-element.89), channel_id=1, source_target_pairs={{0,4},{4,0},{8,12},{12,8},{16,20},{20,16},{24,28},{28,24},{1,5},{5... | collective-permute-start | bytes 1572872 | tf_op jit(solution)/shard_map/ppermute | solution.py:325
  157.9 15.7 %collective-permute-start.3 = (bf16[2,512,256]{2,1,0:T(8,128)(2,1)}, bf16[2,512,256]{2,1,0:T(8,128)(2,1)S(1)}, u32[]{:S(2)}, u32[]{:S(2)}) collective-permute-start(bf16[2,512,256]{2,1,0:T(8,128)(2,1)} %get-tuple-element.90), channel_id=1, source_target_pairs={{0,8},{4,12},{8,0},{12,4},{16,24},{20,28},{24,16},{28,20},{1,9},{5... | collective-permute-start | bytes 1572872 | tf_op jit(solution)/shard_map/ppermute | solution.py:325
  157.9 22.3 %collective-permute-start.4 = (bf16[2,512,256]{2,1,0:T(8,128)(2,1)}, bf16[2,512,256]{2,1,0:T(8,128)(2,1)S(1)}, u32[]{:S(2)}, u32[]{:S(2)}) collective-permute-start(bf16[2,512,256]{2,1,0:T(8,128)(2,1)} %get-tuple-element.91), channel_id=1, source_target_pairs={{0,12},{4,8},{8,4},{12,0},{16,28},{20,24},{24,20},{28,16},{1,13},{... | collective-permute-start | bytes 1572872 | tf_op jit(solution)/shard_map/ppermute | solution.py:325
  160.5 19.7 %copy-start.19 = (bf16[2,512,256]{2,1,0:T(8,128)(2,1)S(1)}, bf16[2,512,256]{2,1,0:T(8,128)(2,1)}, u32[]{:S(2)}) copy-start(bf16[2,512,256]{2,1,0:T(8,128)(2,1)} %get-tuple-element.101) | copy-start | bytes 1572868
  160.5 21.4 %copy-start.17 = (bf16[2,512,256]{2,1,0:T(8,128)(2,1)S(1)}, bf16[2,512,256]{2,1,0:T(8,128)(2,1)}, u32[]{:S(2)}) copy-start(bf16[2,512,256]{2,1,0:T(8,128)(2,1)} %get-tuple-element.102) | copy-start | bytes 1572868
  160.5 21.7 %copy-start.15 = (bf16[2,512,256]{2,1,0:T(8,128)(2,1)S(1)}, bf16[2,512,256]{2,1,0:T(8,128)(2,1)}, u32[]{:S(2)}) copy-start(bf16[2,512,256]{2,1,0:T(8,128)(2,1)} %get-tuple-element.103) | copy-start | bytes 1572868
  173.5 10.2 %copy-start.21 = (bf16[2,512,256]{2,1,0:T(8,128)(2,1)}, bf16[2,512,256]{2,1,0:T(8,128)(2,1)S(1)}, u32[]{:S(2)}) copy-start(bf16[2,512,256]{2,1,0:T(8,128)(2,1)S(1)} %collective-permute-done.2.refs_1_) | copy-start | bytes 1572868
  173.6 10.2 %copy-start.22 = (bf16[2,512,256]{2,1,0:T(8,128)(2,1)}, bf16[2,512,256]{2,1,0:T(8,128)(2,1)S(1)}, u32[]{:S(2)}) copy-start(bf16[2,512,256]{2,1,0:T(8,128)(2,1)S(1)} %collective-permute-done.3.refs_2_) | copy-start | bytes 1572868
  180.2 3.5 copy-start.23
  180.2 69.9 %collective-permute-start.5 = (bf16[2,512,256]{2,1,0:T(8,128)(2,1)S(1)}, bf16[2,512,256]{2,1,0:T(8,128)(2,1)S(1)}, u32[]{:S(2)}, u32[]{:S(2)}) collective-permute-start(bf16[2,512,256]{2,1,0:T(8,128)(2,1)S(1)} %copy-done.19), channel_id=1, source_target_pairs={{0,4},{4,0},{8,12},{12,8},{16,20},{20,16},{24,28},{28,24},{1,5},{5... | collective-permute-start | bytes 1572872 | tf_op jit(solution)/shard_map/ppermute | solution.py:325
  181.9 68.2 %collective-permute-start.6 = (bf16[2,512,256]{2,1,0:T(8,128)(2,1)S(1)}, bf16[2,512,256]{2,1,0:T(8,128)(2,1)S(1)}, u32[]{:S(2)}, u32[]{:S(2)}) collective-permute-start(bf16[2,512,256]{2,1,0:T(8,128)(2,1)S(1)} %copy-done.17), channel_id=1, source_target_pairs={{0,8},{4,12},{8,0},{12,4},{16,24},{20,28},{24,16},{28,20},{1,9},{5... | collective-permute-start | bytes 1572872 | tf_op jit(solution)/shard_map/ppermute | solution.py:325
  182.2 69.6 %collective-permute-start.7 = (bf16[2,512,256]{2,1,0:T(8,128)(2,1)S(1)}, bf16[2,512,256]{2,1,0:T(8,128)(2,1)}, u32[]{:S(2)}, u32[]{:S(2)}) collective-permute-start(bf16[2,512,256]{2,1,0:T(8,128)(2,1)S(1)} %copy-done.15), channel_id=1, source_target_pairs={{0,12},{4,8},{8,4},{12,0},{16,28},{20,24},{24,20},{28,16},{1,13},{... | collective-permute-start | bytes 1572872 | tf_op jit(solution)/shard_map/ppermute | solution.py:325
  250.1 10.4 %copy-start.14 = (bf16[2,512,256]{2,1,0:T(8,128)(2,1)S(1)}, bf16[2,512,256]{2,1,0:T(8,128)(2,1)}, u32[]{:S(2)}) copy-start(bf16[2,512,256]{2,1,0:T(8,128)(2,1)} %get-tuple-element.117) | copy-start | bytes 1572868
  250.1 0.8 copy-start.24
  250.9 0.8 copy-start.25
  251.7 78.9 %all-to-all-start = ((bf16[8,512,256]{2,1,0:T(8,128)(2,1)}), bf16[8,512,256]{2,1,0:T(8,128)(2,1)S(1)}, u32[]{:S(2)}, u32[]{:S(2)}) async-start(bf16[8,512,256]{2,1,0:T(8,128)(2,1)} %attend_pair.4), calls=%async_computation | async-start | bytes 4194304 | tf_op jit(solution)/shard_map/all_to_all | solution.py:407
  257.0 73.2 %copy-start.13 = (bf16[2,512,256]{2,1,0:T(8,128)(2,1)S(1)}, bf16[2,512,256]{2,1,0:T(8,128)(2,1)}, u32[]{:S(2)}) copy-start(bf16[2,512,256]{2,1,0:T(8,128)(2,1)} %get-tuple-element.143) | copy-start | bytes 1572868
  257.0 69.7 %collective-permute-start.10 = (bf16[2,512,256]{2,1,0:T(8,128)(2,1)}, bf16[2,512,256]{2,1,0:T(8,128)(2,1)S(1)}, u32[]{:S(2)}, u32[]{:S(2)}) collective-permute-start(bf16[2,512,256]{2,1,0:T(8,128)(2,1)} %get-tuple-element.118), channel_id=1, source_target_pairs={{0,8},{4,12},{8,0},{12,4},{16,24},{20,28},{24,16},{28,20},{1,9},{5... | collective-permute-start | bytes 1572872 | tf_op jit(solution)/shard_map/ppermute | solution.py:325
  259.0 67.7 %collective-permute-start.11 = (bf16[2,512,256]{2,1,0:T(8,128)(2,1)}, bf16[2,512,256]{2,1,0:T(8,128)(2,1)S(1)}, u32[]{:S(2)}, u32[]{:S(2)}) collective-permute-start(bf16[2,512,256]{2,1,0:T(8,128)(2,1)} %get-tuple-element.119), channel_id=1, source_target_pairs={{0,12},{4,8},{8,4},{12,0},{16,28},{20,24},{24,20},{28,16},{1,13},{... | collective-permute-start | bytes 1572872 | tf_op jit(solution)/shard_map/ppermute | solution.py:325
  260.5 66.2 %collective-permute-start.9 = (bf16[2,512,256]{2,1,0:T(8,128)(2,1)S(1)}, bf16[2,512,256]{2,1,0:T(8,128)(2,1)S(1)}, u32[]{:S(2)}, u32[]{:S(2)}) collective-permute-start(bf16[2,512,256]{2,1,0:T(8,128)(2,1)S(1)} %copy-done.14), channel_id=1, source_target_pairs={{0,4},{4,0},{8,12},{12,8},{16,20},{20,16},{24,28},{28,24},{1,5},{5... | collective-permute-start | bytes 1572872 | tf_op jit(solution)/shard_map/ppermute | solution.py:325
  326.7 3.5 copy-start.16
  326.7 3.5 copy-start.18
  326.7 3.5 copy-start.20
  326.7 25.1 %collective-permute-start.12 = (bf16[2,512,256]{2,1,0:T(8,128)(2,1)}, bf16[2,512,256]{2,1,0:T(8,128)(2,1)}, u32[]{:S(2)}, u32[]{:S(2)}) collective-permute-start(bf16[2,512,256]{2,1,0:T(8,128)(2,1)} %get-tuple-element.141), channel_id=1, source_target_pairs={{0,4},{4,0},{8,12},{12,8},{16,20},{20,16},{24,28},{28,24},{1,5},{5... | collective-permute-start | bytes 1572872 | tf_op jit(solution)/shard_map/ppermute | solution.py:325
  328.7 89.6 %collective-permute-start.13 = (bf16[2,512,256]{2,1,0:T(8,128)(2,1)}, bf16[2,512,256]{2,1,0:T(8,128)(2,1)}, u32[]{:S(2)}, u32[]{:S(2)}) collective-permute-start(bf16[2,512,256]{2,1,0:T(8,128)(2,1)} %get-tuple-element.142), channel_id=1, source_target_pairs={{0,8},{4,12},{8,0},{12,4},{16,24},{20,28},{24,16},{28,20},{1,9},{5... | collective-permute-start | bytes 1572872 | tf_op jit(solution)/shard_map/ppermute | solution.py:325
  330.2 88.2 %collective-permute-start.14 = (bf16[2,512,256]{2,1,0:T(8,128)(2,1)S(1)}, bf16[2,512,256]{2,1,0:T(8,128)(2,1)}, u32[]{:S(2)}, u32[]{:S(2)}) collective-permute-start(bf16[2,512,256]{2,1,0:T(8,128)(2,1)S(1)} %copy-done.13), channel_id=1, source_target_pairs={{0,12},{4,8},{8,4},{12,0},{16,28},{20,24},{24,20},{28,16},{1,13},{... | collective-permute-start | bytes 1572872 | tf_op jit(solution)/shard_map/ppermute | solution.py:325
  330.7 6.1 copy-start.3
  330.7 87.7 %all-to-all-start.1 = ((bf16[8,512,256]{2,1,0:T(8,128)(2,1)}), bf16[8,512,256]{2,1,0:T(8,128)(2,1)}, u32[]{:S(2)}, u32[]{:S(2)}) async-start(bf16[8,512,256]{2,1,0:T(8,128)(2,1)} %attend_pair.5), calls=%async_computation.1 | async-start | bytes 4194304 | tf_op jit(solution)/shard_map/all_to_all | solution.py:407
  350.3 92.7 %collective-permute-start.15 = (bf16[8,40,1024]{2,1,0:T(8,128)(2,1)}, bf16[8,40,1024]{2,1,0:T(8,128)(2,1)S(1)}, u32[]{:S(2)}, u32[]{:S(2)}) collective-permute-start(bf16[8,40,1024]{2,1,0:T(8,128)(2,1)} %get-tuple-element.205), channel_id=1, source_target_pairs={{0,1},{1,0},{2,3},{3,2},{4,5},{5,4},{6,7},{7,6},{8,9},{9,8},{10,11... | collective-permute-start | bytes 1966088 | tf_op jit(solution)/shard_map/ppermute | solution.py:325
  350.3 92.7 %collective-permute-start.16 = (bf16[8,40,1024]{2,1,0:T(8,128)(2,1)}, bf16[8,40,1024]{2,1,0:T(8,128)(2,1)}, u32[]{:S(2)}, u32[]{:S(2)}) collective-permute-start(bf16[8,40,1024]{2,1,0:T(8,128)(2,1)} %get-tuple-element.206), channel_id=1, source_target_pairs={{0,2},{1,3},{2,0},{3,1},{4,6},{5,7},{6,4},{7,5},{8,10},{9,11},{10,... | collective-permute-start | bytes 1966088 | tf_op jit(solution)/shard_map/ppermute | solution.py:325
  351.8 91.2 %collective-permute-start.17 = (bf16[8,40,1024]{2,1,0:T(8,128)(2,1)S(1)}, bf16[8,40,1024]{2,1,0:T(8,128)(2,1)}, u32[]{:S(2)}, u32[]{:S(2)}) collective-permute-start(bf16[8,40,1024]{2,1,0:T(8,128)(2,1)S(1)} %get-tuple-element.207), channel_id=1, source_target_pairs={{0,3},{1,2},{2,1},{3,0},{4,7},{5,6},{6,5},{7,4},{8,11},{9,10},{10,... | collective-permute-start | bytes 1966088 | tf_op jit(solution)/shard_map/ppermute | solution.py:325
  418.4 92.9 %all-to-all-start.2 = ((bf16[8,512,256]{2,1,0:T(8,128)(2,1)}), bf16[8,512,256]{2,1,0:T(8,128)(2,1)S(1)}, u32[]{:S(2)}, u32[]{:S(2)}) async-start(bf16[8,512,256]{2,1,0:T(8,128)(2,1)} %attend_pair.6), calls=%async_computation.2 | async-start | bytes 4194304 | tf_op jit(solution)/shard_map/all_to_all | solution.py:407
  511.3 8.4 %copy-start.4 = (bf16[8,512,256]{2,1,0:T(8,128)(2,1)}, bf16[8,512,256]{2,1,0:T(8,128)(2,1)S(1)}, u32[]{:S(2)}) copy-start(bf16[8,512,256]{2,1,0:T(8,128)(2,1)S(1)} %all-to-all-done.2.refs_2_.refs_0_.refs_1_) | copy-start | bytes 6291460
  511.3 70.4 %all-to-all-start.3 = ((bf16[8,512,256]{2,1,0:T(8,128)(2,1)}), bf16[8,512,256]{2,1,0:T(8,128)(2,1)}, u32[]{:S(2)}, u32[]{:S(2)}) async-start(bf16[8,512,256]{2,1,0:T(8,128)(2,1)} %attend_pair.7), calls=%async_computation.3 | async-start | bytes 4194304 | tf_op jit(solution)/shard_map/all_to_all | solution.py:419
  519.8 16.3 %collective-permute-start.18 = (bf16[8,40,1024]{2,1,0:T(8,128)(2,1)S(1)}, bf16[8,40,1024]{2,1,0:T(8,128)(2,1)S(1)}, u32[]{:S(2)}, u32[]{:S(2)}) collective-permute-start(bf16[8,40,1024]{2,1,0:T(8,128)(2,1)S(1)} %get-tuple-element.199), channel_id=1, source_target_pairs={{0,1},{1,0},{2,3},{3,2},{4,5},{5,4},{6,7},{7,6},{8,9},{9,8},{10,11... | collective-permute-start | bytes 1966088 | tf_op jit(solution)/shard_map/ppermute | solution.py:325
  520.6 17.6 %collective-permute-start.19 = (bf16[8,40,1024]{2,1,0:T(8,128)(2,1)S(1)}, bf16[8,40,1024]{2,1,0:T(8,128)(2,1)S(1)}, u32[]{:S(2)}, u32[]{:S(2)}) collective-permute-start(bf16[8,40,1024]{2,1,0:T(8,128)(2,1)S(1)} %get-tuple-element.200), channel_id=1, source_target_pairs={{0,2},{1,3},{2,0},{3,1},{4,6},{5,7},{6,4},{7,5},{8,10},{9,11},{10,... | collective-permute-start | bytes 1966088 | tf_op jit(solution)/shard_map/ppermute | solution.py:325
  521.4 29.1 %collective-permute-start.20 = (bf16[8,40,1024]{2,1,0:T(8,128)(2,1)S(1)}, bf16[8,40,1024]{2,1,0:T(8,128)(2,1)S(1)}, u32[]{:S(2)}, u32[]{:S(2)}) collective-permute-start(bf16[8,40,1024]{2,1,0:T(8,128)(2,1)S(1)} %get-tuple-element.201), channel_id=1, source_target_pairs={{0,3},{1,2},{2,1},{3,0},{4,7},{5,6},{6,5},{7,4},{8,11},{9,10},{10,... | collective-permute-start | bytes 1966088 | tf_op jit(solution)/shard_map/ppermute | solution.py:325
  534.5 17.8 %collective-permute-start.21 = (bf16[8,40,1024]{2,1,0:T(8,128)(2,1)S(1)}, bf16[8,40,1024]{2,1,0:T(8,128)(2,1)S(1)}, u32[]{:S(2)}, u32[]{:S(2)}) collective-permute-start(bf16[8,40,1024]{2,1,0:T(8,128)(2,1)S(1)} %get-tuple-element.202), channel_id=1, source_target_pairs={{0,1},{1,0},{2,3},{3,2},{4,5},{5,4},{6,7},{7,6},{8,9},{9,8},{10,11... | collective-permute-start | bytes 1966088 | tf_op jit(solution)/shard_map/ppermute | solution.py:325
  535.3 31.0 %collective-permute-start.22 = (bf16[8,40,1024]{2,1,0:T(8,128)(2,1)S(1)}, bf16[8,40,1024]{2,1,0:T(8,128)(2,1)S(1)}, u32[]{:S(2)}, u32[]{:S(2)}) collective-permute-start(bf16[8,40,1024]{2,1,0:T(8,128)(2,1)S(1)} %get-tuple-element.204), channel_id=1, source_target_pairs={{0,2},{1,3},{2,0},{3,1},{4,6},{5,7},{6,4},{7,5},{8,10},{9,11},{10,... | collective-permute-start | bytes 1966088 | tf_op jit(solution)/shard_map/ppermute | solution.py:325
  536.0 42.6 %collective-permute-start.23 = (bf16[8,40,1024]{2,1,0:T(8,128)(2,1)S(1)}, bf16[8,40,1024]{2,1,0:T(8,128)(2,1)S(1)}, u32[]{:S(2)}, u32[]{:S(2)}) collective-permute-start(bf16[8,40,1024]{2,1,0:T(8,128)(2,1)S(1)} %get-tuple-element.203), channel_id=1, source_target_pairs={{0,3},{1,2},{2,1},{3,0},{4,7},{5,6},{6,5},{7,4},{8,11},{9,10},{10,... | collective-permute-start | bytes 1966088 | tf_op jit(solution)/shard_map/ppermute | solution.py:325
  581.8 71.2 %all-to-all-start.4 = ((bf16[8,40,3072]{2,1,0:T(8,128)(2,1)}), bf16[8,40,3072]{2,1,0:T(8,128)(2,1)}, u32[]{:S(2)}, u32[]{:S(2)}) async-start(bf16[8,40,3072]{2,1,0:T(8,128)(2,1)} %pad_maximum_fusion), calls=%async_computation.4 | async-start | bytes 3932160 | tf_op jit(solution)/shard_map/all_to_all | solution.py:341
  601.3 54.3 %collective-permute-start.24 = (bf16[8,40,1024]{2,1,0:T(8,128)(2,1)}, bf16[8,40,1024]{2,1,0:T(8,128)(2,1)}, u32[]{:S(2)}, u32[]{:S(2)}) collective-permute-start(bf16[8,40,1024]{2,1,0:T(8,128)(2,1)} %get-tuple-element.196), channel_id=1, source_target_pairs={{0,1},{1,0},{2,3},{3,2},{4,5},{5,4},{6,7},{7,6},{8,9},{9,8},{10,11... | collective-permute-start | bytes 1966088 | tf_op jit(solution)/shard_map/ppermute | solution.py:325
  601.7 53.9 %collective-permute-start.25 = (bf16[8,40,1024]{2,1,0:T(8,128)(2,1)}, bf16[8,40,1024]{2,1,0:T(8,128)(2,1)}, u32[]{:S(2)}, u32[]{:S(2)}) collective-permute-start(bf16[8,40,1024]{2,1,0:T(8,128)(2,1)} %get-tuple-element.198), channel_id=1, source_target_pairs={{0,2},{1,3},{2,0},{3,1},{4,6},{5,7},{6,4},{7,5},{8,10},{9,11},{10,... | collective-permute-start | bytes 1966088 | tf_op jit(solution)/shard_map/ppermute | solution.py:325
  603.1 23.5 %copy-start.1 = (bf16[512,2,1280]{2,1,0:T(2,128)(2,1)S(1)}, bf16[512,2,1280]{2,1,0:T(2,128)(2,1)}, u32[]{:S(2)}) copy-start(bf16[512,2,1280]{2,1,0:T(2,128)(2,1)} %param.6) | copy-start | bytes 7864324
  603.1 23.5 %copy-start.7 = (f32[2,1280]{1,0:T(2,128)S(1)}, f32[2,1280]{1,0:T(2,128)}, u32[]{:S(2)}) copy-start(f32[2,1280]{1,0:T(2,128)} %copy-done.6) | copy-start | bytes 30724
  603.1 23.5 %copy-start.9 = (f32[2,1280]{1,0:T(2,128)S(1)}, f32[2,1280]{1,0:T(2,128)}, u32[]{:S(2)}) copy-start(f32[2,1280]{1,0:T(2,128)} %copy-done.8) | copy-start | bytes 30724
  603.1 23.5 %copy-start.11 = (f32[1280]{0:T(1024)S(1)}, f32[1280]{0:T(1024)}, u32[]{:S(2)}) copy-start(f32[1280]{0:T(1024)} %param.8) | copy-start | bytes 15364
  603.1 52.5 %collective-permute-start.26 = (bf16[8,40,1024]{2,1,0:T(8,128)(2,1)S(1)}, bf16[8,40,1024]{2,1,0:T(8,128)(2,1)}, u32[]{:S(2)}, u32[]{:S(2)}) collective-permute-start(bf16[8,40,1024]{2,1,0:T(8,128)(2,1)S(1)} %get-tuple-element.197), channel_id=1, source_target_pairs={{0,3},{1,2},{2,1},{3,0},{4,7},{5,6},{6,5},{7,4},{8,11},{9,10},{10,... | collective-permute-start | bytes 1966088 | tf_op jit(solution)/shard_map/ppermute | solution.py:325
  658.8 18.8 %all-to-all-start.5 = ((bf16[8,40,1024]{2,1,0:T(8,128)(2,1)}), bf16[8,40,1024]{2,1,0:T(8,128)(2,1)S(1)}, u32[]{:S(2)}, u32[]{:S(2)}) async-start(bf16[8,40,1024]{2,1,0:T(8,128)(2,1)} %fusion.27), calls=%async_computation.5 | async-start | bytes 1310720 | tf_op jit(solution)/shard_map/all_to_all | solution.py:341
  672.6 4.2 copy-start.5
  681.8 14.7 %all-to-all-start.6 = ((f32[32,1,1280]{2,1,0:T(1,128)}), f32[32,1,1280]{2,1,0:T(1,128)S(1)}, u32[]{:S(2)}, u32[]{:S(2)}) async-start(f32[32,1,1280]{2,1,0:T(1,128)} %reshape.109), calls=%async_computation.6 | async-start | bytes 327680 | tf_op jit(solution)/shard_map/all_to_all | solution.py:442
Sparse Core Ops, SparseCore 0:
  9.6 14.0 all-gather.2
  25.2 20.2 all-gather.4

commit v2 on v1

--- a/solution.py
+++ b/solution.py
@@ -146,24 +146,25 @@
     return piece if head % 2 == slot % 2 else pltpu.roll(piece, HEAD, 1)
 
 
-def project_body(count, groups, me_ref, norm_ref, grad_ref, wq_ref, wk_ref, wv_ref, *outs):
+def project_body(count, groups, unit_ref, norm_ref, grad_ref, wq_ref, wk_ref, wv_ref, *outs):
     first = lax.broadcasted_iota(jnp.int32, (1, HALF), 1) < HEAD
     width = count * HEAD
+    halves, tokens, channels = norm_ref.shape
     weights = jnp.concatenate([wq_ref[...], wk_ref[...], wv_ref[...]], axis=1)
-    projected = dot(norm_ref[0], weights)
+    projected = dot(norm_ref[...].reshape(halves * tokens, channels), weights)
     query, key, value = (projected[:, part * width : (part + 1) * width] for part in range(3))
-    grad = grad_ref[0].astype(jnp.float32)
+    grad = grad_ref[...].reshape(halves * tokens, width).astype(jnp.float32)
     packs = []
     for head in range(count):
         left = jnp.where(first, lane_piece(key, head, 0), lane_piece(value, head, 1))
         right = jnp.where(first, lane_piece(query, head, 0), lane_piece(grad, head, 1))
-        packs.append(low(jnp.concatenate([left, right], axis=1)))
+        packs.append(low(jnp.concatenate([left, right], axis=1)).reshape(halves, tokens, PACK))
     for flip in range(groups):
 
-        @pl.when(pl.program_id(1) == flip)
+        @pl.when(pl.program_id(0) == flip)
         def _():
             for head in range(count):
-                outs[head * groups + flip][0] = packs[head]
+                outs[head * groups + flip][...] = packs[head]
 
 
 def project(normed, grads, full_qkv, unit, heads, offset, count):
@@ -171,11 +172,10 @@
     groups = HEADS // heads
     width = count * HEAD
     steps = heads // count
-    rows = pl.BlockSpec((1, tokens, channels), lambda i, j, unit: (i, 0, 0))
 
     def columns(part):
         return pl.BlockSpec(
-            (channels, width), lambda i, j, unit: (0, (part * groups + (j ^ unit[0])) * steps + offset // count)
+            (channels, width), lambda j, unit: (0, (part * groups + (j ^ unit[0])) * steps + offset // count)
         )
 
     results = pl.pallas_call(
@@ -183,15 +183,15 @@
         out_shape=[jax.ShapeDtypeStruct((halves, tokens, PACK), jnp.bfloat16)] * (count * groups),
         grid_spec=pltpu.PrefetchScalarGridSpec(
             num_scalar_prefetch=1,
-            grid=(halves, groups),
+            grid=(groups,),
             in_specs=[
-                rows,
-                pl.BlockSpec((1, tokens, width), lambda i, j, unit: (i, 0, j ^ unit[0])),
+                pl.BlockSpec((halves, tokens, channels), lambda j, unit: (0, 0, 0)),
+                pl.BlockSpec((halves, tokens, width), lambda j, unit: (0, 0, j ^ unit[0])),
                 columns(0),
                 columns(1),
                 columns(2),
             ],
-            out_specs=[pl.BlockSpec((1, tokens, PACK), lambda i, j, unit: (i, 0, 0))] * (count * groups),
+            out_specs=[pl.BlockSpec((halves, tokens, PACK), lambda j, unit: (0, 0, 0))] * (count * groups),
         ),
         compiler_params=pltpu.CompilerParams(vmem_limit_bytes=VMEM),
         cost_estimate=pl.CostEstimate(
@@ -214,35 +214,77 @@
     return [[packed[head, flip] for flip in range(groups)] for head in range(count)]
 
 
-def weight_body(images, norm_ref, cot_ref, *refs):
-    grad_refs, o_ref = refs[:images], refs[images]
-    grads = jnp.concatenate([ref[0] for ref in grad_refs], axis=0)
-    split = lax.broadcasted_iota(jnp.int32, (1, PACK), 1) < 3 * HEAD
-    zero = jnp.bfloat16(0)
-    o_ref[...] = dot(norm_ref[...], jnp.where(split, grads, zero)) + dot(cot_ref[...], jnp.where(split, zero, grads))
-
-
-def weight_grads(normed_t, cotangent_t, grads, images):
+def weight_body(images, here_ref, norm_ref, cot_ref, grad_ref, *refs):
+    outs, (grads, total) = refs[:-2], refs[-2:]
+    groups, tokens = grad_ref.shape[0] // images, grad_ref.shape[1]
+    first = lax.broadcasted_iota(jnp.int32, (1, HALF), 1) < HEAD
+    split = groups * 3 * HEAD
+
+    @pl.when(pl.program_id(0) == 0)
+    def _():
+        for image in range(images):
+            rows = slice(image * tokens, (image + 1) * tokens)
+            for group in range(0, groups, 2):
+                pair = [grad_ref[image * groups + group + odd] for odd in range(2)]
+                for odd in range(2):
+                    grads[rows, (group + odd) * HALF : (group + odd + 1) * HALF] = pair[odd][:, 0:HALF]
+                left, right = (part[:, HALF:PACK].astype(jnp.float32) for part in pair)
+                query = groups * HALF + group * HEAD
+                grads[rows, query : query + HALF] = low(jnp.where(first, left, pltpu.roll(right, HEAD, 1)))
+                out = split + group * HEAD
+                grads[rows, out : out + HALF] = low(jnp.where(first, pltpu.roll(left, HEAD, 1), right))
+
+    total[:, 0:split] = dot(norm_ref[...], grads[:, 0:split])
+    total[:, split:] = dot(cot_ref[...], grads[:, split:])
+    rep, far, block, _ = outs[0].shape
+    for place in range(far):
+        for own, out in enumerate(outs):
+            for row in range(rep):
+                start = (place * rep * len(outs) + (here_ref[0] ^ (row * len(outs) + own))) * block
+                out[row, place] = low(total[pl.ds(pl.multiple_of(start, 8), block), :])
+
+
+def weight_grads(normed_t, cotangent_t, grads, here, images, near, far):
+    own = lax.axis_size("own")
     channels, rows = normed_t.shape
     groups = grads.shape[0] // images
     tokens = grads.shape[1]
-    whole = pl.BlockSpec((channels, rows), lambda g: (0, 0))
-
-    def block(image):
-        return pl.BlockSpec((1, tokens, PACK), lambda g: (image * groups + g, 0, 0))
-
+    steps = 2
+    part = channels // steps
+    block = channels // (near * far)
     return pl.pallas_call(
         functools.partial(weight_body, images),
-        out_shape=jax.ShapeDtypeStruct((channels, groups * PACK), jnp.float32),
-        grid=(groups,),
-        in_specs=[whole, whole] + [block(image) for image in range(images)],
-        out_specs=pl.BlockSpec((channels, PACK), lambda g: (0, g)),
+        out_shape=[jax.ShapeDtypeStruct((near // own, far, block, groups * PACK), jnp.bfloat16)] * own,
+        grid=(steps,),
+        in_specs=[
+            pl.BlockSpec(memory_space=pltpu.SMEM),
+            pl.BlockSpec((part, rows), lambda g: (g, 0)),
+            pl.BlockSpec((part, rows), lambda g: (g, 0)),
+            pl.BlockSpec(grads.shape, lambda g: (0, 0, 0)),
+        ],
+        out_specs=[pl.BlockSpec((near // own, far // steps, block, groups * PACK), lambda g: (0, g, 0, 0))] * own,
+        scratch_shapes=[
+            pltpu.VMEM((images * tokens, groups * PACK), jnp.bfloat16),
+            pltpu.VMEM((part, groups * PACK), jnp.float32),
+        ],
         compiler_params=pltpu.CompilerParams(vmem_limit_bytes=VMEM),
         cost_estimate=pl.CostEstimate(
-            flops=4 * channels * rows * groups * PACK, bytes_accessed=2**23, transcendentals=0
+            flops=2 * channels * rows * groups * PACK, bytes_accessed=2**23, transcendentals=0
         ),
         name="weight_grads",
-    )(normed_t, cotangent_t, *([grads] * images))
+    )(here, normed_t, cotangent_t, grads)
+
+
+def weight_grads_plain(normed_t, cotangent_t, grads, here, images, near, far):
+    channels, rows = normed_t.shape
+    groups, tokens = grads.shape[0] // images, grads.shape[1]
+    cut = grads.reshape(images, groups, tokens, 4, HEAD).transpose(0, 2, 1, 3, 4).reshape(rows, groups, 4, HEAD)
+    left = jnp.concatenate([cut[:, :, 0:2].reshape(rows, -1), cut[:, :, 2].reshape(rows, -1)], axis=1)
+    total = jnp.concatenate([dot(normed_t, left), dot(cotangent_t, cut[:, :, 3].reshape(rows, -1))], axis=1)
+    total = low(total).reshape(far, near, -1, groups * PACK)
+    parts = [lax.dynamic_index_in_dim(total, here[0] ^ flip, 1, keepdims=False) for flip in range(near)]
+    own = lax.axis_size("own")
+    return [jnp.stack(parts[flip::own]) for flip in range(own)]
 
 
 def gather_heads(parts, slot):
@@ -259,53 +301,116 @@
     return low(jnp.concatenate(pieces, axis=1))
 
 
-def back_body(heads, *refs):
-    grads, (wq_ref, wk_ref, wv_ref, wo_ref, mix_ref, norm_ref) = refs[:heads], refs[heads:]
-    g = pl.program_id(1)
-    parts = [ref[0].astype(jnp.float32) for ref in grads]
-    back = (
-        dot(gather_heads(parts, 2), wq_ref[...], NT)
-        + dot(gather_heads(parts, 0), wk_ref[...], NT)
-        + dot(gather_heads(parts, 1), wv_ref[...], NT)
-    )
+def back_body(count, steps, *refs):
+    grads = refs[:count]
+    wq_ref, wk_ref, wv_ref, wo_ref = refs[count : count + 4]
+    parts = [ref[...].reshape(-1, PACK).astype(jnp.float32) for ref in grads]
+    stacked = jnp.concatenate([gather_heads(parts, slot) for slot in (2, 0, 1)], axis=1)
+    weights = jnp.concatenate([wq_ref[...], wk_ref[...], wv_ref[...]], axis=1)
+    back = dot(stacked, weights, NT)
     mixed = dot(gather_heads(parts, 3), wo_ref[...])
+    g = pl.program_id(0)
+    if len(refs) == count + 6:
+        back_ref, mix_ref = refs[count + 4 :]
+
+        @pl.when(g == 0)
+        def _():
+            back_ref[...] = back
+            mix_ref[...] = mixed
+
+        @pl.when(g > 0)
+        def _():
+            back_ref[...] += back
+            mix_ref[...] += mixed
+
+        return
+    back_in, mix_in, row_ref, mean_ref, inv_ref, gain_ref, back_ref, mix_ref, sum_ref, mix = refs[count + 4 :]
 
     @pl.when(g == 0)
     def _():
-        norm_ref[0] = back
-        mix_ref[0] = mixed
+        back_ref[...] = back_in[...] + back
+        mix[...] = mix_in[...] + mixed
 
     @pl.when(g > 0)
     def _():
-        norm_ref[0] += back
-        mix_ref[0] += mixed
-
-
-def project_back(grads, full_qkv, full_out, images):
-    heads = len(grads)
+        back_ref[...] += back
+        mix[...] += mixed
+
+    @pl.when(g == steps - 1)
+    def _():
+        images, tokens, channels = row_ref.shape
+        size = min(64, tokens)
+        for image in range(images):
+            mean, inv, gain = mean_ref[image], inv_ref[image], gain_ref[...]
+
+            def piece(j, sums):
+                inner = pl.ds(pl.multiple_of(j * size, size), size)
+                outer = pl.ds(pl.multiple_of(image * tokens + j * size, size), size)
+                values = row_ref[image, inner, :].astype(jnp.float32)
+                mix_ref[image, inner, :] = low(values + mix[outer, :])
+                grad = back_ref[outer, :] * gain
+                return (
+                    sums[0] + eight_rows(grad, jnp.sum),
+                    sums[1] + eight_rows(grad * ((values - mean) * inv), jnp.sum),
+                )
+
+            zero = jnp.zeros((8, channels), jnp.float32)
+            sums = lax.fori_loop(0, tokens // size, piece, (zero, zero))
+            for kind in range(2):
+                sum_ref[kind, image] = jnp.sum(sums[kind], axis=0, keepdims=True)
+
+
+def project_back(grads, full_qkv, full_out, heads, offset, images, tail=None):
+    count = len(grads)
     groups = HEADS // heads
+    steps = heads // count
     tokens = grads[0].shape[1]
     channels = full_qkv.shape[0]
-    width = heads * HEAD
+    width = count * HEAD
 
     def columns(part):
-        return pl.BlockSpec((channels, width), lambda i, g: (0, part * groups + g))
-
-    rows = pl.BlockSpec((1, tokens, channels), lambda i, g: (i, 0, 0))
-    block = pl.BlockSpec((1, tokens, PACK), lambda i, g: (i * groups + g, 0, 0))
+        return pl.BlockSpec((channels, width), lambda g: (0, (part * groups + g) * steps + offset // count))
+
+    def whole(shape):
+        return pl.BlockSpec(shape, lambda g: (0,) * len(shape))
+
+    def once(shape):
+        return pl.BlockSpec(shape, lambda g: (0,) * len(shape), pipeline_mode=pl.Buffered(1))
+
+    flat = (images * tokens, channels)
+    shape = (images, tokens, channels)
+    line = (images, 1, channels)
+    in_specs = [pl.BlockSpec((images, 1, tokens, PACK), lambda g: (0, g, 0, 0))] * count + [
+        columns(0),
+        columns(1),
+        columns(2),
+        pl.BlockSpec((width, channels), lambda g: (g * steps + offset // count, 0)),
+    ]
+    operands = [grad.reshape(images, groups, tokens, PACK) for grad in grads] + [full_qkv] * 3 + [full_out]
+    out_shape = [jax.ShapeDtypeStruct(flat, jnp.float32)]
+    out_specs = [whole(flat)]
+    scratch = []
+    if tail is None:
+        out_shape, out_specs = out_shape * 2, out_specs * 2
+    else:
+        in_specs += [once(flat), once(flat), once(shape), whole(line), whole(line), whole((1, channels))]
+        operands += list(tail)
+        out_shape += [jax.ShapeDtypeStruct(shape, jnp.bfloat16), jax.ShapeDtypeStruct((2, *line), jnp.float32)]
+        out_specs += [whole(shape), whole((2, *line))]
+        scratch = [pltpu.VMEM(flat, jnp.float32)]
     return pl.pallas_call(
-        functools.partial(back_body, heads),
-        out_shape=[jax.ShapeDtypeStruct((images, tokens, channels), jnp.float32)] * 2,
-        grid=(images, groups),
-        in_specs=[block] * heads
-        + [columns(0), columns(1), columns(2), pl.BlockSpec((width, channels), lambda i, g: (g, 0))],
-        out_specs=[rows, rows],
+        functools.partial(back_body, count, groups),
+        out_shape=out_shape,
+        grid=(groups,),
+        in_specs=in_specs,
+        out_specs=out_specs,
+        scratch_shapes=scratch,
         compiler_params=pltpu.CompilerParams(vmem_limit_bytes=VMEM),
         cost_estimate=pl.CostEstimate(
-            flops=2 * images * tokens * channels * 4 * HEADS * HEAD, bytes_accessed=2**25, transcendentals=0
+            flops=2 * images * tokens * channels * 4 * groups * width, bytes_accessed=2**24, transcendentals=0
         ),
         name="project_back",
-    )(*grads, full_qkv, full_qkv, full_qkv, full_out)
+    )(*operands)
 
 
 def project_back_plain(grads, full_qkv, full_out, images):
@@ -325,21 +430,50 @@
     return lax.ppermute(array, axis, [(i, i ^ flip) for i in range(lax.axis_size(axis))])
 
 
-def sum_near(partial, seq_count):
-    rep, own = lax.axis_size("rep"), lax.axis_size("own")
-    columns = partial.shape[1]
-    cut = partial.reshape(seq_count, rep * own, -1, columns)
-    here = lax.axis_index("rep") * own + lax.axis_index("own")
-    total = lax.dynamic_index_in_dim(cut, here, 1, keepdims=False)
-    for flip in range(1, rep * own):
-        sent = low(lax.dynamic_index_in_dim(cut, here ^ flip, 1, keepdims=False))
-        total = total + flipped(sent, ("rep", "own"), flip).astype(jnp.float32)
-    return low(total)
-
-
-def sum_far(near):
-    pieces = lax.all_to_all(near, "seq", split_axis=0, concat_axis=0, tiled=True)
-    return jnp.sum(pieces.astype(jnp.float32), axis=0)
+def wide(array):
+    return array.astype(jnp.float32)
+
+
+def sum_near(parts, steps):
+    rep = parts[0].shape[0]
+    if steps == 1:
+        total = wide(parts[0][0])
+        for own, part in enumerate(parts):
+            for row in range(rep):
+                if own or row:
+                    total = total + wide(flipped(part[row], ("rep", "own"), row * len(parts) + own))
+        return total
+    total = wide(parts[0])
+    for own in range(1, len(parts)):
+        total = total + wide(flipped(parts[own], "own", own))
+    return total
+
+
+def sum_rep(total):
+    mine = total[0]
+    for row in range(1, total.shape[0]):
+        mine = mine + wide(flipped(low(total[row]), "rep", row))
+    return mine
+
+
+def sum_far(near, groups):
+    place = lax.axis_index("seq")
+    cut = near.reshape(2, groups, *near.shape[1:])
+
+    def pick(array, index, dim):
+        return lax.dynamic_index_in_dim(array, index, dim, keepdims=False)
+
+    total = pick(cut, place % groups, 1)
+    for flip in range(1, groups):
+        total = total + wide(flipped(low(pick(cut, (place % groups) ^ flip, 1)), "seq", flip))
+    half = place // groups
+    return pick(total, half, 0) + wide(flipped(low(pick(total, 1 - half, 0)), "seq", groups))
+
+
+def sum_seq(array):
+    for bit in reversed(range(lax.axis_size("seq").bit_length() - 1)):
+        array = array + flipped(array, "seq", 1 << bit)
+    return array
 
 
 def shards(latent, cotangent, norm_gain, norm_shift, proj_qkv, proj_out):
@@ -350,14 +484,20 @@
     total_count = tokens * seq_count * per_group
     groups = seq_count // images
     heads = HEADS // groups
-    aligned = heads * HEAD % HALF == 0
+    near = devices // seq_count
+    block = channels // devices
+    aligned = heads * HEAD % HALF == 0 and block % 8 == 0 and seq_count % 2 == 0
+    here = (lax.axis_index("rep") * lax.axis_size("own") + lax.axis_index("own")).astype(jnp.int32).reshape(1)
+
+    def weight_parts(grad):
+        kernel = weight_grads if aligned else weight_grads_plain
+        return kernel(normed_t, cotangent_t, grad, here, images, near, seq_count)
 
     full_qkv = lax.all_gather(proj_qkv, "own", axis=0, tiled=True)
     full_out = lax.all_gather(proj_out, "own", axis=0, tiled=True)
 
-    def group_sums(*arrays):
-        sums = jnp.stack([jnp.sum(a, axis=1).reshape(images, GROUPS, per_group).sum(axis=2) for a in arrays])
-        return lax.psum(sums, "seq") / total_count
+    def mean_groups(sums):
+        return sum_seq(sums.reshape(2, images, GROUPS, per_group).sum(axis=3)) / total_count
 
     def spread(array):
         return jnp.repeat(array, per_group, axis=1)[:, None, :]
@@ -381,10 +521,11 @@
     for offset in offsets:
         part = full_out.reshape(groups, heads, HEAD, channels)[:, offset : offset + count]
         part = part.reshape(groups * count * HEAD, channels)
-        grad_parts.append(swapped(low(jnp.einsum("itc,dc->itd", cot_rows, part, preferred_element_type=jnp.float32))))
+        grad_parts.append(low(jnp.einsum("itc,dc->itd", cot_rows, part, preferred_element_type=jnp.float32)))
 
     values = rows.astype(jnp.float32)
-    group_mean, group_meansq = group_sums(values, values * values)
+    sums = jnp.stack([jnp.sum(values, axis=1), jnp.sum(values * values, axis=1)])
+    group_mean, group_meansq = mean_groups(sums)
     group_inv = lax.rsqrt(group_meansq - group_mean * group_mean + EPS)
     mean, inv_std = spread(group_mean), spread(group_inv)
     centred = (values - mean) * inv_std
@@ -394,7 +535,10 @@
     work_normed = low((work - pick(mean, image)) * pick(inv_std, image) * norm_gain + norm_shift)
 
     sends = []
-    for offset, part in zip(offsets, grad_parts):
+    for index, offset in enumerate(offsets):
+        part = swapped(grad_parts[index])
+        if index + 1 < len(grad_parts):
+            part, grad_parts[index + 1] = lax.optimization_barrier((part, grad_parts[index + 1]))
         sends += (project if aligned else project_plain)(work_normed, part, full_qkv, unit, heads, offset, count)
     grads, nears = [], []
     result = None
@@ -408,37 +552,62 @@
         if head + 1 < heads:
             pieces, sends[head + 1] = lax.optimization_barrier((pieces, sends[head + 1]))
         if head >= 2:
-            partial = weight_grads(normed_t, cotangent_t, grads[head - 2], images)
-            pieces, partial, grads[head - 2] = lax.optimization_barrier((pieces, partial, grads[head - 2]))
-            nears.append(sum_near(partial, seq_count))
+            parts = weight_parts(grads[head - 2])
+            pieces, parts, grads[head - 2] = lax.optimization_barrier((pieces, parts, grads[head - 2]))
+            nears.append(sum_near(parts, 1))
         if head >= 3:
             pieces, nears[head - 3] = lax.optimization_barrier((pieces, nears[head - 3]))
         result = attend_pair(pieces, me)
     if heads > 1:
-        result, grads[-1] = lax.optimization_barrier((result, grads[-1]))
+        result, grads[-1], nears = lax.optimization_barrier((result, grads[-1], nears))
     grads.append(lax.all_to_all(result, "seq", split_axis=0, concat_axis=0, tiled=True))
-    for grad in grads[len(nears) :]:
-        nears.append(sum_near(weight_grads(normed_t, cotangent_t, grad, images), seq_count))
+    for index in range(len(nears), heads - 1):
+        nears.append(sum_rep(sum_near(weight_parts(grads[index]), 2)))
+    if aligned and heads > count:
+        back, mixed = project_back(grads[:count], full_qkv, full_out, heads, 0, images)
+        back, mixed, grads[-1], nears = lax.optimization_barrier((back, mixed, grads[-1], nears))
+    last = sum_near(weight_parts(grads[-1]), 2)
+    if heads > 1:
+        last, grads[-1], nears = lax.optimization_barrier((last, grads[-1], nears))
+    nears.append(sum_rep(last))
+    gain = norm_gain[None, :]
+    if aligned:
+        if heads == count:
+            back = mixed = jnp.zeros((images * tokens, channels), jnp.float32)
+        offset = heads - count
+        tail = (back, mixed, rows, mean, inv_std, gain)
+        back, mixed_out, sums = project_back(grads[offset:], full_qkv, full_out, heads, offset, images, tail)
+        back = back.reshape(images, tokens, channels)
+        sums = sums.reshape(2, images, channels)
+    else:
+        mixed, back = project_back_plain(grads, full_qkv, full_out, images)
+        mixed_out = low(values + mixed)
+        sums = jnp.stack([jnp.sum(back * norm_gain, axis=1), jnp.sum(back * norm_gain * centred, axis=1)])
+    sums, nears[-1] = lax.optimization_barrier((sums, nears[-1]))
     weight_sums = []
     if heads > 1:
-        early = sum_far(jnp.concatenate(nears[:-1], axis=2))
+        early = sum_far(jnp.concatenate(nears[:-1], axis=2), groups)
         early, nears[-1] = lax.optimization_barrier((early, nears[-1]))
         weight_sums = jnp.split(early, heads - 1, axis=1)
-    weight_sums.append(sum_far(nears[-1]))
-
-    mixed, back = (project_back if aligned else project_back_plain)(grads, full_qkv, full_out, images)
-    mixed_out = low(values + mixed).transpose(1, 0, 2)
-    grad_centred = back * norm_gain
-    mean_one, mean_two = group_sums(grad_centred, grad_centred * centred)
-    grad_values = inv_std * (grad_centred - spread(mean_one) - centred * spread(mean_two))
+    weight_sums.append(sum_far(nears[-1], groups))
+
+    mixed_out = mixed_out.transpose(1, 0, 2)
+    mean_one, mean_two = mean_groups(sums)
+    grad_values = inv_std * (back * norm_gain - spread(mean_one) - centred * spread(mean_two))
     grad_latent = low(cot_rows.astype(jnp.float32) + grad_values).transpose(1, 0, 2)
 
-    own_rows = channels // devices
-    summed = jnp.stack(weight_sums).reshape(heads, own_rows, groups, 4, HEAD)
-    summed = summed.transpose(1, 3, 2, 0, 4).reshape(own_rows, 4, HEADS * HEAD)
-    grad_qkv = jnp.concatenate([summed[:, 2], summed[:, 0], summed[:, 1]], axis=1)
+    summed = jnp.stack(weight_sums)
+    split = groups * HALF
+
+    def columns(part):
+        part = part.reshape(heads, block, groups, -1, HEAD).transpose(3, 1, 2, 0, 4)
+        return part.reshape(-1, block, HEADS * HEAD)
+
+    keys_values = columns(summed[:, :, :split])
+    queries_outs = [columns(part)[0] for part in jnp.split(summed[:, :, split:], 2, axis=2)]
+    grad_qkv = jnp.concatenate([queries_outs[0], keys_values[0], keys_values[1]], axis=1)
     out_rows = HEADS * HEAD // devices
-    pieces = summed[:, 3].reshape(own_rows, devices, out_rows).transpose(1, 2, 0)
+    pieces = queries_outs[1].reshape(block, devices, out_rows).transpose(1, 2, 0)
     pieces = lax.all_to_all(pieces, ALL, split_axis=0, concat_axis=0, tiled=True)
     grad_out = pieces.transpose(1, 0, 2).reshape(out_rows, channels)
     return (mixed_out, grad_latent, grad_qkv, grad_out)

time: 716 us -> 664 us (0.927)
  blocking collectives: 64.2 us -> 0 us
  waiting for transfers between devices: 92.7 us -> 119 us
  starting transfers between devices: 94.7 us -> 74.2 us
    psum x2 -> x0, blocking collectives: 64.2 us -> none  [group_sums(): return lax.psum(sums, 'seq') / total_count]
    add x0 -> x13, other arithmetic: none -> 15.1 us  [the longest x2 4.54 us: sum_near(): total + wide(flipped(part[row], ('rep', 'own'), row * len(parts) + own))]
    all_to_all x4, waiting for transfers between devices: 0.01 us -> 14.5 us  [shards(): lax.all_to_all(result, 'seq', split_axis=0, concat_axis=0, tiled=True)]
    ppermute x27 -> x39, waiting for transfers between devices: 83.5 us -> 97.4 us  [flipped(): lax.ppermute(array, axis, [(i, i ^ flip) for i in range(lax.axis_size(axi...]
    all_to_all x2 -> x0, starting transfers between devices: 9.77 us -> none  [sum_far(): lax.all_to_all(near, 'seq', split_axis=0, concat_axis=0, tiled=True)]
    pallas_call x5 -> x6, Pallas kernels: 63.5 us -> 73.2 us  [the longest x2 43.3 us: project_back(): pl.pallas_call(functools.partial(back_body, count, groups), out_shape=out...]
    all_to_all x4, starting transfers between devices: 31.9 us -> 22.2 us  [shards(): lax.all_to_all(result, 'seq', split_axis=0, concat_axis=0, tiled=True)]
    convert_element_type x4 -> x6, local copies, waits for them, and re-layouts: 11.8 us -> 2.64 us  [low(): return array.astype(jnp.bfloat16)]
  transfers between devices with their start and end apart: 36 -> 46, of which waited for: 8 -> 12; matrix products, arithmetic and copies ran while one was open for 10% -> 11% of each run, Pallas kernels for 50% -> 54%
where the time goes in v2:
time: 664 us; the launch traced here: 655 us
  Pallas kernels  361 us (54%)
  waiting for transfers between devices  119 us (18%)
  starting transfers between devices  74.2 us (11%)
  local copies, waits for them, and re-layouts  49.3 us (7%)
  other arithmetic  31.3 us (5%)
  between operations  15 us (2%)
    pallas_call x4, Pallas kernels, attend_pair(): pl.pallas_call(functools.partial(pair_body, bq, kb), out_shape=jax.ShapeD...  265 us
    ppermute x39, waiting for transfers between devices, flipped(): lax.ppermute(array, axis, [(i, i ^ flip) for i in range(lax.axis_size(axi...  97.4 us
    ppermute x39, starting transfers between devices, flipped(): lax.ppermute(array, axis, [(i, i ^ flip) for i in range(lax.axis_size(axi...  48.5 us
    pallas_call x2, Pallas kernels, project_back(): pl.pallas_call(functools.partial(back_body, count, groups), out_shape=out...  43.3 us
    pallas_call x4, Pallas kernels, weight_grads(): pl.pallas_call(functools.partial(weight_body, images), out_shape=[jax.Sha...  29.9 us
    pallas_call x2, Pallas kernels, project(): pl.pallas_call(functools.partial(project_body, count, groups), out_shape=...  22.8 us
    all_to_all x4, starting transfers between devices, shards(): lax.all_to_all(result, 'seq', split_axis=0, concat_axis=0, tiled=True)  22.2 us
    unnamed x75, local copies, waits for them, and re-layouts  20 us
  transfers between devices with their start and end apart: 46, of which 12 were waited for; matrix products, arithmetic and copies ran while one was open for 11% of the time, Pallas kernels for 54%

profile of v2, /device:TPU:0, one launch (start us, length us, event | category | flops | bytes accessed | tf_op | source)
XLA Modules:
  0.0 654.9 jit_solution(13484730474462833269)
XLA Ops:
  9.9 4.1 collective-permute-start.1
  14.0 1.8 copy.122
  15.8 3.4 dynamic-slice_bitcast_fusion.1
  19.2 1.9 collective-permute-start.2
  21.1 26.5 %collective-permute-done.2 = f32[2,2,32]{2,1,0:T(2,128)S(1)} collective-permute-done((f32[2,2,32]{2,1,0:T(2,128)S(1)}, f32[2,2,32]{2,1,0:T(2,128)S(1)}, u32[]{:S(2)}, u32[]{:S(2)}) %collective-permute-start.2) | collective-permute-done | bytes 544 | tf_op jit(solution)/shard_map/ppermute | solution.py:430
  47.7 1.5 collective-permute-start.3
  49.2 3.6 copy.78
  52.7 4.5 copy.80
  57.3 3.2 fusion.46
  60.4 1.5 fusion.15
  62.8 4.6 collective-permute-start.4
  68.1 3.7 fusion.18
  71.8 29.5 %collective-permute-done.4 = bf16[512,512]{1,0:T(8,128)(2,1)} collective-permute-done((bf16[512,512]{1,0:T(8,128)(2,1)}, bf16[512,512]{1,0:T(8,128)(2,1)}, u32[]{:S(2)}, u32[]{:S(2)}) %collective-permute-start.4) | collective-permute-done | bytes 524320 | tf_op jit(solution)/shard_map/ppermute | solution.py:430
  101.2 2.1 pad_maximum_fusion.1.grad_ref
  104.3 4.6 fusion.5
  108.9 4.4 copy.79
  113.3 11.4 %project.2 = (bf16[2,512,256]{2,1,0:T(8,128)(2,1)}, bf16[2,512,256]{2,1,0:T(8,128)(2,1)}, bf16[2,512,256]{2,1,0:T(8,128)(2,1)}, bf16[2,512,256]{2,1,0:T(8,128)(2...) custom-call(s32[1]{0:T(128)S(6)} %select_n.72.unit_ref, ...), custom_call_target="tpu_custom_call" | custom-call | flops 5368709120 | bytes 16777216 | tf_op jit(solution)/shard_map/project/pallas_call | solution.py:181
  126.2 1.7 collective-permute-start.6
  129.1 2.1 pad_maximum_fusion.2.grad_ref
  131.3 11.4 %project.3 = (bf16[2,512,256]{2,1,0:T(8,128)(2,1)}, bf16[2,512,256]{2,1,0:T(8,128)(2,1)}, bf16[2,512,256]{2,1,0:T(8,128)(2,1)}, bf16[2,512,256]{2,1,0:T(8,128)(2...) custom-call(s32[1]{0:T(128)S(6)} %select_n.72.unit_ref, ...), custom_call_target="tpu_custom_call" | custom-call | flops 5368709120 | bytes 16777216 | tf_op jit(solution)/shard_map/project/pallas_call | solution.py:181
  142.7 9.7 %collective-permute-done.7.refs_3_ = bf16[2,512,256]{2,1,0:T(8,128)(2,1)S(1)} collective-permute-done((bf16[2,512,256]{2,1,0:T(8,128)(2,1)}, bf16[2,512,256]{2,1,0:T(8,128)(2,1)S(1)}, u32[]{:S(2)}, u32[]{:S(2)}) %collective-permute-start.7) | collective-permute-done | bytes 524320 | tf_op jit(solution)/shard_map/ppermute | solution.py:430
  154.1 1.8 collective-permute-start.9
  155.9 66.6 %attend_pair.4 = bf16[8,512,256]{2,1,0:T(8,128)(2,1)} custom-call(s32[1]{0:T(128)} %bitcast.me_ref, bf16[2,512,256]{2,1,0:T(8,128)(2,1)} %get-tuple-element.135.refs_0_, bf16[2,512,256]{2,1,0:T(8,128)(2,1)} %copy-done.28, bf16[2,512,256]{2,1,0:T(8,128)(2,1)} %copy-done.29, bf16[2,512,256]{2,1,0:T(8,128)(2,1)} %copy-done.30), custom_call_target="tpu_custom_call" | custom-call | flops 51539607552 | bytes 4194304 | tf_op jit(solution)/shard_map/attend_pair/pallas_call | solution.py:123
  225.9 1.8 collective-permute-start.14
  227.6 3.6 all-to-all-start
  231.3 66.3 %attend_pair.5 = bf16[8,512,256]{2,1,0:T(8,128)(2,1)} custom-call(s32[1]{0:T(128)} %bitcast.me_ref, bf16[2,512,256]{2,1,0:T(8,128)(2,1)} %get-tuple-element.152.refs_0_, bf16[2,512,256]{2,1,0:T(8,128)(2,1)} %copy-done.32, bf16[2,512,256]{2,1,0:T(8,128)(2,1)} %copy-done.33, bf16[2,512,256]{2,1,0:T(8,128)(2,1)} %copy-done.31), custom_call_target="tpu_custom_call" | custom-call | flops 51539607552 | bytes 4194304 | tf_op jit(solution)/shard_map/attend_pair/pallas_call | solution.py:123
  297.6 1.9 collective-permute-start.15
  301.2 6.1 all-to-all-start.1
  307.3 7.5 %weight_grads.4 = (bf16[2,8,40,1024]{3,2,1,0:T(8,128)(2,1)}, bf16[2,8,40,1024]{3,2,1,0:T(8,128)(2,1)}) custom-call(s32[1]{0:T(128)} %bitcast.21.here_ref, bf16[1280,1024]{1,0:T(8,128)(2,1)} %bitcast.191, bf16[1280,1024]{1,0:T(8,128)(2,1)} %bitcast.187, bf16[8,512,256]{2,1,0:T(8,128)(2,1)} %copy-done.5), custom_call_target="tpu_custom_call" | custom-call | flops 2684354560 | bytes 8388608 | tf_op jit(solution)/shard_map/weight_grads/pallas_call | solution.py:255
  314.8 66.2 %attend_pair.6 = bf16[8,512,256]{2,1,0:T(8,128)(2,1)} custom-call(s32[1]{0:T(128)} %bitcast.me_ref, bf16[2,512,256]{2,1,0:T(8,128)(2,1)} %get-tuple-element.177.refs_0_, bf16[2,512,256]{2,1,0:T(8,128)(2,1)} %collective-permute-done.12.refs_1_, bf16[2,512,256]{2,1,0:T(8,128)(2,1)} %collective-permute-done.13.refs_2_, ...), custom_call_target="tpu_custom_call" | custom-call | flops 51539607552 | bytes 4194304 | tf_op jit(solution)/shard_map/attend_pair/pallas_call | solution.py:123
  381.3 1.6 collective-permute-start.20
  384.8 6.2 all-to-all-start.2
  391.0 7.5 %weight_grads.5 = (bf16[2,8,40,1024]{3,2,1,0:T(8,128)(2,1)}, bf16[2,8,40,1024]{3,2,1,0:T(8,128)(2,1)}) custom-call(s32[1]{0:T(128)} %bitcast.21.here_ref, bf16[1280,1024]{1,0:T(8,128)(2,1)} %bitcast.192, bf16[1280,1024]{1,0:T(8,128)(2,1)} %bitcast.188, bf16[8,512,256]{2,1,0:T(8,128)(2,1)} %all-to-all-done.1.grad_ref), custom_call_target="tpu_custom_call" | custom-call | flops 2684354560 | bytes 8388608 | tf_op jit(solution)/shard_map/weight_grads/pallas_call | solution.py:255
  398.5 1.5 slice_bitcast_fusion.2
  402.4 10.6 %collective-permute-done.18 = bf16[8,40,1024]{2,1,0:T(8,128)(2,1)} collective-permute-done((bf16[8,40,1024]{2,1,0:T(8,128)(2,1)}, bf16[8,40,1024]{2,1,0:T(8,128)(2,1)}, u32[]{:S(2)}, u32[]{:S(2)}) %collective-permute-start.18) | collective-permute-done | bytes 655392 | tf_op jit(solution)/shard_map/ppermute | solution.py:430
  413.1 1.9 fusion.25
  415.0 66.1 %attend_pair.7 = bf16[8,512,256]{2,1,0:T(8,128)(2,1)} custom-call(s32[1]{0:T(128)} %bitcast.me_ref, bf16[2,512,256]{2,1,0:T(8,128)(2,1)} %get-tuple-element.194.refs_0_, bf16[2,512,256]{2,1,0:T(8,128)(2,1)} %collective-permute-done.15.refs_1_, bf16[2,512,256]{2,1,0:T(8,128)(2,1)} %collective-permute-done.16.refs_2_, ...), custom_call_target="tpu_custom_call" | custom-call | flops 51539607552 | bytes 4194304 | tf_op jit(solution)/shard_map/attend_pair/pallas_call | solution.py:123
  481.1 2.6 fusion.23
  483.7 6.3 all-to-all-start.3
  490.0 7.4 %weight_grads.6 = (bf16[2,8,40,1024]{3,2,1,0:T(8,128)(2,1)}, bf16[2,8,40,1024]{3,2,1,0:T(8,128)(2,1)}) custom-call(s32[1]{0:T(128)} %bitcast.21.here_ref, bf16[1280,1024]{1,0:T(8,128)(2,1)} %bitcast.193, bf16[1280,1024]{1,0:T(8,128)(2,1)} %bitcast.189, bf16[8,512,256]{2,1,0:T(8,128)(2,1)} %copy-done.4), custom_call_target="tpu_custom_call" | custom-call | flops 2684354560 | bytes 8388608 | tf_op jit(solution)/shard_map/weight_grads/pallas_call | solution.py:255
  497.5 3.2 collective-permute-done.24
  500.7 1.8 convert_add_fusion.1
  502.7 1.5 collective-permute-start.25
  504.2 18.6 %project_back.2 = (f32[1024,1280]{1,0:T(8,128)}, f32[1024,1280]{1,0:T(8,128)}) custom-call(bf16[2,4,512,256]{3,2,1,0:T(8,128)(2,1)} %bitcast.183, bf16[2,4,512,256]{3,2,1,0:T(8,128)(2,1)} %bitcast.32.refs_1_, bf16[1280,3072]{1,0:T(8,128)(2,1)} %all-gather.5.cloned.1.call-done.wq_ref.wk_ref.wv_ref.refs_2_.refs_3_.refs_4_, ...), custom_call_target="tpu_custom_call" | custom-call | flops 5368709120 | bytes 16777216 | tf_op jit(solution)/shard_map/project_back/pallas_call | solution.py:401
  523.0 14.5 %all-to-all-done.3.grad_ref = bf16[8,512,256]{2,1,0:T(8,128)(2,1)} async-done(((bf16[8,512,256]{2,1,0:T(8,128)(2,1)}), bf16[8,512,256]{2,1,0:T(8,128)(2,1)}, u32[]{:S(2)}, u32[]{:S(2)}) %all-to-all-start.3) | async-done | bytes 2097184 | tf_op jit(solution)/shard_map/all_to_all | solution.py:563
  537.5 7.5 %weight_grads.7 = (bf16[2,8,40,1024]{3,2,1,0:T(8,128)(2,1)}, bf16[2,8,40,1024]{3,2,1,0:T(8,128)(2,1)}) custom-call(s32[1]{0:T(128)} %bitcast.21.here_ref, bf16[1280,1024]{1,0:T(8,128)(2,1)} %bitcast.194, bf16[1280,1024]{1,0:T(8,128)(2,1)} %bitcast.190, bf16[8,512,256]{2,1,0:T(8,128)(2,1)} %all-to-all-done.3.grad_ref), custom_call_target="tpu_custom_call" | custom-call | flops 2684354560 | bytes 8388608 | tf_op jit(solution)/shard_map/weight_grads/pallas_call | solution.py:255
  545.6 2.8 collective-permute-done.26
  548.3 2.3 convert_add_fusion
  550.8 1.5 collective-permute-start.27
  552.6 1.9 copy-done.3
  557.1 2.0 collective-permute-start.33
  559.1 24.7 %project_back.3 = (f32[1024,1280]{1,0:T(8,128)}, bf16[2,512,1280]{2,1,0:T(8,128)(2,1)}, f32[2,2,1,1280]{3,2,1,0:T(1,128)}) custom-call(bf16[2,4,512,256]{3,2,1,0:T(8,128)(2,1)} %bitcast.182, bf16[2,4,512,256]{3,2,1,0:T(8,128)(2,1)} %bitcast.35.refs_1_, bf16[1280,3072]{1,0:T(8,128)(2,1)} %all-gather.5.cloned.1.call-done.wq_ref.wk_ref.wv_ref.refs_2_.refs_3_.refs_4_, ...), custom_call_target="tpu_custom_call" | custom-call | flops 5368709120 | bytes 16777216 | tf_op jit(solution)/shard_map/project_back/pallas_call | solution.py:401
  584.7 2.4 bitcast_add_fusion
  587.5 4.2 copy.92
  591.8 2.0 collective-permute-start.29
  593.8 1.7 fusion.27
  597.0 2.7 collective-permute-start.34
  600.0 9.2 %collective-permute-done.34 = bf16[40,3072]{1,0:T(8,128)(2,1)S(1)} collective-permute-done((bf16[40,3072]{1,0:T(8,128)(2,1)S(1)}, bf16[40,3072]{1,0:T(8,128)(2,1)S(1)}, u32[]{:S(2)}, u32[]{:S(2)}) %collective-permute-start.34) | collective-permute-done | bytes 245792 | tf_op jit(solution)/shard_map/ppermute | solution.py:430
  612.7 2.4 collective-permute-start.37
  615.1 4.3 fusion.10
  619.4 4.2 copy.93
  625.7 4.7 collective-permute-done.38
  632.7 3.4 all-to-all-start.4
  639.2 5.5 all-to-all-done.4
  (198 shorter events, 40.0 us)
Async XLA Ops:
  7.2 50.1 %all-gather.3.cloned.1.call-start = ((), (), s32[]{:S(2)}) async-start(), calls=%async_computation.5 | async-start | bytes 3932160 | tf_op jit(solution)/shard_map/all_gather | solution.py:497
  7.9 105.4 %all-gather.5.cloned.1.call-start = ((), (), s32[]{:S(2)}) async-start(), calls=%async_computation.6 | async-start | bytes 11796480 | tf_op jit(solution)/shard_map/all_gather | solution.py:496
  9.9 9.3 %collective-permute-start.1 = (f32[2,2,32]{2,1,0:T(2,128)S(1)}, f32[2,2,32]{2,1,0:T(2,128)S(1)}, u32[]{:S(2)}, u32[]{:S(2)}) collective-permute-start(f32[2,2,32]{2,1,0:T(2,128)S(1)} %maximum_reduce_fusion), channel_id=1, source_target_pairs={{0,16},{4,20},{8,24},{12,28},{16,0},{20,4},{24,8},{28,12},{1,17},{... | collective-permute-start | bytes 1544 | tf_op jit(solution)/shard_map/ppermute | solution.py:430
  19.2 85.0 %collective-permute-start = (bf16[512,1280]{1,0:T(8,128)(2,1)}, bf16[512,1280]{1,0:T(8,128)(2,1)}, u32[]{:S(2)}, u32[]{:S(2)}) collective-permute-start(bf16[512,1280]{1,0:T(8,128)(2,1)} %get-tuple-element.262), channel_id=1, source_target_pairs={{0,16},{4,20},{8,24},{12,28},{16,0},{20,4},{24,8},{28,12},{1,17},{... | collective-permute-start | bytes 3932168 | tf_op jit(solution)/shard_map/ppermute | solution.py:430
  19.2 28.4 %collective-permute-start.2 = (f32[2,2,32]{2,1,0:T(2,128)S(1)}, f32[2,2,32]{2,1,0:T(2,128)S(1)}, u32[]{:S(2)}, u32[]{:S(2)}) collective-permute-start(f32[2,2,32]{2,1,0:T(2,128)S(1)} %add.159), channel_id=1, source_target_pairs={{0,8},{4,12},{8,0},{12,4},{16,24},{20,28},{24,16},{28,20},{1,9},{5... | collective-permute-start | bytes 1544 | tf_op jit(solution)/shard_map/ppermute | solution.py:430
  47.7 9.5 %collective-permute-start.3 = (f32[2,2,32]{2,1,0:T(2,128)S(1)}, f32[2,2,32]{2,1,0:T(2,128)S(1)}, u32[]{:S(2)}, u32[]{:S(2)}) collective-permute-start(f32[2,2,32]{2,1,0:T(2,128)S(1)} %add.160), channel_id=1, source_target_pairs={{0,4},{4,0},{8,12},{12,8},{16,20},{20,16},{24,28},{28,24},{1,5},{5... | collective-permute-start | bytes 1544 | tf_op jit(solution)/shard_map/ppermute | solution.py:430
  62.8 38.4 %collective-permute-start.4 = (bf16[512,512]{1,0:T(8,128)(2,1)}, bf16[512,512]{1,0:T(8,128)(2,1)}, u32[]{:S(2)}, u32[]{:S(2)}) collective-permute-start(bf16[512,512]{1,0:T(8,128)(2,1)} %get-tuple-element.273), channel_id=1, source_target_pairs={{0,16},{4,20},{8,24},{12,28},{16,0},{20,4},{24,8},{28,12},{1,17},{... | collective-permute-start | bytes 1572872 | tf_op jit(solution)/shard_map/ppermute | solution.py:430
  67.7 36.5 %copy-start.14 = (f32[2,1280]{1,0:T(2,128)}, f32[2,1280]{1,0:T(2,128)S(1)}, u32[]{:S(2)}) copy-start(f32[2,1280]{1,0:T(2,128)S(1)} %mul.72) | copy-start | bytes 30724
  68.0 36.3 %copy-start.16 = (f32[2,1280]{1,0:T(2,128)}, f32[2,1280]{1,0:T(2,128)S(1)}, u32[]{:S(2)}) copy-start(f32[2,1280]{1,0:T(2,128)S(1)} %sub.55) | copy-start | bytes 30724
  71.8 32.5 %copy-start.6 = (bf16[1,512,1280]{2,1,0:T(8,128)(2,1)S(1)}, bf16[1,512,1280]{2,1,0:T(8,128)(2,1)}, u32[]{:S(2)}) copy-start(bf16[1,512,1280]{2,1,0:T(8,128)(2,1)} %get-tuple-element.261) | copy-start | bytes 3932164
  71.8 32.5 %copy-start.18 = (f32[1280]{0:T(1024)S(1)}, f32[1280]{0:T(1024)}, u32[]{:S(2)}) copy-start(f32[1280]{0:T(1024)} %param.8) | copy-start | bytes 15364
  71.8 32.5 %copy-start.22 = (f32[1280]{0:T(1024)S(1)}, f32[1280]{0:T(1024)}, u32[]{:S(2)}) copy-start(f32[1280]{0:T(1024)} %param.9) | copy-start | bytes 15364
  104.3 24.9 %collective-permute-start.11 = (bf16[512,512]{1,0:T(8,128)(2,1)}, bf16[512,512]{1,0:T(8,128)(2,1)}, u32[]{:S(2)}, u32[]{:S(2)}) collective-permute-start(bf16[512,512]{1,0:T(8,128)(2,1)} %get-tuple-element.271), channel_id=1, source_target_pairs={{0,16},{4,20},{8,24},{12,28},{16,0},{20,4},{24,8},{28,12},{1,17},{... | collective-permute-start | bytes 1572872 | tf_op jit(solution)/shard_map/ppermute | solution.py:430
  124.7 17.9 %collective-permute-start.5 = (bf16[2,512,256]{2,1,0:T(8,128)(2,1)}, bf16[2,512,256]{2,1,0:T(8,128)(2,1)S(1)}, u32[]{:S(2)}, u32[]{:S(2)}) collective-permute-start(bf16[2,512,256]{2,1,0:T(8,128)(2,1)} %get-tuple-element.120), channel_id=1, source_target_pairs={{0,4},{4,0},{8,12},{12,8},{16,20},{20,16},{24,28},{28,24},{1,5},{5... | collective-permute-start | bytes 1572872 | tf_op jit(solution)/shard_map/ppermute | solution.py:430
  126.2 16.4 %collective-permute-start.6 = (bf16[2,512,256]{2,1,0:T(8,128)(2,1)}, bf16[2,512,256]{2,1,0:T(8,128)(2,1)S(1)}, u32[]{:S(2)}, u32[]{:S(2)}) collective-permute-start(bf16[2,512,256]{2,1,0:T(8,128)(2,1)} %get-tuple-element.121), channel_id=1, source_target_pairs={{0,8},{4,12},{8,0},{12,4},{16,24},{20,28},{24,16},{28,20},{1,9},{5... | collective-permute-start | bytes 1572872 | tf_op jit(solution)/shard_map/ppermute | solution.py:430
  128.0 24.4 %collective-permute-start.7 = (bf16[2,512,256]{2,1,0:T(8,128)(2,1)}, bf16[2,512,256]{2,1,0:T(8,128)(2,1)S(1)}, u32[]{:S(2)}, u32[]{:S(2)}) collective-permute-start(bf16[2,512,256]{2,1,0:T(8,128)(2,1)} %get-tuple-element.122), channel_id=1, source_target_pairs={{0,12},{4,8},{8,4},{12,0},{16,28},{20,24},{24,20},{28,16},{1,13},{... | collective-permute-start | bytes 1572872 | tf_op jit(solution)/shard_map/ppermute | solution.py:430
  131.2 21.2 %copy-start.27 = (bf16[2,512,256]{2,1,0:T(8,128)(2,1)S(1)}, bf16[2,512,256]{2,1,0:T(8,128)(2,1)}, u32[]{:S(2)}) copy-start(bf16[2,512,256]{2,1,0:T(8,128)(2,1)} %get-tuple-element.134) | copy-start | bytes 1572868
  131.2 22.4 %copy-start.26 = (bf16[2,512,256]{2,1,0:T(8,128)(2,1)S(1)}, bf16[2,512,256]{2,1,0:T(8,128)(2,1)}, u32[]{:S(2)}) copy-start(bf16[2,512,256]{2,1,0:T(8,128)(2,1)} %get-tuple-element.132) | copy-start | bytes 1572868
  131.2 22.9 %copy-start.25 = (bf16[2,512,256]{2,1,0:T(8,128)(2,1)S(1)}, bf16[2,512,256]{2,1,0:T(8,128)(2,1)}, u32[]{:S(2)}) copy-start(bf16[2,512,256]{2,1,0:T(8,128)(2,1)} %get-tuple-element.133) | copy-start | bytes 1572868
  142.6 13.3 %copy-start.28 = (bf16[2,512,256]{2,1,0:T(8,128)(2,1)}, bf16[2,512,256]{2,1,0:T(8,128)(2,1)S(1)}, u32[]{:S(2)}) copy-start(bf16[2,512,256]{2,1,0:T(8,128)(2,1)S(1)} %collective-permute-done.5.refs_1_) | copy-start | bytes 1572868
  142.7 13.3 %copy-start.29 = (bf16[2,512,256]{2,1,0:T(8,128)(2,1)}, bf16[2,512,256]{2,1,0:T(8,128)(2,1)S(1)}, u32[]{:S(2)}) copy-start(bf16[2,512,256]{2,1,0:T(8,128)(2,1)S(1)} %collective-permute-done.6.refs_2_) | copy-start | bytes 1572868
  152.4 70.1 %collective-permute-start.10 = (bf16[2,512,256]{2,1,0:T(8,128)(2,1)S(1)}, bf16[2,512,256]{2,1,0:T(8,128)(2,1)S(1)}, u32[]{:S(2)}, u32[]{:S(2)}) collective-permute-start(bf16[2,512,256]{2,1,0:T(8,128)(2,1)S(1)} %copy-done.27), channel_id=1, source_target_pairs={{0,12},{4,8},{8,4},{12,0},{16,28},{20,24},{24,20},{28,16},{1,13},{... | collective-permute-start | bytes 1572872 | tf_op jit(solution)/shard_map/ppermute | solution.py:430
  153.6 68.9 %collective-permute-start.8 = (bf16[2,512,256]{2,1,0:T(8,128)(2,1)S(1)}, bf16[2,512,256]{2,1,0:T(8,128)(2,1)S(1)}, u32[]{:S(2)}, u32[]{:S(2)}) collective-permute-start(bf16[2,512,256]{2,1,0:T(8,128)(2,1)S(1)} %copy-done.26), channel_id=1, source_target_pairs={{0,4},{4,0},{8,12},{12,8},{16,20},{20,16},{24,28},{28,24},{1,5},{5... | collective-permute-start | bytes 1572872 | tf_op jit(solution)/shard_map/ppermute | solution.py:430
  154.1 68.4 %collective-permute-start.9 = (bf16[2,512,256]{2,1,0:T(8,128)(2,1)S(1)}, bf16[2,512,256]{2,1,0:T(8,128)(2,1)S(1)}, u32[]{:S(2)}, u32[]{:S(2)}) collective-permute-start(bf16[2,512,256]{2,1,0:T(8,128)(2,1)S(1)} %copy-done.25), channel_id=1, source_target_pairs={{0,8},{4,12},{8,0},{12,4},{16,24},{20,28},{24,16},{28,20},{1,9},{5... | collective-permute-start | bytes 1572872 | tf_op jit(solution)/shard_map/ppermute | solution.py:430
  224.2 73.4 %collective-permute-start.12 = (bf16[2,512,256]{2,1,0:T(8,128)(2,1)}, bf16[2,512,256]{2,1,0:T(8,128)(2,1)}, u32[]{:S(2)}, u32[]{:S(2)}) collective-permute-start(bf16[2,512,256]{2,1,0:T(8,128)(2,1)} %get-tuple-element.149), channel_id=1, source_target_pairs={{0,4},{4,0},{8,12},{12,8},{16,20},{20,16},{24,28},{28,24},{1,5},{5... | collective-permute-start | bytes 1572872 | tf_op jit(solution)/shard_map/ppermute | solution.py:430
  224.7 72.9 %collective-permute-start.13 = (bf16[2,512,256]{2,1,0:T(8,128)(2,1)}, bf16[2,512,256]{2,1,0:T(8,128)(2,1)}, u32[]{:S(2)}, u32[]{:S(2)}) collective-permute-start(bf16[2,512,256]{2,1,0:T(8,128)(2,1)} %get-tuple-element.150), channel_id=1, source_target_pairs={{0,8},{4,12},{8,0},{12,4},{16,24},{20,28},{24,16},{28,20},{1,9},{5... | collective-permute-start | bytes 1572872 | tf_op jit(solution)/shard_map/ppermute | solution.py:430
  225.9 71.7 %collective-permute-start.14 = (bf16[2,512,256]{2,1,0:T(8,128)(2,1)}, bf16[2,512,256]{2,1,0:T(8,128)(2,1)}, u32[]{:S(2)}, u32[]{:S(2)}) collective-permute-start(bf16[2,512,256]{2,1,0:T(8,128)(2,1)} %get-tuple-element.151), channel_id=1, source_target_pairs={{0,12},{4,8},{8,4},{12,0},{16,28},{20,24},{24,20},{28,16},{1,13},{... | collective-permute-start | bytes 1572872 | tf_op jit(solution)/shard_map/ppermute | solution.py:430
  227.6 73.5 %all-to-all-start = ((bf16[8,512,256]{2,1,0:T(8,128)(2,1)}), bf16[8,512,256]{2,1,0:T(8,128)(2,1)S(1)}, u32[]{:S(2)}, u32[]{:S(2)}) async-start(bf16[8,512,256]{2,1,0:T(8,128)(2,1)} %attend_pair.4), calls=%async_computation | async-start | bytes 4194304 | tf_op jit(solution)/shard_map/all_to_all | solution.py:551
  231.3 68.3 %copy-start.24 = (bf16[2,512,256]{2,1,0:T(8,128)(2,1)S(1)}, bf16[2,512,256]{2,1,0:T(8,128)(2,1)}, u32[]{:S(2)}) copy-start(bf16[2,512,256]{2,1,0:T(8,128)(2,1)} %get-tuple-element.166) | copy-start | bytes 1572868
  231.3 69.8 %copy-start.23 = (bf16[2,512,256]{2,1,0:T(8,128)(2,1)S(1)}, bf16[2,512,256]{2,1,0:T(8,128)(2,1)}, u32[]{:S(2)}) copy-start(bf16[2,512,256]{2,1,0:T(8,128)(2,1)} %get-tuple-element.167) | copy-start | bytes 1572868
  297.6 83.4 %collective-permute-start.15 = (bf16[2,512,256]{2,1,0:T(8,128)(2,1)}, bf16[2,512,256]{2,1,0:T(8,128)(2,1)}, u32[]{:S(2)}, u32[]{:S(2)}) collective-permute-start(bf16[2,512,256]{2,1,0:T(8,128)(2,1)} %get-tuple-element.165), channel_id=1, source_target_pairs={{0,4},{4,0},{8,12},{12,8},{16,20},{20,16},{24,28},{28,24},{1,5},{5... | collective-permute-start | bytes 1572872 | tf_op jit(solution)/shard_map/ppermute | solution.py:430
  299.5 81.5 %collective-permute-start.16 = (bf16[2,512,256]{2,1,0:T(8,128)(2,1)S(1)}, bf16[2,512,256]{2,1,0:T(8,128)(2,1)}, u32[]{:S(2)}, u32[]{:S(2)}) collective-permute-start(bf16[2,512,256]{2,1,0:T(8,128)(2,1)S(1)} %copy-done.24), channel_id=1, source_target_pairs={{0,8},{4,12},{8,0},{12,4},{16,24},{20,28},{24,16},{28,20},{1,9},{5... | collective-permute-start | bytes 1572872 | tf_op jit(solution)/shard_map/ppermute | solution.py:430
  301.0 80.0 %collective-permute-start.17 = (bf16[2,512,256]{2,1,0:T(8,128)(2,1)S(1)}, bf16[2,512,256]{2,1,0:T(8,128)(2,1)}, u32[]{:S(2)}, u32[]{:S(2)}) collective-permute-start(bf16[2,512,256]{2,1,0:T(8,128)(2,1)S(1)} %copy-done.23), channel_id=1, source_target_pairs={{0,12},{4,8},{8,4},{12,0},{16,28},{20,24},{24,20},{28,16},{1,13},{... | collective-permute-start | bytes 1572872 | tf_op jit(solution)/shard_map/ppermute | solution.py:430
  301.2 83.6 %all-to-all-start.1 = ((bf16[8,512,256]{2,1,0:T(8,128)(2,1)}), bf16[8,512,256]{2,1,0:T(8,128)(2,1)}, u32[]{:S(2)}, u32[]{:S(2)}) async-start(bf16[8,512,256]{2,1,0:T(8,128)(2,1)} %attend_pair.5), calls=%async_computation.1 | async-start | bytes 4194304 | tf_op jit(solution)/shard_map/all_to_all | solution.py:551
  314.8 66.3 %copy-start.10 = (bf16[2,8,40,1024]{3,2,1,0:T(8,128)(2,1)S(1)}, bf16[2,8,40,1024]{3,2,1,0:T(8,128)(2,1)}, u32[]{:S(2)}) copy-start(bf16[2,8,40,1024]{3,2,1,0:T(8,128)(2,1)} %get-tuple-element.193) | copy-start | bytes 3932164
  381.2 20.2 %collective-permute-start.19 = (bf16[8,40,1024]{2,1,0:T(8,128)(2,1)S(1)}, bf16[8,40,1024]{2,1,0:T(8,128)(2,1)}, u32[]{:S(2)}, u32[]{:S(2)}) collective-permute-start(bf16[8,40,1024]{2,1,0:T(8,128)(2,1)S(1)} %get-tuple-element.268), channel_id=1, source_target_pairs={{0,1},{1,0},{2,3},{3,2},{4,5},{5,4},{6,7},{7,6},{8,9},{9,8},{10,11... | collective-permute-start | bytes 1966088 | tf_op jit(solution)/shard_map/ppermute | solution.py:430
  381.3 21.2 %collective-permute-start.20 = (bf16[8,40,1024]{2,1,0:T(8,128)(2,1)S(1)}, bf16[8,40,1024]{2,1,0:T(8,128)(2,1)}, u32[]{:S(2)}, u32[]{:S(2)}) collective-permute-start(bf16[8,40,1024]{2,1,0:T(8,128)(2,1)S(1)} %get-tuple-element.269), channel_id=1, source_target_pairs={{0,3},{1,2},{2,1},{3,0},{4,7},{5,6},{6,5},{7,4},{8,11},{9,10},{10,... | collective-permute-start | bytes 1966088 | tf_op jit(solution)/shard_map/ppermute | solution.py:430
  383.8 29.3 %collective-permute-start.18 = (bf16[8,40,1024]{2,1,0:T(8,128)(2,1)}, bf16[8,40,1024]{2,1,0:T(8,128)(2,1)}, u32[]{:S(2)}, u32[]{:S(2)}) collective-permute-start(bf16[8,40,1024]{2,1,0:T(8,128)(2,1)} %slice_bitcast_fusion.6), channel_id=1, source_target_pairs={{0,2},{1,3},{2,0},{3,1},{4,6},{5,7},{6,4},{7,5},{8,10},{9,11},{10,... | collective-permute-start | bytes 1966088 | tf_op jit(solution)/shard_map/ppermute | solution.py:430
  384.8 99.0 %all-to-all-start.2 = ((bf16[8,512,256]{2,1,0:T(8,128)(2,1)}), bf16[8,512,256]{2,1,0:T(8,128)(2,1)S(1)}, u32[]{:S(2)}, u32[]{:S(2)}) async-start(bf16[8,512,256]{2,1,0:T(8,128)(2,1)} %attend_pair.6), calls=%async_computation.2 | async-start | bytes 4194304 | tf_op jit(solution)/shard_map/all_to_all | solution.py:551
  398.5 14.6 %copy-start.12 = (bf16[2,8,40,1024]{3,2,1,0:T(8,128)(2,1)S(1)}, bf16[2,8,40,1024]{3,2,1,0:T(8,128)(2,1)}, u32[]{:S(2)}) copy-start(bf16[2,8,40,1024]{3,2,1,0:T(8,128)(2,1)} %get-tuple-element.192) | copy-start | bytes 3932164
  400.1 81.0 %collective-permute-start.22 = (bf16[8,40,1024]{2,1,0:T(8,128)(2,1)S(1)}, bf16[8,40,1024]{2,1,0:T(8,128)(2,1)S(1)}, u32[]{:S(2)}, u32[]{:S(2)}) collective-permute-start(bf16[8,40,1024]{2,1,0:T(8,128)(2,1)S(1)} %get-tuple-element.266), channel_id=1, source_target_pairs={{0,1},{1,0},{2,3},{3,2},{4,5},{5,4},{6,7},{7,6},{8,9},{9,8},{10,11... | collective-permute-start | bytes 1966088 | tf_op jit(solution)/shard_map/ppermute | solution.py:430
  400.2 81.0 %collective-permute-start.23 = (bf16[8,40,1024]{2,1,0:T(8,128)(2,1)S(1)}, bf16[8,40,1024]{2,1,0:T(8,128)(2,1)S(1)}, u32[]{:S(2)}, u32[]{:S(2)}) collective-permute-start(bf16[8,40,1024]{2,1,0:T(8,128)(2,1)S(1)} %get-tuple-element.267), channel_id=1, source_target_pairs={{0,3},{1,2},{2,1},{3,0},{4,7},{5,6},{6,5},{7,4},{8,11},{9,10},{10,... | collective-permute-start | bytes 1966088 | tf_op jit(solution)/shard_map/ppermute | solution.py:430
  401.4 79.7 %collective-permute-start.21 = (bf16[8,40,1024]{2,1,0:T(8,128)(2,1)S(1)}, bf16[8,40,1024]{2,1,0:T(8,128)(2,1)}, u32[]{:S(2)}, u32[]{:S(2)}) collective-permute-start(bf16[8,40,1024]{2,1,0:T(8,128)(2,1)S(1)} %slice_bitcast_fusion.3), channel_id=1, source_target_pairs={{0,2},{1,3},{2,0},{3,1},{4,6},{5,7},{6,4},{7,5},{8,10},{9,11},{10,... | collective-permute-start | bytes 1966088 | tf_op jit(solution)/shard_map/ppermute | solution.py:430
  483.7 53.7 %all-to-all-start.3 = ((bf16[8,512,256]{2,1,0:T(8,128)(2,1)}), bf16[8,512,256]{2,1,0:T(8,128)(2,1)}, u32[]{:S(2)}, u32[]{:S(2)}) async-start(bf16[8,512,256]{2,1,0:T(8,128)(2,1)} %attend_pair.7), calls=%async_computation.3 | async-start | bytes 4194304 | tf_op jit(solution)/shard_map/all_to_all | solution.py:563
  497.5 3.2 collective-permute-start.24
  502.7 20.1 %collective-permute-start.25 = (bf16[8,40,1024]{2,1,0:T(8,128)(2,1)S(1)}, bf16[8,40,1024]{2,1,0:T(8,128)(2,1)S(1)}, u32[]{:S(2)}, u32[]{:S(2)}) collective-permute-start(bf16[8,40,1024]{2,1,0:T(8,128)(2,1)S(1)} %fusion.28), channel_id=1, source_target_pairs={{0,2},{2,0},{1,3},{3,1},{4,6},{6,4},{5,7},{7,5},{8,10},{10,8},{9,1... | collective-permute-start | bytes 1966088 | tf_op jit(solution)/shard_map/ppermute | solution.py:430
  537.5 7.5 %copy-start.19 = (f32[1280]{0:T(1024)S(1)}, f32[1280]{0:T(1024)}, u32[]{:S(2)}) copy-start(f32[1280]{0:T(1024)} %param.8) | copy-start | bytes 15364
  545.0 3.4 collective-permute-start.26
  550.8 33.9 %collective-permute-start.27 = (bf16[8,40,1024]{2,1,0:T(8,128)(2,1)S(1)}, bf16[8,40,1024]{2,1,0:T(8,128)(2,1)}, u32[]{:S(2)}, u32[]{:S(2)}) collective-permute-start(bf16[8,40,1024]{2,1,0:T(8,128)(2,1)S(1)} %fusion.29), channel_id=1, source_target_pairs={{0,2},{2,0},{1,3},{3,1},{4,6},{6,4},{5,7},{7,5},{8,10},{10,8},{9,1... | collective-permute-start | bytes 1966088 | tf_op jit(solution)/shard_map/ppermute | solution.py:430
  555.6 38.2 %collective-permute-start.31 = (bf16[2,40,3072]{2,1,0:T(8,128)(2,1)}, bf16[2,40,3072]{2,1,0:T(8,128)(2,1)S(1)}, u32[]{:S(2)}, u32[]{:S(2)}) collective-permute-start(bf16[2,40,3072]{2,1,0:T(8,128)(2,1)} %get-tuple-element.254), channel_id=1, source_target_pairs={{0,4},{4,0},{8,12},{12,8},{16,20},{20,16},{24,28},{28,24},{1,5},{5... | collective-permute-start | bytes 1474568 | tf_op jit(solution)/shard_map/ppermute | solution.py:430
  557.1 36.8 %collective-permute-start.32 = (bf16[2,40,3072]{2,1,0:T(8,128)(2,1)}, bf16[2,40,3072]{2,1,0:T(8,128)(2,1)}, u32[]{:S(2)}, u32[]{:S(2)}) collective-permute-start(bf16[2,40,3072]{2,1,0:T(8,128)(2,1)} %get-tuple-element.255), channel_id=1, source_target_pairs={{0,8},{4,12},{8,0},{12,4},{16,24},{20,28},{24,16},{28,20},{1,9},{5... | collective-permute-start | bytes 1474568 | tf_op jit(solution)/shard_map/ppermute | solution.py:430
  557.1 36.8 %collective-permute-start.33 = (bf16[2,40,3072]{2,1,0:T(8,128)(2,1)}, bf16[2,40,3072]{2,1,0:T(8,128)(2,1)}, u32[]{:S(2)}, u32[]{:S(2)}) collective-permute-start(bf16[2,40,3072]{2,1,0:T(8,128)(2,1)} %get-tuple-element.256), channel_id=1, source_target_pairs={{0,12},{4,8},{8,4},{12,0},{16,28},{20,24},{24,20},{28,16},{1,13},{... | collective-permute-start | bytes 1474568 | tf_op jit(solution)/shard_map/ppermute | solution.py:430
  587.2 4.5 collective-permute-start.28
  591.8 23.3 %copy-start.1 = (bf16[512,2,1280]{2,1,0:T(2,128)(2,1)S(1)}, bf16[512,2,1280]{2,1,0:T(2,128)(2,1)}, u32[]{:S(2)}) copy-start(bf16[512,2,1280]{2,1,0:T(2,128)(2,1)} %param.6) | copy-start | bytes 7864324
  591.8 23.3 %copy-start.15 = (f32[2,1280]{1,0:T(2,128)S(1)}, f32[2,1280]{1,0:T(2,128)}, u32[]{:S(2)}) copy-start(f32[2,1280]{1,0:T(2,128)} %copy-done.14) | copy-start | bytes 30724
  591.8 23.3 %copy-start.17 = (f32[2,1280]{1,0:T(2,128)S(1)}, f32[2,1280]{1,0:T(2,128)}, u32[]{:S(2)}) copy-start(f32[2,1280]{1,0:T(2,128)} %copy-done.16) | copy-start | bytes 30724
  591.8 3.8 collective-permute-start.29
  595.6 4.1 collective-permute-start.30
  597.0 12.3 %collective-permute-start.34 = (bf16[40,3072]{1,0:T(8,128)(2,1)S(1)}, bf16[40,3072]{1,0:T(8,128)(2,1)S(1)}, u32[]{:S(2)}, u32[]{:S(2)}) collective-permute-start(bf16[40,3072]{1,0:T(8,128)(2,1)S(1)} %fusion.35), channel_id=1, source_target_pairs={{0,16},{4,20},{8,24},{12,28},{16,0},{20,4},{24,8},{28,12},{1,17},{... | collective-permute-start | bytes 737288 | tf_op jit(solution)/shard_map/ppermute | solution.py:430
  611.5 12.1 %collective-permute-start.35 = (bf16[2,40,1024]{2,1,0:T(8,128)(2,1)S(1)}, bf16[2,40,1024]{2,1,0:T(8,128)(2,1)S(1)}, u32[]{:S(2)}, u32[]{:S(2)}) collective-permute-start(bf16[2,40,1024]{2,1,0:T(8,128)(2,1)S(1)} %get-tuple-element.263), channel_id=1, source_target_pairs={{0,4},{4,0},{8,12},{12,8},{16,20},{20,16},{24,28},{28,24},{1,5},{5... | collective-permute-start | bytes 491528 | tf_op jit(solution)/shard_map/ppermute | solution.py:430
  612.7 10.9 %collective-permute-start.36 = (bf16[2,40,1024]{2,1,0:T(8,128)(2,1)S(1)}, bf16[2,40,1024]{2,1,0:T(8,128)(2,1)S(1)}, u32[]{:S(2)}, u32[]{:S(2)}) collective-permute-start(bf16[2,40,1024]{2,1,0:T(8,128)(2,1)S(1)} %get-tuple-element.264), channel_id=1, source_target_pairs={{0,8},{4,12},{8,0},{12,4},{16,24},{20,28},{24,16},{28,20},{1,9},{5... | collective-permute-start | bytes 491528 | tf_op jit(solution)/shard_map/ppermute | solution.py:430
  612.7 10.9 %collective-permute-start.37 = (bf16[2,40,1024]{2,1,0:T(8,128)(2,1)S(1)}, bf16[2,40,1024]{2,1,0:T(8,128)(2,1)S(1)}, u32[]{:S(2)}, u32[]{:S(2)}) collective-permute-start(bf16[2,40,1024]{2,1,0:T(8,128)(2,1)S(1)} %get-tuple-element.265), channel_id=1, source_target_pairs={{0,12},{4,8},{8,4},{12,0},{16,28},{20,24},{24,20},{28,16},{1,13},{... | collective-permute-start | bytes 491528 | tf_op jit(solution)/shard_map/ppermute | solution.py:430
  624.7 5.7 collective-permute-start.38
  632.7 12.0 %all-to-all-start.4 = ((f32[32,1,1280]{2,1,0:T(1,128)}), f32[32,1,1280]{2,1,0:T(1,128)S(1)}, u32[]{:S(2)}, u32[]{:S(2)}) async-start(f32[32,1,1280]{2,1,0:T(1,128)} %reshape.130), calls=%async_computation.4 | async-start | bytes 327680 | tf_op jit(solution)/shard_map/all_to_all | solution.py:611
  (16 other events, 47.0 us)
Sparse Core Ops, SparseCore 0:
  9.6 14.0 all-gather.2
  25.2 20.2 all-gather.4

commit v3 on v2

--- a/solution.py
+++ b/solution.py
@@ -146,19 +146,18 @@
     return piece if head % 2 == slot % 2 else pltpu.roll(piece, HEAD, 1)
 
 
-def project_body(count, groups, unit_ref, norm_ref, grad_ref, wq_ref, wk_ref, wv_ref, *outs):
+def project_body(count, groups, unit_ref, here_ref, there_ref, grad_here, grad_there, wq_ref, wk_ref, wv_ref, *outs):
     first = lax.broadcasted_iota(jnp.int32, (1, HALF), 1) < HEAD
     width = count * HEAD
-    halves, tokens, channels = norm_ref.shape
     weights = jnp.concatenate([wq_ref[...], wk_ref[...], wv_ref[...]], axis=1)
-    projected = dot(norm_ref[...].reshape(halves * tokens, channels), weights)
+    projected = dot(jnp.concatenate([here_ref[...], there_ref[...]], axis=0), weights)
     query, key, value = (projected[:, part * width : (part + 1) * width] for part in range(3))
-    grad = grad_ref[...].reshape(halves * tokens, width).astype(jnp.float32)
+    grad = jnp.concatenate([grad_here[...], grad_there[...]], axis=0).astype(jnp.float32)
     packs = []
     for head in range(count):
         left = jnp.where(first, lane_piece(key, head, 0), lane_piece(value, head, 1))
         right = jnp.where(first, lane_piece(query, head, 0), lane_piece(grad, head, 1))
-        packs.append(low(jnp.concatenate([left, right], axis=1)).reshape(halves, tokens, PACK))
+        packs.append(low(jnp.concatenate([left, right], axis=1)).reshape(2, -1, PACK))
     for flip in range(groups):
 
         @pl.when(pl.program_id(0) == flip)
@@ -168,14 +167,14 @@
 
 
 def project(normed, grads, full_qkv, unit, heads, offset, count):
-    halves, tokens, channels = normed.shape
+    halves, (tokens, channels) = len(normed), normed[0].shape
     groups = HEADS // heads
     width = count * HEAD
     steps = heads // count
 
-    def columns(part):
+    def columns(kind):
         return pl.BlockSpec(
-            (channels, width), lambda j, unit: (0, (part * groups + (j ^ unit[0])) * steps + offset // count)
+            (channels, width), lambda j, unit: (0, (kind * groups + (j ^ unit[0])) * steps + offset // count)
         )
 
     results = pl.pallas_call(
@@ -185,8 +184,10 @@
             num_scalar_prefetch=1,
             grid=(groups,),
             in_specs=[
-                pl.BlockSpec((halves, tokens, channels), lambda j, unit: (0, 0, 0)),
-                pl.BlockSpec((halves, tokens, width), lambda j, unit: (0, 0, j ^ unit[0])),
+                pl.BlockSpec((tokens, channels), lambda j, unit: (0, 0)),
+                pl.BlockSpec((tokens, channels), lambda j, unit: (0, 0)),
+                pl.BlockSpec((tokens, width), lambda j, unit: (0, j ^ unit[0])),
+                pl.BlockSpec((tokens, width), lambda j, unit: (0, j ^ unit[0])),
                 columns(0),
                 columns(1),
                 columns(2),
@@ -195,14 +196,15 @@
         ),
         compiler_params=pltpu.CompilerParams(vmem_limit_bytes=VMEM),
         cost_estimate=pl.CostEstimate(
-            flops=2 * halves * tokens * channels * 4 * groups * width, bytes_accessed=2**24, transcendentals=0
+            flops=2 * halves * tokens * channels * groups * width, bytes_accessed=2**16, transcendentals=0
         ),
         name="project",
-    )(unit, normed, grads, full_qkv, full_qkv, full_qkv)
+    )(unit, *normed, *grads, full_qkv, full_qkv, full_qkv)
     return [results[head * groups : (head + 1) * groups] for head in range(count)]
 
 
 def project_plain(normed, grads, full_qkv, unit, heads, offset, count):
+    normed, grads = jnp.stack(normed), jnp.stack(grads)
     halves, tokens, channels = normed.shape
     groups = HEADS // heads
     qkv = low(jnp.einsum("itc,cd->itd", normed, full_qkv, preferred_element_type=jnp.float32))
@@ -301,116 +303,94 @@
     return low(jnp.concatenate(pieces, axis=1))
 
 
-def back_body(count, steps, *refs):
-    grads = refs[:count]
-    wq_ref, wk_ref, wv_ref, wo_ref = refs[count : count + 4]
-    parts = [ref[...].reshape(-1, PACK).astype(jnp.float32) for ref in grads]
-    stacked = jnp.concatenate([gather_heads(parts, slot) for slot in (2, 0, 1)], axis=1)
-    weights = jnp.concatenate([wq_ref[...], wk_ref[...], wv_ref[...]], axis=1)
-    back = dot(stacked, weights, NT)
-    mixed = dot(gather_heads(parts, 3), wo_ref[...])
-    g = pl.program_id(0)
-    if len(refs) == count + 6:
-        back_ref, mix_ref = refs[count + 4 :]
-
-        @pl.when(g == 0)
-        def _():
-            back_ref[...] = back
-            mix_ref[...] = mixed
-
-        @pl.when(g > 0)
-        def _():
-            back_ref[...] += back
-            mix_ref[...] += mixed
-
+def back_body(offset, heads, *refs):
+    refs, (stacked, attended) = refs[:-2], refs[-2:]
+    count = len(refs) - 4 if len(refs) < 12 else len(refs) - 11
+    grads, refs = refs[:count], refs[count:]
+    qkv_ref, out_ref = refs[:2]
+    images_groups, tokens, _ = grads[0].shape
+    groups = HEADS // heads
+    images = images_groups // groups
+    width = count * HEAD
+
+    @pl.when(pl.program_id(0) == 0)
+    def _():
+        for image in range(images):
+            rows = slice(image * tokens, (image + 1) * tokens)
+            for group in range(groups):
+                parts = [wide(ref[image * groups + group]) for ref in grads]
+                attended[rows, group * width : (group + 1) * width] = gather_heads(parts, 3)
+                for kind, slot in enumerate((2, 0, 1)):
+                    start = (kind * groups + group) * width
+                    stacked[rows, start : start + width] = gather_heads(parts, slot)
+
+    starts = [group * heads * HEAD + offset * HEAD for group in range(groups)]
+    inner = HEADS * HEAD
+    weights = [qkv_ref[:, kind * inner + start :][:, :width] for kind in range(3) for start in starts]
+    back = dot(stacked[...], jnp.concatenate(weights, axis=1), NT)
+    mixed = dot(attended[...], jnp.concatenate([out_ref[start : start + width, :] for start in starts], axis=0))
+    if len(refs) == 4:
+        refs[2][...] = back
+        refs[3][...] = mixed
         return
-    back_in, mix_in, row_ref, mean_ref, inv_ref, gain_ref, back_ref, mix_ref, sum_ref, mix = refs[count + 4 :]
-
-    @pl.when(g == 0)
-    def _():
-        back_ref[...] = back_in[...] + back
-        mix[...] = mix_in[...] + mixed
-
-    @pl.when(g > 0)
-    def _():
-        back_ref[...] += back
-        mix[...] += mixed
-
-    @pl.when(g == steps - 1)
-    def _():
-        images, tokens, channels = row_ref.shape
-        size = min(64, tokens)
-        for image in range(images):
-            mean, inv, gain = mean_ref[image], inv_ref[image], gain_ref[...]
-
-            def piece(j, sums):
-                inner = pl.ds(pl.multiple_of(j * size, size), size)
-                outer = pl.ds(pl.multiple_of(image * tokens + j * size, size), size)
-                values = row_ref[image, inner, :].astype(jnp.float32)
-                mix_ref[image, inner, :] = low(values + mix[outer, :])
-                grad = back_ref[outer, :] * gain
-                return (
-                    sums[0] + eight_rows(grad, jnp.sum),
-                    sums[1] + eight_rows(grad * ((values - mean) * inv), jnp.sum),
-                )
-
-            zero = jnp.zeros((8, channels), jnp.float32)
-            sums = lax.fori_loop(0, tokens // size, piece, (zero, zero))
-            for kind in range(2):
-                sum_ref[kind, image] = jnp.sum(sums[kind], axis=0, keepdims=True)
+    back_in, mix_in, row_ref, mean_ref, inv_ref, gain_ref, back_ref, mix_ref, sum_ref = refs[2:]
+    back = back + back_in[...]
+    mixed = mixed + mix_in[...]
+    back_ref[...] = back
+    for image in range(images):
+        rows = slice(image * tokens, (image + 1) * tokens)
+        values = wide(row_ref[image])
+        mix_ref[image] = low(values + mixed[rows])
+        grad = back[rows] * gain_ref[...]
+        centred = (values - mean_ref[image]) * inv_ref[image]
+        sum_ref[0, image] = jnp.sum(grad, axis=0, keepdims=True)
+        sum_ref[1, image] = jnp.sum(grad * centred, axis=0, keepdims=True)
 
 
 def project_back(grads, full_qkv, full_out, heads, offset, images, tail=None):
     count = len(grads)
     groups = HEADS // heads
-    steps = heads // count
     tokens = grads[0].shape[1]
-    channels = full_qkv.shape[0]
-    width = count * HEAD
-
-    def columns(part):
-        return pl.BlockSpec((channels, width), lambda g: (0, (part * groups + g) * steps + offset // count))
-
-    def whole(shape):
-        return pl.BlockSpec(shape, lambda g: (0,) * len(shape))
-
-    def once(shape):
-        return pl.BlockSpec(shape, lambda g: (0,) * len(shape), pipeline_mode=pl.Buffered(1))
-
-    flat = (images * tokens, channels)
-    shape = (images, tokens, channels)
-    line = (images, 1, channels)
-    in_specs = [pl.BlockSpec((images, 1, tokens, PACK), lambda g: (0, g, 0, 0))] * count + [
-        columns(0),
-        columns(1),
-        columns(2),
-        pl.BlockSpec((width, channels), lambda g: (g * steps + offset // count, 0)),
+    channels, columns = full_qkv.shape
+    step = 256 if channels % 256 == 0 else channels
+    flat = (images * tokens, step)
+    line = (images, 1, step)
+
+    def across(shape):
+        return pl.BlockSpec(shape, lambda n: (0,) * (len(shape) - 1) + (n,))
+
+    in_specs = [pl.BlockSpec(grads[0].shape, lambda n: (0, 0, 0))] * count + [
+        pl.BlockSpec((step, columns), lambda n: (n, 0)),
+        across((HEADS * HEAD, step)),
     ]
-    operands = [grad.reshape(images, groups, tokens, PACK) for grad in grads] + [full_qkv] * 3 + [full_out]
-    out_shape = [jax.ShapeDtypeStruct(flat, jnp.float32)]
-    out_specs = [whole(flat)]
-    scratch = []
+    out_shape = [jax.ShapeDtypeStruct((images * tokens, channels), jnp.float32)]
+    out_specs = [across(flat)]
     if tail is None:
         out_shape, out_specs = out_shape * 2, out_specs * 2
     else:
-        in_specs += [once(flat), once(flat), once(shape), whole(line), whole(line), whole((1, channels))]
-        operands += list(tail)
-        out_shape += [jax.ShapeDtypeStruct(shape, jnp.bfloat16), jax.ShapeDtypeStruct((2, *line), jnp.float32)]
-        out_specs += [whole(shape), whole((2, *line))]
-        scratch = [pltpu.VMEM(flat, jnp.float32)]
+        rows = across((images, tokens, step))
+        in_specs += [across(flat), across(flat), rows, across(line), across(line), across((1, step))]
+        out_shape += [
+            jax.ShapeDtypeStruct((images, tokens, channels), jnp.bfloat16),
+            jax.ShapeDtypeStruct((2, images, 1, channels), jnp.float32),
+        ]
+        out_specs += [rows, across((2, *line))]
     return pl.pallas_call(
-        functools.partial(back_body, count, groups),
+        functools.partial(back_body, offset, heads),
         out_shape=out_shape,
-        grid=(groups,),
+        grid=(channels // step,),
         in_specs=in_specs,
         out_specs=out_specs,
-        scratch_shapes=scratch,
+        scratch_shapes=[
+            pltpu.VMEM((images * tokens, 3 * groups * count * HEAD), jnp.bfloat16),
+            pltpu.VMEM((images * tokens, groups * count * HEAD), jnp.bfloat16),
+        ],
         compiler_params=pltpu.CompilerParams(vmem_limit_bytes=VMEM),
         cost_estimate=pl.CostEstimate(
-            flops=2 * images * tokens * channels * 4 * groups * width, bytes_accessed=2**24, transcendentals=0
+            flops=2 * images * tokens * channels * 4 * groups * count * HEAD, bytes_accessed=2**24, transcendentals=0
         ),
         name="project_back",
-    )(*operands)
+    )(*grads, full_qkv, full_out, *(tail or ()))
 
 
 def project_back_plain(grads, full_qkv, full_out, images):
@@ -428,6 +408,10 @@
 
 def flipped(array, axis, flip):
     return lax.ppermute(array, axis, [(i, i ^ flip) for i in range(lax.axis_size(axis))])
+
+
+def after(value, *others):
+    return lax.optimization_barrier((value, others))[0]
 
 
 def wide(array):
@@ -470,8 +454,11 @@
     return pick(total, half, 0) + wide(flipped(low(pick(total, 1 - half, 0)), "seq", groups))
 
 
-def sum_seq(array):
-    for bit in reversed(range(lax.axis_size("seq").bit_length() - 1)):
+def sum_seq(array, hold=()):
+    bits = lax.axis_size("seq").bit_length() - 1
+    for bit in range(bits):
+        if bit == bits - 1:
+            array = after(array, hold)
         array = array + flipped(array, "seq", 1 << bit)
     return array
 
@@ -496,8 +483,8 @@
     full_qkv = lax.all_gather(proj_qkv, "own", axis=0, tiled=True)
     full_out = lax.all_gather(proj_out, "own", axis=0, tiled=True)
 
-    def mean_groups(sums):
-        return sum_seq(sums.reshape(2, images, GROUPS, per_group).sum(axis=3)) / total_count
+    def mean_groups(sums, hold=()):
+        return sum_seq(sums.reshape(2, images, GROUPS, per_group).sum(axis=3), hold) / total_count
 
     def spread(array):
         return jnp.repeat(array, per_group, axis=1)[:, None, :]
@@ -510,11 +497,10 @@
         return lax.dynamic_index_in_dim(array, index, 0, keepdims=False)
 
     def swapped(array):
-        return jnp.stack([pick(array, image), flipped(pick(array, 1 - image), "seq", groups)])
+        return [pick(array, image), flipped(pick(array, 1 - image), "seq", groups)]
 
     rows = latent.transpose(1, 0, 2)
     cot_rows = cotangent.transpose(1, 0, 2)
-    work = swapped(rows).astype(jnp.float32)
     count = 2 if aligned else heads
     offsets = range(0, heads, count)
     grad_parts = []
@@ -522,53 +508,52 @@
         part = full_out.reshape(groups, heads, HEAD, channels)[:, offset : offset + count]
         part = part.reshape(groups * count * HEAD, channels)
         grad_parts.append(low(jnp.einsum("itc,dc->itd", cot_rows, part, preferred_element_type=jnp.float32)))
+    work = swapped(rows)
+    first_grad = grad_parts[0]
+    grad_parts[0] = swapped(grad_parts[0])
+    grad_parts[1:] = [swapped(after(part, grad_parts[0])) for part in grad_parts[1:]]
 
     values = rows.astype(jnp.float32)
     sums = jnp.stack([jnp.sum(values, axis=1), jnp.sum(values * values, axis=1)])
-    group_mean, group_meansq = mean_groups(sums)
+    group_mean, group_meansq = mean_groups(sums, first_grad)
     group_inv = lax.rsqrt(group_meansq - group_mean * group_mean + EPS)
     mean, inv_std = spread(group_mean), spread(group_inv)
     centred = (values - mean) * inv_std
     normed = low(centred * norm_gain + norm_shift)
     normed_t = normed.reshape(images * tokens, channels).T
     cotangent_t = cot_rows.reshape(images * tokens, channels).T
-    work_normed = low((work - pick(mean, image)) * pick(inv_std, image) * norm_gain + norm_shift)
-
+    work[1] = after(work[1], normed_t, cotangent_t)
+    work_mean, work_inv = pick(mean, image), pick(inv_std, image)
+    work = [low((wide(part) - work_mean) * work_inv * norm_gain + norm_shift) for part in work]
+    kernel = project if aligned else project_plain
     sends = []
-    for index, offset in enumerate(offsets):
-        part = swapped(grad_parts[index])
-        if index + 1 < len(grad_parts):
-            part, grad_parts[index + 1] = lax.optimization_barrier((part, grad_parts[index + 1]))
-        sends += (project if aligned else project_plain)(work_normed, part, full_qkv, unit, heads, offset, count)
+    for offset, grad_part in zip(offsets, grad_parts):
+        sends += kernel(work, grad_part, full_qkv, unit, heads, offset, count)
     grads, nears = [], []
     result = None
     for head in range(heads):
         pieces = [sends[head][0]] + [flipped(sends[head][flip], "seq", flip) for flip in range(1, groups)]
-        if head == 0:
-            pieces, normed_t, cotangent_t = lax.optimization_barrier((pieces, normed_t, cotangent_t))
         if head >= 1:
             pieces, result = lax.optimization_barrier((pieces, result))
             grads.append(lax.all_to_all(result, "seq", split_axis=0, concat_axis=0, tiled=True))
-        if head + 1 < heads:
-            pieces, sends[head + 1] = lax.optimization_barrier((pieces, sends[head + 1]))
+        if head + 2 < heads:
+            pieces = after(pieces, sends[head + 2])
         if head >= 2:
             parts = weight_parts(grads[head - 2])
-            pieces, parts, grads[head - 2] = lax.optimization_barrier((pieces, parts, grads[head - 2]))
+            pieces = after(pieces, parts)
             nears.append(sum_near(parts, 1))
-        if head >= 3:
-            pieces, nears[head - 3] = lax.optimization_barrier((pieces, nears[head - 3]))
         result = attend_pair(pieces, me)
     if heads > 1:
-        result, grads[-1], nears = lax.optimization_barrier((result, grads[-1], nears))
+        result = after(result, grads[-1], nears)
     grads.append(lax.all_to_all(result, "seq", split_axis=0, concat_axis=0, tiled=True))
     for index in range(len(nears), heads - 1):
         nears.append(sum_rep(sum_near(weight_parts(grads[index]), 2)))
     if aligned and heads > count:
         back, mixed = project_back(grads[:count], full_qkv, full_out, heads, 0, images)
-        back, mixed, grads[-1], nears = lax.optimization_barrier((back, mixed, grads[-1], nears))
+        grads[-1] = after(grads[-1], back, mixed, nears)
     last = sum_near(weight_parts(grads[-1]), 2)
     if heads > 1:
-        last, grads[-1], nears = lax.optimization_barrier((last, grads[-1], nears))
+        grads[-1], nears = after((grads[-1], nears), last)
     nears.append(sum_rep(last))
     gain = norm_gain[None, :]
     if aligned:
@@ -583,11 +568,10 @@
         mixed, back = project_back_plain(grads, full_qkv, full_out, images)
         mixed_out = low(values + mixed)
         sums = jnp.stack([jnp.sum(back * norm_gain, axis=1), jnp.sum(back * norm_gain * centred, axis=1)])
-    sums, nears[-1] = lax.optimization_barrier((sums, nears[-1]))
+    sums = after(sums, nears[-1])
     weight_sums = []
     if heads > 1:
         early = sum_far(jnp.concatenate(nears[:-1], axis=2), groups)
-        early, nears[-1] = lax.optimization_barrier((early, nears[-1]))
         weight_sums = jnp.split(early, heads - 1, axis=1)
     weight_sums.append(sum_far(nears[-1], groups))
 

time: 664 us -> 635 us (0.956)
  waiting for transfers between devices: 119 us -> 105 us
  Pallas kernels: 361 us -> 351 us
    ppermute x39, waiting for transfers between devices: 97.4 us -> 77.6 us  [flipped(): lax.ppermute(array, axis, [(i, i ^ flip) for i in range(lax.axis_size(axi...]
    pallas_call x2, Pallas kernels: 43.3 us -> 33.5 us  [project_back(): pl.pallas_call(functools.partial(back_body, offset, heads), out_shape=out...]
    unnamed x75 -> x83, local copies, waits for them, and re-layouts: 20 us -> 23.4 us
  transfers between devices with their start and end apart: 46 -> 46, of which waited for: 12 -> 15; matrix products, arithmetic and copies ran while one was open for 11% -> 11% of each run, Pallas kernels for 54% -> 55%
where the time goes in v3:
time: 635 us; the launch traced here: 625 us
  Pallas kernels  351 us (55%)
  waiting for transfers between devices  105 us (17%)
  starting transfers between devices  67.9 us (11%)
  local copies, waits for them, and re-layouts  54 us (9%)
  other arithmetic  27.2 us (4%)
  between operations  15.2 us (2%)
    pallas_call x4, Pallas kernels, attend_pair(): pl.pallas_call(functools.partial(pair_body, bq, kb), out_shape=jax.ShapeD...  265 us
    ppermute x39, waiting for transfers between devices, flipped(): lax.ppermute(array, axis, [(i, i ^ flip) for i in range(lax.axis_size(axi...  77.6 us
    ppermute x39, starting transfers between devices, flipped(): lax.ppermute(array, axis, [(i, i ^ flip) for i in range(lax.axis_size(axi...  43.8 us
    pallas_call x2, Pallas kernels, project_back(): pl.pallas_call(functools.partial(back_body, offset, heads), out_shape=out...  33.5 us
    pallas_call x4, Pallas kernels, weight_grads(): pl.pallas_call(functools.partial(weight_body, images), out_shape=[jax.Sha...  30 us
    unnamed x83, local copies, waits for them, and re-layouts  23.4 us
    pallas_call x2, Pallas kernels, project(): pl.pallas_call(functools.partial(project_body, count, groups), out_shape=...  23 us
    all_to_all x4, starting transfers between devices, shards(): lax.all_to_all(result, 'seq', split_axis=0, concat_axis=0, tiled=True)  20.8 us
  transfers between devices with their start and end apart: 46, of which 15 were waited for; matrix products, arithmetic and copies ran while one was open for 11% of the time, Pallas kernels for 55%

profile of v3, /device:TPU:0, one launch (start us, length us, event | category | flops | bytes accessed | tf_op | source)
XLA Modules:
  0.0 625.2 jit_solution(5692077885558981401)
XLA Ops:
  8.9 1.8 copy.123
  10.7 2.6 dynamic-slice_bitcast_fusion
  13.3 4.0 collective-permute-start.3
  18.3 1.6 collective-permute-start
  19.9 2.1 collective-permute-done
  22.0 1.6 collective-permute-start.1
  23.6 3.6 copy.78
  27.1 4.5 copy.81
  31.6 14.2 %collective-permute-done.1 = f32[2,2,32]{2,1,0:T(2,128)S(1)} collective-permute-done((f32[2,2,32]{2,1,0:T(2,128)S(1)}, f32[2,2,32]{2,1,0:T(2,128)S(1)}, u32[]{:S(2)}, u32[]{:S(2)}) %collective-permute-start.1) | collective-permute-done | bytes 544 | tf_op jit(solution)/shard_map/ppermute | solution.py:410
  45.7 2.1 fusion.51
  48.3 1.5 fusion.19
  49.8 2.4 collective-permute-start.2
  52.2 2.5 fusion.22
  56.4 30.2 %collective-permute-done.2 = f32[2,2,32]{2,1,0:T(2,128)S(1)} collective-permute-done((f32[2,2,32]{2,1,0:T(2,128)S(1)}, f32[2,2,32]{2,1,0:T(2,128)S(1)}, u32[]{:S(2)}, u32[]{:S(2)}) %collective-permute-start.2) | collective-permute-done | bytes 544 | tf_op jit(solution)/shard_map/ppermute | solution.py:410
  87.2 2.5 fusion.5
  89.7 4.7 copy.80
  94.5 2.5 collective-permute-done.4.grad_there
  97.0 2.4 dynamic-slice_bitcast_fusion.1
  99.4 3.9 add_convert_fusion
  103.3 11.4 %project.3 = (bf16[2,512,256]{2,1,0:T(8,128)(2,1)}, bf16[2,512,256]{2,1,0:T(8,128)(2,1)}, bf16[2,512,256]{2,1,0:T(8,128)(2,1)}, bf16[2,512,256]{2,1,0:T(8,128)(2...) custom-call(s32[1]{0:T(128)S(6)} %select_n.72.unit_ref, ...), custom_call_target="tpu_custom_call" | custom-call | flops 1342177280 | bytes 65536 | tf_op jit(solution)/shard_map/project/pallas_call | solution.py:180
  114.7 1.6 collective-permute-start.15
  116.3 4.0 collective-permute-start.16
  120.3 4.6 collective-permute-done.5.grad_there
  125.8 11.6 %project.2 = (bf16[2,512,256]{2,1,0:T(8,128)(2,1)}, bf16[2,512,256]{2,1,0:T(8,128)(2,1)}, bf16[2,512,256]{2,1,0:T(8,128)(2,1)}, bf16[2,512,256]{2,1,0:T(8,128)(2...) custom-call(s32[1]{0:T(128)S(6)} %select_n.72.unit_ref, ...), custom_call_target="tpu_custom_call" | custom-call | flops 1342177280 | bytes 65536 | tf_op jit(solution)/shard_map/project/pallas_call | solution.py:180
  139.5 2.1 collective-permute-start.13
  141.5 6.6 %collective-permute-done.17.refs_3_ = bf16[2,512,256]{2,1,0:T(8,128)(2,1)S(1)} collective-permute-done((bf16[2,512,256]{2,1,0:T(8,128)(2,1)}, bf16[2,512,256]{2,1,0:T(8,128)(2,1)S(1)}, u32[]{:S(2)}, u32[]{:S(2)}) %collective-permute-start.17) | collective-permute-done | bytes 524320 | tf_op jit(solution)/shard_map/ppermute | solution.py:410
  149.0 66.3 %attend_pair.4 = bf16[8,512,256]{2,1,0:T(8,128)(2,1)} custom-call(s32[1]{0:T(128)} %bitcast.me_ref, bf16[2,512,256]{2,1,0:T(8,128)(2,1)} %get-tuple-element.93.refs_0_, bf16[2,512,256]{2,1,0:T(8,128)(2,1)} %copy-done.32, bf16[2,512,256]{2,1,0:T(8,128)(2,1)} %copy-done.33, bf16[2,512,256]{2,1,0:T(8,128)(2,1)} %copy-done.34), custom_call_target="tpu_custom_call" | custom-call | flops 51539607552 | bytes 4194304 | tf_op jit(solution)/shard_map/attend_pair/pallas_call | solution.py:123
  215.3 2.2 collective-permute-start.11
  219.1 3.6 all-to-all-start
  222.7 66.2 %attend_pair.5 = bf16[8,512,256]{2,1,0:T(8,128)(2,1)} custom-call(s32[1]{0:T(128)} %bitcast.me_ref, bf16[2,512,256]{2,1,0:T(8,128)(2,1)} %get-tuple-element.101.refs_0_, bf16[2,512,256]{2,1,0:T(8,128)(2,1)} %copy-done.35, bf16[2,512,256]{2,1,0:T(8,128)(2,1)} %copy-done.36, bf16[2,512,256]{2,1,0:T(8,128)(2,1)} %copy-done.37), custom_call_target="tpu_custom_call" | custom-call | flops 51539607552 | bytes 4194304 | tf_op jit(solution)/shard_map/attend_pair/pallas_call | solution.py:123
  288.9 2.8 collective-permute-start.8
  291.8 4.8 all-to-all-start.2
  296.5 7.5 %weight_grads.4 = (bf16[2,8,40,1024]{3,2,1,0:T(8,128)(2,1)}, bf16[2,8,40,1024]{3,2,1,0:T(8,128)(2,1)}) custom-call(s32[1]{0:T(128)} %bitcast.20.here_ref, bf16[1280,1024]{1,0:T(8,128)(2,1)} %bitcast.189, bf16[1280,1024]{1,0:T(8,128)(2,1)} %bitcast.185, bf16[8,512,256]{2,1,0:T(8,128)(2,1)} %copy-done.9), custom_call_target="tpu_custom_call" | custom-call | flops 2684354560 | bytes 8388608 | tf_op jit(solution)/shard_map/weight_grads/pallas_call | solution.py:257
  304.0 66.2 %attend_pair.6 = bf16[8,512,256]{2,1,0:T(8,128)(2,1)} custom-call(s32[1]{0:T(128)} %bitcast.me_ref, bf16[2,512,256]{2,1,0:T(8,128)(2,1)} %get-tuple-element.112.refs_0_, bf16[2,512,256]{2,1,0:T(8,128)(2,1)} %collective-permute-done.9.refs_1_, bf16[2,512,256]{2,1,0:T(8,128)(2,1)} %collective-permute-done.10.refs_2_, ...), custom_call_target="tpu_custom_call" | custom-call | flops 51539607552 | bytes 4194304 | tf_op jit(solution)/shard_map/attend_pair/pallas_call | solution.py:123
  372.6 6.2 all-to-all-start.1
  378.8 7.5 %weight_grads.5 = (bf16[2,8,40,1024]{3,2,1,0:T(8,128)(2,1)}, bf16[2,8,40,1024]{3,2,1,0:T(8,128)(2,1)}) custom-call(s32[1]{0:T(128)} %bitcast.20.here_ref, bf16[1280,1024]{1,0:T(8,128)(2,1)} %bitcast.190, bf16[1280,1024]{1,0:T(8,128)(2,1)} %bitcast.186, bf16[8,512,256]{2,1,0:T(8,128)(2,1)} %all-to-all-done.2.grad_ref.refs_1_), custom_call_target="tpu_custom_call" | custom-call | flops 2684354560 | bytes 8388608 | tf_op jit(solution)/shard_map/weight_grads/pallas_call | solution.py:257
  387.8 1.4 slice_bitcast_fusion.3
  392.3 66.1 %attend_pair.7 = bf16[8,512,256]{2,1,0:T(8,128)(2,1)} custom-call(s32[1]{0:T(128)} %bitcast.me_ref, bf16[2,512,256]{2,1,0:T(8,128)(2,1)} %get-tuple-element.124.refs_0_, bf16[2,512,256]{2,1,0:T(8,128)(2,1)} %copy-done.27, bf16[2,512,256]{2,1,0:T(8,128)(2,1)} %collective-permute-done.7.refs_2_, bf16[2,512,256]{2,1,0:T(8,128)(2,1)} %collective-permute-done.8.refs_3_), custom_call_target="tpu_custom_call" | custom-call | flops 51539607552 | bytes 4194304 | tf_op jit(solution)/shard_map/attend_pair/pallas_call | solution.py:123
  458.4 1.9 fusion.30
  460.4 3.0 fusion.28
  463.4 6.3 %all-to-all-start.3 = ((bf16[8,512,256]{2,1,0:T(8,128)(2,1)}), bf16[8,512,256]{2,1,0:T(8,128)(2,1)}, u32[]{:S(2)}, u32[]{:S(2)}) async-start(bf16[8,512,256]{2,1,0:T(8,128)(2,1)} %attend_pair.7), calls=%async_computation.3 | async-start | bytes 4194304 | tf_op jit(solution)/shard_map/all_to_all | solution.py:548
  469.7 7.5 %weight_grads.6 = (bf16[2,8,40,1024]{3,2,1,0:T(8,128)(2,1)}, bf16[2,8,40,1024]{3,2,1,0:T(8,128)(2,1)}) custom-call(s32[1]{0:T(128)} %bitcast.20.here_ref, bf16[1280,1024]{1,0:T(8,128)(2,1)} %bitcast.191, bf16[1280,1024]{1,0:T(8,128)(2,1)} %bitcast.187, bf16[8,512,256]{2,1,0:T(8,128)(2,1)} %copy-done.5), custom_call_target="tpu_custom_call" | custom-call | flops 2684354560 | bytes 8388608 | tf_op jit(solution)/shard_map/weight_grads/pallas_call | solution.py:257
  477.2 3.2 collective-permute-done.24
  480.4 1.8 convert_add_fusion.1
  483.4 14.8 %project_back.2 = (f32[1024,1280]{1,0:T(8,128)}, f32[1024,1280]{1,0:T(8,128)}) custom-call(bf16[8,512,256]{2,1,0:T(8,128)(2,1)} %copy-done.9, bf16[8,512,256]{2,1,0:T(8,128)(2,1)} %all-to-all-done.2.grad_ref.refs_1_, bf16[1280,3072]{1,0:T(8,128)(2,1)} %all-gather.5.cloned.1.call-done.wq_ref.wk_ref.wv_ref.refs_2_, ...), custom_call_target="tpu_custom_call" | custom-call | flops 5368709120 | bytes 16777216 | tf_op jit(solution)/shard_map/project_back/pallas_call | solution.py:378
  499.3 18.6 %all-to-all-done.3.grad_ref.refs_1_ = bf16[8,512,256]{2,1,0:T(8,128)(2,1)} async-done(((bf16[8,512,256]{2,1,0:T(8,128)(2,1)}), bf16[8,512,256]{2,1,0:T(8,128)(2,1)}, u32[]{:S(2)}, u32[]{:S(2)}) %all-to-all-start.3) | async-done | bytes 2097184 | tf_op jit(solution)/shard_map/all_to_all | solution.py:548
  518.0 7.5 %weight_grads.7 = (bf16[2,8,40,1024]{3,2,1,0:T(8,128)(2,1)}, bf16[2,8,40,1024]{3,2,1,0:T(8,128)(2,1)}) custom-call(s32[1]{0:T(128)} %bitcast.20.here_ref, bf16[1280,1024]{1,0:T(8,128)(2,1)} %bitcast.192, bf16[1280,1024]{1,0:T(8,128)(2,1)} %bitcast.188, bf16[8,512,256]{2,1,0:T(8,128)(2,1)} %all-to-all-done.3.grad_ref.refs_1_), custom_call_target="tpu_custom_call" | custom-call | flops 2684354560 | bytes 8388608 | tf_op jit(solution)/shard_map/weight_grads/pallas_call | solution.py:257
  526.0 2.8 collective-permute-done.26
  528.8 2.3 convert_add_fusion
  532.5 1.9 copy-done.4
  535.5 2.9 collective-permute-start.32
  539.0 18.7 %project_back.3 = (f32[1024,1280]{1,0:T(8,128)}, bf16[2,512,1280]{2,1,0:T(8,128)(2,1)}, f32[2,2,1,1280]{3,2,1,0:T(1,128)}) custom-call(bf16[8,512,256]{2,1,0:T(8,128)(2,1)} %copy-done.5, bf16[8,512,256]{2,1,0:T(8,128)(2,1)} %all-to-all-done.3.grad_ref.refs_1_, bf16[1280,3072]{1,0:T(8,128)(2,1)} %all-gather.5.cloned.1.call-done.wq_ref.wk_ref.wv_ref.refs_2_, ...), custom_call_target="tpu_custom_call" | custom-call | flops 5368709120 | bytes 16777216 | tf_op jit(solution)/shard_map/project_back/pallas_call | solution.py:378
  557.8 5.9 copy.93
  565.3 1.5 collective-permute-start.28
  566.8 1.7 fusion.32
  569.5 2.3 collective-permute-start.34
  573.3 1.9 fusion.41
  575.2 2.1 collective-permute-start.37
  578.7 3.8 collective-permute-done.30
  582.9 4.1 fusion.10
  587.1 4.2 copy.94
  592.8 5.6 collective-permute-done.38
  602.9 3.2 all-to-all-start.4
  607.0 7.8 %all-to-all-done.4 = f32[32,1,1280]{2,1,0:T(1,128)S(1)} async-done(((f32[32,1,1280]{2,1,0:T(1,128)}), f32[32,1,1280]{2,1,0:T(1,128)S(1)}, u32[]{:S(2)}, u32[]{:S(2)}) %all-to-all-start.4) | async-done | bytes 163872 | tf_op jit(solution)/shard_map/all_to_all | solution.py:595
  (205 shorter events, 39.2 us)
Async XLA Ops:
  7.2 38.6 %all-gather.3.cloned.1.call-start = ((), (), s32[]{:S(2)}) async-start(), calls=%async_computation.5 | async-start | bytes 3932160 | tf_op jit(solution)/shard_map/all_gather | solution.py:484
  7.9 95.4 %all-gather.5.cloned.1.call-start = ((), (), s32[]{:S(2)}) async-start(), calls=%async_computation.6 | async-start | bytes 11796480 | tf_op jit(solution)/shard_map/all_gather | solution.py:483
  13.3 81.1 %collective-permute-start.3 = (bf16[512,1280]{1,0:T(8,128)(2,1)}, bf16[512,1280]{1,0:T(8,128)(2,1)}, u32[]{:S(2)}, u32[]{:S(2)}) collective-permute-start(bf16[512,1280]{1,0:T(8,128)(2,1)} %dynamic-slice_bitcast_fusion), channel_id=1, source_target_pairs={{0,16},{4,20},{8,24},{12,28},{16,0},{20,4},{24,8},{28,12},{1,17},{... | collective-permute-start | bytes 3932168 | tf_op jit(solution)/shard_map/ppermute | solution.py:410
  18.3 3.7 collective-permute-start
  22.0 23.8 %collective-permute-start.1 = (f32[2,2,32]{2,1,0:T(2,128)S(1)}, f32[2,2,32]{2,1,0:T(2,128)S(1)}, u32[]{:S(2)}, u32[]{:S(2)}) collective-permute-start(f32[2,2,32]{2,1,0:T(2,128)S(1)} %add.166), channel_id=1, source_target_pairs={{0,8},{4,12},{8,0},{12,4},{16,24},{20,28},{24,16},{28,20},{1,9},{5... | collective-permute-start | bytes 1544 | tf_op jit(solution)/shard_map/ppermute | solution.py:410
  49.8 36.8 %collective-permute-start.2 = (f32[2,2,32]{2,1,0:T(2,128)S(1)}, f32[2,2,32]{2,1,0:T(2,128)S(1)}, u32[]{:S(2)}, u32[]{:S(2)}) collective-permute-start(f32[2,2,32]{2,1,0:T(2,128)S(1)} %add.167), channel_id=1, source_target_pairs={{0,16},{4,20},{8,24},{12,28},{16,0},{20,4},{24,8},{28,12},{1,17},{... | collective-permute-start | bytes 1544 | tf_op jit(solution)/shard_map/ppermute | solution.py:410
  52.2 35.0 %copy-start.17 = (f32[1280]{0:T(1024)S(1)}, f32[1280]{0:T(1024)}, u32[]{:S(2)}) copy-start(f32[1280]{0:T(1024)} %param.8) | copy-start | bytes 15364
  52.2 35.0 %copy-start.25 = (f32[1280]{0:T(1024)S(1)}, f32[1280]{0:T(1024)}, u32[]{:S(2)}) copy-start(f32[1280]{0:T(1024)} %param.9) | copy-start | bytes 15364
  55.8 41.2 %collective-permute-start.4 = (bf16[512,512]{1,0:T(8,128)(2,1)}, bf16[512,512]{1,0:T(8,128)(2,1)S(1)}, u32[]{:S(2)}, u32[]{:S(2)}) collective-permute-start(bf16[512,512]{1,0:T(8,128)(2,1)} %get-tuple-element.182), channel_id=1, source_target_pairs={{0,16},{4,20},{8,24},{12,28},{16,0},{20,4},{24,8},{28,12},{1,17},{... | collective-permute-start | bytes 1572872 | tf_op jit(solution)/shard_map/ppermute | solution.py:410
  86.9 7.5 %copy-start.23 = (f32[2,1,1280]{2,1,0:T(1,128)}, f32[2,1,1280]{2,1,0:T(1,128)S(1)}, u32[]{:S(2)}) copy-start(f32[2,1,1280]{2,1,0:T(1,128)S(1)} %broadcast_in_dim_reshape.9.refs_8_) | copy-start | bytes 30724
  87.2 7.2 %copy-start.24 = (f32[2,1,1280]{2,1,0:T(1,128)}, f32[2,1,1280]{2,1,0:T(1,128)S(1)}, u32[]{:S(2)}) copy-start(f32[2,1,1280]{2,1,0:T(1,128)S(1)} %broadcast_in_dim_reshape.8.refs_7_) | copy-start | bytes 30724
  89.7 9.7 %copy-start.2 = (bf16[512,2,1280]{2,0,1:T(8,128)(2,1)S(1)}, bf16[512,2,1280]{2,0,1:T(8,128)(2,1)}, u32[]{:S(2)}) copy-start(bf16[512,2,1280]{2,0,1:T(8,128)(2,1)} %copy.123) | copy-start | bytes 7864324
  99.4 25.6 %collective-permute-start.5 = (bf16[512,512]{1,0:T(8,128)(2,1)}, bf16[512,512]{1,0:T(8,128)(2,1)S(1)}, u32[]{:S(2)}, u32[]{:S(2)}) collective-permute-start(bf16[512,512]{1,0:T(8,128)(2,1)} %get-tuple-element.180), channel_id=1, source_target_pairs={{0,16},{4,20},{8,24},{12,28},{16,0},{20,4},{24,8},{28,12},{1,17},{... | collective-permute-start | bytes 1572872 | tf_op jit(solution)/shard_map/ppermute | solution.py:410
  114.7 23.9 %collective-permute-start.15 = (bf16[2,512,256]{2,1,0:T(8,128)(2,1)}, bf16[2,512,256]{2,1,0:T(8,128)(2,1)S(1)}, u32[]{:S(2)}, u32[]{:S(2)}) collective-permute-start(bf16[2,512,256]{2,1,0:T(8,128)(2,1)} %get-tuple-element.90), channel_id=1, source_target_pairs={{0,4},{4,0},{8,12},{12,8},{16,20},{20,16},{24,28},{28,24},{1,5},{5... | collective-permute-start | bytes 1572872 | tf_op jit(solution)/shard_map/ppermute | solution.py:410
  116.3 23.2 %collective-permute-start.16 = (bf16[2,512,256]{2,1,0:T(8,128)(2,1)}, bf16[2,512,256]{2,1,0:T(8,128)(2,1)S(1)}, u32[]{:S(2)}, u32[]{:S(2)}) collective-permute-start(bf16[2,512,256]{2,1,0:T(8,128)(2,1)} %get-tuple-element.91), channel_id=1, source_target_pairs={{0,8},{4,12},{8,0},{12,4},{16,24},{20,28},{24,16},{28,20},{1,9},{5... | collective-permute-start | bytes 1572872 | tf_op jit(solution)/shard_map/ppermute | solution.py:410
  120.3 27.8 %collective-permute-start.17 = (bf16[2,512,256]{2,1,0:T(8,128)(2,1)}, bf16[2,512,256]{2,1,0:T(8,128)(2,1)S(1)}, u32[]{:S(2)}, u32[]{:S(2)}) collective-permute-start(bf16[2,512,256]{2,1,0:T(8,128)(2,1)} %get-tuple-element.92), channel_id=1, source_target_pairs={{0,12},{4,8},{8,4},{12,0},{16,28},{20,24},{24,20},{28,16},{1,13},{... | collective-permute-start | bytes 1572872 | tf_op jit(solution)/shard_map/ppermute | solution.py:410
  125.8 12.9 %copy-start.31 = (bf16[2,512,256]{2,1,0:T(8,128)(2,1)S(1)}, bf16[2,512,256]{2,1,0:T(8,128)(2,1)}, u32[]{:S(2)}) copy-start(bf16[2,512,256]{2,1,0:T(8,128)(2,1)} %get-tuple-element.86) | copy-start | bytes 1572868
  125.8 13.7 %copy-start.30 = (bf16[2,512,256]{2,1,0:T(8,128)(2,1)S(1)}, bf16[2,512,256]{2,1,0:T(8,128)(2,1)}, u32[]{:S(2)}) copy-start(bf16[2,512,256]{2,1,0:T(8,128)(2,1)} %get-tuple-element.87) | copy-start | bytes 1572868
  125.8 22.4 %copy-start.29 = (bf16[2,512,256]{2,1,0:T(8,128)(2,1)S(1)}, bf16[2,512,256]{2,1,0:T(8,128)(2,1)}, u32[]{:S(2)}) copy-start(bf16[2,512,256]{2,1,0:T(8,128)(2,1)} %get-tuple-element.88) | copy-start | bytes 1572868
  137.3 151.5 %collective-permute-start.9 = (bf16[2,512,256]{2,1,0:T(8,128)(2,1)}, bf16[2,512,256]{2,1,0:T(8,128)(2,1)}, u32[]{:S(2)}, u32[]{:S(2)}) collective-permute-start(bf16[2,512,256]{2,1,0:T(8,128)(2,1)} %get-tuple-element.82), channel_id=1, source_target_pairs={{0,4},{4,0},{8,12},{12,8},{16,20},{20,16},{24,28},{28,24},{1,5},{5... | collective-permute-start | bytes 1572872 | tf_op jit(solution)/shard_map/ppermute | solution.py:410
  138.6 153.1 %collective-permute-start.10 = (bf16[2,512,256]{2,1,0:T(8,128)(2,1)}, bf16[2,512,256]{2,1,0:T(8,128)(2,1)}, u32[]{:S(2)}, u32[]{:S(2)}) collective-permute-start(bf16[2,512,256]{2,1,0:T(8,128)(2,1)} %get-tuple-element.83), channel_id=1, source_target_pairs={{0,8},{4,12},{8,0},{12,4},{16,24},{20,28},{24,16},{28,20},{1,9},{5... | collective-permute-start | bytes 1572872 | tf_op jit(solution)/shard_map/ppermute | solution.py:410
  138.6 9.6 %copy-start.32 = (bf16[2,512,256]{2,1,0:T(8,128)(2,1)}, bf16[2,512,256]{2,1,0:T(8,128)(2,1)S(1)}, u32[]{:S(2)}) copy-start(bf16[2,512,256]{2,1,0:T(8,128)(2,1)S(1)} %collective-permute-done.15.refs_1_) | copy-start | bytes 1572868
  138.6 76.6 %collective-permute-start.12 = (bf16[2,512,256]{2,1,0:T(8,128)(2,1)S(1)}, bf16[2,512,256]{2,1,0:T(8,128)(2,1)S(1)}, u32[]{:S(2)}, u32[]{:S(2)}) collective-permute-start(bf16[2,512,256]{2,1,0:T(8,128)(2,1)S(1)} %copy-done.31), channel_id=1, source_target_pairs={{0,4},{4,0},{8,12},{12,8},{16,20},{20,16},{24,28},{28,24},{1,5},{5... | collective-permute-start | bytes 1572872 | tf_op jit(solution)/shard_map/ppermute | solution.py:410
  139.5 8.7 %copy-start.33 = (bf16[2,512,256]{2,1,0:T(8,128)(2,1)}, bf16[2,512,256]{2,1,0:T(8,128)(2,1)S(1)}, u32[]{:S(2)}) copy-start(bf16[2,512,256]{2,1,0:T(8,128)(2,1)S(1)} %collective-permute-done.16.refs_2_) | copy-start | bytes 1572868
  139.5 78.0 %collective-permute-start.13 = (bf16[2,512,256]{2,1,0:T(8,128)(2,1)S(1)}, bf16[2,512,256]{2,1,0:T(8,128)(2,1)S(1)}, u32[]{:S(2)}, u32[]{:S(2)}) collective-permute-start(bf16[2,512,256]{2,1,0:T(8,128)(2,1)S(1)} %copy-done.30), channel_id=1, source_target_pairs={{0,8},{4,12},{8,0},{12,4},{16,24},{20,28},{24,16},{28,20},{1,9},{5... | collective-permute-start | bytes 1572872 | tf_op jit(solution)/shard_map/ppermute | solution.py:410
  148.2 70.0 %collective-permute-start.14 = (bf16[2,512,256]{2,1,0:T(8,128)(2,1)S(1)}, bf16[2,512,256]{2,1,0:T(8,128)(2,1)S(1)}, u32[]{:S(2)}, u32[]{:S(2)}) collective-permute-start(bf16[2,512,256]{2,1,0:T(8,128)(2,1)S(1)} %copy-done.29), channel_id=1, source_target_pairs={{0,12},{4,8},{8,4},{12,0},{16,28},{20,24},{24,20},{28,16},{1,13},{... | collective-permute-start | bytes 1572872 | tf_op jit(solution)/shard_map/ppermute | solution.py:410
  215.3 76.4 %collective-permute-start.11 = (bf16[2,512,256]{2,1,0:T(8,128)(2,1)}, bf16[2,512,256]{2,1,0:T(8,128)(2,1)}, u32[]{:S(2)}, u32[]{:S(2)}) collective-permute-start(bf16[2,512,256]{2,1,0:T(8,128)(2,1)} %get-tuple-element.84), channel_id=1, source_target_pairs={{0,12},{4,8},{8,4},{12,0},{16,28},{20,24},{24,20},{28,16},{1,13},{... | collective-permute-start | bytes 1572872 | tf_op jit(solution)/shard_map/ppermute | solution.py:410
  217.5 152.8 %collective-permute-start.6 = (bf16[2,512,256]{2,1,0:T(8,128)(2,1)}, bf16[2,512,256]{2,1,0:T(8,128)(2,1)S(1)}, u32[]{:S(2)}, u32[]{:S(2)}) collective-permute-start(bf16[2,512,256]{2,1,0:T(8,128)(2,1)} %get-tuple-element.78), channel_id=1, source_target_pairs={{0,4},{4,0},{8,12},{12,8},{16,20},{20,16},{24,28},{28,24},{1,5},{5... | collective-permute-start | bytes 1572872 | tf_op jit(solution)/shard_map/ppermute | solution.py:410
  218.3 152.0 %collective-permute-start.7 = (bf16[2,512,256]{2,1,0:T(8,128)(2,1)}, bf16[2,512,256]{2,1,0:T(8,128)(2,1)}, u32[]{:S(2)}, u32[]{:S(2)}) collective-permute-start(bf16[2,512,256]{2,1,0:T(8,128)(2,1)} %get-tuple-element.79), channel_id=1, source_target_pairs={{0,8},{4,12},{8,0},{12,4},{16,24},{20,28},{24,16},{28,20},{1,9},{5... | collective-permute-start | bytes 1572872 | tf_op jit(solution)/shard_map/ppermute | solution.py:410
  219.1 72.7 %all-to-all-start = ((bf16[8,512,256]{2,1,0:T(8,128)(2,1)}), bf16[8,512,256]{2,1,0:T(8,128)(2,1)S(1)}, u32[]{:S(2)}, u32[]{:S(2)}) async-start(bf16[8,512,256]{2,1,0:T(8,128)(2,1)} %attend_pair.4), calls=%async_computation | async-start | bytes 4194304 | tf_op jit(solution)/shard_map/all_to_all | solution.py:538
  222.7 66.2 %copy-start.28 = (bf16[2,512,256]{2,1,0:T(8,128)(2,1)S(1)}, bf16[2,512,256]{2,1,0:T(8,128)(2,1)}, u32[]{:S(2)}) copy-start(bf16[2,512,256]{2,1,0:T(8,128)(2,1)} %get-tuple-element.80) | copy-start | bytes 1572868
  288.9 82.2 %collective-permute-start.8 = (bf16[2,512,256]{2,1,0:T(8,128)(2,1)S(1)}, bf16[2,512,256]{2,1,0:T(8,128)(2,1)}, u32[]{:S(2)}, u32[]{:S(2)}) collective-permute-start(bf16[2,512,256]{2,1,0:T(8,128)(2,1)S(1)} %copy-done.28), channel_id=1, source_target_pairs={{0,12},{4,8},{8,4},{12,0},{16,28},{20,24},{24,20},{28,16},{1,13},{... | collective-permute-start | bytes 1572872 | tf_op jit(solution)/shard_map/ppermute | solution.py:410
  291.8 80.9 %all-to-all-start.2 = ((bf16[8,512,256]{2,1,0:T(8,128)(2,1)}), bf16[8,512,256]{2,1,0:T(8,128)(2,1)}, u32[]{:S(2)}, u32[]{:S(2)}) async-start(bf16[8,512,256]{2,1,0:T(8,128)(2,1)} %attend_pair.5), calls=%async_computation.2 | async-start | bytes 4194304 | tf_op jit(solution)/shard_map/all_to_all | solution.py:538
  304.0 67.1 %copy-start.10 = (bf16[2,8,40,1024]{3,2,1,0:T(8,128)(2,1)S(1)}, bf16[2,8,40,1024]{3,2,1,0:T(8,128)(2,1)}, u32[]{:S(2)}) copy-start(bf16[2,8,40,1024]{3,2,1,0:T(8,128)(2,1)} %get-tuple-element.111) | copy-start | bytes 3932164
  371.2 20.3 %collective-permute-start.20 = (bf16[8,40,1024]{2,1,0:T(8,128)(2,1)S(1)}, bf16[8,40,1024]{2,1,0:T(8,128)(2,1)}, u32[]{:S(2)}, u32[]{:S(2)}) collective-permute-start(bf16[8,40,1024]{2,1,0:T(8,128)(2,1)S(1)} %get-tuple-element.179), channel_id=1, source_target_pairs={{0,3},{1,2},{2,1},{3,0},{4,7},{5,6},{6,5},{7,4},{8,11},{9,10},{10,... | collective-permute-start | bytes 1966088 | tf_op jit(solution)/shard_map/ppermute | solution.py:410
  372.6 90.7 %all-to-all-start.1 = ((bf16[8,512,256]{2,1,0:T(8,128)(2,1)}), bf16[8,512,256]{2,1,0:T(8,128)(2,1)S(1)}, u32[]{:S(2)}, u32[]{:S(2)}) async-start(bf16[8,512,256]{2,1,0:T(8,128)(2,1)} %attend_pair.6), calls=%async_computation.1 | async-start | bytes 4194304 | tf_op jit(solution)/shard_map/all_to_all | solution.py:538
  378.8 8.2 %copy-start.14 = (bf16[8,40,1024]{2,1,0:T(8,128)(2,1)S(1)}, bf16[8,40,1024]{2,1,0:T(8,128)(2,1)}, u32[]{:S(2)}) copy-start(bf16[8,40,1024]{2,1,0:T(8,128)(2,1)} %slice_bitcast_fusion.7) | copy-start | bytes 1966084
  386.4 72.0 %collective-permute-start.19 = (bf16[8,40,1024]{2,1,0:T(8,128)(2,1)S(1)}, bf16[8,40,1024]{2,1,0:T(8,128)(2,1)}, u32[]{:S(2)}, u32[]{:S(2)}) collective-permute-start(bf16[8,40,1024]{2,1,0:T(8,128)(2,1)S(1)} %get-tuple-element.178), channel_id=1, source_target_pairs={{0,1},{1,0},{2,3},{3,2},{4,5},{5,4},{6,7},{7,6},{8,9},{9,8},{10,11... | collective-permute-start | bytes 1966088 | tf_op jit(solution)/shard_map/ppermute | solution.py:410
  387.0 71.4 %collective-permute-start.18 = (bf16[8,40,1024]{2,1,0:T(8,128)(2,1)S(1)}, bf16[8,40,1024]{2,1,0:T(8,128)(2,1)}, u32[]{:S(2)}, u32[]{:S(2)}) collective-permute-start(bf16[8,40,1024]{2,1,0:T(8,128)(2,1)S(1)} %copy-done.14), channel_id=1, source_target_pairs={{0,2},{1,3},{2,0},{3,1},{4,6},{5,7},{6,4},{7,5},{8,10},{9,11},{10,... | collective-permute-start | bytes 1966088 | tf_op jit(solution)/shard_map/ppermute | solution.py:410
  389.2 71.2 %collective-permute-start.23 = (bf16[8,40,1024]{2,1,0:T(8,128)(2,1)S(1)}, bf16[8,40,1024]{2,1,0:T(8,128)(2,1)}, u32[]{:S(2)}, u32[]{:S(2)}) collective-permute-start(bf16[8,40,1024]{2,1,0:T(8,128)(2,1)S(1)} %get-tuple-element.177), channel_id=1, source_target_pairs={{0,3},{1,2},{2,1},{3,0},{4,7},{5,6},{6,5},{7,4},{8,11},{9,10},{10,... | collective-permute-start | bytes 1966088 | tf_op jit(solution)/shard_map/ppermute | solution.py:410
  389.9 70.4 %collective-permute-start.22 = (bf16[8,40,1024]{2,1,0:T(8,128)(2,1)S(1)}, bf16[8,40,1024]{2,1,0:T(8,128)(2,1)}, u32[]{:S(2)}, u32[]{:S(2)}) collective-permute-start(bf16[8,40,1024]{2,1,0:T(8,128)(2,1)S(1)} %get-tuple-element.176), channel_id=1, source_target_pairs={{0,1},{1,0},{2,3},{3,2},{4,5},{5,4},{6,7},{7,6},{8,9},{9,8},{10,11... | collective-permute-start | bytes 1966088 | tf_op jit(solution)/shard_map/ppermute | solution.py:410
  391.5 66.9 %copy-start.12 = (bf16[2,8,40,1024]{3,2,1,0:T(8,128)(2,1)S(1)}, bf16[2,8,40,1024]{3,2,1,0:T(8,128)(2,1)}, u32[]{:S(2)}) copy-start(bf16[2,8,40,1024]{3,2,1,0:T(8,128)(2,1)} %get-tuple-element.110) | copy-start | bytes 3932164
  391.5 68.9 %collective-permute-start.21 = (bf16[8,40,1024]{2,1,0:T(8,128)(2,1)}, bf16[8,40,1024]{2,1,0:T(8,128)(2,1)}, u32[]{:S(2)}, u32[]{:S(2)}) collective-permute-start(bf16[8,40,1024]{2,1,0:T(8,128)(2,1)} %slice_bitcast_fusion.4), channel_id=1, source_target_pairs={{0,2},{1,3},{2,0},{3,1},{4,6},{5,7},{6,4},{7,5},{8,10},{9,11},{10,... | collective-permute-start | bytes 1966088 | tf_op jit(solution)/shard_map/ppermute | solution.py:410
  463.4 54.6 %all-to-all-start.3 = ((bf16[8,512,256]{2,1,0:T(8,128)(2,1)}), bf16[8,512,256]{2,1,0:T(8,128)(2,1)}, u32[]{:S(2)}, u32[]{:S(2)}) async-start(bf16[8,512,256]{2,1,0:T(8,128)(2,1)} %attend_pair.7), calls=%async_computation.3 | async-start | bytes 4194304 | tf_op jit(solution)/shard_map/all_to_all | solution.py:548
  477.2 3.2 collective-permute-start.24
  482.3 16.8 %collective-permute-start.25 = (bf16[8,40,1024]{2,1,0:T(8,128)(2,1)S(1)}, bf16[8,40,1024]{2,1,0:T(8,128)(2,1)S(1)}, u32[]{:S(2)}, u32[]{:S(2)}) collective-permute-start(bf16[8,40,1024]{2,1,0:T(8,128)(2,1)S(1)} %fusion.33), channel_id=1, source_target_pairs={{0,2},{2,0},{1,3},{3,1},{4,6},{6,4},{5,7},{7,5},{8,10},{10,8},{9,1... | collective-permute-start | bytes 1966088 | tf_op jit(solution)/shard_map/ppermute | solution.py:410
  517.9 7.5 %copy-start.18 = (f32[1280]{0:T(1024)S(1)}, f32[1280]{0:T(1024)}, u32[]{:S(2)}) copy-start(f32[1280]{0:T(1024)} %param.8) | copy-start | bytes 15364
  525.4 3.4 collective-permute-start.26
  531.2 32.5 %collective-permute-start.27 = (bf16[8,40,1024]{2,1,0:T(8,128)(2,1)S(1)}, bf16[8,40,1024]{2,1,0:T(8,128)(2,1)S(1)}, u32[]{:S(2)}, u32[]{:S(2)}) collective-permute-start(bf16[8,40,1024]{2,1,0:T(8,128)(2,1)S(1)} %fusion.34), channel_id=1, source_target_pairs={{0,2},{2,0},{1,3},{3,1},{4,6},{6,4},{5,7},{7,5},{8,10},{10,8},{9,1... | collective-permute-start | bytes 1966088 | tf_op jit(solution)/shard_map/ppermute | solution.py:410
  535.5 31.3 %collective-permute-start.33 = (bf16[2,40,3072]{2,1,0:T(8,128)(2,1)}, bf16[2,40,3072]{2,1,0:T(8,128)(2,1)S(1)}, u32[]{:S(2)}, u32[]{:S(2)}) collective-permute-start(bf16[2,40,3072]{2,1,0:T(8,128)(2,1)} %get-tuple-element.168), channel_id=1, source_target_pairs={{0,12},{4,8},{8,4},{12,0},{16,28},{20,24},{24,20},{28,16},{1,13},{... | collective-permute-start | bytes 1474568 | tf_op jit(solution)/shard_map/ppermute | solution.py:410
  535.5 31.3 %collective-permute-start.32 = (bf16[2,40,3072]{2,1,0:T(8,128)(2,1)}, bf16[2,40,3072]{2,1,0:T(8,128)(2,1)}, u32[]{:S(2)}, u32[]{:S(2)}) collective-permute-start(bf16[2,40,3072]{2,1,0:T(8,128)(2,1)} %get-tuple-element.167), channel_id=1, source_target_pairs={{0,8},{4,12},{8,0},{12,4},{16,24},{20,28},{24,16},{28,20},{1,9},{5... | collective-permute-start | bytes 1474568 | tf_op jit(solution)/shard_map/ppermute | solution.py:410
  538.5 28.3 %collective-permute-start.31 = (bf16[2,40,3072]{2,1,0:T(8,128)(2,1)}, bf16[2,40,3072]{2,1,0:T(8,128)(2,1)}, u32[]{:S(2)}, u32[]{:S(2)}) collective-permute-start(bf16[2,40,3072]{2,1,0:T(8,128)(2,1)} %get-tuple-element.166), channel_id=1, source_target_pairs={{0,4},{4,0},{8,12},{12,8},{16,20},{20,16},{24,28},{28,24},{1,5},{5... | collective-permute-start | bytes 1474568 | tf_op jit(solution)/shard_map/ppermute | solution.py:410
  565.1 17.8 %copy-start.1 = (bf16[512,2,1280]{2,1,0:T(2,128)(2,1)S(1)}, bf16[512,2,1280]{2,1,0:T(2,128)(2,1)}, u32[]{:S(2)}) copy-start(bf16[512,2,1280]{2,1,0:T(2,128)(2,1)} %param.6) | copy-start | bytes 7864324
  565.1 17.8 %copy-start.20 = (f32[2,1280]{1,0:T(2,128)S(1)}, f32[2,1280]{1,0:T(2,128)}, u32[]{:S(2)}) copy-start(f32[2,1280]{1,0:T(2,128)} %copy-done.19) | copy-start | bytes 30724
  565.1 17.9 %copy-start.22 = (f32[2,1280]{1,0:T(2,128)S(1)}, f32[2,1280]{1,0:T(2,128)}, u32[]{:S(2)}) copy-start(f32[2,1280]{1,0:T(2,128)} %copy-done.21) | copy-start | bytes 30724
  565.3 3.7 collective-permute-start.28
  568.9 3.6 collective-permute-start.29
  569.5 21.7 %collective-permute-start.34 = (bf16[40,3072]{1,0:T(8,128)(2,1)S(1)}, bf16[40,3072]{1,0:T(8,128)(2,1)S(1)}, u32[]{:S(2)}, u32[]{:S(2)}) collective-permute-start(bf16[40,3072]{1,0:T(8,128)(2,1)S(1)} %fusion.40), channel_id=1, source_target_pairs={{0,16},{4,20},{8,24},{12,28},{16,0},{20,4},{24,8},{28,12},{1,17},{... | collective-permute-start | bytes 737288 | tf_op jit(solution)/shard_map/ppermute | solution.py:410
  572.5 10.0 %collective-permute-start.30 = (f32[2,2,32]{2,1,0:T(2,128)S(1)}, f32[2,2,32]{2,1,0:T(2,128)S(1)}, u32[]{:S(2)}, u32[]{:S(2)}) collective-permute-start(f32[2,2,32]{2,1,0:T(2,128)S(1)} %add.189), channel_id=1, source_target_pairs={{0,16},{4,20},{8,24},{12,28},{16,0},{20,4},{24,8},{28,12},{1,17},{... | collective-permute-start | bytes 1544 | tf_op jit(solution)/shard_map/ppermute | solution.py:410
  575.2 16.1 %collective-permute-start.37 = (bf16[2,40,1024]{2,1,0:T(8,128)(2,1)}, bf16[2,40,1024]{2,1,0:T(8,128)(2,1)}, u32[]{:S(2)}, u32[]{:S(2)}) collective-permute-start(bf16[2,40,1024]{2,1,0:T(8,128)(2,1)} %get-tuple-element.175), channel_id=1, source_target_pairs={{0,12},{4,8},{8,4},{12,0},{16,28},{20,24},{24,20},{28,16},{1,13},{... | collective-permute-start | bytes 491528 | tf_op jit(solution)/shard_map/ppermute | solution.py:410
  577.3 14.0 %collective-permute-start.36 = (bf16[2,40,1024]{2,1,0:T(8,128)(2,1)S(1)}, bf16[2,40,1024]{2,1,0:T(8,128)(2,1)}, u32[]{:S(2)}, u32[]{:S(2)}) collective-permute-start(bf16[2,40,1024]{2,1,0:T(8,128)(2,1)S(1)} %get-tuple-element.174), channel_id=1, source_target_pairs={{0,8},{4,12},{8,0},{12,4},{16,24},{20,28},{24,16},{28,20},{1,9},{5... | collective-permute-start | bytes 491528 | tf_op jit(solution)/shard_map/ppermute | solution.py:410
  577.4 14.0 %collective-permute-start.35 = (bf16[2,40,1024]{2,1,0:T(8,128)(2,1)S(1)}, bf16[2,40,1024]{2,1,0:T(8,128)(2,1)}, u32[]{:S(2)}, u32[]{:S(2)}) collective-permute-start(bf16[2,40,1024]{2,1,0:T(8,128)(2,1)S(1)} %get-tuple-element.173), channel_id=1, source_target_pairs={{0,4},{4,0},{8,12},{12,8},{16,20},{20,16},{24,28},{28,24},{1,5},{5... | collective-permute-start | bytes 491528 | tf_op jit(solution)/shard_map/ppermute | solution.py:410
  592.7 5.8 collective-permute-start.38
  602.9 11.8 %all-to-all-start.4 = ((f32[32,1,1280]{2,1,0:T(1,128)}), f32[32,1,1280]{2,1,0:T(1,128)S(1)}, u32[]{:S(2)}, u32[]{:S(2)}) async-start(f32[32,1,1280]{2,1,0:T(1,128)} %reshape.122), calls=%async_computation.4 | async-start | bytes 327680 | tf_op jit(solution)/shard_map/all_to_all | solution.py:595
  (20 other events, 52.5 us)
Sparse Core Ops, SparseCore 0:
  9.6 14.0 all-gather.2
  25.2 20.2 all-gather.4

commit v4 on v3

--- a/solution.py
+++ b/solution.py
@@ -32,12 +32,21 @@
     return op(array.reshape(array.shape[0] // 8, 8, array.shape[1]), axis=0)
 
 
-def pair_body(bq, kb, me_ref, *refs):
+def pair_body(bq, kb, flips, places, me_ref, *refs):
     ins, (o_ref, x_ref, kv_t, s_buf, dp_buf, acc, done) = refs[:-7], refs[-7:]
     length = x_ref.shape[0]
-    piece = length // len(ins)
-    for j, ref in enumerate(ins):
-        x_ref[j * piece : (j + 1) * piece, :] = ref[...].reshape(piece, PACK)
+    piece = length // flips
+    left = lax.broadcasted_iota(jnp.int32, (1, HALF), 1) < HEAD
+    for j in range(flips):
+        kinds = []
+        for group, lane, _ in places:
+            kinds.append(ins[group * flips + j][:, :, lane : lane + HALF].reshape(piece, HALF))
+        query, grad = wide(kinds[1]), wide(kinds[2])
+        query = query if places[1][2] == 0 else pltpu.roll(query, HEAD, 1)
+        grad = grad if places[2][2] == 1 else pltpu.roll(grad, HEAD, 1)
+        rows = slice(j * piece, (j + 1) * piece)
+        x_ref[rows, 0:HALF] = kinds[0]
+        x_ref[rows, HALF:PACK] = low(jnp.where(left, query, grad))
     key_blocks, query_blocks = length // kb, length // bq
     step_len = min(512, length)
     first = lax.broadcasted_iota(jnp.int32, (1, HALF), 1) < HEAD
@@ -106,22 +115,24 @@
     lax.fori_loop(0, query_blocks, step, finish_top(top))
 
     tokens = o_ref.shape[1]
-    for j in range(len(ins)):
+    for j in range(flips):
         for half in range(2):
             rows = slice((2 * j + half) * tokens, (2 * j + half + 1) * tokens)
-            owner = me_ref[0] ^ (half * len(ins) + j)
+            owner = me_ref[0] ^ (half * flips + j)
             o_ref[owner, :, 0:HALF] = low(acc[rows, :])
             o_ref[owner, :, HALF:PACK] = done[rows, :]
 
 
-def attend_pair(pieces, me):
+def attend_pair(groups, places, me):
+    pieces = [piece for group in groups for piece in group]
+    flips = len(groups[0])
     tokens = pieces[0].shape[1]
-    blocks = 2 * len(pieces)
+    blocks = 2 * flips
     length = blocks * tokens
     bq, kb = min(256, length), min(256, length)
     vmem = pl.BlockSpec(memory_space=pltpu.VMEM)
     return pl.pallas_call(
-        functools.partial(pair_body, bq, kb),
+        functools.partial(pair_body, bq, kb, flips, places),
         out_shape=jax.ShapeDtypeStruct((blocks, tokens, PACK), jnp.bfloat16),
         in_specs=[pl.BlockSpec(memory_space=pltpu.SMEM)] + [vmem] * len(pieces),
         out_specs=vmem,
@@ -141,79 +152,63 @@
     )(me, *pieces)
 
 
-def lane_piece(array, head, slot):
-    piece = array[:, head * HEAD // HALF * HALF :][:, :HALF]
-    return piece if head % 2 == slot % 2 else pltpu.roll(piece, HEAD, 1)
-
-
-def project_body(count, groups, unit_ref, here_ref, there_ref, grad_here, grad_there, wq_ref, wk_ref, wv_ref, *outs):
+def project_body(groups, unit_ref, here_ref, there_ref, wq_ref, wk_ref, wv_ref, *outs):
     first = lax.broadcasted_iota(jnp.int32, (1, HALF), 1) < HEAD
-    width = count * HEAD
     weights = jnp.concatenate([wq_ref[...], wk_ref[...], wv_ref[...]], axis=1)
     projected = dot(jnp.concatenate([here_ref[...], there_ref[...]], axis=0), weights)
-    query, key, value = (projected[:, part * width : (part + 1) * width] for part in range(3))
-    grad = jnp.concatenate([grad_here[...], grad_there[...]], axis=0).astype(jnp.float32)
-    packs = []
-    for head in range(count):
-        left = jnp.where(first, lane_piece(key, head, 0), lane_piece(value, head, 1))
-        right = jnp.where(first, lane_piece(query, head, 0), lane_piece(grad, head, 1))
-        packs.append(low(jnp.concatenate([left, right], axis=1)).reshape(2, -1, PACK))
+    query, key, value = (projected[:, kind * HALF : (kind + 1) * HALF] for kind in range(3))
+    pieces = [
+        jnp.where(first, key, pltpu.roll(value, HEAD, 1)),
+        query,
+        jnp.where(first, pltpu.roll(key, HEAD, 1), value),
+    ]
+    packed = low(jnp.concatenate(pieces, axis=1)).reshape(2, -1, 3 * HALF)
     for flip in range(groups):
 
         @pl.when(pl.program_id(0) == flip)
         def _():
-            for head in range(count):
-                outs[head * groups + flip][...] = packs[head]
-
-
-def project(normed, grads, full_qkv, unit, heads, offset, count):
-    halves, (tokens, channels) = len(normed), normed[0].shape
+            lane = 0
+            for out in outs[flip::groups]:
+                out[...] = packed[:, :, lane : lane + out.shape[2]]
+                lane += out.shape[2]
+
+
+def project(normed, full_qkv, unit, heads, offset, widths):
+    tokens, channels = normed[0].shape
     groups = HEADS // heads
-    width = count * HEAD
-    steps = heads // count
+    steps = heads // 2
 
     def columns(kind):
-        return pl.BlockSpec(
-            (channels, width), lambda j, unit: (0, (kind * groups + (j ^ unit[0])) * steps + offset // count)
-        )
-
+        return pl.BlockSpec((channels, HALF), lambda j, unit: (0, (kind * groups + (j ^ unit[0])) * steps + offset // 2))
+
+    shapes = [(2, tokens, width) for width in widths for _ in range(groups)]
+    rows = pl.BlockSpec((tokens, channels), lambda j, unit: (0, 0))
     results = pl.pallas_call(
-        functools.partial(project_body, count, groups),
-        out_shape=[jax.ShapeDtypeStruct((halves, tokens, PACK), jnp.bfloat16)] * (count * groups),
+        functools.partial(project_body, groups),
+        out_shape=[jax.ShapeDtypeStruct(shape, jnp.bfloat16) for shape in shapes],
         grid_spec=pltpu.PrefetchScalarGridSpec(
             num_scalar_prefetch=1,
             grid=(groups,),
-            in_specs=[
-                pl.BlockSpec((tokens, channels), lambda j, unit: (0, 0)),
-                pl.BlockSpec((tokens, channels), lambda j, unit: (0, 0)),
-                pl.BlockSpec((tokens, width), lambda j, unit: (0, j ^ unit[0])),
-                pl.BlockSpec((tokens, width), lambda j, unit: (0, j ^ unit[0])),
-                columns(0),
-                columns(1),
-                columns(2),
-            ],
-            out_specs=[pl.BlockSpec((halves, tokens, PACK), lambda j, unit: (0, 0, 0))] * (count * groups),
+            in_specs=[rows, rows, columns(0), columns(1), columns(2)],
+            out_specs=[pl.BlockSpec(shape, lambda j, unit: (0, 0, 0)) for shape in shapes],
         ),
         compiler_params=pltpu.CompilerParams(vmem_limit_bytes=VMEM),
         cost_estimate=pl.CostEstimate(
-            flops=2 * halves * tokens * channels * groups * width, bytes_accessed=2**16, transcendentals=0
+            flops=4 * tokens * channels * groups * 3 * HALF, bytes_accessed=2**16, transcendentals=0
         ),
         name="project",
-    )(unit, *normed, *grads, full_qkv, full_qkv, full_qkv)
-    return [results[head * groups : (head + 1) * groups] for head in range(count)]
-
-
-def project_plain(normed, grads, full_qkv, unit, heads, offset, count):
-    normed, grads = jnp.stack(normed), jnp.stack(grads)
-    halves, tokens, channels = normed.shape
+    )(unit, *normed, full_qkv, full_qkv, full_qkv)
+    return [results[index * groups : (index + 1) * groups] for index in range(len(widths))]
+
+
+def project_plain(normed, full_qkv, unit, heads, offset):
+    normed = jnp.stack(normed)
     groups = HEADS // heads
     qkv = low(jnp.einsum("itc,cd->itd", normed, full_qkv, preferred_element_type=jnp.float32))
-    split = qkv.reshape(halves, tokens, 3, groups, heads, HEAD)[:, :, :, :, offset : offset + count]
-    grads = grads.reshape(halves, tokens, 1, groups, count, HEAD)
-    packed = jnp.concatenate([split[:, :, 1:3], split[:, :, 0:1], grads], axis=2)
-    packed = packed.transpose(4, 3, 0, 1, 2, 5).reshape(count, groups, halves, tokens, PACK)
-    packed = jnp.take(packed, jnp.arange(groups) ^ unit[0], axis=1)
-    return [[packed[head, flip] for flip in range(groups)] for head in range(count)]
+    split = qkv.reshape(*normed.shape[:2], 3, groups, heads, HEAD)[:, :, :, :, offset]
+    packed = jnp.concatenate([split[:, :, 1:3], split[:, :, 0:1], jnp.zeros_like(split[:, :, 0:1])], axis=2)
+    packed = packed.transpose(3, 0, 1, 2, 4).reshape(groups, *normed.shape[:2], PACK)
+    return [[lax.dynamic_index_in_dim(packed, unit[0] ^ flip, 0, keepdims=False) for flip in range(groups)]]
 
 
 def weight_body(images, here_ref, norm_ref, cot_ref, grad_ref, *refs):
@@ -271,7 +266,7 @@
         ],
         compiler_params=pltpu.CompilerParams(vmem_limit_bytes=VMEM),
         cost_estimate=pl.CostEstimate(
-            flops=2 * channels * rows * groups * PACK, bytes_accessed=2**23, transcendentals=0
+            flops=channels * rows, bytes_accessed=2**12, transcendentals=0
         ),
         name="weight_grads",
     )(here, normed_t, cotangent_t, grads)
@@ -387,7 +382,7 @@
         ],
         compiler_params=pltpu.CompilerParams(vmem_limit_bytes=VMEM),
         cost_estimate=pl.CostEstimate(
-            flops=2 * images * tokens * channels * 4 * groups * count * HEAD, bytes_accessed=2**24, transcendentals=0
+            flops=images * tokens * channels, bytes_accessed=2**12, transcendentals=0
         ),
         name="project_back",
     )(*grads, full_qkv, full_out, *(tail or ()))
@@ -418,15 +413,17 @@
     return array.astype(jnp.float32)
 
 
-def sum_near(parts, steps):
+def move_near(parts):
     rep = parts[0].shape[0]
-    if steps == 1:
-        total = wide(parts[0][0])
-        for own, part in enumerate(parts):
-            for row in range(rep):
-                if own or row:
-                    total = total + wide(flipped(part[row], ("rep", "own"), row * len(parts) + own))
-        return total
+    moved = []
+    for own, part in enumerate(parts):
+        for row in range(rep):
+            flip = row * len(parts) + own
+            moved.append(flipped(part[row], ("rep", "own"), flip) if flip else part[row])
+    return moved
+
+
+def sum_own(parts):
     total = wide(parts[0])
     for own in range(1, len(parts)):
         total = total + wide(flipped(parts[own], "own", own))
@@ -440,25 +437,28 @@
     return mine
 
 
-def sum_far(near, groups):
-    place = lax.axis_index("seq")
+def sum_half(near, groups):
+    place = lax.axis_index("seq") % groups
     cut = near.reshape(2, groups, *near.shape[1:])
-
-    def pick(array, index, dim):
-        return lax.dynamic_index_in_dim(array, index, dim, keepdims=False)
-
-    total = pick(cut, place % groups, 1)
+    total = lax.dynamic_index_in_dim(cut, place, 1, keepdims=False)
     for flip in range(1, groups):
-        total = total + wide(flipped(low(pick(cut, (place % groups) ^ flip, 1)), "seq", flip))
-    half = place // groups
-    return pick(total, half, 0) + wide(flipped(low(pick(total, 1 - half, 0)), "seq", groups))
+        sent = lax.dynamic_index_in_dim(cut, place ^ flip, 1, keepdims=False)
+        total = total + wide(flipped(low(sent), "seq", flip))
+    return total
+
+
+def sum_halves(total, groups):
+    half = lax.axis_index("seq") // groups
+    sent = lax.dynamic_index_in_dim(total, 1 - half, 0, keepdims=False)
+    return lax.dynamic_index_in_dim(total, half, 0, keepdims=False) + wide(flipped(low(sent), "seq", groups))
 
 
 def sum_seq(array, hold=()):
     bits = lax.axis_size("seq").bit_length() - 1
-    for bit in range(bits):
-        if bit == bits - 1:
+    for step in range(bits):
+        if step == bits - 1:
             array = after(array, hold)
+        bit = step - 1 if step else bits - 1
         array = array + flipped(array, "seq", 1 << bit)
     return array
 
@@ -501,7 +501,7 @@
 
     rows = latent.transpose(1, 0, 2)
     cot_rows = cotangent.transpose(1, 0, 2)
-    count = 2 if aligned else heads
+    count = 2 if aligned else 1
     offsets = range(0, heads, count)
     grad_parts = []
     for offset in offsets:
@@ -511,7 +511,6 @@
     work = swapped(rows)
     first_grad = grad_parts[0]
     grad_parts[0] = swapped(grad_parts[0])
-    grad_parts[1:] = [swapped(after(part, grad_parts[0])) for part in grad_parts[1:]]
 
     values = rows.astype(jnp.float32)
     sums = jnp.stack([jnp.sum(values, axis=1), jnp.sum(values * values, axis=1)])
@@ -525,40 +524,92 @@
     work[1] = after(work[1], normed_t, cotangent_t)
     work_mean, work_inv = pick(mean, image), pick(inv_std, image)
     work = [low((wide(part) - work_mean) * work_inv * norm_gain + norm_shift) for part in work]
-    kernel = project if aligned else project_plain
-    sends = []
-    for offset, grad_part in zip(offsets, grad_parts):
-        sends += kernel(work, grad_part, full_qkv, unit, heads, offset, count)
+
+    def exchanged(pieces):
+        return [pieces[0]] + [flipped(pieces[flip], "seq", flip) for flip in range(1, groups)]
+
+    def grad_pieces(halves):
+        pieces = []
+        for flip in range(groups):
+            start = (unit[0] ^ flip) * (count * HEAD)
+            both = [lax.dynamic_slice_in_dim(half, start, count * HEAD, 1) for half in halves]
+            pieces.append(jnp.pad(jnp.stack(both), ((0, 0), (0, 0), (0, HALF - count * HEAD))))
+        return pieces
+
+    arrays, heads_plan, moved = [], [], {}
+    for index, offset in enumerate(offsets):
+        base = len(arrays)
+        if not aligned:
+            arrays += project_plain(work, full_qkv, unit, heads, offset)
+            heads_plan.append(((base, 0, 0), (base, HALF, 0), (base + 1, 0, 0)))
+        elif index == 0:
+            arrays += project(work, full_qkv, unit, heads, offset, (PACK, HALF))
+            heads_plan.append(((base, 0, 0), (base, HALF, 0), (base + 2, 0, 0)))
+            heads_plan.append(((base + 1, 0, 0), (base, HALF, 1), (base + 2, 0, 1)))
+        else:
+            arrays += project(work, full_qkv, unit, heads, offset, (PACK + HALF,))
+            heads_plan.append(((base, 0, 0), (base, HALF, 0), (base + 1, 0, 0)))
+            heads_plan.append(((base, PACK, 0), (base, HALF, 1), (base + 1, 0, 1)))
+        if index:
+            arrays.append(grad_parts[index])
+        else:
+            arrays.append(None)
+    early = arrays[2 if aligned else 1 :][1:2]
+    moved[0] = exchanged(arrays[0])
+    first = 2 if aligned else 1
+    arrays[first] = grad_pieces(after(grad_parts[0], moved[0], early))
+    moved[first] = exchanged(arrays[first])
+    for index in range(1, len(arrays)):
+        if index != first:
+            arrays[index] = after(arrays[index], moved[first])
+
     grads, nears = [], []
     result = None
     for head in range(heads):
-        pieces = [sends[head][0]] + [flipped(sends[head][flip], "seq", flip) for flip in range(1, groups)]
+        used = sorted({place[0] for place in heads_plan[head]})
+        late = heads_plan[head][2][0]
+        if late != first and late not in moved:
+            halves = swapped(arrays[late])
+            moved[late] = exchanged(grad_pieces(after(halves, first_result)))
+        for index in used:
+            if index not in moved:
+                moved[index] = exchanged(arrays[index])
+        operands = [moved[index] for index in used]
         if head >= 1:
-            pieces, result = lax.optimization_barrier((pieces, result))
+            operands, result = lax.optimization_barrier((operands, result))
             grads.append(lax.all_to_all(result, "seq", split_axis=0, concat_axis=0, tiled=True))
-        if head + 2 < heads:
-            pieces = after(pieces, sends[head + 2])
         if head >= 2:
-            parts = weight_parts(grads[head - 2])
-            pieces = after(pieces, parts)
-            nears.append(sum_near(parts, 1))
-        result = attend_pair(pieces, me)
+            operands = after(operands, grads[head - 2])
+        if head == 2:
+            parts = weight_parts(grads[0])
+            operands = after(operands, parts)
+            near_moved = move_near(parts)
+        places = tuple((used.index(index), lane, half) for index, lane, half in heads_plan[head])
+        result = attend_pair(operands, places, me)
+        if head == 0:
+            first_result = result
     if heads > 1:
-        result = after(result, grads[-1], nears)
+        result = after(result, grads[-1])
+    if heads > 2:
+        result = after(result, near_moved)
+        nears.append(sum(wide(part) for part in near_moved))
+        grads[1:] = after(grads[1:], result)
     grads.append(lax.all_to_all(result, "seq", split_axis=0, concat_axis=0, tiled=True))
-    for index in range(len(nears), heads - 1):
-        nears.append(sum_rep(sum_near(weight_parts(grads[index]), 2)))
+    back = mixed = jnp.zeros((images * tokens, channels), jnp.float32)
     if aligned and heads > count:
         back, mixed = project_back(grads[:count], full_qkv, full_out, heads, 0, images)
-        grads[-1] = after(grads[-1], back, mixed, nears)
-    last = sum_near(weight_parts(grads[-1]), 2)
+        grads[-1] = after(grads[-1], back, mixed)
+    middle = [sum_own(weight_parts(grads[index])) for index in range(len(nears), heads - 1)]
+    if middle:
+        middle = [sum_rep(total) for total in middle]
+        nears += middle
+        grads[-1] = after(grads[-1], middle)
+    last = sum_own(weight_parts(grads[-1]))
     if heads > 1:
         grads[-1], nears = after((grads[-1], nears), last)
     nears.append(sum_rep(last))
     gain = norm_gain[None, :]
     if aligned:
-        if heads == count:
-            back = mixed = jnp.zeros((images * tokens, channels), jnp.float32)
         offset = heads - count
         tail = (back, mixed, rows, mean, inv_std, gain)
         back, mixed_out, sums = project_back(grads[offset:], full_qkv, full_out, heads, offset, images, tail)
@@ -571,11 +622,12 @@
     sums = after(sums, nears[-1])
     weight_sums = []
     if heads > 1:
-        early = sum_far(jnp.concatenate(nears[:-1], axis=2), groups)
+        early = sum_halves(sum_half(jnp.concatenate(nears[:-1], axis=2), groups), groups)
         weight_sums = jnp.split(early, heads - 1, axis=1)
-    weight_sums.append(sum_far(nears[-1], groups))
-
-    mixed_out = mixed_out.transpose(1, 0, 2)
+    last_sum = sum_half(nears[-1], groups)
+    weight_sums.append(sum_halves(last_sum, groups))
+
+    mixed_out = after(mixed_out, last_sum).transpose(1, 0, 2)
     mean_one, mean_two = mean_groups(sums)
     grad_values = inv_std * (back * norm_gain - spread(mean_one) - centred * spread(mean_two))
     grad_latent = low(cot_rows.astype(jnp.float32) + grad_values).transpose(1, 0, 2)

time: 635 us -> 624 us (0.983)
  waiting for transfers between devices: 105 us -> 78.9 us
  starting transfers between devices: 67.9 us -> 81.3 us
    all_to_all x4, waiting for transfers between devices: 18.6 us -> 0.01 us  [shards(): lax.all_to_all(result, 'seq', split_axis=0, concat_axis=0, tiled=True)]
    ppermute x39 -> x41, starting transfers between devices: 43.8 us -> 56.4 us  [flipped(): lax.ppermute(array, axis, [(i, i ^ flip) for i in range(lax.axis_size(axi...]
    ppermute x39 -> x41, waiting for transfers between devices: 77.6 us -> 71.9 us  [flipped(): lax.ppermute(array, axis, [(i, i ^ flip) for i in range(lax.axis_size(axi...]
    unnamed x83 -> x89, local copies, waits for them, and re-layouts: 23.4 us -> 21.2 us
  transfers between devices with their start and end apart: 46 -> 48, of which waited for: 15 -> 11; matrix products, arithmetic and copies ran while one was open for 11% -> 11% of each run, Pallas kernels for 55% -> 56%
where the time goes in v4:
time: 624 us; the launch traced here: 614 us
  Pallas kernels  354 us (57%)
  starting transfers between devices  81.3 us (13%)
  waiting for transfers between devices  78.9 us (13%)
  local copies, waits for them, and re-layouts  52.8 us (8%)
  other arithmetic  28.8 us (5%)
  between operations  15 us (2%)
    pallas_call x4, Pallas kernels, attend_pair(): pl.pallas_call(functools.partial(pair_body, bq, kb, flips, places), out_s...  268 us
    ppermute x41, waiting for transfers between devices, flipped(): lax.ppermute(array, axis, [(i, i ^ flip) for i in range(lax.axis_size(axi...  71.9 us
    ppermute x41, starting transfers between devices, flipped(): lax.ppermute(array, axis, [(i, i ^ flip) for i in range(lax.axis_size(axi...  56.4 us
    pallas_call x2, Pallas kernels, project_back(): pl.pallas_call(functools.partial(back_body, offset, heads), out_shape=out...  33.5 us
    pallas_call x4, Pallas kernels, weight_grads(): pl.pallas_call(functools.partial(weight_body, images), out_shape=[jax.Sha...  30 us
    all_to_all x4, starting transfers between devices, shards(): lax.all_to_all(result, 'seq', split_axis=0, concat_axis=0, tiled=True)  22.3 us
    pallas_call x2, Pallas kernels, project(): pl.pallas_call(functools.partial(project_body, groups), out_shape=[jax.Sh...  21.5 us
    unnamed x89, local copies, waits for them, and re-layouts  21.2 us
  transfers between devices with their start and end apart: 48, of which 11 were waited for; matrix products, arithmetic and copies ran while one was open for 11% of the time, Pallas kernels for 56%

profile of v4, /device:TPU:0, one launch (start us, length us, event | category | flops | bytes accessed | tf_op | source)
XLA Modules:
  0.0 613.5 jit_solution(2083067652606415140)
XLA Ops:
  9.9 4.1 collective-permute-start
  14.0 1.8 copy.123
  15.8 2.5 dynamic-slice_bitcast_fusion
  18.4 1.8 collective-permute-start.1
  20.2 3.9 copy.78
  24.1 4.4 copy.81
  28.6 3.2 fusion.51
  31.8 1.5 fusion.19
  35.6 2.7 collective-permute-start.4
  38.4 9.5 %collective-permute-done.2 = f32[2,2,32]{2,1,0:T(2,128)S(1)} collective-permute-done((f32[2,2,32]{2,1,0:T(2,128)S(1)}, f32[2,2,32]{2,1,0:T(2,128)S(1)}, u32[]{:S(2)}, u32[]{:S(2)}) %collective-permute-start.2) | collective-permute-done | bytes 544 | tf_op jit(solution)/shard_map/ppermute | solution.py:405
  48.5 2.5 fusion.5
  51.0 4.6 copy.80
  55.6 34.6 %collective-permute-done.3 = bf16[512,1280]{1,0:T(8,128)(2,1)} collective-permute-done((bf16[512,1280]{1,0:T(8,128)(2,1)}, bf16[512,1280]{1,0:T(8,128)(2,1)}, u32[]{:S(2)}, u32[]{:S(2)}) %collective-permute-start.3) | collective-permute-done | bytes 1310752 | tf_op jit(solution)/shard_map/ppermute | solution.py:405
  90.3 3.9 add_convert_fusion
  94.2 10.7 %project.3 = (bf16[2,512,256]{2,1,0:T(8,128)(2,1)}, bf16[2,512,256]{2,1,0:T(8,128)(2,1)}, bf16[2,512,256]{2,1,0:T(8,128)(2,1)}, bf16[2,512,256]{2,1,0:T(8,128)(2...) custom-call(s32[1]{0:T(128)S(6)} %select_n.84.unit_ref, ...), custom_call_target="tpu_custom_call" | custom-call | flops 4026531840 | bytes 65536 | tf_op jit(solution)/shard_map/project/pallas_call | solution.py:186
  106.5 1.9 collective-permute-start.7
  108.4 10.8 %project.2 = (bf16[2,512,384]{2,1,0:T(8,128)(2,1)}, bf16[2,512,384]{2,1,0:T(8,128)(2,1)}, bf16[2,512,384]{2,1,0:T(8,128)(2,1)}, bf16[2,512,384]{2,1,0:T(8,128)(2,1)}) custom-call(s32[1]{0:T(128)S(6)} %select_n.84.unit_ref, bf16[512,1280]{1,0:T(8,128)(2,1)} %get-tuple-element.280.here_ref, bf16[512,1280]{1,0:T(8,128)(2,1)} %get-tuple-element.279.there_ref, ...), custom_call_target="tpu_custom_call" | custom-call | flops 4026531840 | bytes 65536 | tf_op jit(solution)/shard_map/project/pallas_call | solution.py:186
  119.2 2.3 collective-permute-done.6.refs_2_
  121.5 7.6 %collective-permute-done.7.refs_3_ = bf16[2,512,256]{2,1,0:T(8,128)(2,1)S(1)} collective-permute-done((bf16[2,512,256]{2,1,0:T(8,128)(2,1)}, bf16[2,512,256]{2,1,0:T(8,128)(2,1)S(1)}, u32[]{:S(2)}, u32[]{:S(2)}) %collective-permute-start.7) | collective-permute-done | bytes 524320 | tf_op jit(solution)/shard_map/ppermute | solution.py:405
  130.5 1.6 collective-permute-start.8
  132.6 1.7 collective-permute-start.10
  134.3 1.6 fusion.22
  136.6 2.8 collective-permute-done.8.refs_5_.refs_9_
  139.6 2.9 collective-permute-done.10.refs_7_.refs_11_
  146.9 3.1 collective-permute-start.14
  151.5 67.0 %attend_pair.4 = bf16[8,512,256]{2,1,0:T(8,128)(2,1)} custom-call(s32[1]{0:T(128)} %bitcast.me_ref, bf16[2,512,256]{2,1,0:T(8,128)(2,1)} %get-tuple-element.138.refs_0_, bf16[2,512,256]{2,1,0:T(8,128)(2,1)} %copy-done.28, bf16[2,512,256]{2,1,0:T(8,128)(2,1)} %copy-done.29, bf16[2,512,256]{2,1,0:T(8,128)(2,1)} %copy-done.30, ...), custom_call_target="tpu_custom_call" | custom-call | flops 51539607552 | bytes 4194304 | tf_op jit(solution)/shard_map/attend_pair/pallas_call | solution.py:134
  218.6 1.8 collective-permute-start.12
  221.1 3.6 all-to-all-start.1
  224.9 2.0 collective-permute-start.15
  228.7 67.2 %attend_pair.5 = bf16[8,512,256]{2,1,0:T(8,128)(2,1)} custom-call(s32[1]{0:T(128)} %bitcast.me_ref, bf16[2,512,256]{2,1,0:T(8,128)(2,1)} %get-tuple-element.138.refs_0_, bf16[2,512,256]{2,1,0:T(8,128)(2,1)} %copy-done.28, bf16[2,512,256]{2,1,0:T(8,128)(2,1)} %copy-done.29, bf16[2,512,256]{2,1,0:T(8,128)(2,1)} %copy-done.30, ...), custom_call_target="tpu_custom_call" | custom-call | flops 51539607552 | bytes 4194304 | tf_op jit(solution)/shard_map/attend_pair/pallas_call | solution.py:134
  298.1 6.2 %all-to-all-start = ((bf16[8,512,256]{2,1,0:T(8,128)(2,1)}), bf16[8,512,256]{2,1,0:T(8,128)(2,1)}, u32[]{:S(2)}, u32[]{:S(2)}) async-start(bf16[8,512,256]{2,1,0:T(8,128)(2,1)} %attend_pair.5), calls=%async_computation | async-start | bytes 4194304 | tf_op jit(solution)/shard_map/all_to_all | solution.py:580
  304.3 7.4 %weight_grads.4 = (bf16[2,8,40,1024]{3,2,1,0:T(8,128)(2,1)}, bf16[2,8,40,1024]{3,2,1,0:T(8,128)(2,1)}) custom-call(s32[1]{0:T(128)} %bitcast.40.here_ref, bf16[1280,1024]{1,0:T(8,128)(2,1)} %bitcast.214, bf16[1280,1024]{1,0:T(8,128)(2,1)} %bitcast.210, bf16[8,512,256]{2,1,0:T(8,128)(2,1)} %copy-done.3), custom_call_target="tpu_custom_call" | custom-call | flops 1310720 | bytes 4096 | tf_op jit(solution)/shard_map/weight_grads/pallas_call | solution.py:252
  311.7 2.0 slice_bitcast_fusion.5
  315.1 1.5 collective-permute-start.21
  317.3 67.1 %attend_pair.6 = bf16[8,512,256]{2,1,0:T(8,128)(2,1)} custom-call(s32[1]{0:T(128)} %bitcast.me_ref, bf16[2,512,384]{2,1,0:T(8,128)(2,1)} %get-tuple-element.187.refs_0_, bf16[2,512,384]{2,1,0:T(8,128)(2,1)} %collective-permute-done.11.refs_1_, bf16[2,512,384]{2,1,0:T(8,128)(2,1)} %collective-permute-done.12.refs_2_, ...), custom_call_target="tpu_custom_call" | custom-call | flops 51539607552 | bytes 4194304 | tf_op jit(solution)/shard_map/attend_pair/pallas_call | solution.py:134
  384.4 6.0 all-to-all-start.2
  390.4 67.1 %attend_pair.7 = bf16[8,512,256]{2,1,0:T(8,128)(2,1)} custom-call(s32[1]{0:T(128)} %bitcast.me_ref, bf16[2,512,384]{2,1,0:T(8,128)(2,1)} %get-tuple-element.187.refs_0_, bf16[2,512,384]{2,1,0:T(8,128)(2,1)} %collective-permute-done.11.refs_1_, bf16[2,512,384]{2,1,0:T(8,128)(2,1)} %collective-permute-done.12.refs_2_, ...), custom_call_target="tpu_custom_call" | custom-call | flops 51539607552 | bytes 4194304 | tf_op jit(solution)/shard_map/attend_pair/pallas_call | solution.py:134
  457.6 6.5 %all-to-all-start.3 = ((bf16[8,512,256]{2,1,0:T(8,128)(2,1)}), bf16[8,512,256]{2,1,0:T(8,128)(2,1)}, u32[]{:S(2)}, u32[]{:S(2)}) async-start(bf16[8,512,256]{2,1,0:T(8,128)(2,1)} %attend_pair.7), calls=%async_computation.3 | async-start | bytes 4194304 | tf_op jit(solution)/shard_map/all_to_all | solution.py:597
  464.1 7.4 %weight_grads.6 = (bf16[2,8,40,1024]{3,2,1,0:T(8,128)(2,1)}, bf16[2,8,40,1024]{3,2,1,0:T(8,128)(2,1)}) custom-call(s32[1]{0:T(128)} %bitcast.40.here_ref, bf16[1280,1024]{1,0:T(8,128)(2,1)} %bitcast.215, bf16[1280,1024]{1,0:T(8,128)(2,1)} %bitcast.211, bf16[8,512,256]{2,1,0:T(8,128)(2,1)} %copy-done.4), custom_call_target="tpu_custom_call" | custom-call | flops 1310720 | bytes 4096 | tf_op jit(solution)/shard_map/weight_grads/pallas_call | solution.py:252
  471.6 7.6 %weight_grads.5 = (bf16[2,8,40,1024]{3,2,1,0:T(8,128)(2,1)}, bf16[2,8,40,1024]{3,2,1,0:T(8,128)(2,1)}) custom-call(s32[1]{0:T(128)} %bitcast.40.here_ref, bf16[1280,1024]{1,0:T(8,128)(2,1)} %bitcast.216, bf16[1280,1024]{1,0:T(8,128)(2,1)} %bitcast.212, bf16[8,512,256]{2,1,0:T(8,128)(2,1)} %all-to-all-done.refs_1_.grad_ref), custom_call_target="tpu_custom_call" | custom-call | flops 1310720 | bytes 4096 | tf_op jit(solution)/shard_map/weight_grads/pallas_call | solution.py:252
  480.2 1.5 collective-permute-start.27
  483.1 1.6 collective-permute-start.25
  484.6 15.0 %project_back.2 = (f32[1024,1280]{1,0:T(8,128)}, f32[1024,1280]{1,0:T(8,128)}) custom-call(bf16[8,512,256]{2,1,0:T(8,128)(2,1)} %copy-done.3, bf16[8,512,256]{2,1,0:T(8,128)(2,1)} %all-to-all-done.refs_1_.grad_ref, bf16[1280,3072]{1,0:T(8,128)(2,1)} %all-gather.5.cloned.1.call-done.wq_ref.wk_ref.wv_ref.refs_2_, ...), custom_call_target="tpu_custom_call" | custom-call | flops 1310720 | bytes 4096 | tf_op jit(solution)/shard_map/project_back/pallas_call | solution.py:373
  501.0 10.1 %collective-permute-done.25 = bf16[8,40,1024]{2,1,0:T(8,128)(2,1)S(1)} collective-permute-done((bf16[8,40,1024]{2,1,0:T(8,128)(2,1)S(1)}, bf16[8,40,1024]{2,1,0:T(8,128)(2,1)S(1)}, u32[]{:S(2)}, u32[]{:S(2)}) %collective-permute-start.25) | collective-permute-done | bytes 655392 | tf_op jit(solution)/shard_map/ppermute | solution.py:405
  512.4 7.6 %weight_grads.7 = (bf16[2,8,40,1024]{3,2,1,0:T(8,128)(2,1)}, bf16[2,8,40,1024]{3,2,1,0:T(8,128)(2,1)}) custom-call(s32[1]{0:T(128)} %bitcast.40.here_ref, bf16[1280,1024]{1,0:T(8,128)(2,1)} %bitcast.217, bf16[1280,1024]{1,0:T(8,128)(2,1)} %bitcast.213, bf16[8,512,256]{2,1,0:T(8,128)(2,1)} %all-to-all-done.3.grad_ref.refs_1_), custom_call_target="tpu_custom_call" | custom-call | flops 1310720 | bytes 4096 | tf_op jit(solution)/shard_map/weight_grads/pallas_call | solution.py:252
  520.0 2.0 convert_add_fusion.3
  524.3 2.0 convert_add_fusion
  526.3 1.5 collective-permute-start.29
  528.4 1.8 copy-done.7
  531.4 2.0 collective-permute-start.36
  535.5 18.6 %project_back.3 = (f32[1024,1280]{1,0:T(8,128)}, bf16[2,512,1280]{2,1,0:T(8,128)(2,1)}, f32[2,2,1,1280]{3,2,1,0:T(1,128)}) custom-call(bf16[8,512,256]{2,1,0:T(8,128)(2,1)} %copy-done.4, bf16[8,512,256]{2,1,0:T(8,128)(2,1)} %all-to-all-done.3.grad_ref.refs_1_, bf16[1280,3072]{1,0:T(8,128)(2,1)} %all-gather.5.cloned.1.call-done.wq_ref.wk_ref.wv_ref.refs_2_, ...), custom_call_target="tpu_custom_call" | custom-call | flops 1310720 | bytes 4096 | tf_op jit(solution)/shard_map/project_back/pallas_call | solution.py:373
  554.8 2.3 fusion.25
  557.3 3.0 collective-permute-start.33
  560.3 1.9 fusion.29
  562.2 1.7 collective-permute-start.34
  563.9 2.4 collective-permute-start.39
  567.8 1.9 fusion.39
  571.4 1.8 collective-permute-start.32
  573.6 4.1 fusion.10
  577.8 4.2 copy.94
  583.5 2.1 collective-permute-start.40
  585.6 4.2 copy.93
  592.1 2.6 all-to-all-start.4
  597.7 5.5 all-to-all-done.4
  (227 shorter events, 48.3 us)
Async XLA Ops:
  7.2 21.4 %all-gather.3.cloned.1.call-start = ((), (), s32[]{:S(2)}) async-start(), calls=%async_computation.5 | async-start | bytes 3932160 | tf_op jit(solution)/shard_map/all_gather | solution.py:484
  7.9 86.3 %all-gather.5.cloned.1.call-start = ((), (), s32[]{:S(2)}) async-start(), calls=%async_computation.6 | async-start | bytes 11796480 | tf_op jit(solution)/shard_map/all_gather | solution.py:483
  9.9 8.5 %collective-permute-start = (f32[2,2,32]{2,1,0:T(2,128)S(1)}, f32[2,2,32]{2,1,0:T(2,128)S(1)}, u32[]{:S(2)}, u32[]{:S(2)}) collective-permute-start(f32[2,2,32]{2,1,0:T(2,128)S(1)} %maximum_reduce_fusion), channel_id=1, source_target_pairs={{0,16},{4,20},{8,24},{12,28},{16,0},{20,4},{24,8},{28,12},{1,17},{... | collective-permute-start | bytes 1544 | tf_op jit(solution)/shard_map/ppermute | solution.py:405
  18.3 71.9 %collective-permute-start.3 = (bf16[512,1280]{1,0:T(8,128)(2,1)}, bf16[512,1280]{1,0:T(8,128)(2,1)}, u32[]{:S(2)}, u32[]{:S(2)}) collective-permute-start(bf16[512,1280]{1,0:T(8,128)(2,1)} %dynamic-slice_bitcast_fusion), channel_id=1, source_target_pairs={{0,16},{4,20},{8,24},{12,28},{16,0},{20,4},{24,8},{28,12},{1,17},{... | collective-permute-start | bytes 3932168 | tf_op jit(solution)/shard_map/ppermute | solution.py:405
  18.4 10.2 %collective-permute-start.1 = (f32[2,2,32]{2,1,0:T(2,128)S(1)}, f32[2,2,32]{2,1,0:T(2,128)S(1)}, u32[]{:S(2)}, u32[]{:S(2)}) collective-permute-start(f32[2,2,32]{2,1,0:T(2,128)S(1)} %add.181), channel_id=1, source_target_pairs={{0,4},{4,0},{8,12},{12,8},{16,20},{20,16},{24,28},{28,24},{1,5},{5... | collective-permute-start | bytes 1544 | tf_op jit(solution)/shard_map/ppermute | solution.py:405
  31.8 16.8 %copy-start.19 = (f32[1280]{0:T(1024)S(1)}, f32[1280]{0:T(1024)}, u32[]{:S(2)}) copy-start(f32[1280]{0:T(1024)} %param.8) | copy-start | bytes 15364
  31.8 16.8 %copy-start.27 = (f32[1280]{0:T(1024)S(1)}, f32[1280]{0:T(1024)}, u32[]{:S(2)}) copy-start(f32[1280]{0:T(1024)} %param.9) | copy-start | bytes 15364
  33.3 14.6 %collective-permute-start.2 = (f32[2,2,32]{2,1,0:T(2,128)S(1)}, f32[2,2,32]{2,1,0:T(2,128)S(1)}, u32[]{:S(2)}, u32[]{:S(2)}) collective-permute-start(f32[2,2,32]{2,1,0:T(2,128)S(1)} %add.182), channel_id=1, source_target_pairs={{0,8},{4,12},{8,0},{12,4},{16,24},{20,28},{24,16},{28,20},{1,9},{5... | collective-permute-start | bytes 1544 | tf_op jit(solution)/shard_map/ppermute | solution.py:405
  35.6 83.6 %collective-permute-start.4 = (bf16[512,512]{1,0:T(8,128)(2,1)}, bf16[512,512]{1,0:T(8,128)(2,1)}, u32[]{:S(2)}, u32[]{:S(2)}) collective-permute-start(bf16[512,512]{1,0:T(8,128)(2,1)} %get-tuple-element.254), channel_id=1, source_target_pairs={{0,16},{4,20},{8,24},{12,28},{16,0},{20,4},{24,8},{28,12},{1,17},{... | collective-permute-start | bytes 1572872 | tf_op jit(solution)/shard_map/ppermute | solution.py:405
  48.2 42.1 %copy-start.25 = (f32[2,1,1280]{2,1,0:T(1,128)}, f32[2,1,1280]{2,1,0:T(1,128)S(1)}, u32[]{:S(2)}) copy-start(f32[2,1,1280]{2,1,0:T(1,128)S(1)} %broadcast_in_dim_reshape.8.refs_7_) | copy-start | bytes 30724
  48.5 41.7 %copy-start.26 = (f32[2,1,1280]{2,1,0:T(1,128)}, f32[2,1,1280]{2,1,0:T(1,128)S(1)}, u32[]{:S(2)}) copy-start(f32[2,1,1280]{2,1,0:T(1,128)S(1)} %broadcast_in_dim_reshape.9.refs_8_) | copy-start | bytes 30724
  51.0 39.3 %copy-start.2 = (bf16[512,2,1280]{2,0,1:T(8,128)(2,1)S(1)}, bf16[512,2,1280]{2,0,1:T(8,128)(2,1)}, u32[]{:S(2)}) copy-start(bf16[512,2,1280]{2,0,1:T(8,128)(2,1)} %copy.123) | copy-start | bytes 7864324
  104.9 14.3 %collective-permute-start.5 = (bf16[2,512,256]{2,1,0:T(8,128)(2,1)}, bf16[2,512,256]{2,1,0:T(8,128)(2,1)S(1)}, u32[]{:S(2)}, u32[]{:S(2)}) collective-permute-start(bf16[2,512,256]{2,1,0:T(8,128)(2,1)} %get-tuple-element.118), channel_id=1, source_target_pairs={{0,4},{4,0},{8,12},{12,8},{16,20},{20,16},{24,28},{28,24},{1,5},{5... | collective-permute-start | bytes 1572872 | tf_op jit(solution)/shard_map/ppermute | solution.py:405
  106.5 15.1 %collective-permute-start.6 = (bf16[2,512,256]{2,1,0:T(8,128)(2,1)}, bf16[2,512,256]{2,1,0:T(8,128)(2,1)S(1)}, u32[]{:S(2)}, u32[]{:S(2)}) collective-permute-start(bf16[2,512,256]{2,1,0:T(8,128)(2,1)} %get-tuple-element.119), channel_id=1, source_target_pairs={{0,8},{4,12},{8,0},{12,4},{16,24},{20,28},{24,16},{28,20},{1,9},{5... | collective-permute-start | bytes 1572872 | tf_op jit(solution)/shard_map/ppermute | solution.py:405
  106.5 22.7 %collective-permute-start.7 = (bf16[2,512,256]{2,1,0:T(8,128)(2,1)}, bf16[2,512,256]{2,1,0:T(8,128)(2,1)S(1)}, u32[]{:S(2)}, u32[]{:S(2)}) collective-permute-start(bf16[2,512,256]{2,1,0:T(8,128)(2,1)} %get-tuple-element.120), channel_id=1, source_target_pairs={{0,12},{4,8},{8,4},{12,0},{16,28},{20,24},{24,20},{28,16},{1,13},{... | collective-permute-start | bytes 1572872 | tf_op jit(solution)/shard_map/ppermute | solution.py:405
  108.4 25.9 %copy-start.13 = (bf16[4,2,64,1280]{3,2,1,0:T(8,128)(2,1)S(1)}, bf16[4,2,64,1280]{3,2,1,0:T(8,128)(2,1)}, u32[]{:S(2)}) copy-start(bf16[4,2,64,1280]{3,2,1,0:T(8,128)(2,1)} %get-tuple-element.245) | copy-start | bytes 3932164
  119.2 15.1 %copy-start.6 = (bf16[512,2,1280]{2,1,0:T(2,128)(2,1)S(1)}, bf16[512,2,1280]{2,1,0:T(2,128)(2,1)}, u32[]{:S(2)}) copy-start(bf16[512,2,1280]{2,1,0:T(2,128)(2,1)} %param.7) | copy-start | bytes 7864324
  119.2 16.6 %copy-start.28 = (bf16[2,512,256]{2,1,0:T(8,128)(2,1)}, bf16[2,512,256]{2,1,0:T(8,128)(2,1)S(1)}, u32[]{:S(2)}) copy-start(bf16[2,512,256]{2,1,0:T(8,128)(2,1)S(1)} %collective-permute-done.5.refs_1_) | copy-start | bytes 1572868
  121.5 14.3 %copy-start.29 = (bf16[2,512,256]{2,1,0:T(8,128)(2,1)}, bf16[2,512,256]{2,1,0:T(8,128)(2,1)S(1)}, u32[]{:S(2)}) copy-start(bf16[2,512,256]{2,1,0:T(8,128)(2,1)S(1)} %collective-permute-done.6.refs_2_) | copy-start | bytes 1572868
  130.5 8.9 %collective-permute-start.8 = (bf16[2,512,128]{2,1,0:T(8,128)(2,1)S(1)}, bf16[2,512,128]{2,1,0:T(8,128)(2,1)S(1)}, u32[]{:S(2)}, u32[]{:S(2)}) collective-permute-start(bf16[2,512,128]{2,1,0:T(8,128)(2,1)S(1)} %pad_maximum_fusion.4), channel_id=1, source_target_pairs={{0,4},{4,0},{8,12},{12,8},{16,20},{20,16},{24,28},{28,24},{1,5},{5... | collective-permute-start | bytes 786440 | tf_op jit(solution)/shard_map/ppermute | solution.py:405
  132.2 7.4 %collective-permute-start.9 = (bf16[2,512,128]{2,1,0:T(8,128)(2,1)S(1)}, bf16[2,512,128]{2,1,0:T(8,128)(2,1)S(1)}, u32[]{:S(2)}, u32[]{:S(2)}) collective-permute-start(bf16[2,512,128]{2,1,0:T(8,128)(2,1)S(1)} %pad_maximum_fusion.5), channel_id=1, source_target_pairs={{0,8},{4,12},{8,0},{12,4},{16,24},{20,28},{24,16},{28,20},{1,9},{5... | collective-permute-start | bytes 786440 | tf_op jit(solution)/shard_map/ppermute | solution.py:405
  132.6 9.9 %collective-permute-start.10 = (bf16[2,512,128]{2,1,0:T(8,128)(2,1)S(1)}, bf16[2,512,128]{2,1,0:T(8,128)(2,1)S(1)}, u32[]{:S(2)}, u32[]{:S(2)}) collective-permute-start(bf16[2,512,128]{2,1,0:T(8,128)(2,1)S(1)} %pad_maximum_fusion.6), channel_id=1, source_target_pairs={{0,12},{4,8},{8,4},{12,0},{16,28},{20,24},{24,20},{28,16},{1,13},{... | collective-permute-start | bytes 786440 | tf_op jit(solution)/shard_map/ppermute | solution.py:405
  135.9 9.5 %copy-start.31 = (bf16[2,512,128]{2,1,0:T(8,128)(2,1)S(1)}, bf16[2,512,128]{2,1,0:T(8,128)(2,1)}, u32[]{:S(2)}) copy-start(bf16[2,512,128]{2,1,0:T(8,128)(2,1)} %get-tuple-element.137) | copy-start | bytes 786436
  139.5 12.0 %copy-start.34 = (bf16[2,512,128]{2,1,0:T(8,128)(2,1)}, bf16[2,512,128]{2,1,0:T(8,128)(2,1)S(1)}, u32[]{:S(2)}) copy-start(bf16[2,512,128]{2,1,0:T(8,128)(2,1)S(1)} %collective-permute-done.8.refs_5_.refs_9_) | copy-start | bytes 786436
  139.6 12.0 %copy-start.35 = (bf16[2,512,128]{2,1,0:T(8,128)(2,1)}, bf16[2,512,128]{2,1,0:T(8,128)(2,1)S(1)}, u32[]{:S(2)}) copy-start(bf16[2,512,128]{2,1,0:T(8,128)(2,1)S(1)} %collective-permute-done.9.refs_6_.refs_10_) | copy-start | bytes 786436
  142.4 9.1 %copy-start.36 = (bf16[2,512,128]{2,1,0:T(8,128)(2,1)}, bf16[2,512,128]{2,1,0:T(8,128)(2,1)S(1)}, u32[]{:S(2)}) copy-start(bf16[2,512,128]{2,1,0:T(8,128)(2,1)S(1)} %collective-permute-done.10.refs_7_.refs_11_) | copy-start | bytes 786436
  143.4 75.2 %collective-permute-start.18 = (bf16[2,512,128]{2,1,0:T(8,128)(2,1)S(1)}, bf16[2,512,128]{2,1,0:T(8,128)(2,1)S(1)}, u32[]{:S(2)}, u32[]{:S(2)}) collective-permute-start(bf16[2,512,128]{2,1,0:T(8,128)(2,1)S(1)} %copy-done.33), channel_id=1, source_target_pairs={{0,4},{4,0},{8,12},{12,8},{16,20},{20,16},{24,28},{28,24},{1,5},{5... | collective-permute-start | bytes 786440 | tf_op jit(solution)/shard_map/ppermute | solution.py:405
  144.9 75.4 %collective-permute-start.19 = (bf16[2,512,128]{2,1,0:T(8,128)(2,1)S(1)}, bf16[2,512,128]{2,1,0:T(8,128)(2,1)S(1)}, u32[]{:S(2)}, u32[]{:S(2)}) collective-permute-start(bf16[2,512,128]{2,1,0:T(8,128)(2,1)S(1)} %copy-done.32), channel_id=1, source_target_pairs={{0,8},{4,12},{8,0},{12,4},{16,24},{20,28},{24,16},{28,20},{1,9},{5... | collective-permute-start | bytes 786440 | tf_op jit(solution)/shard_map/ppermute | solution.py:405
  145.4 75.6 %collective-permute-start.20 = (bf16[2,512,128]{2,1,0:T(8,128)(2,1)S(1)}, bf16[2,512,128]{2,1,0:T(8,128)(2,1)}, u32[]{:S(2)}, u32[]{:S(2)}) collective-permute-start(bf16[2,512,128]{2,1,0:T(8,128)(2,1)S(1)} %copy-done.31), channel_id=1, source_target_pairs={{0,12},{4,8},{8,4},{12,0},{16,28},{20,24},{24,20},{28,16},{1,13},{... | collective-permute-start | bytes 786440 | tf_op jit(solution)/shard_map/ppermute | solution.py:405
  146.9 77.8 %collective-permute-start.14 = (bf16[512,512]{1,0:T(8,128)(2,1)}, bf16[512,512]{1,0:T(8,128)(2,1)S(1)}, u32[]{:S(2)}, u32[]{:S(2)}) collective-permute-start(bf16[512,512]{1,0:T(8,128)(2,1)} %get-tuple-element.252), channel_id=1, source_target_pairs={{0,16},{4,20},{8,24},{12,28},{16,0},{20,4},{24,8},{28,12},{1,17},{... | collective-permute-start | bytes 1572872 | tf_op jit(solution)/shard_map/ppermute | solution.py:405
  150.0 78.6 %collective-permute-start.11 = (bf16[2,512,384]{2,1,0:T(8,128)(2,1)}, bf16[2,512,384]{2,1,0:T(8,128)(2,1)}, u32[]{:S(2)}, u32[]{:S(2)}) collective-permute-start(bf16[2,512,384]{2,1,0:T(8,128)(2,1)} %get-tuple-element.124), channel_id=1, source_target_pairs={{0,4},{4,0},{8,12},{12,8},{16,20},{20,16},{24,28},{28,24},{1,5},{5... | collective-permute-start | bytes 2359304 | tf_op jit(solution)/shard_map/ppermute | solution.py:405
  218.6 78.1 %collective-permute-start.12 = (bf16[2,512,384]{2,1,0:T(8,128)(2,1)}, bf16[2,512,384]{2,1,0:T(8,128)(2,1)}, u32[]{:S(2)}, u32[]{:S(2)}) collective-permute-start(bf16[2,512,384]{2,1,0:T(8,128)(2,1)} %get-tuple-element.125), channel_id=1, source_target_pairs={{0,8},{4,12},{8,0},{12,4},{16,24},{20,28},{24,16},{28,20},{1,9},{5... | collective-permute-start | bytes 2359304 | tf_op jit(solution)/shard_map/ppermute | solution.py:405
  220.4 76.3 %collective-permute-start.13 = (bf16[2,512,384]{2,1,0:T(8,128)(2,1)}, bf16[2,512,384]{2,1,0:T(8,128)(2,1)}, u32[]{:S(2)}, u32[]{:S(2)}) collective-permute-start(bf16[2,512,384]{2,1,0:T(8,128)(2,1)} %get-tuple-element.126), channel_id=1, source_target_pairs={{0,12},{4,8},{8,4},{12,0},{16,28},{20,24},{24,20},{28,16},{1,13},{... | collective-permute-start | bytes 2359304 | tf_op jit(solution)/shard_map/ppermute | solution.py:405
  221.1 77.0 %all-to-all-start.1 = ((bf16[8,512,256]{2,1,0:T(8,128)(2,1)}), bf16[8,512,256]{2,1,0:T(8,128)(2,1)S(1)}, u32[]{:S(2)}, u32[]{:S(2)}) async-start(bf16[8,512,256]{2,1,0:T(8,128)(2,1)} %attend_pair.4), calls=%async_computation.1 | async-start | bytes 4194304 | tf_op jit(solution)/shard_map/all_to_all | solution.py:580
  224.9 71.7 %collective-permute-start.15 = (bf16[2,512,128]{2,1,0:T(8,128)(2,1)S(1)}, bf16[2,512,128]{2,1,0:T(8,128)(2,1)S(1)}, u32[]{:S(2)}, u32[]{:S(2)}) collective-permute-start(bf16[2,512,128]{2,1,0:T(8,128)(2,1)S(1)} %pad_maximum_fusion.8), channel_id=1, source_target_pairs={{0,4},{4,0},{8,12},{12,8},{16,20},{20,16},{24,28},{28,24},{1,5},{5... | collective-permute-start | bytes 786440 | tf_op jit(solution)/shard_map/ppermute | solution.py:405
  227.0 69.7 %collective-permute-start.16 = (bf16[2,512,128]{2,1,0:T(8,128)(2,1)S(1)}, bf16[2,512,128]{2,1,0:T(8,128)(2,1)S(1)}, u32[]{:S(2)}, u32[]{:S(2)}) collective-permute-start(bf16[2,512,128]{2,1,0:T(8,128)(2,1)S(1)} %pad_maximum_fusion.9), channel_id=1, source_target_pairs={{0,8},{4,12},{8,0},{12,4},{16,24},{20,28},{24,16},{28,20},{1,9},{5... | collective-permute-start | bytes 786440 | tf_op jit(solution)/shard_map/ppermute | solution.py:405
  228.6 69.5 %collective-permute-start.17 = (bf16[2,512,128]{2,1,0:T(8,128)(2,1)S(1)}, bf16[2,512,128]{2,1,0:T(8,128)(2,1)}, u32[]{:S(2)}, u32[]{:S(2)}) collective-permute-start(bf16[2,512,128]{2,1,0:T(8,128)(2,1)S(1)} %pad_maximum_fusion.10), channel_id=1, source_target_pairs={{0,12},{4,8},{8,4},{12,0},{16,28},{20,24},{24,20},{28,16},{1,13},{... | collective-permute-start | bytes 786440 | tf_op jit(solution)/shard_map/ppermute | solution.py:405
  298.1 86.4 %all-to-all-start = ((bf16[8,512,256]{2,1,0:T(8,128)(2,1)}), bf16[8,512,256]{2,1,0:T(8,128)(2,1)}, u32[]{:S(2)}, u32[]{:S(2)}) async-start(bf16[8,512,256]{2,1,0:T(8,128)(2,1)} %attend_pair.5), calls=%async_computation | async-start | bytes 4194304 | tf_op jit(solution)/shard_map/all_to_all | solution.py:580
  315.1 142.5 %collective-permute-start.21 = (bf16[8,40,1024]{2,1,0:T(8,128)(2,1)}, bf16[8,40,1024]{2,1,0:T(8,128)(2,1)}, u32[]{:S(2)}, u32[]{:S(2)}) collective-permute-start(bf16[8,40,1024]{2,1,0:T(8,128)(2,1)} %slice_bitcast_fusion.5), channel_id=1, source_target_pairs={{0,2},{1,3},{2,0},{3,1},{4,6},{5,7},{6,4},{7,5},{8,10},{9,11},{10,... | collective-permute-start | bytes 1966088 | tf_op jit(solution)/shard_map/ppermute | solution.py:405
  316.6 141.0 %collective-permute-start.23 = (bf16[8,40,1024]{2,1,0:T(8,128)(2,1)S(1)}, bf16[8,40,1024]{2,1,0:T(8,128)(2,1)}, u32[]{:S(2)}, u32[]{:S(2)}) collective-permute-start(bf16[8,40,1024]{2,1,0:T(8,128)(2,1)S(1)} %get-tuple-element.250), channel_id=1, source_target_pairs={{0,3},{1,2},{2,1},{3,0},{4,7},{5,6},{6,5},{7,4},{8,11},{9,10},{10,... | collective-permute-start | bytes 1966088 | tf_op jit(solution)/shard_map/ppermute | solution.py:405
  316.6 141.0 %collective-permute-start.22 = (bf16[8,40,1024]{2,1,0:T(8,128)(2,1)S(1)}, bf16[8,40,1024]{2,1,0:T(8,128)(2,1)}, u32[]{:S(2)}, u32[]{:S(2)}) collective-permute-start(bf16[8,40,1024]{2,1,0:T(8,128)(2,1)S(1)} %get-tuple-element.251), channel_id=1, source_target_pairs={{0,1},{1,0},{2,3},{3,2},{4,5},{5,4},{6,7},{7,6},{8,9},{9,8},{10,11... | collective-permute-start | bytes 1966088 | tf_op jit(solution)/shard_map/ppermute | solution.py:405
  384.4 73.1 %all-to-all-start.2 = ((bf16[8,512,256]{2,1,0:T(8,128)(2,1)}), bf16[8,512,256]{2,1,0:T(8,128)(2,1)S(1)}, u32[]{:S(2)}, u32[]{:S(2)}) async-start(bf16[8,512,256]{2,1,0:T(8,128)(2,1)} %attend_pair.6), calls=%async_computation.2 | async-start | bytes 4194304 | tf_op jit(solution)/shard_map/all_to_all | solution.py:580
  457.6 54.8 %all-to-all-start.3 = ((bf16[8,512,256]{2,1,0:T(8,128)(2,1)}), bf16[8,512,256]{2,1,0:T(8,128)(2,1)}, u32[]{:S(2)}, u32[]{:S(2)}) async-start(bf16[8,512,256]{2,1,0:T(8,128)(2,1)} %attend_pair.7), calls=%async_computation.3 | async-start | bytes 4194304 | tf_op jit(solution)/shard_map/all_to_all | solution.py:597
  471.6 8.0 %collective-permute-start.26 = (bf16[2,8,40,1024]{3,2,1,0:T(8,128)(2,1)}, bf16[2,8,40,1024]{3,2,1,0:T(8,128)(2,1)S(1)}, u32[]{:S(2)}, u32[]{:S(2)}) collective-permute-start(bf16[2,8,40,1024]{3,2,1,0:T(8,128)(2,1)} %get-tuple-element.205), channel_id=1, source_target_pairs={{0,1},{1,0},{2,3},{3,2},{4,5},{5,4},{6,7},{7,6},{8,9},{9,8},{10,11... | collective-permute-start | bytes 3932168 | tf_op jit(solution)/shard_map/ppermute | solution.py:405
  479.2 3.3 collective-permute-start.24
  480.2 19.4 %collective-permute-start.27 = (bf16[8,40,1024]{2,1,0:T(8,128)(2,1)S(1)}, bf16[8,40,1024]{2,1,0:T(8,128)(2,1)S(1)}, u32[]{:S(2)}, u32[]{:S(2)}) collective-permute-start(bf16[8,40,1024]{2,1,0:T(8,128)(2,1)S(1)} %fusion.31), channel_id=1, source_target_pairs={{0,2},{2,0},{1,3},{3,1},{4,6},{6,4},{5,7},{7,5},{8,10},{10,8},{9,1... | collective-permute-start | bytes 1966088 | tf_op jit(solution)/shard_map/ppermute | solution.py:405
  483.1 28.0 %collective-permute-start.25 = (bf16[8,40,1024]{2,1,0:T(8,128)(2,1)S(1)}, bf16[8,40,1024]{2,1,0:T(8,128)(2,1)S(1)}, u32[]{:S(2)}, u32[]{:S(2)}) collective-permute-start(bf16[8,40,1024]{2,1,0:T(8,128)(2,1)S(1)} %fusion.30), channel_id=1, source_target_pairs={{0,2},{2,0},{1,3},{3,1},{4,6},{6,4},{5,7},{7,5},{8,10},{10,8},{9,1... | collective-permute-start | bytes 1966088 | tf_op jit(solution)/shard_map/ppermute | solution.py:405
  519.9 3.2 collective-permute-start.28
  526.3 28.4 %collective-permute-start.29 = (bf16[8,40,1024]{2,1,0:T(8,128)(2,1)S(1)}, bf16[8,40,1024]{2,1,0:T(8,128)(2,1)}, u32[]{:S(2)}, u32[]{:S(2)}) collective-permute-start(bf16[8,40,1024]{2,1,0:T(8,128)(2,1)S(1)} %fusion.32), channel_id=1, source_target_pairs={{0,2},{2,0},{1,3},{3,1},{4,6},{6,4},{5,7},{7,5},{8,10},{10,8},{9,1... | collective-permute-start | bytes 1966088 | tf_op jit(solution)/shard_map/ppermute | solution.py:405
  531.4 28.9 %collective-permute-start.36 = (bf16[2,40,3072]{2,1,0:T(8,128)(2,1)}, bf16[2,40,3072]{2,1,0:T(8,128)(2,1)}, u32[]{:S(2)}, u32[]{:S(2)}) collective-permute-start(bf16[2,40,3072]{2,1,0:T(8,128)(2,1)} %get-tuple-element.240), channel_id=1, source_target_pairs={{0,4},{4,0},{8,12},{12,8},{16,20},{20,16},{24,28},{28,24},{1,5},{5... | collective-permute-start | bytes 1474568 | tf_op jit(solution)/shard_map/ppermute | solution.py:405
  533.4 26.9 %collective-permute-start.37 = (bf16[2,40,3072]{2,1,0:T(8,128)(2,1)}, bf16[2,40,3072]{2,1,0:T(8,128)(2,1)}, u32[]{:S(2)}, u32[]{:S(2)}) collective-permute-start(bf16[2,40,3072]{2,1,0:T(8,128)(2,1)} %get-tuple-element.241), channel_id=1, source_target_pairs={{0,8},{4,12},{8,0},{12,4},{16,24},{20,28},{24,16},{28,20},{1,9},{5... | collective-permute-start | bytes 1474568 | tf_op jit(solution)/shard_map/ppermute | solution.py:405
  534.9 25.4 %collective-permute-start.38 = (bf16[2,40,3072]{2,1,0:T(8,128)(2,1)}, bf16[2,40,3072]{2,1,0:T(8,128)(2,1)}, u32[]{:S(2)}, u32[]{:S(2)}) collective-permute-start(bf16[2,40,3072]{2,1,0:T(8,128)(2,1)} %get-tuple-element.242), channel_id=1, source_target_pairs={{0,12},{4,8},{8,4},{12,0},{16,28},{20,24},{24,20},{28,16},{1,13},{... | collective-permute-start | bytes 1474568 | tf_op jit(solution)/shard_map/ppermute | solution.py:405
  557.1 16.5 %copy-start.1 = (bf16[512,2,1280]{2,1,0:T(2,128)(2,1)S(1)}, bf16[512,2,1280]{2,1,0:T(2,128)(2,1)}, u32[]{:S(2)}) copy-start(bf16[512,2,1280]{2,1,0:T(2,128)(2,1)} %param.6) | copy-start | bytes 7864324
  557.1 16.5 %copy-start.22 = (f32[2,1280]{1,0:T(2,128)S(1)}, f32[2,1280]{1,0:T(2,128)}, u32[]{:S(2)}) copy-start(f32[2,1280]{1,0:T(2,128)} %copy-done.21) | copy-start | bytes 30724
  557.1 16.5 %copy-start.24 = (f32[2,1280]{1,0:T(2,128)S(1)}, f32[2,1280]{1,0:T(2,128)}, u32[]{:S(2)}) copy-start(f32[2,1280]{1,0:T(2,128)} %copy-done.23) | copy-start | bytes 30724
  557.3 4.9 collective-permute-start.33
  562.2 4.1 collective-permute-start.34
  563.9 18.1 %collective-permute-start.39 = (bf16[40,3072]{1,0:T(8,128)(2,1)S(1)}, bf16[40,3072]{1,0:T(8,128)(2,1)S(1)}, u32[]{:S(2)}, u32[]{:S(2)}) collective-permute-start(bf16[40,3072]{1,0:T(8,128)(2,1)S(1)} %fusion.38), channel_id=1, source_target_pairs={{0,16},{4,20},{8,24},{12,28},{16,0},{20,4},{24,8},{28,12},{1,17},{... | collective-permute-start | bytes 737288 | tf_op jit(solution)/shard_map/ppermute | solution.py:405
  566.3 6.9 %collective-permute-start.35 = (f32[2,2,32]{2,1,0:T(2,128)S(1)}, f32[2,2,32]{2,1,0:T(2,128)S(1)}, u32[]{:S(2)}, u32[]{:S(2)}) collective-permute-start(f32[2,2,32]{2,1,0:T(2,128)S(1)} %add.215), channel_id=1, source_target_pairs={{0,8},{4,12},{8,0},{12,4},{16,24},{20,28},{24,16},{28,20},{1,9},{5... | collective-permute-start | bytes 1544 | tf_op jit(solution)/shard_map/ppermute | solution.py:405
  569.7 12.3 %collective-permute-start.30 = (bf16[2,40,1024]{2,1,0:T(8,128)(2,1)}, bf16[2,40,1024]{2,1,0:T(8,128)(2,1)}, u32[]{:S(2)}, u32[]{:S(2)}) collective-permute-start(bf16[2,40,1024]{2,1,0:T(8,128)(2,1)} %get-tuple-element.247), channel_id=1, source_target_pairs={{0,4},{4,0},{8,12},{12,8},{16,20},{20,16},{24,28},{28,24},{1,5},{5... | collective-permute-start | bytes 491528 | tf_op jit(solution)/shard_map/ppermute | solution.py:405
  570.8 11.2 %collective-permute-start.31 = (bf16[2,40,1024]{2,1,0:T(8,128)(2,1)S(1)}, bf16[2,40,1024]{2,1,0:T(8,128)(2,1)}, u32[]{:S(2)}, u32[]{:S(2)}) collective-permute-start(bf16[2,40,1024]{2,1,0:T(8,128)(2,1)S(1)} %get-tuple-element.248), channel_id=1, source_target_pairs={{0,8},{4,12},{8,0},{12,4},{16,24},{20,28},{24,16},{28,20},{1,9},{5... | collective-permute-start | bytes 491528 | tf_op jit(solution)/shard_map/ppermute | solution.py:405
  571.4 10.6 %collective-permute-start.32 = (bf16[2,40,1024]{2,1,0:T(8,128)(2,1)S(1)}, bf16[2,40,1024]{2,1,0:T(8,128)(2,1)}, u32[]{:S(2)}, u32[]{:S(2)}) collective-permute-start(bf16[2,40,1024]{2,1,0:T(8,128)(2,1)S(1)} %get-tuple-element.249), channel_id=1, source_target_pairs={{0,12},{4,8},{8,4},{12,0},{16,28},{20,24},{24,20},{28,16},{1,13},{... | collective-permute-start | bytes 491528 | tf_op jit(solution)/shard_map/ppermute | solution.py:405
  583.5 6.3 %collective-permute-start.40 = (bf16[40,1024]{1,0:T(8,128)(2,1)S(1)}, bf16[40,1024]{1,0:T(8,128)(2,1)S(1)}, u32[]{:S(2)}, u32[]{:S(2)}) collective-permute-start(bf16[40,1024]{1,0:T(8,128)(2,1)S(1)} %fusion.43), channel_id=1, source_target_pairs={{0,16},{4,20},{8,24},{12,28},{16,0},{20,4},{24,8},{28,12},{1,17},{... | collective-permute-start | bytes 245768 | tf_op jit(solution)/shard_map/ppermute | solution.py:405
  592.1 11.2 %all-to-all-start.4 = ((f32[32,1,1280]{2,1,0:T(1,128)}), f32[32,1,1280]{2,1,0:T(1,128)S(1)}, u32[]{:S(2)}, u32[]{:S(2)}) async-start(f32[32,1,1280]{2,1,0:T(1,128)} %reshape.131), calls=%async_computation.4 | async-start | bytes 327680 | tf_op jit(solution)/shard_map/all_to_all | solution.py:647
  (25 other events, 99.5 us)
Sparse Core Ops, SparseCore 0:
  9.6 14.0 all-gather.2
  25.2 20.2 all-gather.4

commit v5 on v4

--- a/solution.py
+++ b/solution.py
@@ -382,7 +382,7 @@
         ],
         compiler_params=pltpu.CompilerParams(vmem_limit_bytes=VMEM),
         cost_estimate=pl.CostEstimate(
-            flops=images * tokens * channels, bytes_accessed=2**12, transcendentals=0
+            flops=images * tokens * channels * (1 if tail is None else 2**14), bytes_accessed=2**12, transcendentals=0
         ),
         name="project_back",
     )(*grads, full_qkv, full_out, *(tail or ()))
@@ -413,16 +413,6 @@
     return array.astype(jnp.float32)
 
 
-def move_near(parts):
-    rep = parts[0].shape[0]
-    moved = []
-    for own, part in enumerate(parts):
-        for row in range(rep):
-            flip = row * len(parts) + own
-            moved.append(flipped(part[row], ("rep", "own"), flip) if flip else part[row])
-    return moved
-
-
 def sum_own(parts):
     total = wide(parts[0])
     for own in range(1, len(parts)):
@@ -430,21 +420,21 @@
     return total
 
 
-def sum_rep(total):
-    mine = total[0]
-    for row in range(1, total.shape[0]):
-        mine = mine + wide(flipped(low(total[row]), "rep", row))
-    return mine
-
-
-def sum_half(near, groups):
+def sum_rep(total, hold=()):
+    moved = [flipped(low(total[row]), "rep", row) for row in range(1, total.shape[0])]
+    return total[0] + sum(wide(part) for part in after(moved, hold))
+
+
+def half_pieces(near, groups):
     place = lax.axis_index("seq") % groups
     cut = near.reshape(2, groups, *near.shape[1:])
-    total = lax.dynamic_index_in_dim(cut, place, 1, keepdims=False)
-    for flip in range(1, groups):
-        sent = lax.dynamic_index_in_dim(cut, place ^ flip, 1, keepdims=False)
-        total = total + wide(flipped(low(sent), "seq", flip))
-    return total
+    pieces = [lax.dynamic_index_in_dim(cut, place ^ flip, 1, keepdims=False) for flip in range(groups)]
+    return pieces[:1] + [low(piece) for piece in pieces[1:]]
+
+
+def sum_half(pieces, hold=()):
+    moved = [flipped(pieces[flip], "seq", flip) for flip in range(1, len(pieces))]
+    return pieces[0] + sum(wide(part) for part in after(moved, hold))
 
 
 def sum_halves(total, groups):
@@ -510,7 +500,7 @@
         grad_parts.append(low(jnp.einsum("itc,dc->itd", cot_rows, part, preferred_element_type=jnp.float32)))
     work = swapped(rows)
     first_grad = grad_parts[0]
-    grad_parts[0] = swapped(grad_parts[0])
+    grad_parts[0] = swapped(after(grad_parts[0], work[1]))
 
     values = rows.astype(jnp.float32)
     sums = jnp.stack([jnp.sum(values, axis=1), jnp.sum(values * values, axis=1)])
@@ -563,7 +553,7 @@
         if index != first:
             arrays[index] = after(arrays[index], moved[first])
 
-    grads, nears = [], []
+    grads = []
     result = None
     for head in range(heads):
         used = sorted({place[0] for place in heads_plan[head]})
@@ -580,34 +570,25 @@
             grads.append(lax.all_to_all(result, "seq", split_axis=0, concat_axis=0, tiled=True))
         if head >= 2:
             operands = after(operands, grads[head - 2])
-        if head == 2:
-            parts = weight_parts(grads[0])
-            operands = after(operands, parts)
-            near_moved = move_near(parts)
         places = tuple((used.index(index), lane, half) for index, lane, half in heads_plan[head])
         result = attend_pair(operands, places, me)
         if head == 0:
             first_result = result
     if heads > 1:
         result = after(result, grads[-1])
-    if heads > 2:
-        result = after(result, near_moved)
-        nears.append(sum(wide(part) for part in near_moved))
-        grads[1:] = after(grads[1:], result)
+        token = flipped(result[0, :16, :HALF], "seq", 1)
+        grads = after(grads, result, token)
     grads.append(lax.all_to_all(result, "seq", split_axis=0, concat_axis=0, tiled=True))
     back = mixed = jnp.zeros((images * tokens, channels), jnp.float32)
     if aligned and heads > count:
         back, mixed = project_back(grads[:count], full_qkv, full_out, heads, 0, images)
         grads[-1] = after(grads[-1], back, mixed)
-    middle = [sum_own(weight_parts(grads[index])) for index in range(len(nears), heads - 1)]
-    if middle:
-        middle = [sum_rep(total) for total in middle]
-        nears += middle
-        grads[-1] = after(grads[-1], middle)
+    nears = [sum_own(weight_parts(grads[index])) for index in range(heads - 1)]
+    grads[-1] = after(grads[-1], nears)
     last = sum_own(weight_parts(grads[-1]))
     if heads > 1:
-        grads[-1], nears = after((grads[-1], nears), last)
-    nears.append(sum_rep(last))
+        grads[-1] = after(grads[-1], last)
+        nears = [sum_rep(total) for total in nears]
     gain = norm_gain[None, :]
     if aligned:
         offset = heads - count
@@ -619,12 +600,14 @@
         mixed, back = project_back_plain(grads, full_qkv, full_out, images)
         mixed_out = low(values + mixed)
         sums = jnp.stack([jnp.sum(back * norm_gain, axis=1), jnp.sum(back * norm_gain * centred, axis=1)])
-    sums = after(sums, nears[-1])
+    last_pieces = half_pieces(sum_rep(last, back), groups)
+    sums = after(sums, last_pieces)
     weight_sums = []
     if heads > 1:
-        early = sum_halves(sum_half(jnp.concatenate(nears[:-1], axis=2), groups), groups)
+        early = half_pieces(jnp.concatenate(after(nears, last), axis=2), groups)
+        early = sum_halves(sum_half(early, back), groups)
         weight_sums = jnp.split(early, heads - 1, axis=1)
-    last_sum = sum_half(nears[-1], groups)
+    last_sum = sum_half(last_pieces)
     weight_sums.append(sum_halves(last_sum, groups))
 
     mixed_out = after(mixed_out, last_sum).transpose(1, 0, 2)

time: 624 us -> 646 us (1.035)
  waiting for transfers between devices: 78.9 us -> 115 us
  starting transfers between devices: 81.3 us -> 73.6 us
    ppermute x41 -> x40, waiting for transfers between devices: 71.9 us -> 106 us  [flipped(): lax.ppermute(array, axis, [(i, i ^ flip) for i in range(lax.axis_size(axi...]
    ppermute x41 -> x40, starting transfers between devices: 56.4 us -> 47.7 us  [flipped(): lax.ppermute(array, axis, [(i, i ^ flip) for i in range(lax.axis_size(axi...]
    unnamed x89 -> x87, local copies, waits for them, and re-layouts: 21.2 us -> 18.9 us
  transfers between devices with their start and end apart: 48 -> 47, of which waited for: 11 -> 15; matrix products, arithmetic and copies ran while one was open for 11% -> 10% of each run, Pallas kernels for 56% -> 56%
where the time goes in v5:
time: 646 us; the launch traced here: 635 us
  Pallas kernels  354 us (55%)
  waiting for transfers between devices  115 us (18%)
  starting transfers between devices  73.6 us (11%)
  local copies, waits for them, and re-layouts  48 us (7%)
  other arithmetic  26.4 us (4%)
  between operations  15.4 us (2%)
    pallas_call x4, Pallas kernels, attend_pair(): pl.pallas_call(functools.partial(pair_body, bq, kb, flips, places), out_s...  269 us
    ppermute x40, waiting for transfers between devices, flipped(): lax.ppermute(array, axis, [(i, i ^ flip) for i in range(lax.axis_size(axi...  106 us
    ppermute x40, starting transfers between devices, flipped(): lax.ppermute(array, axis, [(i, i ^ flip) for i in range(lax.axis_size(axi...  47.7 us
    pallas_call x2, Pallas kernels, project_back(): pl.pallas_call(functools.partial(back_body, offset, heads), out_shape=out...  33.4 us
    pallas_call x4, Pallas kernels, weight_grads(): pl.pallas_call(functools.partial(weight_body, images), out_shape=[jax.Sha...  30 us
    all_to_all x4, starting transfers between devices, shards(): lax.all_to_all(result, 'seq', split_axis=0, concat_axis=0, tiled=True)  22.8 us
    pallas_call x2, Pallas kernels, project(): pl.pallas_call(functools.partial(project_body, groups), out_shape=[jax.Sh...  21.7 us
    unnamed x87, local copies, waits for them, and re-layouts  18.9 us
  transfers between devices with their start and end apart: 47, of which 15 were waited for; matrix products, arithmetic and copies ran while one was open for 10% of the time, Pallas kernels for 56%

profile of v5, /device:TPU:0, one launch (start us, length us, event | category | flops | bytes accessed | tf_op | source)
XLA Modules:
  0.0 635.1 jit_solution(2996863659522651694)
XLA Ops:
  8.9 1.8 copy.123
  10.7 2.5 dynamic-slice_bitcast_fusion
  13.2 4.0 collective-permute-start.3
  18.3 56.1 %collective-permute-done = f32[2,2,32]{2,1,0:T(2,128)S(1)} collective-permute-done((f32[2,2,32]{2,1,0:T(2,128)S(1)}, f32[2,2,32]{2,1,0:T(2,128)S(1)}, u32[]{:S(2)}, u32[]{:S(2)}) %collective-permute-start) | collective-permute-done | bytes 544 | tf_op jit(solution)/shard_map/ppermute | solution.py:405
  74.5 1.6 collective-permute-start.1
  76.0 3.6 copy.78
  79.6 4.5 copy.81
  84.1 3.2 fusion.49
  87.3 1.5 fusion.19
  90.5 3.4 collective-permute-start.7
  94.5 2.5 fusion.5
  97.0 4.6 copy.80
  101.6 3.8 add_convert_fusion
  105.5 10.7 %project.2 = (bf16[2,512,256]{2,1,0:T(8,128)(2,1)}, bf16[2,512,256]{2,1,0:T(8,128)(2,1)}, bf16[2,512,256]{2,1,0:T(8,128)(2,1)}, bf16[2,512,256]{2,1,0:T(8,128)(2...) custom-call(s32[1]{0:T(128)S(6)} %select_n.84.unit_ref, ...), custom_call_target="tpu_custom_call" | custom-call | flops 4026531840 | bytes 65536 | tf_op jit(solution)/shard_map/project/pallas_call | solution.py:186
  116.7 3.0 collective-permute-start.6
  119.6 11.0 %project.3 = (bf16[2,512,384]{2,1,0:T(8,128)(2,1)}, bf16[2,512,384]{2,1,0:T(8,128)(2,1)}, bf16[2,512,384]{2,1,0:T(8,128)(2,1)}, bf16[2,512,384]{2,1,0:T(8,128)(2,1)}) custom-call(s32[1]{0:T(128)S(6)} %select_n.84.unit_ref, bf16[512,1280]{1,0:T(8,128)(2,1)} %get-tuple-element.280.here_ref, bf16[512,1280]{1,0:T(8,128)(2,1)} %get-tuple-element.279.there_ref, ...), custom_call_target="tpu_custom_call" | custom-call | flops 4026531840 | bytes 65536 | tf_op jit(solution)/shard_map/project/pallas_call | solution.py:186
  131.7 10.1 %collective-permute-done.6.refs_3_ = bf16[2,512,256]{2,1,0:T(8,128)(2,1)S(1)} collective-permute-done((bf16[2,512,256]{2,1,0:T(8,128)(2,1)}, bf16[2,512,256]{2,1,0:T(8,128)(2,1)S(1)}, u32[]{:S(2)}, u32[]{:S(2)}) %collective-permute-start.6) | collective-permute-done | bytes 524320 | tf_op jit(solution)/shard_map/ppermute | solution.py:405
  141.8 1.3 dynamic-slice_bitcast_fusion.14
  144.3 2.7 collective-permute-start.10
  147.1 1.6 fusion.22
  149.4 2.6 collective-permute-done.8.refs_5_.refs_9_
  152.7 3.9 collective-permute-done.10.refs_7_.refs_11_
  157.6 2.4 collective-permute-start.13
  161.5 67.0 %attend_pair.4 = bf16[8,512,256]{2,1,0:T(8,128)(2,1)} custom-call(s32[1]{0:T(128)} %bitcast.me_ref, bf16[2,512,256]{2,1,0:T(8,128)(2,1)} %get-tuple-element.140.refs_0_, bf16[2,512,256]{2,1,0:T(8,128)(2,1)} %copy-done.26, bf16[2,512,256]{2,1,0:T(8,128)(2,1)} %copy-done.27, bf16[2,512,256]{2,1,0:T(8,128)(2,1)} %copy-done.28, ...), custom_call_target="tpu_custom_call" | custom-call | flops 51539607552 | bytes 4194304 | tf_op jit(solution)/shard_map/attend_pair/pallas_call | solution.py:134
  228.6 1.6 collective-permute-start.15
  230.2 1.6 collective-permute-start.16
  231.8 4.1 all-to-all-start
  236.1 2.1 collective-permute-start.18
  238.2 1.5 collective-permute-start.19
  239.9 67.2 %attend_pair.5 = bf16[8,512,256]{2,1,0:T(8,128)(2,1)} custom-call(s32[1]{0:T(128)} %bitcast.me_ref, bf16[2,512,256]{2,1,0:T(8,128)(2,1)} %get-tuple-element.140.refs_0_, bf16[2,512,256]{2,1,0:T(8,128)(2,1)} %copy-done.26, bf16[2,512,256]{2,1,0:T(8,128)(2,1)} %copy-done.27, bf16[2,512,256]{2,1,0:T(8,128)(2,1)} %copy-done.28, ...), custom_call_target="tpu_custom_call" | custom-call | flops 51539607552 | bytes 4194304 | tf_op jit(solution)/shard_map/attend_pair/pallas_call | solution.py:134
  307.9 6.5 %all-to-all-start.1 = ((bf16[8,512,256]{2,1,0:T(8,128)(2,1)}), bf16[8,512,256]{2,1,0:T(8,128)(2,1)}, u32[]{:S(2)}, u32[]{:S(2)}) async-start(bf16[8,512,256]{2,1,0:T(8,128)(2,1)} %attend_pair.5), calls=%async_computation.1 | async-start | bytes 4194304 | tf_op jit(solution)/shard_map/all_to_all | solution.py:570
  314.4 67.2 %attend_pair.6 = bf16[8,512,256]{2,1,0:T(8,128)(2,1)} custom-call(s32[1]{0:T(128)} %bitcast.me_ref, bf16[2,512,384]{2,1,0:T(8,128)(2,1)} %get-tuple-element.178.refs_0_, bf16[2,512,384]{2,1,0:T(8,128)(2,1)} %collective-permute-done.14.refs_1_, bf16[2,512,384]{2,1,0:T(8,128)(2,1)} %collective-permute-done.15.refs_2_, ...), custom_call_target="tpu_custom_call" | custom-call | flops 51539607552 | bytes 4194304 | tf_op jit(solution)/shard_map/attend_pair/pallas_call | solution.py:134
  381.6 6.0 all-to-all-start.2
  387.6 67.1 %attend_pair.7 = bf16[8,512,256]{2,1,0:T(8,128)(2,1)} custom-call(s32[1]{0:T(128)} %bitcast.me_ref, bf16[2,512,384]{2,1,0:T(8,128)(2,1)} %get-tuple-element.178.refs_0_, bf16[2,512,384]{2,1,0:T(8,128)(2,1)} %collective-permute-done.14.refs_1_, bf16[2,512,384]{2,1,0:T(8,128)(2,1)} %collective-permute-done.15.refs_2_, ...), custom_call_target="tpu_custom_call" | custom-call | flops 51539607552 | bytes 4194304 | tf_op jit(solution)/shard_map/attend_pair/pallas_call | solution.py:134
  454.7 6.3 all-to-all-start.3
  461.0 7.5 %weight_grads.4 = (bf16[2,8,40,1024]{3,2,1,0:T(8,128)(2,1)}, bf16[2,8,40,1024]{3,2,1,0:T(8,128)(2,1)}) custom-call(s32[1]{0:T(128)} %bitcast.40.here_ref, bf16[1280,1024]{1,0:T(8,128)(2,1)} %bitcast.203, bf16[1280,1024]{1,0:T(8,128)(2,1)} %bitcast.199, bf16[8,512,256]{2,1,0:T(8,128)(2,1)} %copy-done.2), custom_call_target="tpu_custom_call" | custom-call | flops 1310720 | bytes 4096 | tf_op jit(solution)/shard_map/weight_grads/pallas_call | solution.py:252
  468.5 7.4 %weight_grads.5 = (bf16[2,8,40,1024]{3,2,1,0:T(8,128)(2,1)}, bf16[2,8,40,1024]{3,2,1,0:T(8,128)(2,1)}) custom-call(s32[1]{0:T(128)} %bitcast.40.here_ref, bf16[1280,1024]{1,0:T(8,128)(2,1)} %bitcast.204, bf16[1280,1024]{1,0:T(8,128)(2,1)} %bitcast.200, bf16[8,512,256]{2,1,0:T(8,128)(2,1)} %all-to-all-done.1.refs_1_.grad_ref), custom_call_target="tpu_custom_call" | custom-call | flops 1310720 | bytes 4096 | tf_op jit(solution)/shard_map/weight_grads/pallas_call | solution.py:252
  476.4 7.4 %weight_grads.6 = (bf16[2,8,40,1024]{3,2,1,0:T(8,128)(2,1)}, bf16[2,8,40,1024]{3,2,1,0:T(8,128)(2,1)}) custom-call(s32[1]{0:T(128)} %bitcast.40.here_ref, bf16[1280,1024]{1,0:T(8,128)(2,1)} %bitcast.205, bf16[1280,1024]{1,0:T(8,128)(2,1)} %bitcast.201, bf16[8,512,256]{2,1,0:T(8,128)(2,1)} %copy-done.6), custom_call_target="tpu_custom_call" | custom-call | flops 1310720 | bytes 4096 | tf_op jit(solution)/shard_map/weight_grads/pallas_call | solution.py:252
  484.6 1.6 collective-permute-start.32
  490.6 1.4 collective-permute-start.34
  492.0 14.9 %project_back.2 = (f32[1024,1280]{1,0:T(8,128)}, f32[1024,1280]{1,0:T(8,128)}) custom-call(bf16[8,512,256]{2,1,0:T(8,128)(2,1)} %copy-done.2, bf16[8,512,256]{2,1,0:T(8,128)(2,1)} %all-to-all-done.1.refs_1_.grad_ref, bf16[1280,3072]{1,0:T(8,128)(2,1)} %all-gather.5.cloned.1.call-done.wq_ref.wk_ref.wv_ref.refs_2_, ...), custom_call_target="tpu_custom_call" | custom-call | flops 1310720 | bytes 4096 | tf_op jit(solution)/shard_map/project_back/pallas_call | solution.py:373
  506.9 7.6 %weight_grads.7 = (bf16[2,8,40,1024]{3,2,1,0:T(8,128)(2,1)}, bf16[2,8,40,1024]{3,2,1,0:T(8,128)(2,1)}) custom-call(s32[1]{0:T(128)} %bitcast.40.here_ref, bf16[1280,1024]{1,0:T(8,128)(2,1)} %bitcast.206, bf16[1280,1024]{1,0:T(8,128)(2,1)} %bitcast.202, bf16[8,512,256]{2,1,0:T(8,128)(2,1)} %all-to-all-done.3.grad_ref.refs_1_), custom_call_target="tpu_custom_call" | custom-call | flops 1310720 | bytes 4096 | tf_op jit(solution)/shard_map/weight_grads/pallas_call | solution.py:252
  516.4 13.5 %collective-permute-done.34 = bf16[8,40,1024]{2,1,0:T(8,128)(2,1)} collective-permute-done((bf16[8,40,1024]{2,1,0:T(8,128)(2,1)}, bf16[8,40,1024]{2,1,0:T(8,128)(2,1)}, u32[]{:S(2)}, u32[]{:S(2)}) %collective-permute-start.34) | collective-permute-done | bytes 655392 | tf_op jit(solution)/shard_map/ppermute | solution.py:405
  531.2 1.4 fusion.26
  533.8 1.8 convert_add_fusion
  535.8 1.6 collective-permute-start.25
  538.7 2.0 collective-permute-start.35
  540.8 1.5 collective-permute-start.36
  542.2 18.5 %project_back.3 = (f32[1024,1280]{1,0:T(8,128)}, bf16[2,512,1280]{2,1,0:T(8,128)(2,1)}, f32[2,2,1,1280]{3,2,1,0:T(1,128)}) custom-call(bf16[8,512,256]{2,1,0:T(8,128)(2,1)} %copy-done.6, bf16[8,512,256]{2,1,0:T(8,128)(2,1)} %all-to-all-done.3.grad_ref.refs_1_, bf16[1280,3072]{1,0:T(8,128)(2,1)} %all-gather.5.cloned.1.call-done.wq_ref.wk_ref.wv_ref.refs_2_, ...), custom_call_target="tpu_custom_call" | custom-call | flops 21474836480 | bytes 4096 | tf_op jit(solution)/shard_map/project_back/pallas_call | solution.py:373
  561.5 1.9 collective-permute-done.37
  563.5 1.5 bitcast_add_fusion
  566.3 1.8 collective-permute-start.26
  568.1 1.5 collective-permute-start.27
  569.9 2.7 collective-permute-start.38
  572.8 5.6 collective-permute-done.27
  578.4 2.7 collective-permute-done.28
  582.0 3.9 collective-permute-done.29
  587.2 2.3 collective-permute-done.30
  590.2 6.1 copy.93
  596.2 2.4 collective-permute-start.39
  599.0 4.4 fusion.10
  603.4 4.2 copy.94
  613.0 3.0 all-to-all-start.4
  616.9 7.8 %all-to-all-done.4 = f32[32,1,1280]{2,1,0:T(1,128)S(1)} async-done(((f32[32,1,1280]{2,1,0:T(1,128)}), f32[32,1,1280]{2,1,0:T(1,128)S(1)}, u32[]{:S(2)}, u32[]{:S(2)}) %all-to-all-start.4) | async-done | bytes 163872 | tf_op jit(solution)/shard_map/all_to_all | solution.py:630
  (223 shorter events, 39.5 us)
Async XLA Ops:
  7.2 76.9 %all-gather.3.cloned.1.call-start = ((), (), s32[]{:S(2)}) async-start(), calls=%async_computation.5 | async-start | bytes 3932160 | tf_op jit(solution)/shard_map/all_gather | solution.py:474
  7.9 97.5 %all-gather.5.cloned.1.call-start = ((), (), s32[]{:S(2)}) async-start(), calls=%async_computation.6 | async-start | bytes 11796480 | tf_op jit(solution)/shard_map/all_gather | solution.py:473
  13.2 76.4 %collective-permute-start.3 = (bf16[512,1280]{1,0:T(8,128)(2,1)}, bf16[512,1280]{1,0:T(8,128)(2,1)}, u32[]{:S(2)}, u32[]{:S(2)}) collective-permute-start(bf16[512,1280]{1,0:T(8,128)(2,1)} %dynamic-slice_bitcast_fusion), channel_id=1, source_target_pairs={{0,16},{4,20},{8,24},{12,28},{16,0},{20,4},{24,8},{28,12},{1,17},{... | collective-permute-start | bytes 3932168 | tf_op jit(solution)/shard_map/ppermute | solution.py:405
  18.2 56.2 %collective-permute-start = (f32[2,2,32]{2,1,0:T(2,128)S(1)}, f32[2,2,32]{2,1,0:T(2,128)S(1)}, u32[]{:S(2)}, u32[]{:S(2)}) collective-permute-start(f32[2,2,32]{2,1,0:T(2,128)S(1)} %maximum_reduce_fusion), channel_id=1, source_target_pairs={{0,16},{4,20},{8,24},{12,28},{16,0},{20,4},{24,8},{28,12},{1,17},{... | collective-permute-start | bytes 1544 | tf_op jit(solution)/shard_map/ppermute | solution.py:405
  74.5 9.6 %collective-permute-start.1 = (f32[2,2,32]{2,1,0:T(2,128)S(1)}, f32[2,2,32]{2,1,0:T(2,128)S(1)}, u32[]{:S(2)}, u32[]{:S(2)}) collective-permute-start(f32[2,2,32]{2,1,0:T(2,128)S(1)} %add.178), channel_id=1, source_target_pairs={{0,4},{4,0},{8,12},{12,8},{16,20},{20,16},{24,28},{28,24},{1,5},{5... | collective-permute-start | bytes 1544 | tf_op jit(solution)/shard_map/ppermute | solution.py:405
  88.8 5.0 collective-permute-start.2
  90.5 40.2 %collective-permute-start.7 = (bf16[512,512]{1,0:T(8,128)(2,1)}, bf16[512,512]{1,0:T(8,128)(2,1)}, u32[]{:S(2)}, u32[]{:S(2)}) collective-permute-start(bf16[512,512]{1,0:T(8,128)(2,1)} %get-tuple-element.254), channel_id=1, source_target_pairs={{0,16},{4,20},{8,24},{12,28},{16,0},{20,4},{24,8},{28,12},{1,17},{... | collective-permute-start | bytes 1572872 | tf_op jit(solution)/shard_map/ppermute | solution.py:405
  116.1 14.5 %collective-permute-start.4 = (bf16[2,512,256]{2,1,0:T(8,128)(2,1)}, bf16[2,512,256]{2,1,0:T(8,128)(2,1)S(1)}, u32[]{:S(2)}, u32[]{:S(2)}) collective-permute-start(bf16[2,512,256]{2,1,0:T(8,128)(2,1)} %get-tuple-element.114), channel_id=1, source_target_pairs={{0,4},{4,0},{8,12},{12,8},{16,20},{20,16},{24,28},{28,24},{1,5},{5... | collective-permute-start | bytes 1572872 | tf_op jit(solution)/shard_map/ppermute | solution.py:405
  116.7 15.1 %collective-permute-start.5 = (bf16[2,512,256]{2,1,0:T(8,128)(2,1)}, bf16[2,512,256]{2,1,0:T(8,128)(2,1)S(1)}, u32[]{:S(2)}, u32[]{:S(2)}) collective-permute-start(bf16[2,512,256]{2,1,0:T(8,128)(2,1)} %get-tuple-element.115), channel_id=1, source_target_pairs={{0,8},{4,12},{8,0},{12,4},{16,24},{20,28},{24,16},{28,20},{1,9},{5... | collective-permute-start | bytes 1572872 | tf_op jit(solution)/shard_map/ppermute | solution.py:405
  116.7 25.1 %collective-permute-start.6 = (bf16[2,512,256]{2,1,0:T(8,128)(2,1)}, bf16[2,512,256]{2,1,0:T(8,128)(2,1)S(1)}, u32[]{:S(2)}, u32[]{:S(2)}) collective-permute-start(bf16[2,512,256]{2,1,0:T(8,128)(2,1)} %get-tuple-element.116), channel_id=1, source_target_pairs={{0,12},{4,8},{8,4},{12,0},{16,28},{20,24},{24,20},{28,16},{1,13},{... | collective-permute-start | bytes 1572872 | tf_op jit(solution)/shard_map/ppermute | solution.py:405
  119.6 27.4 %copy-start.11 = (bf16[4,2,64,1280]{3,2,1,0:T(8,128)(2,1)S(1)}, bf16[4,2,64,1280]{3,2,1,0:T(8,128)(2,1)}, u32[]{:S(2)}) copy-start(bf16[4,2,64,1280]{3,2,1,0:T(8,128)(2,1)} %get-tuple-element.247) | copy-start | bytes 3932164
  130.6 16.4 %copy-start.4 = (bf16[512,2,1280]{2,1,0:T(2,128)(2,1)S(1)}, bf16[512,2,1280]{2,1,0:T(2,128)(2,1)}, u32[]{:S(2)}) copy-start(bf16[512,2,1280]{2,1,0:T(2,128)(2,1)} %param.7) | copy-start | bytes 7864324
  130.6 18.0 %copy-start.26 = (bf16[2,512,256]{2,1,0:T(8,128)(2,1)}, bf16[2,512,256]{2,1,0:T(8,128)(2,1)S(1)}, u32[]{:S(2)}) copy-start(bf16[2,512,256]{2,1,0:T(8,128)(2,1)S(1)} %collective-permute-done.4.refs_1_) | copy-start | bytes 1572868
  131.7 16.9 %copy-start.27 = (bf16[2,512,256]{2,1,0:T(8,128)(2,1)}, bf16[2,512,256]{2,1,0:T(8,128)(2,1)S(1)}, u32[]{:S(2)}) copy-start(bf16[2,512,256]{2,1,0:T(8,128)(2,1)S(1)} %collective-permute-done.5.refs_2_) | copy-start | bytes 1572868
  143.3 8.6 %collective-permute-start.8 = (bf16[2,512,128]{2,1,0:T(8,128)(2,1)S(1)}, bf16[2,512,128]{2,1,0:T(8,128)(2,1)S(1)}, u32[]{:S(2)}, u32[]{:S(2)}) collective-permute-start(bf16[2,512,128]{2,1,0:T(8,128)(2,1)S(1)} %pad_maximum_fusion.4), channel_id=1, source_target_pairs={{0,4},{4,0},{8,12},{12,8},{16,20},{20,16},{24,28},{28,24},{1,5},{5... | collective-permute-start | bytes 786440 | tf_op jit(solution)/shard_map/ppermute | solution.py:405
  143.9 8.8 %collective-permute-start.9 = (bf16[2,512,128]{2,1,0:T(8,128)(2,1)S(1)}, bf16[2,512,128]{2,1,0:T(8,128)(2,1)S(1)}, u32[]{:S(2)}, u32[]{:S(2)}) collective-permute-start(bf16[2,512,128]{2,1,0:T(8,128)(2,1)S(1)} %pad_maximum_fusion.5), channel_id=1, source_target_pairs={{0,8},{4,12},{8,0},{12,4},{16,24},{20,28},{24,16},{28,20},{1,9},{5... | collective-permute-start | bytes 786440 | tf_op jit(solution)/shard_map/ppermute | solution.py:405
  144.3 12.3 %collective-permute-start.10 = (bf16[2,512,128]{2,1,0:T(8,128)(2,1)S(1)}, bf16[2,512,128]{2,1,0:T(8,128)(2,1)S(1)}, u32[]{:S(2)}, u32[]{:S(2)}) collective-permute-start(bf16[2,512,128]{2,1,0:T(8,128)(2,1)S(1)} %pad_maximum_fusion.6), channel_id=1, source_target_pairs={{0,12},{4,8},{8,4},{12,0},{16,28},{20,24},{24,20},{28,16},{1,13},{... | collective-permute-start | bytes 786440 | tf_op jit(solution)/shard_map/ppermute | solution.py:405
  147.0 9.5 %copy-start.31 = (bf16[2,512,128]{2,1,0:T(8,128)(2,1)S(1)}, bf16[2,512,128]{2,1,0:T(8,128)(2,1)}, u32[]{:S(2)}) copy-start(bf16[2,512,128]{2,1,0:T(8,128)(2,1)} %get-tuple-element.129) | copy-start | bytes 786436
  147.0 10.0 %copy-start.30 = (bf16[2,512,128]{2,1,0:T(8,128)(2,1)S(1)}, bf16[2,512,128]{2,1,0:T(8,128)(2,1)}, u32[]{:S(2)}) copy-start(bf16[2,512,128]{2,1,0:T(8,128)(2,1)} %get-tuple-element.130) | copy-start | bytes 786436
  147.0 10.6 %copy-start.29 = (bf16[2,512,128]{2,1,0:T(8,128)(2,1)S(1)}, bf16[2,512,128]{2,1,0:T(8,128)(2,1)}, u32[]{:S(2)}) copy-start(bf16[2,512,128]{2,1,0:T(8,128)(2,1)} %get-tuple-element.131) | copy-start | bytes 786436
  151.9 9.6 %copy-start.32 = (bf16[2,512,128]{2,1,0:T(8,128)(2,1)}, bf16[2,512,128]{2,1,0:T(8,128)(2,1)S(1)}, u32[]{:S(2)}) copy-start(bf16[2,512,128]{2,1,0:T(8,128)(2,1)S(1)} %collective-permute-done.8.refs_5_.refs_9_) | copy-start | bytes 786436
  152.7 8.8 %copy-start.33 = (bf16[2,512,128]{2,1,0:T(8,128)(2,1)}, bf16[2,512,128]{2,1,0:T(8,128)(2,1)S(1)}, u32[]{:S(2)}) copy-start(bf16[2,512,128]{2,1,0:T(8,128)(2,1)S(1)} %collective-permute-done.9.refs_6_.refs_10_) | copy-start | bytes 786436
  156.6 72.0 %collective-permute-start.11 = (bf16[2,512,128]{2,1,0:T(8,128)(2,1)S(1)}, bf16[2,512,128]{2,1,0:T(8,128)(2,1)S(1)}, u32[]{:S(2)}, u32[]{:S(2)}) collective-permute-start(bf16[2,512,128]{2,1,0:T(8,128)(2,1)S(1)} %copy-done.31), channel_id=1, source_target_pairs={{0,4},{4,0},{8,12},{12,8},{16,20},{20,16},{24,28},{28,24},{1,5},{5... | collective-permute-start | bytes 786440 | tf_op jit(solution)/shard_map/ppermute | solution.py:405
  157.1 73.1 %collective-permute-start.12 = (bf16[2,512,128]{2,1,0:T(8,128)(2,1)S(1)}, bf16[2,512,128]{2,1,0:T(8,128)(2,1)S(1)}, u32[]{:S(2)}, u32[]{:S(2)}) collective-permute-start(bf16[2,512,128]{2,1,0:T(8,128)(2,1)S(1)} %copy-done.30), channel_id=1, source_target_pairs={{0,8},{4,12},{8,0},{12,4},{16,24},{20,28},{24,16},{28,20},{1,9},{5... | collective-permute-start | bytes 786440 | tf_op jit(solution)/shard_map/ppermute | solution.py:405
  157.6 74.2 %collective-permute-start.13 = (bf16[2,512,128]{2,1,0:T(8,128)(2,1)S(1)}, bf16[2,512,128]{2,1,0:T(8,128)(2,1)}, u32[]{:S(2)}, u32[]{:S(2)}) collective-permute-start(bf16[2,512,128]{2,1,0:T(8,128)(2,1)S(1)} %copy-done.29), channel_id=1, source_target_pairs={{0,12},{4,8},{8,4},{12,0},{16,28},{20,24},{24,20},{28,16},{1,13},{... | collective-permute-start | bytes 786440 | tf_op jit(solution)/shard_map/ppermute | solution.py:405
  160.0 79.7 %collective-permute-start.14 = (bf16[2,512,384]{2,1,0:T(8,128)(2,1)}, bf16[2,512,384]{2,1,0:T(8,128)(2,1)}, u32[]{:S(2)}, u32[]{:S(2)}) collective-permute-start(bf16[2,512,384]{2,1,0:T(8,128)(2,1)} %get-tuple-element.134), channel_id=1, source_target_pairs={{0,4},{4,0},{8,12},{12,8},{16,20},{20,16},{24,28},{28,24},{1,5},{5... | collective-permute-start | bytes 2359304 | tf_op jit(solution)/shard_map/ppermute | solution.py:405
  161.4 74.5 %collective-permute-start.17 = (bf16[512,512]{1,0:T(8,128)(2,1)}, bf16[512,512]{1,0:T(8,128)(2,1)S(1)}, u32[]{:S(2)}, u32[]{:S(2)}) collective-permute-start(bf16[512,512]{1,0:T(8,128)(2,1)} %get-tuple-element.252), channel_id=1, source_target_pairs={{0,16},{4,20},{8,24},{12,28},{16,0},{20,4},{24,8},{28,12},{1,17},{... | collective-permute-start | bytes 1572872 | tf_op jit(solution)/shard_map/ppermute | solution.py:405
  228.6 79.3 %collective-permute-start.15 = (bf16[2,512,384]{2,1,0:T(8,128)(2,1)}, bf16[2,512,384]{2,1,0:T(8,128)(2,1)}, u32[]{:S(2)}, u32[]{:S(2)}) collective-permute-start(bf16[2,512,384]{2,1,0:T(8,128)(2,1)} %get-tuple-element.135), channel_id=1, source_target_pairs={{0,8},{4,12},{8,0},{12,4},{16,24},{20,28},{24,16},{28,20},{1,9},{5... | collective-permute-start | bytes 2359304 | tf_op jit(solution)/shard_map/ppermute | solution.py:405
  230.2 77.6 %collective-permute-start.16 = (bf16[2,512,384]{2,1,0:T(8,128)(2,1)}, bf16[2,512,384]{2,1,0:T(8,128)(2,1)}, u32[]{:S(2)}, u32[]{:S(2)}) collective-permute-start(bf16[2,512,384]{2,1,0:T(8,128)(2,1)} %get-tuple-element.136), channel_id=1, source_target_pairs={{0,12},{4,8},{8,4},{12,0},{16,28},{20,24},{24,20},{28,16},{1,13},{... | collective-permute-start | bytes 2359304 | tf_op jit(solution)/shard_map/ppermute | solution.py:405
  231.8 76.1 %all-to-all-start = ((bf16[8,512,256]{2,1,0:T(8,128)(2,1)}), bf16[8,512,256]{2,1,0:T(8,128)(2,1)S(1)}, u32[]{:S(2)}, u32[]{:S(2)}) async-start(bf16[8,512,256]{2,1,0:T(8,128)(2,1)} %attend_pair.4), calls=%async_computation | async-start | bytes 4194304 | tf_op jit(solution)/shard_map/all_to_all | solution.py:570
  236.1 71.7 %collective-permute-start.18 = (bf16[2,512,128]{2,1,0:T(8,128)(2,1)S(1)}, bf16[2,512,128]{2,1,0:T(8,128)(2,1)S(1)}, u32[]{:S(2)}, u32[]{:S(2)}) collective-permute-start(bf16[2,512,128]{2,1,0:T(8,128)(2,1)S(1)} %pad_maximum_fusion.8), channel_id=1, source_target_pairs={{0,4},{4,0},{8,12},{12,8},{16,20},{20,16},{24,28},{28,24},{1,5},{5... | collective-permute-start | bytes 786440 | tf_op jit(solution)/shard_map/ppermute | solution.py:405
  238.2 69.6 %collective-permute-start.19 = (bf16[2,512,128]{2,1,0:T(8,128)(2,1)S(1)}, bf16[2,512,128]{2,1,0:T(8,128)(2,1)S(1)}, u32[]{:S(2)}, u32[]{:S(2)}) collective-permute-start(bf16[2,512,128]{2,1,0:T(8,128)(2,1)S(1)} %pad_maximum_fusion.9), channel_id=1, source_target_pairs={{0,8},{4,12},{8,0},{12,4},{16,24},{20,28},{24,16},{28,20},{1,9},{5... | collective-permute-start | bytes 786440 | tf_op jit(solution)/shard_map/ppermute | solution.py:405
  239.8 68.1 %collective-permute-start.20 = (bf16[2,512,128]{2,1,0:T(8,128)(2,1)S(1)}, bf16[2,512,128]{2,1,0:T(8,128)(2,1)S(1)}, u32[]{:S(2)}, u32[]{:S(2)}) collective-permute-start(bf16[2,512,128]{2,1,0:T(8,128)(2,1)S(1)} %pad_maximum_fusion.10), channel_id=1, source_target_pairs={{0,12},{4,8},{8,4},{12,0},{16,28},{20,24},{24,20},{28,16},{1,13},{... | collective-permute-start | bytes 786440 | tf_op jit(solution)/shard_map/ppermute | solution.py:405
  307.9 73.7 %copy-start.2 = (bf16[8,512,256]{2,1,0:T(8,128)(2,1)}, bf16[8,512,256]{2,1,0:T(8,128)(2,1)S(1)}, u32[]{:S(2)}) copy-start(bf16[8,512,256]{2,1,0:T(8,128)(2,1)S(1)} %all-to-all-done.refs_0_.grad_ref) | copy-start | bytes 6291460
  307.9 73.7 %all-to-all-start.1 = ((bf16[8,512,256]{2,1,0:T(8,128)(2,1)}), bf16[8,512,256]{2,1,0:T(8,128)(2,1)}, u32[]{:S(2)}, u32[]{:S(2)}) async-start(bf16[8,512,256]{2,1,0:T(8,128)(2,1)} %attend_pair.5), calls=%async_computation.1 | async-start | bytes 4194304 | tf_op jit(solution)/shard_map/all_to_all | solution.py:570
  381.6 73.1 %all-to-all-start.2 = ((bf16[8,512,256]{2,1,0:T(8,128)(2,1)}), bf16[8,512,256]{2,1,0:T(8,128)(2,1)S(1)}, u32[]{:S(2)}, u32[]{:S(2)}) async-start(bf16[8,512,256]{2,1,0:T(8,128)(2,1)} %attend_pair.6), calls=%async_computation.2 | async-start | bytes 4194304 | tf_op jit(solution)/shard_map/all_to_all | solution.py:570
  454.7 13.8 %copy-start.6 = (bf16[8,512,256]{2,1,0:T(8,128)(2,1)}, bf16[8,512,256]{2,1,0:T(8,128)(2,1)S(1)}, u32[]{:S(2)}) copy-start(bf16[8,512,256]{2,1,0:T(8,128)(2,1)S(1)} %all-to-all-done.2.grad_ref.refs_0_) | copy-start | bytes 6291460
  454.7 52.2 %all-to-all-start.3 = ((bf16[8,512,256]{2,1,0:T(8,128)(2,1)}), bf16[8,512,256]{2,1,0:T(8,128)(2,1)}, u32[]{:S(2)}, u32[]{:S(2)}) async-start(bf16[8,512,256]{2,1,0:T(8,128)(2,1)} %attend_pair.7), calls=%async_computation.3 | async-start | bytes 4194304 | tf_op jit(solution)/shard_map/all_to_all | solution.py:581
  468.5 15.5 %collective-permute-start.21 = (bf16[2,8,40,1024]{3,2,1,0:T(8,128)(2,1)}, bf16[2,8,40,1024]{3,2,1,0:T(8,128)(2,1)S(1)}, u32[]{:S(2)}, u32[]{:S(2)}) collective-permute-start(bf16[2,8,40,1024]{3,2,1,0:T(8,128)(2,1)} %get-tuple-element.194), channel_id=1, source_target_pairs={{0,1},{1,0},{2,3},{3,2},{4,5},{5,4},{6,7},{7,6},{8,9},{9,8},{10,11... | collective-permute-start | bytes 3932168 | tf_op jit(solution)/shard_map/ppermute | solution.py:405
  476.0 8.0 %copy-start.15 = (bf16[2,8,40,1024]{3,2,1,0:T(8,128)(2,1)S(1)}, bf16[2,8,40,1024]{3,2,1,0:T(8,128)(2,1)}, u32[]{:S(2)}) copy-start(bf16[2,8,40,1024]{3,2,1,0:T(8,128)(2,1)} %get-tuple-element.193) | copy-start | bytes 3932164
  476.0 10.2 %collective-permute-start.22 = (bf16[2,8,40,1024]{3,2,1,0:T(8,128)(2,1)}, bf16[2,8,40,1024]{3,2,1,0:T(8,128)(2,1)S(1)}, u32[]{:S(2)}, u32[]{:S(2)}) collective-permute-start(bf16[2,8,40,1024]{3,2,1,0:T(8,128)(2,1)} %get-tuple-element.196), channel_id=1, source_target_pairs={{0,1},{1,0},{2,3},{3,2},{4,5},{5,4},{6,7},{7,6},{8,9},{9,8},{10,11... | collective-permute-start | bytes 3932168 | tf_op jit(solution)/shard_map/ppermute | solution.py:405
  483.9 4.5 collective-permute-start.23
  484.6 30.7 %collective-permute-start.32 = (bf16[8,40,1024]{2,1,0:T(8,128)(2,1)S(1)}, bf16[8,40,1024]{2,1,0:T(8,128)(2,1)}, u32[]{:S(2)}, u32[]{:S(2)}) collective-permute-start(bf16[8,40,1024]{2,1,0:T(8,128)(2,1)S(1)} %fusion.30), channel_id=1, source_target_pairs={{0,2},{2,0},{1,3},{3,1},{4,6},{6,4},{5,7},{7,5},{8,10},{10,8},{9,1... | collective-permute-start | bytes 1966088 | tf_op jit(solution)/shard_map/ppermute | solution.py:405
  487.7 28.6 %collective-permute-start.33 = (bf16[8,40,1024]{2,1,0:T(8,128)(2,1)}, bf16[8,40,1024]{2,1,0:T(8,128)(2,1)}, u32[]{:S(2)}, u32[]{:S(2)}) collective-permute-start(bf16[8,40,1024]{2,1,0:T(8,128)(2,1)} %fusion.31), channel_id=1, source_target_pairs={{0,2},{2,0},{1,3},{3,1},{4,6},{6,4},{5,7},{7,5},{8,10},{10,8},{9,1... | collective-permute-start | bytes 1966088 | tf_op jit(solution)/shard_map/ppermute | solution.py:405
  490.6 39.3 %collective-permute-start.34 = (bf16[8,40,1024]{2,1,0:T(8,128)(2,1)}, bf16[8,40,1024]{2,1,0:T(8,128)(2,1)}, u32[]{:S(2)}, u32[]{:S(2)}) collective-permute-start(bf16[8,40,1024]{2,1,0:T(8,128)(2,1)} %fusion.32), channel_id=1, source_target_pairs={{0,2},{2,0},{1,3},{3,1},{4,6},{6,4},{5,7},{7,5},{8,10},{10,8},{9,1... | collective-permute-start | bytes 1966088 | tf_op jit(solution)/shard_map/ppermute | solution.py:405
  514.5 19.3 %collective-permute-start.24 = (bf16[2,8,40,1024]{3,2,1,0:T(8,128)(2,1)}, bf16[2,8,40,1024]{3,2,1,0:T(8,128)(2,1)}, u32[]{:S(2)}, u32[]{:S(2)}) collective-permute-start(bf16[2,8,40,1024]{3,2,1,0:T(8,128)(2,1)} %get-tuple-element.201), channel_id=1, source_target_pairs={{0,1},{1,0},{2,3},{3,2},{4,5},{5,4},{6,7},{7,6},{8,9},{9,8},{10,11... | collective-permute-start | bytes 3932168 | tf_op jit(solution)/shard_map/ppermute | solution.py:405
  515.2 15.9 %copy-start.8 = (f32[2,8,40,1024]{3,2,1,0:T(8,128)S(1)}, f32[2,8,40,1024]{3,2,1,0:T(8,128)}, u32[]{:S(2)}) copy-start(f32[2,8,40,1024]{3,2,1,0:T(8,128)} %copy-done.7) | copy-start | bytes 7864324
  515.2 17.3 %copy-start.10 = (f32[2,8,40,1024]{3,2,1,0:T(8,128)S(1)}, f32[2,8,40,1024]{3,2,1,0:T(8,128)}, u32[]{:S(2)}) copy-start(f32[2,8,40,1024]{3,2,1,0:T(8,128)} %copy-done.9) | copy-start | bytes 7864324
  535.8 29.2 %collective-permute-start.25 = (bf16[8,40,1024]{2,1,0:T(8,128)(2,1)S(1)}, bf16[8,40,1024]{2,1,0:T(8,128)(2,1)}, u32[]{:S(2)}, u32[]{:S(2)}) collective-permute-start(bf16[8,40,1024]{2,1,0:T(8,128)(2,1)S(1)} %fusion.29), channel_id=1, source_target_pairs={{0,2},{2,0},{1,3},{3,1},{4,6},{6,4},{5,7},{7,5},{8,10},{10,8},{9,1... | collective-permute-start | bytes 1966088 | tf_op jit(solution)/shard_map/ppermute | solution.py:405
  538.7 22.8 %collective-permute-start.35 = (bf16[2,40,3072]{2,1,0:T(8,128)(2,1)}, bf16[2,40,3072]{2,1,0:T(8,128)(2,1)S(1)}, u32[]{:S(2)}, u32[]{:S(2)}) collective-permute-start(bf16[2,40,3072]{2,1,0:T(8,128)(2,1)} %get-tuple-element.244), channel_id=1, source_target_pairs={{0,4},{4,0},{8,12},{12,8},{16,20},{20,16},{24,28},{28,24},{1,5},{5... | collective-permute-start | bytes 1474568 | tf_op jit(solution)/shard_map/ppermute | solution.py:405
  540.8 20.8 %collective-permute-start.36 = (bf16[2,40,3072]{2,1,0:T(8,128)(2,1)}, bf16[2,40,3072]{2,1,0:T(8,128)(2,1)}, u32[]{:S(2)}, u32[]{:S(2)}) collective-permute-start(bf16[2,40,3072]{2,1,0:T(8,128)(2,1)} %get-tuple-element.243), channel_id=1, source_target_pairs={{0,8},{4,12},{8,0},{12,4},{16,24},{20,28},{24,16},{28,20},{1,9},{5... | collective-permute-start | bytes 1474568 | tf_op jit(solution)/shard_map/ppermute | solution.py:405
  542.2 21.2 %collective-permute-start.37 = (bf16[2,40,3072]{2,1,0:T(8,128)(2,1)S(1)}, bf16[2,40,3072]{2,1,0:T(8,128)(2,1)}, u32[]{:S(2)}, u32[]{:S(2)}) collective-permute-start(bf16[2,40,3072]{2,1,0:T(8,128)(2,1)S(1)} %get-tuple-element.242), channel_id=1, source_target_pairs={{0,12},{4,8},{8,4},{12,0},{16,28},{20,24},{24,20},{28,16},{1,13},{... | collective-permute-start | bytes 1474568 | tf_op jit(solution)/shard_map/ppermute | solution.py:405
  566.3 6.5 %collective-permute-start.26 = (bf16[2,40,1024]{2,1,0:T(8,128)(2,1)S(1)}, bf16[2,40,1024]{2,1,0:T(8,128)(2,1)S(1)}, u32[]{:S(2)}, u32[]{:S(2)}) collective-permute-start(bf16[2,40,1024]{2,1,0:T(8,128)(2,1)S(1)} %get-tuple-element.251), channel_id=1, source_target_pairs={{0,4},{4,0},{8,12},{12,8},{16,20},{20,16},{24,28},{28,24},{1,5},{5... | collective-permute-start | bytes 491528 | tf_op jit(solution)/shard_map/ppermute | solution.py:405
  568.1 10.3 %collective-permute-start.27 = (bf16[2,40,1024]{2,1,0:T(8,128)(2,1)S(1)}, bf16[2,40,1024]{2,1,0:T(8,128)(2,1)S(1)}, u32[]{:S(2)}, u32[]{:S(2)}) collective-permute-start(bf16[2,40,1024]{2,1,0:T(8,128)(2,1)S(1)} %get-tuple-element.250), channel_id=1, source_target_pairs={{0,8},{4,12},{8,0},{12,4},{16,24},{20,28},{24,16},{28,20},{1,9},{5... | collective-permute-start | bytes 491528 | tf_op jit(solution)/shard_map/ppermute | solution.py:405
  569.6 11.5 %collective-permute-start.28 = (bf16[2,40,1024]{2,1,0:T(8,128)(2,1)S(1)}, bf16[2,40,1024]{2,1,0:T(8,128)(2,1)S(1)}, u32[]{:S(2)}, u32[]{:S(2)}) collective-permute-start(bf16[2,40,1024]{2,1,0:T(8,128)(2,1)S(1)} %get-tuple-element.249), channel_id=1, source_target_pairs={{0,12},{4,8},{8,4},{12,0},{16,28},{20,24},{24,20},{28,16},{1,13},{... | collective-permute-start | bytes 491528 | tf_op jit(solution)/shard_map/ppermute | solution.py:405
  569.9 12.0 %collective-permute-start.38 = (bf16[40,3072]{1,0:T(8,128)(2,1)S(1)}, bf16[40,3072]{1,0:T(8,128)(2,1)S(1)}, u32[]{:S(2)}, u32[]{:S(2)}) collective-permute-start(bf16[40,3072]{1,0:T(8,128)(2,1)S(1)} %fusion.36), channel_id=1, source_target_pairs={{0,16},{4,20},{8,24},{12,28},{16,0},{20,4},{24,8},{28,12},{1,17},{... | collective-permute-start | bytes 737288 | tf_op jit(solution)/shard_map/ppermute | solution.py:405
  581.4 4.5 collective-permute-start.29
  585.9 3.6 collective-permute-start.30
  589.5 9.1 %collective-permute-start.31 = (f32[2,2,32]{2,1,0:T(2,128)S(1)}, f32[2,2,32]{2,1,0:T(2,128)S(1)}, u32[]{:S(2)}, u32[]{:S(2)}) collective-permute-start(f32[2,2,32]{2,1,0:T(2,128)S(1)} %add.208), channel_id=1, source_target_pairs={{0,8},{4,12},{8,0},{12,4},{16,24},{20,28},{24,16},{28,20},{1,9},{5... | collective-permute-start | bytes 1544 | tf_op jit(solution)/shard_map/ppermute | solution.py:405
  590.2 8.9 %copy-start.1 = (bf16[512,2,1280]{2,1,0:T(2,128)(2,1)S(1)}, bf16[512,2,1280]{2,1,0:T(2,128)(2,1)}, u32[]{:S(2)}) copy-start(bf16[512,2,1280]{2,1,0:T(2,128)(2,1)} %param.6) | copy-start | bytes 7864324
  590.2 8.9 %copy-start.20 = (f32[2,1280]{1,0:T(2,128)S(1)}, f32[2,1280]{1,0:T(2,128)}, u32[]{:S(2)}) copy-start(f32[2,1280]{1,0:T(2,128)} %copy-done.19) | copy-start | bytes 30724
  590.2 8.9 %copy-start.22 = (f32[2,1280]{1,0:T(2,128)S(1)}, f32[2,1280]{1,0:T(2,128)}, u32[]{:S(2)}) copy-start(f32[2,1280]{1,0:T(2,128)} %copy-done.21) | copy-start | bytes 30724
  596.2 11.4 %collective-permute-start.39 = (bf16[40,1024]{1,0:T(8,128)(2,1)}, bf16[40,1024]{1,0:T(8,128)(2,1)}, u32[]{:S(2)}, u32[]{:S(2)}) collective-permute-start(bf16[40,1024]{1,0:T(8,128)(2,1)} %fusion.41), channel_id=1, source_target_pairs={{0,16},{4,20},{8,24},{12,28},{16,0},{20,4},{24,8},{28,12},{1,17},{... | collective-permute-start | bytes 245768 | tf_op jit(solution)/shard_map/ppermute | solution.py:405
  613.0 11.6 %all-to-all-start.4 = ((f32[32,1,1280]{2,1,0:T(1,128)}), f32[32,1,1280]{2,1,0:T(1,128)S(1)}, u32[]{:S(2)}, u32[]{:S(2)}) async-start(f32[32,1,1280]{2,1,0:T(1,128)} %reshape.132), calls=%async_computation.4 | async-start | bytes 327680 | tf_op jit(solution)/shard_map/all_to_all | solution.py:630
  (23 other events, 99.4 us)
Sparse Core Ops, SparseCore 0:
  9.6 14.0 all-gather.2
  25.2 20.2 all-gather.4

commit v6 on v4

--- a/solution.py
+++ b/solution.py
@@ -510,7 +510,6 @@
         grad_parts.append(low(jnp.einsum("itc,dc->itd", cot_rows, part, preferred_element_type=jnp.float32)))
     work = swapped(rows)
     first_grad = grad_parts[0]
-    grad_parts[0] = swapped(grad_parts[0])
 
     values = rows.astype(jnp.float32)
     sums = jnp.stack([jnp.sum(values, axis=1), jnp.sum(values * values, axis=1)])
@@ -522,6 +521,7 @@
     normed_t = normed.reshape(images * tokens, channels).T
     cotangent_t = cot_rows.reshape(images * tokens, channels).T
     work[1] = after(work[1], normed_t, cotangent_t)
+    grad_parts[0] = swapped(after(grad_parts[0], work[1]))
     work_mean, work_inv = pick(mean, image), pick(inv_std, image)
     work = [low((wide(part) - work_mean) * work_inv * norm_gain + norm_shift) for part in work]
 

time: 624 us -> 617 us (0.989); the launches traced: 614 us -> 613 us
  transfers between devices with their start and end apart: 48 -> 48, of which waited for: 11 -> 13; matrix products, arithmetic and copies ran while one was open for 11% -> 11% of each run, Pallas kernels for 56% -> 56%
where the time goes in v6:
time: 617 us; the launch traced here: 613 us
  Pallas kernels  354 us (57%)
  waiting for transfers between devices  82.9 us (13%)
  starting transfers between devices  76.5 us (12%)
  local copies, waits for them, and re-layouts  52.4 us (8%)
  other arithmetic  28.7 us (5%)
  between operations  15 us (2%)
    pallas_call x4, Pallas kernels, attend_pair(): pl.pallas_call(functools.partial(pair_body, bq, kb, flips, places), out_s...  268 us
    ppermute x41, waiting for transfers between devices, flipped(): lax.ppermute(array, axis, [(i, i ^ flip) for i in range(lax.axis_size(axi...  74.3 us
    ppermute x41, starting transfers between devices, flipped(): lax.ppermute(array, axis, [(i, i ^ flip) for i in range(lax.axis_size(axi...  51.2 us
    pallas_call x2, Pallas kernels, project_back(): pl.pallas_call(functools.partial(back_body, offset, heads), out_shape=out...  33.5 us
    pallas_call x4, Pallas kernels, weight_grads(): pl.pallas_call(functools.partial(weight_body, images), out_shape=[jax.Sha...  30 us
    all_to_all x4, starting transfers between devices, shards(): lax.all_to_all(result, 'seq', split_axis=0, concat_axis=0, tiled=True)  22.7 us
    pallas_call x2, Pallas kernels, project(): pl.pallas_call(functools.partial(project_body, groups), out_shape=[jax.Sh...  21.5 us
    unnamed x89, local copies, waits for them, and re-layouts  19 us
  transfers between devices with their start and end apart: 48, of which 13 were waited for; matrix products, arithmetic and copies ran while one was open for 11% of the time, Pallas kernels for 56%

profile of v6, /device:TPU:0, one launch (start us, length us, event | category | flops | bytes accessed | tf_op | source)
XLA Modules:
  0.0 613.2 jit_solution(8384560392884314656)
XLA Ops:
  9.9 4.1 collective-permute-start
  14.0 1.8 copy.123
  15.8 2.5 dynamic-slice_bitcast_fusion
  18.3 1.8 collective-permute-start.1
  20.1 1.8 collective-permute-done.1
  21.9 1.7 all-gather.3.cloned.1.call-done.refs_3_
  23.6 3.2 fusion.51
  26.8 2.5 fusion.19
  29.3 1.7 collective-permute-start.2
  31.1 1.8 copy.78
  32.9 5.1 copy.81
  38.0 8.7 %collective-permute-done.2 = f32[2,2,32]{2,1,0:T(2,128)S(1)} collective-permute-done((f32[2,2,32]{2,1,0:T(2,128)S(1)}, f32[2,2,32]{2,1,0:T(2,128)S(1)}, u32[]{:S(2)}, u32[]{:S(2)}) %collective-permute-start.2) | collective-permute-done | bytes 544 | tf_op jit(solution)/shard_map/ppermute | solution.py:405
  47.4 2.5 fusion.5
  49.8 4.6 copy.80
  54.4 23.4 %collective-permute-done.3 = bf16[512,1280]{1,0:T(8,128)(2,1)} collective-permute-done((bf16[512,1280]{1,0:T(8,128)(2,1)}, bf16[512,1280]{1,0:T(8,128)(2,1)}, u32[]{:S(2)}, u32[]{:S(2)}) %collective-permute-start.3) | collective-permute-done | bytes 1310752 | tf_op jit(solution)/shard_map/ppermute | solution.py:405
  77.8 2.1 dynamic-slice_bitcast_fusion.3
  79.9 3.9 add_convert_fusion
  83.8 10.7 %project.3 = (bf16[2,512,256]{2,1,0:T(8,128)(2,1)}, bf16[2,512,256]{2,1,0:T(8,128)(2,1)}, bf16[2,512,256]{2,1,0:T(8,128)(2,1)}, bf16[2,512,256]{2,1,0:T(8,128)(2...) custom-call(s32[1]{0:T(128)S(6)} %select_n.84.unit_ref, ...), custom_call_target="tpu_custom_call" | custom-call | flops 4026531840 | bytes 65536 | tf_op jit(solution)/shard_map/project/pallas_call | solution.py:186
  96.0 1.8 collective-permute-start.6
  98.0 10.8 %project.2 = (bf16[2,512,384]{2,1,0:T(8,128)(2,1)}, bf16[2,512,384]{2,1,0:T(8,128)(2,1)}, bf16[2,512,384]{2,1,0:T(8,128)(2,1)}, bf16[2,512,384]{2,1,0:T(8,128)(2,1)}) custom-call(s32[1]{0:T(128)S(6)} %select_n.84.unit_ref, bf16[512,1280]{1,0:T(8,128)(2,1)} %get-tuple-element.282.here_ref, bf16[512,1280]{1,0:T(8,128)(2,1)} %get-tuple-element.281.there_ref, ...), custom_call_target="tpu_custom_call" | custom-call | flops 4026531840 | bytes 65536 | tf_op jit(solution)/shard_map/project/pallas_call | solution.py:186
  108.8 7.2 %collective-permute-done.6.refs_2_ = bf16[2,512,256]{2,1,0:T(8,128)(2,1)S(1)} collective-permute-done((bf16[2,512,256]{2,1,0:T(8,128)(2,1)}, bf16[2,512,256]{2,1,0:T(8,128)(2,1)S(1)}, u32[]{:S(2)}, u32[]{:S(2)}) %collective-permute-start.6) | collective-permute-done | bytes 524320 | tf_op jit(solution)/shard_map/ppermute | solution.py:405
  116.0 12.1 %collective-permute-done.7.refs_3_ = bf16[2,512,256]{2,1,0:T(8,128)(2,1)S(1)} collective-permute-done((bf16[2,512,256]{2,1,0:T(8,128)(2,1)}, bf16[2,512,256]{2,1,0:T(8,128)(2,1)S(1)}, u32[]{:S(2)}, u32[]{:S(2)}) %collective-permute-start.7) | collective-permute-done | bytes 524320 | tf_op jit(solution)/shard_map/ppermute | solution.py:405
  130.2 3.0 collective-permute-start.10
  135.5 2.2 collective-permute-done.8.refs_5_.refs_9_
  137.8 1.6 collective-permute-done.9.refs_6_.refs_10_
  139.3 5.3 collective-permute-done.10.refs_7_.refs_11_
  146.4 2.7 collective-permute-start.20
  150.0 67.0 %attend_pair.4 = bf16[8,512,256]{2,1,0:T(8,128)(2,1)} custom-call(s32[1]{0:T(128)} %bitcast.me_ref, bf16[2,512,256]{2,1,0:T(8,128)(2,1)} %get-tuple-element.140.refs_0_, bf16[2,512,256]{2,1,0:T(8,128)(2,1)} %copy-done.28, bf16[2,512,256]{2,1,0:T(8,128)(2,1)} %copy-done.29, bf16[2,512,256]{2,1,0:T(8,128)(2,1)} %copy-done.30, ...), custom_call_target="tpu_custom_call" | custom-call | flops 51539607552 | bytes 4194304 | tf_op jit(solution)/shard_map/attend_pair/pallas_call | solution.py:134
  217.0 1.8 collective-permute-start.12
  218.8 1.6 collective-permute-start.13
  220.4 3.6 all-to-all-start.1
  224.3 2.1 collective-permute-start.15
  228.0 67.2 %attend_pair.5 = bf16[8,512,256]{2,1,0:T(8,128)(2,1)} custom-call(s32[1]{0:T(128)} %bitcast.me_ref, bf16[2,512,256]{2,1,0:T(8,128)(2,1)} %get-tuple-element.140.refs_0_, bf16[2,512,256]{2,1,0:T(8,128)(2,1)} %copy-done.28, bf16[2,512,256]{2,1,0:T(8,128)(2,1)} %copy-done.29, bf16[2,512,256]{2,1,0:T(8,128)(2,1)} %copy-done.30, ...), custom_call_target="tpu_custom_call" | custom-call | flops 51539607552 | bytes 4194304 | tf_op jit(solution)/shard_map/attend_pair/pallas_call | solution.py:134
  297.4 6.5 %all-to-all-start = ((bf16[8,512,256]{2,1,0:T(8,128)(2,1)}), bf16[8,512,256]{2,1,0:T(8,128)(2,1)}, u32[]{:S(2)}, u32[]{:S(2)}) async-start(bf16[8,512,256]{2,1,0:T(8,128)(2,1)} %attend_pair.5), calls=%async_computation | async-start | bytes 4194304 | tf_op jit(solution)/shard_map/all_to_all | solution.py:580
  303.9 7.4 %weight_grads.4 = (bf16[2,8,40,1024]{3,2,1,0:T(8,128)(2,1)}, bf16[2,8,40,1024]{3,2,1,0:T(8,128)(2,1)}) custom-call(s32[1]{0:T(128)} %bitcast.40.here_ref, bf16[1280,1024]{1,0:T(8,128)(2,1)} %bitcast.214, bf16[1280,1024]{1,0:T(8,128)(2,1)} %bitcast.210, bf16[8,512,256]{2,1,0:T(8,128)(2,1)} %copy-done.3), custom_call_target="tpu_custom_call" | custom-call | flops 1310720 | bytes 4096 | tf_op jit(solution)/shard_map/weight_grads/pallas_call | solution.py:252
  311.4 2.0 slice_bitcast_fusion.5
  316.9 67.1 %attend_pair.6 = bf16[8,512,256]{2,1,0:T(8,128)(2,1)} custom-call(s32[1]{0:T(128)} %bitcast.me_ref, bf16[2,512,384]{2,1,0:T(8,128)(2,1)} %get-tuple-element.189.refs_0_, bf16[2,512,384]{2,1,0:T(8,128)(2,1)} %collective-permute-done.11.refs_1_, bf16[2,512,384]{2,1,0:T(8,128)(2,1)} %collective-permute-done.12.refs_2_, ...), custom_call_target="tpu_custom_call" | custom-call | flops 51539607552 | bytes 4194304 | tf_op jit(solution)/shard_map/attend_pair/pallas_call | solution.py:134
  384.1 6.0 all-to-all-start.2
  390.1 67.1 %attend_pair.7 = bf16[8,512,256]{2,1,0:T(8,128)(2,1)} custom-call(s32[1]{0:T(128)} %bitcast.me_ref, bf16[2,512,384]{2,1,0:T(8,128)(2,1)} %get-tuple-element.189.refs_0_, bf16[2,512,384]{2,1,0:T(8,128)(2,1)} %collective-permute-done.11.refs_1_, bf16[2,512,384]{2,1,0:T(8,128)(2,1)} %collective-permute-done.12.refs_2_, ...), custom_call_target="tpu_custom_call" | custom-call | flops 51539607552 | bytes 4194304 | tf_op jit(solution)/shard_map/attend_pair/pallas_call | solution.py:134
  457.2 6.5 %all-to-all-start.3 = ((bf16[8,512,256]{2,1,0:T(8,128)(2,1)}), bf16[8,512,256]{2,1,0:T(8,128)(2,1)}, u32[]{:S(2)}, u32[]{:S(2)}) async-start(bf16[8,512,256]{2,1,0:T(8,128)(2,1)} %attend_pair.7), calls=%async_computation.3 | async-start | bytes 4194304 | tf_op jit(solution)/shard_map/all_to_all | solution.py:597
  463.8 7.4 %weight_grads.6 = (bf16[2,8,40,1024]{3,2,1,0:T(8,128)(2,1)}, bf16[2,8,40,1024]{3,2,1,0:T(8,128)(2,1)}) custom-call(s32[1]{0:T(128)} %bitcast.40.here_ref, bf16[1280,1024]{1,0:T(8,128)(2,1)} %bitcast.215, bf16[1280,1024]{1,0:T(8,128)(2,1)} %bitcast.211, bf16[8,512,256]{2,1,0:T(8,128)(2,1)} %copy-done.4), custom_call_target="tpu_custom_call" | custom-call | flops 1310720 | bytes 4096 | tf_op jit(solution)/shard_map/weight_grads/pallas_call | solution.py:252
  471.2 7.6 %weight_grads.5 = (bf16[2,8,40,1024]{3,2,1,0:T(8,128)(2,1)}, bf16[2,8,40,1024]{3,2,1,0:T(8,128)(2,1)}) custom-call(s32[1]{0:T(128)} %bitcast.40.here_ref, bf16[1280,1024]{1,0:T(8,128)(2,1)} %bitcast.216, bf16[1280,1024]{1,0:T(8,128)(2,1)} %bitcast.212, bf16[8,512,256]{2,1,0:T(8,128)(2,1)} %all-to-all-done.refs_1_.grad_ref), custom_call_target="tpu_custom_call" | custom-call | flops 1310720 | bytes 4096 | tf_op jit(solution)/shard_map/weight_grads/pallas_call | solution.py:252
  482.7 1.6 collective-permute-start.25
  484.3 15.0 %project_back.2 = (f32[1024,1280]{1,0:T(8,128)}, f32[1024,1280]{1,0:T(8,128)}) custom-call(bf16[8,512,256]{2,1,0:T(8,128)(2,1)} %copy-done.3, bf16[8,512,256]{2,1,0:T(8,128)(2,1)} %all-to-all-done.refs_1_.grad_ref, bf16[1280,3072]{1,0:T(8,128)(2,1)} %all-gather.5.cloned.1.call-done.wq_ref.wk_ref.wv_ref.refs_2_, ...), custom_call_target="tpu_custom_call" | custom-call | flops 1310720 | bytes 4096 | tf_op jit(solution)/shard_map/project_back/pallas_call | solution.py:373
  500.7 10.1 %collective-permute-done.25 = bf16[8,40,1024]{2,1,0:T(8,128)(2,1)S(1)} collective-permute-done((bf16[8,40,1024]{2,1,0:T(8,128)(2,1)S(1)}, bf16[8,40,1024]{2,1,0:T(8,128)(2,1)S(1)}, u32[]{:S(2)}, u32[]{:S(2)}) %collective-permute-start.25) | collective-permute-done | bytes 655392 | tf_op jit(solution)/shard_map/ppermute | solution.py:405
  512.0 7.6 %weight_grads.7 = (bf16[2,8,40,1024]{3,2,1,0:T(8,128)(2,1)}, bf16[2,8,40,1024]{3,2,1,0:T(8,128)(2,1)}) custom-call(s32[1]{0:T(128)} %bitcast.40.here_ref, bf16[1280,1024]{1,0:T(8,128)(2,1)} %bitcast.217, bf16[1280,1024]{1,0:T(8,128)(2,1)} %bitcast.213, bf16[8,512,256]{2,1,0:T(8,128)(2,1)} %all-to-all-done.3.grad_ref.refs_1_), custom_call_target="tpu_custom_call" | custom-call | flops 1310720 | bytes 4096 | tf_op jit(solution)/shard_map/weight_grads/pallas_call | solution.py:252
  519.6 2.0 convert_add_fusion.3
  523.9 2.0 convert_add_fusion
  528.0 1.8 copy-done.7
  531.0 2.0 collective-permute-start.36
  535.1 18.6 %project_back.3 = (f32[1024,1280]{1,0:T(8,128)}, bf16[2,512,1280]{2,1,0:T(8,128)(2,1)}, f32[2,2,1,1280]{3,2,1,0:T(1,128)}) custom-call(bf16[8,512,256]{2,1,0:T(8,128)(2,1)} %copy-done.4, bf16[8,512,256]{2,1,0:T(8,128)(2,1)} %all-to-all-done.3.grad_ref.refs_1_, bf16[1280,3072]{1,0:T(8,128)(2,1)} %all-gather.5.cloned.1.call-done.wq_ref.wk_ref.wv_ref.refs_2_, ...), custom_call_target="tpu_custom_call" | custom-call | flops 1310720 | bytes 4096 | tf_op jit(solution)/shard_map/project_back/pallas_call | solution.py:373
  554.4 2.3 fusion.25
  556.9 3.0 collective-permute-start.33
  559.9 1.9 fusion.29
  561.8 1.7 collective-permute-start.34
  563.5 2.4 collective-permute-start.39
  567.5 1.9 fusion.39
  571.0 1.8 collective-permute-start.32
  573.2 4.1 fusion.10
  577.4 4.2 copy.94
  583.1 2.1 collective-permute-start.40
  585.3 4.2 copy.93
  591.8 2.6 all-to-all-start.4
  597.4 5.5 all-to-all-done.4
  (227 shorter events, 48.3 us)
Async XLA Ops:
  7.2 16.5 %all-gather.3.cloned.1.call-start = ((), (), s32[]{:S(2)}) async-start(), calls=%async_computation.5 | async-start | bytes 3932160 | tf_op jit(solution)/shard_map/all_gather | solution.py:484
  7.9 75.9 %all-gather.5.cloned.1.call-start = ((), (), s32[]{:S(2)}) async-start(), calls=%async_computation.6 | async-start | bytes 11796480 | tf_op jit(solution)/shard_map/all_gather | solution.py:483
  9.9 8.4 %collective-permute-start = (f32[2,2,32]{2,1,0:T(2,128)S(1)}, f32[2,2,32]{2,1,0:T(2,128)S(1)}, u32[]{:S(2)}, u32[]{:S(2)}) collective-permute-start(f32[2,2,32]{2,1,0:T(2,128)S(1)} %maximum_reduce_fusion), channel_id=1, source_target_pairs={{0,16},{4,20},{8,24},{12,28},{16,0},{20,4},{24,8},{28,12},{1,17},{... | collective-permute-start | bytes 1544 | tf_op jit(solution)/shard_map/ppermute | solution.py:405
  18.3 59.5 %collective-permute-start.3 = (bf16[512,1280]{1,0:T(8,128)(2,1)}, bf16[512,1280]{1,0:T(8,128)(2,1)}, u32[]{:S(2)}, u32[]{:S(2)}) collective-permute-start(bf16[512,1280]{1,0:T(8,128)(2,1)} %dynamic-slice_bitcast_fusion), channel_id=1, source_target_pairs={{0,16},{4,20},{8,24},{12,28},{16,0},{20,4},{24,8},{28,12},{1,17},{... | collective-permute-start | bytes 3932168 | tf_op jit(solution)/shard_map/ppermute | solution.py:405
  18.3 3.6 collective-permute-start.1
  29.3 17.4 %collective-permute-start.2 = (f32[2,2,32]{2,1,0:T(2,128)S(1)}, f32[2,2,32]{2,1,0:T(2,128)S(1)}, u32[]{:S(2)}, u32[]{:S(2)}) collective-permute-start(f32[2,2,32]{2,1,0:T(2,128)S(1)} %add.182), channel_id=1, source_target_pairs={{0,8},{4,12},{8,0},{12,4},{16,24},{20,28},{24,16},{28,20},{1,9},{5... | collective-permute-start | bytes 1544 | tf_op jit(solution)/shard_map/ppermute | solution.py:405
  32.9 14.4 %copy-start.19 = (f32[1280]{0:T(1024)S(1)}, f32[1280]{0:T(1024)}, u32[]{:S(2)}) copy-start(f32[1280]{0:T(1024)} %param.8) | copy-start | bytes 15364
  32.9 14.4 %copy-start.27 = (f32[1280]{0:T(1024)S(1)}, f32[1280]{0:T(1024)}, u32[]{:S(2)}) copy-start(f32[1280]{0:T(1024)} %param.9) | copy-start | bytes 15364
  47.0 32.9 %copy-start.25 = (f32[2,1,1280]{2,1,0:T(1,128)}, f32[2,1,1280]{2,1,0:T(1,128)S(1)}, u32[]{:S(2)}) copy-start(f32[2,1,1280]{2,1,0:T(1,128)S(1)} %broadcast_in_dim_reshape.8.refs_7_) | copy-start | bytes 30724
  47.3 32.5 %copy-start.26 = (f32[2,1,1280]{2,1,0:T(1,128)}, f32[2,1,1280]{2,1,0:T(1,128)S(1)}, u32[]{:S(2)}) copy-start(f32[2,1,1280]{2,1,0:T(1,128)S(1)} %broadcast_in_dim_reshape.9.refs_8_) | copy-start | bytes 30724
  49.8 30.1 %copy-start.2 = (bf16[512,2,1280]{2,0,1:T(8,128)(2,1)S(1)}, bf16[512,2,1280]{2,0,1:T(8,128)(2,1)}, u32[]{:S(2)}) copy-start(bf16[512,2,1280]{2,0,1:T(8,128)(2,1)} %copy.123) | copy-start | bytes 7864324
  79.9 28.9 %collective-permute-start.4 = (bf16[512,512]{1,0:T(8,128)(2,1)}, bf16[512,512]{1,0:T(8,128)(2,1)}, u32[]{:S(2)}, u32[]{:S(2)}) collective-permute-start(bf16[512,512]{1,0:T(8,128)(2,1)} %get-tuple-element.256), channel_id=1, source_target_pairs={{0,16},{4,20},{8,24},{12,28},{16,0},{20,4},{24,8},{28,12},{1,17},{... | collective-permute-start | bytes 1572872 | tf_op jit(solution)/shard_map/ppermute | solution.py:405
  94.5 14.3 %collective-permute-start.5 = (bf16[2,512,256]{2,1,0:T(8,128)(2,1)}, bf16[2,512,256]{2,1,0:T(8,128)(2,1)S(1)}, u32[]{:S(2)}, u32[]{:S(2)}) collective-permute-start(bf16[2,512,256]{2,1,0:T(8,128)(2,1)} %get-tuple-element.120), channel_id=1, source_target_pairs={{0,4},{4,0},{8,12},{12,8},{16,20},{20,16},{24,28},{28,24},{1,5},{5... | collective-permute-start | bytes 1572872 | tf_op jit(solution)/shard_map/ppermute | solution.py:405
  96.0 19.9 %collective-permute-start.6 = (bf16[2,512,256]{2,1,0:T(8,128)(2,1)}, bf16[2,512,256]{2,1,0:T(8,128)(2,1)S(1)}, u32[]{:S(2)}, u32[]{:S(2)}) collective-permute-start(bf16[2,512,256]{2,1,0:T(8,128)(2,1)} %get-tuple-element.121), channel_id=1, source_target_pairs={{0,8},{4,12},{8,0},{12,4},{16,24},{20,28},{24,16},{28,20},{1,9},{5... | collective-permute-start | bytes 1572872 | tf_op jit(solution)/shard_map/ppermute | solution.py:405
  97.8 30.3 %collective-permute-start.7 = (bf16[2,512,256]{2,1,0:T(8,128)(2,1)}, bf16[2,512,256]{2,1,0:T(8,128)(2,1)S(1)}, u32[]{:S(2)}, u32[]{:S(2)}) collective-permute-start(bf16[2,512,256]{2,1,0:T(8,128)(2,1)} %get-tuple-element.122), channel_id=1, source_target_pairs={{0,12},{4,8},{8,4},{12,0},{16,28},{20,24},{24,20},{28,16},{1,13},{... | collective-permute-start | bytes 1572872 | tf_op jit(solution)/shard_map/ppermute | solution.py:405
  98.0 35.2 %copy-start.13 = (bf16[4,2,64,1280]{3,2,1,0:T(8,128)(2,1)S(1)}, bf16[4,2,64,1280]{3,2,1,0:T(8,128)(2,1)}, u32[]{:S(2)}) copy-start(bf16[4,2,64,1280]{3,2,1,0:T(8,128)(2,1)} %get-tuple-element.247) | copy-start | bytes 3932164
  108.8 24.5 %copy-start.6 = (bf16[512,2,1280]{2,1,0:T(2,128)(2,1)S(1)}, bf16[512,2,1280]{2,1,0:T(2,128)(2,1)}, u32[]{:S(2)}) copy-start(bf16[512,2,1280]{2,1,0:T(2,128)(2,1)} %param.7) | copy-start | bytes 7864324
  108.8 26.0 %copy-start.28 = (bf16[2,512,256]{2,1,0:T(8,128)(2,1)}, bf16[2,512,256]{2,1,0:T(8,128)(2,1)S(1)}, u32[]{:S(2)}) copy-start(bf16[2,512,256]{2,1,0:T(8,128)(2,1)S(1)} %collective-permute-done.5.refs_1_) | copy-start | bytes 1572868
  116.0 18.8 %copy-start.29 = (bf16[2,512,256]{2,1,0:T(8,128)(2,1)}, bf16[2,512,256]{2,1,0:T(8,128)(2,1)S(1)}, u32[]{:S(2)}) copy-start(bf16[2,512,256]{2,1,0:T(8,128)(2,1)S(1)} %collective-permute-done.6.refs_2_) | copy-start | bytes 1572868
  129.5 8.3 %collective-permute-start.8 = (bf16[2,512,128]{2,1,0:T(8,128)(2,1)S(1)}, bf16[2,512,128]{2,1,0:T(8,128)(2,1)S(1)}, u32[]{:S(2)}, u32[]{:S(2)}) collective-permute-start(bf16[2,512,128]{2,1,0:T(8,128)(2,1)S(1)} %pad_maximum_fusion.4), channel_id=1, source_target_pairs={{0,4},{4,0},{8,12},{12,8},{16,20},{20,16},{24,28},{28,24},{1,5},{5... | collective-permute-start | bytes 786440 | tf_op jit(solution)/shard_map/ppermute | solution.py:405
  130.0 9.3 %collective-permute-start.9 = (bf16[2,512,128]{2,1,0:T(8,128)(2,1)S(1)}, bf16[2,512,128]{2,1,0:T(8,128)(2,1)S(1)}, u32[]{:S(2)}, u32[]{:S(2)}) collective-permute-start(bf16[2,512,128]{2,1,0:T(8,128)(2,1)S(1)} %pad_maximum_fusion.5), channel_id=1, source_target_pairs={{0,8},{4,12},{8,0},{12,4},{16,24},{20,28},{24,16},{28,20},{1,9},{5... | collective-permute-start | bytes 786440 | tf_op jit(solution)/shard_map/ppermute | solution.py:405
  130.2 14.5 %collective-permute-start.10 = (bf16[2,512,128]{2,1,0:T(8,128)(2,1)S(1)}, bf16[2,512,128]{2,1,0:T(8,128)(2,1)S(1)}, u32[]{:S(2)}, u32[]{:S(2)}) collective-permute-start(bf16[2,512,128]{2,1,0:T(8,128)(2,1)S(1)} %pad_maximum_fusion.6), channel_id=1, source_target_pairs={{0,12},{4,8},{8,4},{12,0},{16,28},{20,24},{24,20},{28,16},{1,13},{... | collective-permute-start | bytes 786440 | tf_op jit(solution)/shard_map/ppermute | solution.py:405
  134.8 10.8 %copy-start.33 = (bf16[2,512,128]{2,1,0:T(8,128)(2,1)S(1)}, bf16[2,512,128]{2,1,0:T(8,128)(2,1)}, u32[]{:S(2)}) copy-start(bf16[2,512,128]{2,1,0:T(8,128)(2,1)} %get-tuple-element.137) | copy-start | bytes 786436
  134.8 11.3 %copy-start.32 = (bf16[2,512,128]{2,1,0:T(8,128)(2,1)S(1)}, bf16[2,512,128]{2,1,0:T(8,128)(2,1)}, u32[]{:S(2)}) copy-start(bf16[2,512,128]{2,1,0:T(8,128)(2,1)} %get-tuple-element.138) | copy-start | bytes 786436
  134.8 11.6 %copy-start.31 = (bf16[2,512,128]{2,1,0:T(8,128)(2,1)S(1)}, bf16[2,512,128]{2,1,0:T(8,128)(2,1)}, u32[]{:S(2)}) copy-start(bf16[2,512,128]{2,1,0:T(8,128)(2,1)} %get-tuple-element.139) | copy-start | bytes 786436
  137.8 12.2 %copy-start.34 = (bf16[2,512,128]{2,1,0:T(8,128)(2,1)}, bf16[2,512,128]{2,1,0:T(8,128)(2,1)S(1)}, u32[]{:S(2)}) copy-start(bf16[2,512,128]{2,1,0:T(8,128)(2,1)S(1)} %collective-permute-done.8.refs_5_.refs_9_) | copy-start | bytes 786436
  145.6 71.4 %collective-permute-start.18 = (bf16[2,512,128]{2,1,0:T(8,128)(2,1)S(1)}, bf16[2,512,128]{2,1,0:T(8,128)(2,1)S(1)}, u32[]{:S(2)}, u32[]{:S(2)}) collective-permute-start(bf16[2,512,128]{2,1,0:T(8,128)(2,1)S(1)} %copy-done.33), channel_id=1, source_target_pairs={{0,4},{4,0},{8,12},{12,8},{16,20},{20,16},{24,28},{28,24},{1,5},{5... | collective-permute-start | bytes 786440 | tf_op jit(solution)/shard_map/ppermute | solution.py:405
  146.1 72.7 %collective-permute-start.19 = (bf16[2,512,128]{2,1,0:T(8,128)(2,1)S(1)}, bf16[2,512,128]{2,1,0:T(8,128)(2,1)S(1)}, u32[]{:S(2)}, u32[]{:S(2)}) collective-permute-start(bf16[2,512,128]{2,1,0:T(8,128)(2,1)S(1)} %copy-done.32), channel_id=1, source_target_pairs={{0,8},{4,12},{8,0},{12,4},{16,24},{20,28},{24,16},{28,20},{1,9},{5... | collective-permute-start | bytes 786440 | tf_op jit(solution)/shard_map/ppermute | solution.py:405
  146.4 74.0 %collective-permute-start.20 = (bf16[2,512,128]{2,1,0:T(8,128)(2,1)S(1)}, bf16[2,512,128]{2,1,0:T(8,128)(2,1)}, u32[]{:S(2)}, u32[]{:S(2)}) collective-permute-start(bf16[2,512,128]{2,1,0:T(8,128)(2,1)S(1)} %copy-done.31), channel_id=1, source_target_pairs={{0,12},{4,8},{8,4},{12,0},{16,28},{20,24},{24,20},{28,16},{1,13},{... | collective-permute-start | bytes 786440 | tf_op jit(solution)/shard_map/ppermute | solution.py:405
  149.1 74.9 %collective-permute-start.14 = (bf16[512,512]{1,0:T(8,128)(2,1)}, bf16[512,512]{1,0:T(8,128)(2,1)S(1)}, u32[]{:S(2)}, u32[]{:S(2)}) collective-permute-start(bf16[512,512]{1,0:T(8,128)(2,1)} %get-tuple-element.254), channel_id=1, source_target_pairs={{0,16},{4,20},{8,24},{12,28},{16,0},{20,4},{24,8},{28,12},{1,17},{... | collective-permute-start | bytes 1572872 | tf_op jit(solution)/shard_map/ppermute | solution.py:405
  149.4 78.5 %collective-permute-start.11 = (bf16[2,512,384]{2,1,0:T(8,128)(2,1)}, bf16[2,512,384]{2,1,0:T(8,128)(2,1)}, u32[]{:S(2)}, u32[]{:S(2)}) collective-permute-start(bf16[2,512,384]{2,1,0:T(8,128)(2,1)} %get-tuple-element.126), channel_id=1, source_target_pairs={{0,4},{4,0},{8,12},{12,8},{16,20},{20,16},{24,28},{28,24},{1,5},{5... | collective-permute-start | bytes 2359304 | tf_op jit(solution)/shard_map/ppermute | solution.py:405
  217.0 79.0 %collective-permute-start.12 = (bf16[2,512,384]{2,1,0:T(8,128)(2,1)}, bf16[2,512,384]{2,1,0:T(8,128)(2,1)}, u32[]{:S(2)}, u32[]{:S(2)}) collective-permute-start(bf16[2,512,384]{2,1,0:T(8,128)(2,1)} %get-tuple-element.127), channel_id=1, source_target_pairs={{0,8},{4,12},{8,0},{12,4},{16,24},{20,28},{24,16},{28,20},{1,9},{5... | collective-permute-start | bytes 2359304 | tf_op jit(solution)/shard_map/ppermute | solution.py:405
  218.8 77.2 %collective-permute-start.13 = (bf16[2,512,384]{2,1,0:T(8,128)(2,1)}, bf16[2,512,384]{2,1,0:T(8,128)(2,1)}, u32[]{:S(2)}, u32[]{:S(2)}) collective-permute-start(bf16[2,512,384]{2,1,0:T(8,128)(2,1)} %get-tuple-element.128), channel_id=1, source_target_pairs={{0,12},{4,8},{8,4},{12,0},{16,28},{20,24},{24,20},{28,16},{1,13},{... | collective-permute-start | bytes 2359304 | tf_op jit(solution)/shard_map/ppermute | solution.py:405
  220.4 77.0 %all-to-all-start.1 = ((bf16[8,512,256]{2,1,0:T(8,128)(2,1)}), bf16[8,512,256]{2,1,0:T(8,128)(2,1)S(1)}, u32[]{:S(2)}, u32[]{:S(2)}) async-start(bf16[8,512,256]{2,1,0:T(8,128)(2,1)} %attend_pair.4), calls=%async_computation.1 | async-start | bytes 4194304 | tf_op jit(solution)/shard_map/all_to_all | solution.py:580
  224.3 71.7 %collective-permute-start.15 = (bf16[2,512,128]{2,1,0:T(8,128)(2,1)S(1)}, bf16[2,512,128]{2,1,0:T(8,128)(2,1)S(1)}, u32[]{:S(2)}, u32[]{:S(2)}) collective-permute-start(bf16[2,512,128]{2,1,0:T(8,128)(2,1)S(1)} %pad_maximum_fusion.8), channel_id=1, source_target_pairs={{0,4},{4,0},{8,12},{12,8},{16,20},{20,16},{24,28},{28,24},{1,5},{5... | collective-permute-start | bytes 786440 | tf_op jit(solution)/shard_map/ppermute | solution.py:405
  226.4 69.6 %collective-permute-start.16 = (bf16[2,512,128]{2,1,0:T(8,128)(2,1)S(1)}, bf16[2,512,128]{2,1,0:T(8,128)(2,1)S(1)}, u32[]{:S(2)}, u32[]{:S(2)}) collective-permute-start(bf16[2,512,128]{2,1,0:T(8,128)(2,1)S(1)} %pad_maximum_fusion.9), channel_id=1, source_target_pairs={{0,8},{4,12},{8,0},{12,4},{16,24},{20,28},{24,16},{28,20},{1,9},{5... | collective-permute-start | bytes 786440 | tf_op jit(solution)/shard_map/ppermute | solution.py:405
  228.0 69.4 %collective-permute-start.17 = (bf16[2,512,128]{2,1,0:T(8,128)(2,1)S(1)}, bf16[2,512,128]{2,1,0:T(8,128)(2,1)}, u32[]{:S(2)}, u32[]{:S(2)}) collective-permute-start(bf16[2,512,128]{2,1,0:T(8,128)(2,1)S(1)} %pad_maximum_fusion.10), channel_id=1, source_target_pairs={{0,12},{4,8},{8,4},{12,0},{16,28},{20,24},{24,20},{28,16},{1,13},{... | collective-permute-start | bytes 786440 | tf_op jit(solution)/shard_map/ppermute | solution.py:405
  297.4 86.7 %all-to-all-start = ((bf16[8,512,256]{2,1,0:T(8,128)(2,1)}), bf16[8,512,256]{2,1,0:T(8,128)(2,1)}, u32[]{:S(2)}, u32[]{:S(2)}) async-start(bf16[8,512,256]{2,1,0:T(8,128)(2,1)} %attend_pair.5), calls=%async_computation | async-start | bytes 4194304 | tf_op jit(solution)/shard_map/all_to_all | solution.py:580
  314.7 142.5 %collective-permute-start.21 = (bf16[8,40,1024]{2,1,0:T(8,128)(2,1)}, bf16[8,40,1024]{2,1,0:T(8,128)(2,1)}, u32[]{:S(2)}, u32[]{:S(2)}) collective-permute-start(bf16[8,40,1024]{2,1,0:T(8,128)(2,1)} %slice_bitcast_fusion.5), channel_id=1, source_target_pairs={{0,2},{1,3},{2,0},{3,1},{4,6},{5,7},{6,4},{7,5},{8,10},{9,11},{10,... | collective-permute-start | bytes 1966088 | tf_op jit(solution)/shard_map/ppermute | solution.py:405
  316.3 140.9 %collective-permute-start.23 = (bf16[8,40,1024]{2,1,0:T(8,128)(2,1)S(1)}, bf16[8,40,1024]{2,1,0:T(8,128)(2,1)}, u32[]{:S(2)}, u32[]{:S(2)}) collective-permute-start(bf16[8,40,1024]{2,1,0:T(8,128)(2,1)S(1)} %get-tuple-element.252), channel_id=1, source_target_pairs={{0,3},{1,2},{2,1},{3,0},{4,7},{5,6},{6,5},{7,4},{8,11},{9,10},{10,... | collective-permute-start | bytes 1966088 | tf_op jit(solution)/shard_map/ppermute | solution.py:405
  316.3 140.9 %collective-permute-start.22 = (bf16[8,40,1024]{2,1,0:T(8,128)(2,1)S(1)}, bf16[8,40,1024]{2,1,0:T(8,128)(2,1)}, u32[]{:S(2)}, u32[]{:S(2)}) collective-permute-start(bf16[8,40,1024]{2,1,0:T(8,128)(2,1)S(1)} %get-tuple-element.253), channel_id=1, source_target_pairs={{0,1},{1,0},{2,3},{3,2},{4,5},{5,4},{6,7},{7,6},{8,9},{9,8},{10,11... | collective-permute-start | bytes 1966088 | tf_op jit(solution)/shard_map/ppermute | solution.py:405
  384.1 73.1 %all-to-all-start.2 = ((bf16[8,512,256]{2,1,0:T(8,128)(2,1)}), bf16[8,512,256]{2,1,0:T(8,128)(2,1)S(1)}, u32[]{:S(2)}, u32[]{:S(2)}) async-start(bf16[8,512,256]{2,1,0:T(8,128)(2,1)} %attend_pair.6), calls=%async_computation.2 | async-start | bytes 4194304 | tf_op jit(solution)/shard_map/all_to_all | solution.py:580
  457.2 54.8 %all-to-all-start.3 = ((bf16[8,512,256]{2,1,0:T(8,128)(2,1)}), bf16[8,512,256]{2,1,0:T(8,128)(2,1)}, u32[]{:S(2)}, u32[]{:S(2)}) async-start(bf16[8,512,256]{2,1,0:T(8,128)(2,1)} %attend_pair.7), calls=%async_computation.3 | async-start | bytes 4194304 | tf_op jit(solution)/shard_map/all_to_all | solution.py:597
  471.2 8.0 %collective-permute-start.26 = (bf16[2,8,40,1024]{3,2,1,0:T(8,128)(2,1)}, bf16[2,8,40,1024]{3,2,1,0:T(8,128)(2,1)S(1)}, u32[]{:S(2)}, u32[]{:S(2)}) collective-permute-start(bf16[2,8,40,1024]{3,2,1,0:T(8,128)(2,1)} %get-tuple-element.207), channel_id=1, source_target_pairs={{0,1},{1,0},{2,3},{3,2},{4,5},{5,4},{6,7},{7,6},{8,9},{9,8},{10,11... | collective-permute-start | bytes 3932168 | tf_op jit(solution)/shard_map/ppermute | solution.py:405
  478.8 3.3 collective-permute-start.24
  479.9 19.4 %collective-permute-start.27 = (bf16[8,40,1024]{2,1,0:T(8,128)(2,1)S(1)}, bf16[8,40,1024]{2,1,0:T(8,128)(2,1)S(1)}, u32[]{:S(2)}, u32[]{:S(2)}) collective-permute-start(bf16[8,40,1024]{2,1,0:T(8,128)(2,1)S(1)} %fusion.31), channel_id=1, source_target_pairs={{0,2},{2,0},{1,3},{3,1},{4,6},{6,4},{5,7},{7,5},{8,10},{10,8},{9,1... | collective-permute-start | bytes 1966088 | tf_op jit(solution)/shard_map/ppermute | solution.py:405
  482.7 28.0 %collective-permute-start.25 = (bf16[8,40,1024]{2,1,0:T(8,128)(2,1)S(1)}, bf16[8,40,1024]{2,1,0:T(8,128)(2,1)S(1)}, u32[]{:S(2)}, u32[]{:S(2)}) collective-permute-start(bf16[8,40,1024]{2,1,0:T(8,128)(2,1)S(1)} %fusion.30), channel_id=1, source_target_pairs={{0,2},{2,0},{1,3},{3,1},{4,6},{6,4},{5,7},{7,5},{8,10},{10,8},{9,1... | collective-permute-start | bytes 1966088 | tf_op jit(solution)/shard_map/ppermute | solution.py:405
  519.6 3.2 collective-permute-start.28
  526.0 28.4 %collective-permute-start.29 = (bf16[8,40,1024]{2,1,0:T(8,128)(2,1)S(1)}, bf16[8,40,1024]{2,1,0:T(8,128)(2,1)}, u32[]{:S(2)}, u32[]{:S(2)}) collective-permute-start(bf16[8,40,1024]{2,1,0:T(8,128)(2,1)S(1)} %fusion.32), channel_id=1, source_target_pairs={{0,2},{2,0},{1,3},{3,1},{4,6},{6,4},{5,7},{7,5},{8,10},{10,8},{9,1... | collective-permute-start | bytes 1966088 | tf_op jit(solution)/shard_map/ppermute | solution.py:405
  531.0 28.9 %collective-permute-start.36 = (bf16[2,40,3072]{2,1,0:T(8,128)(2,1)}, bf16[2,40,3072]{2,1,0:T(8,128)(2,1)}, u32[]{:S(2)}, u32[]{:S(2)}) collective-permute-start(bf16[2,40,3072]{2,1,0:T(8,128)(2,1)} %get-tuple-element.242), channel_id=1, source_target_pairs={{0,4},{4,0},{8,12},{12,8},{16,20},{20,16},{24,28},{28,24},{1,5},{5... | collective-permute-start | bytes 1474568 | tf_op jit(solution)/shard_map/ppermute | solution.py:405
  533.0 26.9 %collective-permute-start.37 = (bf16[2,40,3072]{2,1,0:T(8,128)(2,1)}, bf16[2,40,3072]{2,1,0:T(8,128)(2,1)}, u32[]{:S(2)}, u32[]{:S(2)}) collective-permute-start(bf16[2,40,3072]{2,1,0:T(8,128)(2,1)} %get-tuple-element.243), channel_id=1, source_target_pairs={{0,8},{4,12},{8,0},{12,4},{16,24},{20,28},{24,16},{28,20},{1,9},{5... | collective-permute-start | bytes 1474568 | tf_op jit(solution)/shard_map/ppermute | solution.py:405
  534.5 25.4 %collective-permute-start.38 = (bf16[2,40,3072]{2,1,0:T(8,128)(2,1)}, bf16[2,40,3072]{2,1,0:T(8,128)(2,1)}, u32[]{:S(2)}, u32[]{:S(2)}) collective-permute-start(bf16[2,40,3072]{2,1,0:T(8,128)(2,1)} %get-tuple-element.244), channel_id=1, source_target_pairs={{0,12},{4,8},{8,4},{12,0},{16,28},{20,24},{24,20},{28,16},{1,13},{... | collective-permute-start | bytes 1474568 | tf_op jit(solution)/shard_map/ppermute | solution.py:405
  556.7 16.5 %copy-start.1 = (bf16[512,2,1280]{2,1,0:T(2,128)(2,1)S(1)}, bf16[512,2,1280]{2,1,0:T(2,128)(2,1)}, u32[]{:S(2)}) copy-start(bf16[512,2,1280]{2,1,0:T(2,128)(2,1)} %param.6) | copy-start | bytes 7864324
  556.7 16.5 %copy-start.22 = (f32[2,1280]{1,0:T(2,128)S(1)}, f32[2,1280]{1,0:T(2,128)}, u32[]{:S(2)}) copy-start(f32[2,1280]{1,0:T(2,128)} %copy-done.21) | copy-start | bytes 30724
  556.7 16.5 %copy-start.24 = (f32[2,1280]{1,0:T(2,128)S(1)}, f32[2,1280]{1,0:T(2,128)}, u32[]{:S(2)}) copy-start(f32[2,1280]{1,0:T(2,128)} %copy-done.23) | copy-start | bytes 30724
  556.9 4.9 collective-permute-start.33
  561.8 4.2 collective-permute-start.34
  563.5 18.0 %collective-permute-start.39 = (bf16[40,3072]{1,0:T(8,128)(2,1)S(1)}, bf16[40,3072]{1,0:T(8,128)(2,1)S(1)}, u32[]{:S(2)}, u32[]{:S(2)}) collective-permute-start(bf16[40,3072]{1,0:T(8,128)(2,1)S(1)} %fusion.38), channel_id=1, source_target_pairs={{0,16},{4,20},{8,24},{12,28},{16,0},{20,4},{24,8},{28,12},{1,17},{... | collective-permute-start | bytes 737288 | tf_op jit(solution)/shard_map/ppermute | solution.py:405
  566.0 6.9 %collective-permute-start.35 = (f32[2,2,32]{2,1,0:T(2,128)S(1)}, f32[2,2,32]{2,1,0:T(2,128)S(1)}, u32[]{:S(2)}, u32[]{:S(2)}) collective-permute-start(f32[2,2,32]{2,1,0:T(2,128)S(1)} %add.215), channel_id=1, source_target_pairs={{0,8},{4,12},{8,0},{12,4},{16,24},{20,28},{24,16},{28,20},{1,9},{5... | collective-permute-start | bytes 1544 | tf_op jit(solution)/shard_map/ppermute | solution.py:405
  569.4 12.3 %collective-permute-start.30 = (bf16[2,40,1024]{2,1,0:T(8,128)(2,1)}, bf16[2,40,1024]{2,1,0:T(8,128)(2,1)}, u32[]{:S(2)}, u32[]{:S(2)}) collective-permute-start(bf16[2,40,1024]{2,1,0:T(8,128)(2,1)} %get-tuple-element.249), channel_id=1, source_target_pairs={{0,4},{4,0},{8,12},{12,8},{16,20},{20,16},{24,28},{28,24},{1,5},{5... | collective-permute-start | bytes 491528 | tf_op jit(solution)/shard_map/ppermute | solution.py:405
  570.5 11.2 %collective-permute-start.31 = (bf16[2,40,1024]{2,1,0:T(8,128)(2,1)S(1)}, bf16[2,40,1024]{2,1,0:T(8,128)(2,1)}, u32[]{:S(2)}, u32[]{:S(2)}) collective-permute-start(bf16[2,40,1024]{2,1,0:T(8,128)(2,1)S(1)} %get-tuple-element.250), channel_id=1, source_target_pairs={{0,8},{4,12},{8,0},{12,4},{16,24},{20,28},{24,16},{28,20},{1,9},{5... | collective-permute-start | bytes 491528 | tf_op jit(solution)/shard_map/ppermute | solution.py:405
  571.0 10.6 %collective-permute-start.32 = (bf16[2,40,1024]{2,1,0:T(8,128)(2,1)S(1)}, bf16[2,40,1024]{2,1,0:T(8,128)(2,1)}, u32[]{:S(2)}, u32[]{:S(2)}) collective-permute-start(bf16[2,40,1024]{2,1,0:T(8,128)(2,1)S(1)} %get-tuple-element.251), channel_id=1, source_target_pairs={{0,12},{4,8},{8,4},{12,0},{16,28},{20,24},{24,20},{28,16},{1,13},{... | collective-permute-start | bytes 491528 | tf_op jit(solution)/shard_map/ppermute | solution.py:405
  583.1 6.3 %collective-permute-start.40 = (bf16[40,1024]{1,0:T(8,128)(2,1)S(1)}, bf16[40,1024]{1,0:T(8,128)(2,1)S(1)}, u32[]{:S(2)}, u32[]{:S(2)}) collective-permute-start(bf16[40,1024]{1,0:T(8,128)(2,1)S(1)} %fusion.43), channel_id=1, source_target_pairs={{0,16},{4,20},{8,24},{12,28},{16,0},{20,4},{24,8},{28,12},{1,17},{... | collective-permute-start | bytes 245768 | tf_op jit(solution)/shard_map/ppermute | solution.py:405
  591.8 11.2 %all-to-all-start.4 = ((f32[32,1,1280]{2,1,0:T(1,128)}), f32[32,1,1280]{2,1,0:T(1,128)S(1)}, u32[]{:S(2)}, u32[]{:S(2)}) async-start(f32[32,1,1280]{2,1,0:T(1,128)} %reshape.131), calls=%async_computation.4 | async-start | bytes 327680 | tf_op jit(solution)/shard_map/all_to_all | solution.py:647
  (25 other events, 100.1 us)
Sparse Core Ops, SparseCore 0:
  9.6 14.0 all-gather.2
  25.2 20.2 all-gather.4
